TPU v7x, 32 devices: a whole 2x2x4 slice. The times are simulated.
32 devices in a mesh: elev: 8 (over z, core), valley: 2 (over y), down: 2 (over x).
Axes of the slice: x: 2, y: 2, z: 4, core: 2. Of those that a mesh axis runs over, the one named last changes fastest.
Arguments:
- resid: bfloat16 [8, 8, 4, 128, 256], P('elev', 'valley', 'down'), may hold values from -6 to 6
- direction: bfloat16 [8, 8, 4, 128, 256], P('elev', 'valley', 'down'), may hold values from -6 to 6
- diag_blocks: bfloat16 [8, 8, 4, 256, 256], P('elev', 'valley', 'down'), may hold values from -0.375 to 0.375
- lower_blocks: bfloat16 [8, 8, 4, 256, 256], P('elev', 'valley', 'down')
- upper_blocks: bfloat16 [8, 8, 4, 256, 256], P('elev', 'valley', 'down')
- inv_pivots: bfloat16 [8, 8, 4, 256, 256], P('elev', 'valley', 'down')
- down_coupling: bfloat16 [8, 8, 4, 256, 256], P('elev', 'valley', 'down'), may hold values from -0.375 to 0.375
- valley_coupling: bfloat16 [8, 8, 4, 256, 256], P('elev', 'valley', 'down'), may hold values from -0.375 to 0.375
- coupled_column: int32 [8, 8, 4], P('elev', 'valley', 'down'), may hold values from 0 to 7
Outputs:
- preconditioned: bfloat16 [8, 8, 4, 128, 256], P('elev', 'valley', 'down')
- image: float32 [8, 8, 4, 128, 256], P('elev', 'valley', 'down')
All inputs are finite; a program needn't handle non-finite values.
Results may differ from a plain program's by a relative error of at most 0.015.
Values may be sent and summed in bfloat16 or wider, within the bound.
No kernel may reach another device: no remote copies, remote signals or barrier semaphores. Data moves between devices by JAX's collectives and lax.ppermute only.
A program may use at most 64 MiB of HBM per device.

v0:
```python
import jax
import jax.numpy as jnp
from jax import lax
from jax.sharding import PartitionSpec as P


def from_behind(value, axis, by):
    length = lax.axis_size(axis)
    pairs = [(i, i + by) for i in range(length) if 0 <= i + by < length]
    return lax.ppermute(value, axis, pairs)


def with_halo(block, sides, width):
    for axis, dim in sides:
        count = lax.axis_size(axis)
        forward = [(i, i + 1) for i in range(count - 1)]
        backward = [(target, source) for source, target in forward]
        low = lax.ppermute(
            lax.slice_in_dim(block, block.shape[dim] - width, None, axis=dim), axis, forward
        )
        high = lax.ppermute(lax.slice_in_dim(block, 0, width, axis=dim), axis, backward)
        block = jnp.concatenate([low, block, high], axis=dim)
    return block


def apply_blocks(vectors, blocks):
    return jnp.einsum("bqrs,bqst->bqrt", vectors, blocks, preferred_element_type=jnp.float32)


def local(
    resid,
    direction,
    diag_blocks,
    lower_blocks,
    upper_blocks,
    inv_pivots,
    down_coupling,
    valley_coupling,
    coupled_column,
):
    rhs_local = resid[0]
    lower_local = lower_blocks[0]
    upper_local = upper_blocks[0]
    pivot_local = inv_pivots[0]
    valley_count = rhs_local.shape[0]
    chain_length = lax.axis_size("elev")
    height = lax.axis_index("elev")
    group_count = 1
    span_blocks = valley_count // group_count
    group_shape = (span_blocks,) + rhs_local.shape[1:]

    def forward_step(step, carry):
        incoming, store = carry
        group = step - height
        active = jnp.logical_and(group >= 0, group < group_count)
        chosen = jnp.clip(group, 0, group_count - 1)

        def forward_advance(operands):
            arriving, kept, which = operands
            inner = (rhs_local.astype(jnp.float32) - apply_blocks(arriving, lower_local)).astype(
                jnp.bfloat16
            )
            result = apply_blocks(inner, pivot_local).astype(jnp.bfloat16)
            return (result, result)

        def forward_remain(operands):
            arriving, kept, which = operands
            return (jnp.zeros_like(arriving), kept)

        result, store = lax.cond(active, forward_advance, forward_remain, (incoming, store, chosen))
        incoming = from_behind(result, "elev", 1)
        return (incoming, store)

    start_front = jnp.zeros(group_shape, jnp.bfloat16)
    _, fronts = lax.fori_loop(
        0, chain_length + group_count - 1, forward_step, (start_front, jnp.zeros_like(rhs_local))
    )
    depth = chain_length - 1 - height

    def backward_step(step, carry):
        incoming, store = carry
        group = step - depth
        active = jnp.logical_and(group >= 0, group < group_count)
        chosen = jnp.clip(group, 0, group_count - 1)

        def backward_advance(operands):
            arriving, kept, which = operands
            carried = apply_blocks(arriving, upper_local).astype(jnp.bfloat16)
            result = (fronts.astype(jnp.float32) - apply_blocks(carried, pivot_local)).astype(
                jnp.bfloat16
            )
            return (result, result)

        def backward_remain(operands):
            arriving, kept, which = operands
            return (jnp.zeros_like(arriving), kept)

        result, store = lax.cond(
            active, backward_advance, backward_remain, (incoming, store, chosen)
        )
        incoming = from_behind(result, "elev", -1)
        return (incoming, store)

    _, solved = lax.fori_loop(
        0, chain_length + group_count - 1, backward_step, (start_front, jnp.zeros_like(rhs_local))
    )
    current = direction[0]
    padded = with_halo(direction, (("elev", 0),), 1)
    below_dir = padded[0]
    above_dir = padded[2]
    rim_blocks = from_behind(current[:, -1:], "down", 1)
    upstream = jnp.concatenate([rim_blocks, current[:, :-1]], axis=1)
    partner_index = coupled_column[0]
    piece = lax.all_gather(current, "valley", axis=0, tiled=True)
    count = piece.shape[0]
    columns = jnp.arange(count, dtype=jnp.int32)
    picker = (partner_index[:, :, None] == columns[None, None, :]).astype(jnp.bfloat16)
    partner_sum = jnp.einsum("pqc,cqrs->pqrs", picker, piece, preferred_element_type=jnp.float32)
    partner = partner_sum.astype(jnp.bfloat16)
    total = apply_blocks(current, diag_blocks[0])
    total = total + apply_blocks(below_dir, lower_local)
    total = total + apply_blocks(above_dir, upper_local)
    total = total + apply_blocks(upstream, down_coupling[0])
    total = total + apply_blocks(partner, valley_coupling[0])
    return (solved[None], total[None])


def solution(mesh):
    in_specs = (
        P("elev", "valley", "down", None, None),
        P("elev", "valley", "down", None, None),
        P("elev", "valley", "down", None, None),
        P("elev", "valley", "down", None, None),
        P("elev", "valley", "down", None, None),
        P("elev", "valley", "down", None, None),
        P("elev", "valley", "down", None, None),
        P("elev", "valley", "down", None, None),
        P("elev", "valley", "down"),
    )
    out_specs = (P("elev", "valley", "down", None, None), P("elev", "valley", "down", None, None))
    return jax.shard_map(local, mesh=mesh, in_specs=in_specs, out_specs=out_specs, check_vma=False)
```

profile of v0, /device:TPU:1, one launch (start us, length us, event | category | flops | bytes accessed | tf_op | source)
XLA Modules:
  0.0 252.2 jit_solution(7144582399272150525)
XLA Ops:
  7.2 4.7 %collective-permute-start.2 = (bf16[1,4,2,128,256]{4,3,2,1,0:T(8,128)(2,1)}, bf16[1,4,2,128,256]{4,3,2,1,0:T(8,128)(2,1)}, u32[]{:S(2)}, u32[]{:S(2)}) collective-permute-start(bf16[1,4,2,128,256]{4,3,2,1,0:T(8,128)(2,1)} %param.18), channel_id=1, source_target_pairs={{0,4},{4,8},{8,12},{12,16},{16,20},{20,24},{24,28},{1,5},{5,9},{9,... | collective-permute-start | bytes 1572872 | tf_op jit(solution)/shard_map/ppermute | solution.py:18
  27.7 12.6 %all-gather.3.cloned.1.call-done = bf16[1,8,2,128,256]{4,3,2,0,1:T(8,128)(2,1)} async-done(((bf16[1,4,2,128,256]{4,3,2,0,1:T(8,128)(2,1)}), bf16[1,8,2,128,256]{4,3,2,0,1:T(8,128)(2,1)}) %all-gather.3.cloned.1.call-update) | async-done | bytes 1048592 | tf_op jit(solution)/shard_map/all_gather | solution.py:114
  47.9 96.9 %while.36 = (s32[]{:T(128)}, bf16[4,2,128,256]{3,2,1,0:T(8,128)(2,1)}, bf16[4,2,128,256]{3,2,1,0:T(8,128)(2,1)}, s32[]{:T(128)}, bf16[4,2,128,256]{3,2,1,0:T(8,1...) while((s32[]{:T(128)}, ...), condition=%wide.region_3.0_spmd, body=%wide.region_0.0_spmd.sunk | while | flops 269484032 | bytes 6815963 | solution.py:75
  52.4 6.4 %collective-permute-done = bf16[4,2,128,256]{3,2,1,0:T(8,128)(2,1)} collective-permute-done((bf16[4,2,128,256]{3,2,1,0:T(8,128)(2,1)}, bf16[4,2,128,256]{3,2,1,0:T(8,128)(2,1)}, u32[]{:S(2)}, u32[]{:S(2)}) %collective-permute-start) | collective-permute-done | bytes 524320 | tf_op jit(solution)/shard_map/while/body/eval_jaxpr/ppermute | solution.py:10
  65.1 6.4 %collective-permute-done = bf16[4,2,128,256]{3,2,1,0:T(8,128)(2,1)} collective-permute-done((bf16[4,2,128,256]{3,2,1,0:T(8,128)(2,1)}, bf16[4,2,128,256]{3,2,1,0:T(8,128)(2,1)}, u32[]{:S(2)}, u32[]{:S(2)}) %collective-permute-start) | collective-permute-done | bytes 524320 | tf_op jit(solution)/shard_map/while/body/eval_jaxpr/ppermute | solution.py:10
  72.3 7.9 %collective-permute-start = (bf16[4,2,128,256]{3,2,1,0:T(8,128)(2,1)}, bf16[4,2,128,256]{3,2,1,0:T(8,128)(2,1)}, u32[]{:S(2)}, u32[]{:S(2)}) collective-permute-start(bf16[4,2,128,256]{3,2,1,0:T(8,128)(2,1)} %get-tuple-element.399), channel_id=1, source_target_pairs={{0,4},{4,8},{8,12},{12,16},{16,20},{20,24},{24,28},{1,5},{5,9},{9,... | collective-permute-start | bytes 1572872 | tf_op jit(solution)/shard_map/while/body/eval_jaxpr/ppermute | solution.py:10
  80.2 6.4 %collective-permute-done = bf16[4,2,128,256]{3,2,1,0:T(8,128)(2,1)} collective-permute-done((bf16[4,2,128,256]{3,2,1,0:T(8,128)(2,1)}, bf16[4,2,128,256]{3,2,1,0:T(8,128)(2,1)}, u32[]{:S(2)}, u32[]{:S(2)}) %collective-permute-start) | collective-permute-done | bytes 524320 | tf_op jit(solution)/shard_map/while/body/eval_jaxpr/ppermute | solution.py:10
  87.5 4.4 %collective-permute-start = (bf16[4,2,128,256]{3,2,1,0:T(8,128)(2,1)}, bf16[4,2,128,256]{3,2,1,0:T(8,128)(2,1)}, u32[]{:S(2)}, u32[]{:S(2)}) collective-permute-start(bf16[4,2,128,256]{3,2,1,0:T(8,128)(2,1)} %get-tuple-element.399), channel_id=1, source_target_pairs={{0,4},{4,8},{8,12},{12,16},{16,20},{20,24},{24,28},{1,5},{5,9},{9,... | collective-permute-start | bytes 1572872 | tf_op jit(solution)/shard_map/while/body/eval_jaxpr/ppermute | solution.py:10
  91.9 6.4 %collective-permute-done = bf16[4,2,128,256]{3,2,1,0:T(8,128)(2,1)} collective-permute-done((bf16[4,2,128,256]{3,2,1,0:T(8,128)(2,1)}, bf16[4,2,128,256]{3,2,1,0:T(8,128)(2,1)}, u32[]{:S(2)}, u32[]{:S(2)}) %collective-permute-start) | collective-permute-done | bytes 524320 | tf_op jit(solution)/shard_map/while/body/eval_jaxpr/ppermute | solution.py:10
  99.1 4.4 %collective-permute-start = (bf16[4,2,128,256]{3,2,1,0:T(8,128)(2,1)}, bf16[4,2,128,256]{3,2,1,0:T(8,128)(2,1)}, u32[]{:S(2)}, u32[]{:S(2)}) collective-permute-start(bf16[4,2,128,256]{3,2,1,0:T(8,128)(2,1)} %get-tuple-element.399), channel_id=1, source_target_pairs={{0,4},{4,8},{8,12},{12,16},{16,20},{20,24},{24,28},{1,5},{5,9},{9,... | collective-permute-start | bytes 1572872 | tf_op jit(solution)/shard_map/while/body/eval_jaxpr/ppermute | solution.py:10
  103.5 6.4 %collective-permute-done = bf16[4,2,128,256]{3,2,1,0:T(8,128)(2,1)} collective-permute-done((bf16[4,2,128,256]{3,2,1,0:T(8,128)(2,1)}, bf16[4,2,128,256]{3,2,1,0:T(8,128)(2,1)}, u32[]{:S(2)}, u32[]{:S(2)}) %collective-permute-start) | collective-permute-done | bytes 524320 | tf_op jit(solution)/shard_map/while/body/eval_jaxpr/ppermute | solution.py:10
  110.7 4.4 %collective-permute-start = (bf16[4,2,128,256]{3,2,1,0:T(8,128)(2,1)}, bf16[4,2,128,256]{3,2,1,0:T(8,128)(2,1)}, u32[]{:S(2)}, u32[]{:S(2)}) collective-permute-start(bf16[4,2,128,256]{3,2,1,0:T(8,128)(2,1)} %get-tuple-element.399), channel_id=1, source_target_pairs={{0,4},{4,8},{8,12},{12,16},{16,20},{20,24},{24,28},{1,5},{5,9},{9,... | collective-permute-start | bytes 1572872 | tf_op jit(solution)/shard_map/while/body/eval_jaxpr/ppermute | solution.py:10
  115.1 6.4 %collective-permute-done = bf16[4,2,128,256]{3,2,1,0:T(8,128)(2,1)} collective-permute-done((bf16[4,2,128,256]{3,2,1,0:T(8,128)(2,1)}, bf16[4,2,128,256]{3,2,1,0:T(8,128)(2,1)}, u32[]{:S(2)}, u32[]{:S(2)}) %collective-permute-start) | collective-permute-done | bytes 524320 | tf_op jit(solution)/shard_map/while/body/eval_jaxpr/ppermute | solution.py:10
  126.8 6.4 %collective-permute-done = bf16[4,2,128,256]{3,2,1,0:T(8,128)(2,1)} collective-permute-done((bf16[4,2,128,256]{3,2,1,0:T(8,128)(2,1)}, bf16[4,2,128,256]{3,2,1,0:T(8,128)(2,1)}, u32[]{:S(2)}, u32[]{:S(2)}) %collective-permute-start) | collective-permute-done | bytes 524320 | tf_op jit(solution)/shard_map/while/body/eval_jaxpr/ppermute | solution.py:10
  138.4 6.4 %collective-permute-done = bf16[4,2,128,256]{3,2,1,0:T(8,128)(2,1)} collective-permute-done((bf16[4,2,128,256]{3,2,1,0:T(8,128)(2,1)}, bf16[4,2,128,256]{3,2,1,0:T(8,128)(2,1)}, u32[]{:S(2)}, u32[]{:S(2)}) %collective-permute-start) | collective-permute-done | bytes 524320 | tf_op jit(solution)/shard_map/while/body/eval_jaxpr/ppermute | solution.py:10
  146.5 98.9 %while.37 = (s32[]{:T(128)}, bf16[4,2,128,256]{3,2,1,0:T(8,128)(2,1)}, bf16[4,2,128,256]{3,2,1,0:T(8,128)(2,1)}, s32[]{:T(128)}, bf16[4,2,128,256]{3,2,1,0:T(8,1...) while((s32[]{:T(128)}, ...), condition=%wide.region_7.0_spmd, body=%wide.region_4.0_spmd.sunk | while | flops 269484032 | bytes 6815963 | solution.py:104
  149.2 9.6 %collective-permute-done.1 = bf16[4,2,128,256]{3,2,1,0:T(8,128)(2,1)} collective-permute-done((bf16[4,2,128,256]{3,2,1,0:T(8,128)(2,1)}, bf16[4,2,128,256]{3,2,1,0:T(8,128)(2,1)}, u32[]{:S(2)}, u32[]{:S(2)}) %collective-permute-start.1) | collective-permute-done | bytes 524320 | tf_op jit(solution)/shard_map/while/body/eval_jaxpr/ppermute | solution.py:10
  161.6 8.9 %collective-permute-done.1 = bf16[4,2,128,256]{3,2,1,0:T(8,128)(2,1)} collective-permute-done((bf16[4,2,128,256]{3,2,1,0:T(8,128)(2,1)}, bf16[4,2,128,256]{3,2,1,0:T(8,128)(2,1)}, u32[]{:S(2)}, u32[]{:S(2)}) %collective-permute-start.1) | collective-permute-done | bytes 524320 | tf_op jit(solution)/shard_map/while/body/eval_jaxpr/ppermute | solution.py:10
  173.3 8.9 %collective-permute-done.1 = bf16[4,2,128,256]{3,2,1,0:T(8,128)(2,1)} collective-permute-done((bf16[4,2,128,256]{3,2,1,0:T(8,128)(2,1)}, bf16[4,2,128,256]{3,2,1,0:T(8,128)(2,1)}, u32[]{:S(2)}, u32[]{:S(2)}) %collective-permute-start.1) | collective-permute-done | bytes 524320 | tf_op jit(solution)/shard_map/while/body/eval_jaxpr/ppermute | solution.py:10
  184.9 8.9 %collective-permute-done.1 = bf16[4,2,128,256]{3,2,1,0:T(8,128)(2,1)} collective-permute-done((bf16[4,2,128,256]{3,2,1,0:T(8,128)(2,1)}, bf16[4,2,128,256]{3,2,1,0:T(8,128)(2,1)}, u32[]{:S(2)}, u32[]{:S(2)}) %collective-permute-start.1) | collective-permute-done | bytes 524320 | tf_op jit(solution)/shard_map/while/body/eval_jaxpr/ppermute | solution.py:10
  196.5 8.9 %collective-permute-done.1 = bf16[4,2,128,256]{3,2,1,0:T(8,128)(2,1)} collective-permute-done((bf16[4,2,128,256]{3,2,1,0:T(8,128)(2,1)}, bf16[4,2,128,256]{3,2,1,0:T(8,128)(2,1)}, u32[]{:S(2)}, u32[]{:S(2)}) %collective-permute-start.1) | collective-permute-done | bytes 524320 | tf_op jit(solution)/shard_map/while/body/eval_jaxpr/ppermute | solution.py:10
  208.2 10.5 %collective-permute-done.1 = bf16[4,2,128,256]{3,2,1,0:T(8,128)(2,1)} collective-permute-done((bf16[4,2,128,256]{3,2,1,0:T(8,128)(2,1)}, bf16[4,2,128,256]{3,2,1,0:T(8,128)(2,1)}, u32[]{:S(2)}, u32[]{:S(2)}) %collective-permute-start.1) | collective-permute-done | bytes 524320 | tf_op jit(solution)/shard_map/while/body/eval_jaxpr/ppermute | solution.py:10
  224.9 8.9 %collective-permute-done.1 = bf16[4,2,128,256]{3,2,1,0:T(8,128)(2,1)} collective-permute-done((bf16[4,2,128,256]{3,2,1,0:T(8,128)(2,1)}, bf16[4,2,128,256]{3,2,1,0:T(8,128)(2,1)}, u32[]{:S(2)}, u32[]{:S(2)}) %collective-permute-start.1) | collective-permute-done | bytes 524320 | tf_op jit(solution)/shard_map/while/body/eval_jaxpr/ppermute | solution.py:10
  236.5 8.9 %collective-permute-done.1 = bf16[4,2,128,256]{3,2,1,0:T(8,128)(2,1)} collective-permute-done((bf16[4,2,128,256]{3,2,1,0:T(8,128)(2,1)}, bf16[4,2,128,256]{3,2,1,0:T(8,128)(2,1)}, u32[]{:S(2)}, u32[]{:S(2)}) %collective-permute-start.1) | collective-permute-done | bytes 524320 | tf_op jit(solution)/shard_map/while/body/eval_jaxpr/ppermute | solution.py:10
  (86 shorter events, 95.1 us)
Async XLA Ops:
  7.2 11.1 %copy-start = (bf16[1,4,2,256,256]{4,3,2,1,0:T(8,128)(2,1)S(1)}, bf16[1,4,2,256,256]{4,3,2,1,0:T(8,128)(2,1)}, u32[]{:S(2)}) copy-start(bf16[1,4,2,256,256]{4,3,2,1,0:T(8,128)(2,1)} %param.19) | copy-start | bytes 3145732
  7.2 33.0 %all-gather.3.cloned.1.call-start = ((), (), s32[]{:S(2)}) async-start(), calls=%async_computation | async-start | bytes 1572864 | tf_op jit(solution)/shard_map/all_gather | solution.py:114
  7.2 19.1 %collective-permute-start.2 = (bf16[1,4,2,128,256]{4,3,2,1,0:T(8,128)(2,1)}, bf16[1,4,2,128,256]{4,3,2,1,0:T(8,128)(2,1)}, u32[]{:S(2)}, u32[]{:S(2)}) collective-permute-start(bf16[1,4,2,128,256]{4,3,2,1,0:T(8,128)(2,1)} %param.18), channel_id=1, source_target_pairs={{0,4},{4,8},{8,12},{12,16},{16,20},{20,24},{24,28},{1,5},{5,9},{9,... | collective-permute-start | bytes 1572872 | tf_op jit(solution)/shard_map/ppermute | solution.py:18
  12.0 30.7 %collective-permute-start.3 = (bf16[1,4,2,128,256]{4,3,2,1,0:T(8,128)(2,1)}, bf16[1,4,2,128,256]{4,3,2,1,0:T(8,128)(2,1)}, u32[]{:S(2)}, u32[]{:S(2)}) collective-permute-start(bf16[1,4,2,128,256]{4,3,2,1,0:T(8,128)(2,1)} %param.18), channel_id=1, source_target_pairs={{4,0},{8,4},{12,8},{16,12},{20,16},{24,20},{28,24},{5,1},{9,5},{13... | collective-permute-start | bytes 1572872 | tf_op jit(solution)/shard_map/ppermute | solution.py:21
  15.0 3.3 %copy-start.5 = (bf16[1,4,2,128,256]{4,3,2,1,0:T(8,128)(2,1)S(1)}, bf16[1,4,2,128,256]{4,3,2,1,0:T(8,128)(2,1)}, u32[]{:S(2)}) copy-start(bf16[1,4,2,128,256]{4,3,2,1,0:T(8,128)(2,1)} %param.18) | copy-start | bytes 1572868
  15.0 8.6 %collective-permute-start.4 = (bf16[4,1,128,256]{3,2,1,0:T(8,128)(2,1)S(1)}, bf16[4,1,128,256]{3,2,1,0:T(8,128)(2,1)S(1)}, u32[]{:S(2)}, u32[]{:S(2)}) collective-permute-start(bf16[4,1,128,256]{3,2,1,0:T(8,128)(2,1)S(1)} %get-tuple-element.314), channel_id=1, source_target_pairs={{0,1},{2,3},{4,5},{6,7},{8,9},{10,11},{12,13},{14,15},{16,17},{18,... | collective-permute-start | bytes 786440 | tf_op jit(solution)/shard_map/ppermute | solution.py:10
  23.6 2.7 %copy-start.2 = (bf16[1,4,2,256,256]{4,3,2,1,0:T(8,128)(2,1)S(1)}, bf16[1,4,2,256,256]{4,3,2,1,0:T(8,128)(2,1)}, u32[]{:S(2)}) copy-start(bf16[1,4,2,256,256]{4,3,2,1,0:T(8,128)(2,1)} %param.20) | copy-start | bytes 3145732
  23.6 2.7 %copy-start.6 = (f32[4,2,128,256]{3,2,1,0:T(8,128)S(1)}, f32[4,2,128,256]{3,2,1,0:T(8,128)}, u32[]{:S(2)}) copy-start(f32[4,2,128,256]{3,2,1,0:T(8,128)} %fusion.10) | copy-start | bytes 3145732
  48.7 10.1 %collective-permute-start = (bf16[4,2,128,256]{3,2,1,0:T(8,128)(2,1)}, bf16[4,2,128,256]{3,2,1,0:T(8,128)(2,1)}, u32[]{:S(2)}, u32[]{:S(2)}) collective-permute-start(bf16[4,2,128,256]{3,2,1,0:T(8,128)(2,1)} %get-tuple-element.399), channel_id=1, source_target_pairs={{0,4},{4,8},{8,12},{12,16},{16,20},{20,24},{24,28},{1,5},{5,9},{9,... | collective-permute-start | bytes 1572872 | tf_op jit(solution)/shard_map/while/body/eval_jaxpr/ppermute | solution.py:10
  63.2 8.3 %collective-permute-start = (bf16[4,2,128,256]{3,2,1,0:T(8,128)(2,1)}, bf16[4,2,128,256]{3,2,1,0:T(8,128)(2,1)}, u32[]{:S(2)}, u32[]{:S(2)}) collective-permute-start(bf16[4,2,128,256]{3,2,1,0:T(8,128)(2,1)} %get-tuple-element.399), channel_id=1, source_target_pairs={{0,4},{4,8},{8,12},{12,16},{16,20},{20,24},{24,28},{1,5},{5,9},{9,... | collective-permute-start | bytes 1572872 | tf_op jit(solution)/shard_map/while/body/eval_jaxpr/ppermute | solution.py:10
  72.3 14.3 %collective-permute-start = (bf16[4,2,128,256]{3,2,1,0:T(8,128)(2,1)}, bf16[4,2,128,256]{3,2,1,0:T(8,128)(2,1)}, u32[]{:S(2)}, u32[]{:S(2)}) collective-permute-start(bf16[4,2,128,256]{3,2,1,0:T(8,128)(2,1)} %get-tuple-element.399), channel_id=1, source_target_pairs={{0,4},{4,8},{8,12},{12,16},{16,20},{20,24},{24,28},{1,5},{5,9},{9,... | collective-permute-start | bytes 1572872 | tf_op jit(solution)/shard_map/while/body/eval_jaxpr/ppermute | solution.py:10
  87.5 10.8 %collective-permute-start = (bf16[4,2,128,256]{3,2,1,0:T(8,128)(2,1)}, bf16[4,2,128,256]{3,2,1,0:T(8,128)(2,1)}, u32[]{:S(2)}, u32[]{:S(2)}) collective-permute-start(bf16[4,2,128,256]{3,2,1,0:T(8,128)(2,1)} %get-tuple-element.399), channel_id=1, source_target_pairs={{0,4},{4,8},{8,12},{12,16},{16,20},{20,24},{24,28},{1,5},{5,9},{9,... | collective-permute-start | bytes 1572872 | tf_op jit(solution)/shard_map/while/body/eval_jaxpr/ppermute | solution.py:10
  99.1 10.8 %collective-permute-start = (bf16[4,2,128,256]{3,2,1,0:T(8,128)(2,1)}, bf16[4,2,128,256]{3,2,1,0:T(8,128)(2,1)}, u32[]{:S(2)}, u32[]{:S(2)}) collective-permute-start(bf16[4,2,128,256]{3,2,1,0:T(8,128)(2,1)} %get-tuple-element.399), channel_id=1, source_target_pairs={{0,4},{4,8},{8,12},{12,16},{16,20},{20,24},{24,28},{1,5},{5,9},{9,... | collective-permute-start | bytes 1572872 | tf_op jit(solution)/shard_map/while/body/eval_jaxpr/ppermute | solution.py:10
  110.7 10.8 %collective-permute-start = (bf16[4,2,128,256]{3,2,1,0:T(8,128)(2,1)}, bf16[4,2,128,256]{3,2,1,0:T(8,128)(2,1)}, u32[]{:S(2)}, u32[]{:S(2)}) collective-permute-start(bf16[4,2,128,256]{3,2,1,0:T(8,128)(2,1)} %get-tuple-element.399), channel_id=1, source_target_pairs={{0,4},{4,8},{8,12},{12,16},{16,20},{20,24},{24,28},{1,5},{5,9},{9,... | collective-permute-start | bytes 1572872 | tf_op jit(solution)/shard_map/while/body/eval_jaxpr/ppermute | solution.py:10
  122.4 10.8 %collective-permute-start = (bf16[4,2,128,256]{3,2,1,0:T(8,128)(2,1)}, bf16[4,2,128,256]{3,2,1,0:T(8,128)(2,1)}, u32[]{:S(2)}, u32[]{:S(2)}) collective-permute-start(bf16[4,2,128,256]{3,2,1,0:T(8,128)(2,1)} %get-tuple-element.399), channel_id=1, source_target_pairs={{0,4},{4,8},{8,12},{12,16},{16,20},{20,24},{24,28},{1,5},{5,9},{9,... | collective-permute-start | bytes 1572872 | tf_op jit(solution)/shard_map/while/body/eval_jaxpr/ppermute | solution.py:10
  134.0 10.8 %collective-permute-start = (bf16[4,2,128,256]{3,2,1,0:T(8,128)(2,1)}, bf16[4,2,128,256]{3,2,1,0:T(8,128)(2,1)}, u32[]{:S(2)}, u32[]{:S(2)}) collective-permute-start(bf16[4,2,128,256]{3,2,1,0:T(8,128)(2,1)} %get-tuple-element.399), channel_id=1, source_target_pairs={{0,4},{4,8},{8,12},{12,16},{16,20},{20,24},{24,28},{1,5},{5,9},{9,... | collective-permute-start | bytes 1572872 | tf_op jit(solution)/shard_map/while/body/eval_jaxpr/ppermute | solution.py:10
  147.3 11.6 %collective-permute-start.1 = (bf16[4,2,128,256]{3,2,1,0:T(8,128)(2,1)}, bf16[4,2,128,256]{3,2,1,0:T(8,128)(2,1)}, u32[]{:S(2)}, u32[]{:S(2)}) collective-permute-start(bf16[4,2,128,256]{3,2,1,0:T(8,128)(2,1)} %get-tuple-element.408), channel_id=1, source_target_pairs={{4,0},{8,4},{12,8},{16,12},{20,16},{24,20},{28,24},{5,1},{9,5},{13... | collective-permute-start | bytes 1572872 | tf_op jit(solution)/shard_map/while/body/eval_jaxpr/ppermute | solution.py:10
  159.7 10.8 %collective-permute-start.1 = (bf16[4,2,128,256]{3,2,1,0:T(8,128)(2,1)}, bf16[4,2,128,256]{3,2,1,0:T(8,128)(2,1)}, u32[]{:S(2)}, u32[]{:S(2)}) collective-permute-start(bf16[4,2,128,256]{3,2,1,0:T(8,128)(2,1)} %get-tuple-element.408), channel_id=1, source_target_pairs={{4,0},{8,4},{12,8},{16,12},{20,16},{24,20},{28,24},{5,1},{9,5},{13... | collective-permute-start | bytes 1572872 | tf_op jit(solution)/shard_map/while/body/eval_jaxpr/ppermute | solution.py:10
  171.3 10.8 %collective-permute-start.1 = (bf16[4,2,128,256]{3,2,1,0:T(8,128)(2,1)}, bf16[4,2,128,256]{3,2,1,0:T(8,128)(2,1)}, u32[]{:S(2)}, u32[]{:S(2)}) collective-permute-start(bf16[4,2,128,256]{3,2,1,0:T(8,128)(2,1)} %get-tuple-element.408), channel_id=1, source_target_pairs={{4,0},{8,4},{12,8},{16,12},{20,16},{24,20},{28,24},{5,1},{9,5},{13... | collective-permute-start | bytes 1572872 | tf_op jit(solution)/shard_map/while/body/eval_jaxpr/ppermute | solution.py:10
  183.0 10.8 %collective-permute-start.1 = (bf16[4,2,128,256]{3,2,1,0:T(8,128)(2,1)}, bf16[4,2,128,256]{3,2,1,0:T(8,128)(2,1)}, u32[]{:S(2)}, u32[]{:S(2)}) collective-permute-start(bf16[4,2,128,256]{3,2,1,0:T(8,128)(2,1)} %get-tuple-element.408), channel_id=1, source_target_pairs={{4,0},{8,4},{12,8},{16,12},{20,16},{24,20},{28,24},{5,1},{9,5},{13... | collective-permute-start | bytes 1572872 | tf_op jit(solution)/shard_map/while/body/eval_jaxpr/ppermute | solution.py:10
  194.6 10.8 %collective-permute-start.1 = (bf16[4,2,128,256]{3,2,1,0:T(8,128)(2,1)}, bf16[4,2,128,256]{3,2,1,0:T(8,128)(2,1)}, u32[]{:S(2)}, u32[]{:S(2)}) collective-permute-start(bf16[4,2,128,256]{3,2,1,0:T(8,128)(2,1)} %get-tuple-element.408), channel_id=1, source_target_pairs={{4,0},{8,4},{12,8},{16,12},{20,16},{24,20},{28,24},{5,1},{9,5},{13... | collective-permute-start | bytes 1572872 | tf_op jit(solution)/shard_map/while/body/eval_jaxpr/ppermute | solution.py:10
  206.2 12.4 %collective-permute-start.1 = (bf16[4,2,128,256]{3,2,1,0:T(8,128)(2,1)}, bf16[4,2,128,256]{3,2,1,0:T(8,128)(2,1)}, u32[]{:S(2)}, u32[]{:S(2)}) collective-permute-start(bf16[4,2,128,256]{3,2,1,0:T(8,128)(2,1)} %get-tuple-element.408), channel_id=1, source_target_pairs={{4,0},{8,4},{12,8},{16,12},{20,16},{24,20},{28,24},{5,1},{9,5},{13... | collective-permute-start | bytes 1572872 | tf_op jit(solution)/shard_map/while/body/eval_jaxpr/ppermute | solution.py:10
  223.0 10.8 %collective-permute-start.1 = (bf16[4,2,128,256]{3,2,1,0:T(8,128)(2,1)}, bf16[4,2,128,256]{3,2,1,0:T(8,128)(2,1)}, u32[]{:S(2)}, u32[]{:S(2)}) collective-permute-start(bf16[4,2,128,256]{3,2,1,0:T(8,128)(2,1)} %get-tuple-element.408), channel_id=1, source_target_pairs={{4,0},{8,4},{12,8},{16,12},{20,16},{24,20},{28,24},{5,1},{9,5},{13... | collective-permute-start | bytes 1572872 | tf_op jit(solution)/shard_map/while/body/eval_jaxpr/ppermute | solution.py:10
  234.6 10.8 %collective-permute-start.1 = (bf16[4,2,128,256]{3,2,1,0:T(8,128)(2,1)}, bf16[4,2,128,256]{3,2,1,0:T(8,128)(2,1)}, u32[]{:S(2)}, u32[]{:S(2)}) collective-permute-start(bf16[4,2,128,256]{3,2,1,0:T(8,128)(2,1)} %get-tuple-element.408), channel_id=1, source_target_pairs={{4,0},{8,4},{12,8},{16,12},{20,16},{24,20},{28,24},{5,1},{9,5},{13... | collective-permute-start | bytes 1572872 | tf_op jit(solution)/shard_map/while/body/eval_jaxpr/ppermute | solution.py:10
  (6 other events, 8.9 us)
Sparse Core Ops, SparseCore 0:
  18.4 21.7 all-gather.2
where the time goes:
time: 253 us; the launch traced here: 252 us
  waiting for transfers between devices  140 us (55%)
  starting transfers between devices  60.6 us (24%)
  local copies, waits for them, and re-layouts  21.8 us (9%)
  matrix products  15 us (6%)
  between operations  14.1 us (6%)
    ppermute x17, waiting for transfers between devices, from_behind(): return lax.ppermute(value, axis, pairs)  128 us
    ppermute x17, starting transfers between devices, from_behind(): return lax.ppermute(value, axis, pairs)  53.9 us
    another operation x18, local copies, waits for them, and re-layouts  14.9 us
    dot_general x7, matrix products, apply_blocks(): jnp.einsum('bqrs,bqst->bqrt', vectors, blocks, preferred_element_type=jnp...  12.9 us
    all_gather x1, waiting for transfers between devices, local(): piece = lax.all_gather(current, 'valley', axis=0, tiled=True)  12.6 us
  transfers between devices with their start and end apart: 20, of which 18 were waited for; matrix products, arithmetic and copies ran while one was open for 4% of the time, Pallas kernels for 0%

commit v1 on v0

v1 whole, which is shorter than its diff:
```python
import functools

import jax
import jax.numpy as jnp
from jax import lax
from jax.experimental import pallas as pl
from jax.experimental.pallas import tpu as pltpu
from jax.sharding import PartitionSpec as P

BF16 = jnp.bfloat16
F32 = jnp.float32
VMEM = pltpu.MemorySpace.VMEM
GROUPS = 2


def dot(x, y):
    return jnp.dot(x, y, preferred_element_type=F32)


def call(kernel, outs, *operands, products=1):
    spec = pl.BlockSpec(memory_space=pltpu.VMEM)
    held = [pltpu.with_memory_space_constraint(x, VMEM) for x in operands]
    result = pl.pallas_call(
        kernel,
        out_shape=[VMEM(shape, dtype) for shape, dtype in outs],
        in_specs=[spec] * len(held),
        out_specs=[spec] * len(outs),
        compiler_params=pltpu.CompilerParams(vmem_limit_bytes=8 << 20),
        cost_estimate=pl.CostEstimate(
            flops=products * 2 * 128 * 256 * 256, bytes_accessed=1 << 18, transcendentals=0
        ),
    )(*held)
    return result


def place():
    height = lax.axis_index("elev")
    return height // 2, lax.rem(height, 2)


def swap_cores(value):
    count = lax.axis_size("elev")
    return lax.ppermute(value, "elev", [(i, i ^ 1) for i in range(count)])


def swap_chips(value, low):
    pairs = []
    for i in range(lax.axis_size("elev")):
        chip = i // 2
        pairs.append((i, i + 2 if chip == low else i - 2 if chip == low + 1 else i ^ 1))
    return lax.ppermute(value, "elev", pairs)


def local(
    resid,
    direction,
    diag_blocks,
    lower_blocks,
    upper_blocks,
    inv_pivots,
    down_coupling,
    valley_coupling,
    coupled_column,
):
    _, valleys, downs, rows, size = resid.shape
    chains = valleys * downs
    half = chains // 2
    groups = GROUPS
    width = half // groups
    chips = lax.axis_size("elev") // 2
    vectors = lambda x: x.reshape(chains, rows, size)
    blocks = lambda x: x.reshape(chains, size, size)
    rhs, current = vectors(resid), vectors(direction)
    lower, upper, pivot = blocks(lower_blocks), blocks(upper_blocks), blocks(inv_pivots)

    elev = lax.axis_size("elev")
    beside = swap_cores(current)
    across = lax.ppermute(
        current,
        "elev",
        [(i, i + 1) for i in range(1, elev - 1, 2)] + [(i + 1, i) for i in range(1, elev - 1, 2)],
    )

    def first(l_ref, p_ref, r_ref, keep_ref, send_ref):
        _, core = place()
        for i in range(half):
            for ref, base in ((send_ref, (1 - core) * half), (keep_ref, core * half)):
                block = p_ref[base + i]
                ref[i, :size] = (-dot(l_ref[base + i], block)).astype(BF16)
                ref[i, size:] = dot(r_ref[base + i], block).astype(BF16)

    packed = ((half, size + rows, size), BF16)
    keep1, send1 = call(first, [packed, packed], lower, pivot, rhs, products=3 * chains)
    recv1 = swap_cores(send1)

    def second(u_ref, p_ref, keep_ref, send_ref):
        _, core = place()
        for i in range(half):
            for ref, base in ((send_ref, (1 - core) * half), (keep_ref, core * half)):
                ref[i] = (-dot(u_ref[base + i], p_ref[base + i])).astype(BF16)

    square = ((half, size, size), BF16)
    keep2, send2 = call(second, [square, square], upper, pivot, products=2 * chains)

    def begin(keep_ref, recv_ref, start_ref):
        _, core = place()

        def write(bottom, top):
            for i in range(half):
                start_ref[i] = (
                    top[i, size:].astype(F32) + dot(bottom[i, size:], top[i, :size])
                ).astype(BF16)

        pl.when(core == 0)(lambda: write(keep_ref, recv_ref))
        pl.when(core == 1)(lambda: write(recv_ref, keep_ref))

    (start,) = call(begin, [((half, rows, size), BF16)], keep1, recv1, products=half)

    def join(keep_ref, recv_ref, through_ref):
        _, core = place()

        def write(bottom, top):
            for i in range(half):
                through_ref[i] = dot(bottom[i, :size], top[i, :size]).astype(BF16)

        pl.when(core == 0)(lambda: write(keep_ref, recv_ref))
        pl.when(core == 1)(lambda: write(recv_ref, keep_ref))

    (through,) = call(join, [square], keep1, recv1, products=2 * half)
    recv2 = swap_cores(send2)

    def back(keep_ref, recv_ref, back_ref):
        _, core = place()

        def write(bottom, top):
            for i in range(half):
                back_ref[i] = dot(top[i], bottom[i]).astype(BF16)

        pl.when(core == 0)(lambda: write(keep_ref, recv_ref))
        pl.when(core == 1)(lambda: write(recv_ref, keep_ref))

    (backward,) = call(back, [square], keep2, recv2, products=2 * half)

    message = ((width, rows, size), BF16)
    spans = [slice(g * width, (g + 1) * width) for g in range(groups)]

    def advance(span, low, in_ref, start_ref, through_ref, out_ref):
        chip, _ = place()
        at = span.start

        def step():
            for i in range(width):
                out_ref[i] = (
                    start_ref[at + i].astype(F32) + dot(in_ref[i], through_ref[at + i])
                ).astype(BF16)

        def idle():
            out_ref[...] = in_ref[...]

        pl.when(chip == low)(step)
        pl.when(chip != low)(idle)

    fronts = [start[span] for span in spans]
    heard = [[] for _ in spans]
    for low in range(chips - 1):
        for g, span in enumerate(spans):
            arrived = swap_chips(fronts[g], low)
            heard[g].append(arrived)
            if low < chips - 2:
                (fronts[g],) = call(
                    functools.partial(advance, span, low + 1),
                    [message],
                    arrived,
                    start,
                    through,
                    products=width,
                )

    def turn(span, *refs):
        heard_refs = refs[: chips - 1]
        start_ref, through_ref, keep1_ref, recv1_ref, keep2_ref, recv2_ref = refs[chips - 1 : -3]
        top_ref, base_ref, in_ref = refs[-3:]
        chip, core = place()
        at = span.start

        @pl.when(chip == 0)
        def _():
            in_ref[...] = jnp.zeros_like(in_ref)

        for low in range(chips - 1):

            @pl.when(chip == low + 1)
            def _():
                in_ref[...] = heard_refs[low][...]

        def write(first_ref, second_ref):
            for i in range(width):
                arrived = in_ref[i]
                top = (
                    start_ref[at + i].astype(F32) + dot(arrived, through_ref[at + i])
                ).astype(BF16)
                low = first_ref[at + i, size:].astype(F32) + dot(arrived, first_ref[at + i, :size])
                top_ref[i] = top
                base_ref[i] = (
                    low.astype(BF16).astype(F32) + dot(top, second_ref[at + i])
                ).astype(BF16)

        pl.when(core == 0)(lambda: write(keep1_ref, keep2_ref))
        pl.when(core == 1)(lambda: write(recv1_ref, recv2_ref))

    tops, bases = [], []
    for g, span in enumerate(spans):
        top, base, _ = call(
            functools.partial(turn, span),
            [message] * 3,
            *heard[g],
            start,
            through,
            keep1,
            recv1,
            keep2,
            recv2,
            products=3 * width,
        )
        tops.append(top)
        bases.append(base)

    def retreat(span, low, in_ref, base_ref, back_ref, out_ref):
        chip, _ = place()
        at = span.start

        def step():
            for i in range(width):
                out_ref[i] = (
                    base_ref[i].astype(F32) + dot(in_ref[i], back_ref[at + i])
                ).astype(BF16)

        def idle():
            out_ref[...] = in_ref[...]

        pl.when(chip == low)(step)
        pl.when(chip != low)(idle)

    solved = list(bases)
    heard = [[] for _ in spans]
    for low in range(chips - 2, -1, -1):
        for g, span in enumerate(spans):
            arrived = swap_chips(solved[g], low)
            heard[g].insert(0, arrived)
            if low > 0:
                (solved[g],) = call(
                    functools.partial(retreat, span, low),
                    [message],
                    arrived,
                    bases[g],
                    backward,
                    products=width,
                )

    def finish(span, *refs):
        heard_refs = refs[: chips - 1]
        top_ref, base_ref, back_ref, keep2_ref, recv2_ref = refs[chips - 1 : -3]
        keep_ref, send_ref, in_ref = refs[-3:]
        chip, core = place()
        at = span.start

        @pl.when(chip == chips - 1)
        def _():
            in_ref[...] = jnp.zeros_like(in_ref)

        for low in range(chips - 1):

            @pl.when(chip == low)
            def _():
                in_ref[...] = heard_refs[low][...]

        def write(top_block, bottom_out, top_out):
            for i in range(width):
                arrived = in_ref[i]
                bottom_out[i] = (
                    base_ref[i].astype(F32) + dot(arrived, back_ref[at + i])
                ).astype(BF16)
                top_out[i] = (
                    top_ref[i].astype(F32) + dot(arrived, top_block[at + i])
                ).astype(BF16)

        pl.when(core == 0)(lambda: write(recv2_ref, keep_ref, send_ref))
        pl.when(core == 1)(lambda: write(keep2_ref, send_ref, keep_ref))

    kept, given = [], []
    for g, span in enumerate(spans):
        keep, send, _ = call(
            functools.partial(finish, span),
            [message] * 3,
            *heard[g],
            tops[g],
            bases[g],
            backward,
            keep2,
            recv2,
            products=2 * width,
        )
        kept.append(keep)
        given.append(swap_cores(send))

    def gather(*refs):
        kept_refs, given_refs, out_ref, sems = refs[:groups], refs[groups:-2], refs[-2], refs[-1]
        _, core = place()
        copies = []
        for g in range(groups):
            for which, (ref, side) in enumerate(((kept_refs[g], core), (given_refs[g], 1 - core))):
                copies.append(
                    pltpu.make_async_copy(
                        ref,
                        out_ref.at[pl.ds(side * half + g * width, width)],
                        sems.at[2 * g + which],
                    )
                )
        for copy in copies:
            copy.start()
        for copy in copies:
            copy.wait()

    spec = pl.BlockSpec(memory_space=pltpu.VMEM)
    parts = [pltpu.with_memory_space_constraint(x, VMEM) for x in kept + given]
    preconditioned = pl.pallas_call(
        gather,
        out_shape=jax.ShapeDtypeStruct((chains, rows, size), BF16),
        in_specs=[spec] * len(parts),
        out_specs=pl.BlockSpec(memory_space=pl.ANY),
        scratch_shapes=[pltpu.SemaphoreType.DMA((2 * groups,))],
        compiler_params=pltpu.CompilerParams(vmem_limit_bytes=8 << 20),
    )(*parts)

    downs_count, valley_count = lax.axis_size("down"), lax.axis_size("valley")
    rim = lax.ppermute(
        direction[0, :, -1],
        "down",
        [(i, (i + 1) % downs_count) for i in range(downs_count)],
    )
    others = [
        lax.ppermute(
            current, "valley", [(i, (i + by) % valley_count) for i in range(valley_count)]
        )
        for by in range(1, valley_count)
    ]

    def near(current_ref, beside_ref, diag_ref, lower_ref, upper_ref, out_ref):
        _, core = place()

        def write(block_ref):
            for i in range(chains):
                out_ref[i] = dot(current_ref[i], diag_ref[i]) + dot(beside_ref[i], block_ref[i])

        pl.when(core == 0)(lambda: write(upper_ref))
        pl.when(core == 1)(lambda: write(lower_ref))

    total_shape = ((chains, rows, size), F32)
    (partial_sum,) = call(
        near,
        [total_shape],
        current,
        beside,
        blocks(diag_blocks),
        lower,
        upper,
        products=2 * chains,
    )

    def far(column_ref, *refs):
        current_ref, across_ref, rim_ref = refs[:3]
        others_refs = refs[3 : 2 + valley_count]
        lower_ref, upper_ref, down_ref, valley_ref, sum_ref = refs[2 + valley_count : -3]
        out_ref, partner_ref, total_ref = refs[-3:]
        chip, core = place()
        mine = lax.axis_index("valley")
        edge = lax.axis_index("down")

        for i in range(chains):
            column = column_ref[i // downs, i % downs]
            owner = column // valleys
            spot = lax.rem(column, valleys) * downs + i % downs
            behind = lax.rem(mine - owner + valley_count, valley_count)

            @pl.when(behind == 0)
            def _():
                partner_ref[i] = current_ref[spot]

            for by in range(1, valley_count):

                @pl.when(behind == by)
                def _():
                    partner_ref[i] = others_refs[by - 1][spot]

        for i in range(chains):
            total = sum_ref[i] + dot(partner_ref[i], valley_ref[i])
            if i % downs:
                total = total + dot(current_ref[i - 1], down_ref[i])
            total_ref[i] = total

        @pl.when(edge > 0)
        def _():
            for i in range(0, chains, downs):
                total_ref[i] += dot(rim_ref[i // downs], down_ref[i])

        @pl.when(jnp.logical_and(core == 0, chip > 0))
        def _():
            for i in range(chains):
                total_ref[i] += dot(across_ref[i], lower_ref[i])

        @pl.when(jnp.logical_and(core == 1, chip < chips - 1))
        def _():
            for i in range(chains):
                total_ref[i] += dot(across_ref[i], upper_ref[i])

        pltpu.sync_copy(total_ref, out_ref)

    operands = [current, across, rim] + others
    operands += [lower, upper, blocks(down_coupling), blocks(valley_coupling), partial_sum]
    operands = [pltpu.with_memory_space_constraint(x, VMEM) for x in operands]
    image = pl.pallas_call(
        far,
        out_shape=jax.ShapeDtypeStruct((chains, rows, size), F32),
        in_specs=[pl.BlockSpec(memory_space=pltpu.SMEM)] + [spec] * len(operands),
        out_specs=pl.BlockSpec(memory_space=pl.ANY),
        scratch_shapes=[
            pltpu.VMEM((chains, rows, size), BF16),
            pltpu.VMEM((chains, rows, size), F32),
        ],
        compiler_params=pltpu.CompilerParams(vmem_limit_bytes=8 << 20),
        cost_estimate=pl.CostEstimate(
            flops=3 * chains * 2 * rows * size * size, bytes_accessed=4 << 20, transcendentals=0
        ),
    )(coupled_column[0], *operands)
    return (preconditioned.reshape(resid.shape), image.reshape(resid.shape))


def solution(mesh):
    spec = P("elev", "valley", "down", None, None)
    in_specs = (spec,) * 8 + (P("elev", "valley", "down"),)
    return jax.shard_map(
        local, mesh=mesh, in_specs=in_specs, out_specs=(spec, spec), check_vma=False
    )
```

time: 253 us -> 67.6 us (0.27)
  waiting for transfers between devices: 140 us -> 13.1 us
  starting transfers between devices: 60.6 us -> 31.3 us
  matrix products: 15 us -> 0 us
  between operations: 14.1 us -> 0.82 us
  Pallas kernels: 0 us -> 11.2 us
  local copies, waits for them, and re-layouts: 21.8 us -> 10.7 us
    ppermute x19 -> x20, waiting for transfers between devices: 128 us -> 13.1 us  [the longest x12 11.9 us: swap_chips(): return lax.ppermute(value, 'elev', pairs)]
    ppermute x19 -> x20, starting transfers between devices: 60.5 us -> 31.3 us  [the longest x1 15.6 us: local(): lax.ppermute(current, 'elev', [(i, i + 1) for i in range(1, elev - 1, 2)]...]
    dot_general x8 -> x0, matrix products: 15 us -> none  [the longest x7 12.9 us: apply_blocks(): jnp.einsum('bqrs,bqst->bqrt', vectors, blocks, preferred_element_type=jnp...]
    another operation x18 -> x0, local copies, waits for them, and re-layouts: 14.9 us -> none
    all_gather x1 -> x0, waiting for transfers between devices: 12.6 us -> none  [local(): piece = lax.all_gather(current, 'valley', axis=0, tiled=True)]
    pallas_call x0 -> x20, Pallas kernels: none -> 11.2 us  [the longest x18 6.4 us: call(): pl.pallas_call(kernel, out_shape=[VMEM(shape, dtype) for shape, dtype in...]
    unnamed x20 -> x28, local copies, waits for them, and re-layouts: 1.92 us -> 9.91 us
    cond x2 -> x0, local copies, waits for them, and re-layouts: 3.75 us -> none
  transfers between devices with their start and end apart: 20 -> 20, of which waited for: 18 -> 7; matrix products, arithmetic and copies ran while one was open for 4% -> 1% of each run, Pallas kernels for 0% -> 13%
where the time goes in v1:
time: 67.6 us; the launch traced here: 67.1 us
  starting transfers between devices  31.3 us (46%)
  waiting for transfers between devices  13.1 us (19%)
  Pallas kernels  11.2 us (17%)
  local copies, waits for them, and re-layouts  10.7 us (16%)
  between operations  0.82 us (1%)
    ppermute x1, starting transfers between devices, local(): lax.ppermute(current, 'elev', [(i, i + 1) for i in range(1, elev - 1, 2)]...  15.6 us
    ppermute x12, waiting for transfers between devices, swap_chips(): return lax.ppermute(value, 'elev', pairs)  11.9 us
    unnamed x28, local copies, waits for them, and re-layouts  9.91 us
    ppermute x12, starting transfers between devices, swap_chips(): return lax.ppermute(value, 'elev', pairs)  9.03 us
    pallas_call x18, Pallas kernels, call(): pl.pallas_call(kernel, out_shape=[VMEM(shape, dtype) for shape, dtype in...  6.4 us
    ppermute x5, starting transfers between devices, swap_cores(): return lax.ppermute(value, 'elev', [(i, i ^ 1) for i in range(count)])  4.23 us
    pallas_call x1, Pallas kernels, local(): pl.pallas_call(far, out_shape=jax.ShapeDtypeStruct((chains, rows, size),...  2.99 us
    pallas_call x1, Pallas kernels, local(): pl.pallas_call(gather, out_shape=jax.ShapeDtypeStruct((chains, rows, size...  1.79 us
  transfers between devices with their start and end apart: 20, of which 7 were waited for; matrix products, arithmetic and copies ran while one was open for 1% of the time, Pallas kernels for 13%

profile of v1, /device:TPU:1, one launch (start us, length us, event | category | flops | bytes accessed | tf_op | source)
XLA Modules:
  0.0 67.1 jit_solution(2480848181695251400)
XLA Ops:
  0.6 1.2 %copy-done = bf16[1,4,2,256,256]{4,3,2,1,0:T(8,128)(2,1)S(1)} copy-done((bf16[1,4,2,256,256]{4,3,2,1,0:T(8,128)(2,1)S(1)}, bf16[1,4,2,256,256]{4,3,2,1,0:T(8,128)(2,1)}, u32[]{:S(2)}) %copy-start) | copy-done | bytes 1048600
  1.9 1.2 %copy-done.3 = bf16[1,4,2,256,256]{4,3,2,1,0:T(8,128)(2,1)S(1)} copy-done((bf16[1,4,2,256,256]{4,3,2,1,0:T(8,128)(2,1)S(1)}, bf16[1,4,2,256,256]{4,3,2,1,0:T(8,128)(2,1)}, u32[]{:S(2)}) %copy-start.3) | copy-done | bytes 1048600
  3.1 1.0 %copy-done.8 = bf16[1,4,2,128,256]{4,3,2,1,0:T(8,128)(2,1)S(1)} copy-done((bf16[1,4,2,128,256]{4,3,2,1,0:T(8,128)(2,1)S(1)}, bf16[1,4,2,128,256]{4,3,2,1,0:T(8,128)(2,1)}, u32[]{:S(2)}) %copy-start.8) | copy-done | bytes 524312
  5.9 1.1 %collective-permute-done.recv_ref.refs_6_ = bf16[4,384,256]{2,1,0:T(8,128)(2,1)S(1)} collective-permute-done((bf16[4,384,256]{2,1,0:T(8,128)(2,1)S(1)}, bf16[4,384,256]{2,1,0:T(8,128)(2,1)S(1)}, u32[]{:S(2)}, u32[]{:S(2)}) %collective-permute-start) | collective-permute-done | bytes 786464 | tf_op jit(solution)/shard_map/ppermute | solution.py:43
  7.3 2.5 %collective-permute-start.8 = (bf16[2,128,256]{2,1,0:T(8,128)(2,1)S(1)}, bf16[2,128,256]{2,1,0:T(8,128)(2,1)S(1)}, u32[]{:S(2)}, u32[]{:S(2)}) collective-permute-start(bf16[2,128,256]{2,1,0:T(8,128)(2,1)S(1)} %get-tuple-element.26), channel_id=1, source_target_pairs={{0,8},{4,12},{8,0},{12,4},{16,20},{20,16},{24,28},{28,24},{1,9},{5... | collective-permute-start | bytes 393224 | tf_op jit(solution)/shard_map/ppermute | solution.py:51
  10.2 3.2 %collective-permute-done.8.in_ref.refs_0_ = bf16[2,128,256]{2,1,0:T(8,128)(2,1)S(1)} collective-permute-done((bf16[2,128,256]{2,1,0:T(8,128)(2,1)S(1)}, bf16[2,128,256]{2,1,0:T(8,128)(2,1)S(1)}, u32[]{:S(2)}, u32[]{:S(2)}) %collective-permute-start.8) | collective-permute-done | bytes 131104 | tf_op jit(solution)/shard_map/ppermute | solution.py:51
  13.4 1.4 %collective-permute-start.9 = (bf16[2,128,256]{2,1,0:T(8,128)(2,1)S(1)}, bf16[2,128,256]{2,1,0:T(8,128)(2,1)S(1)}, u32[]{:S(2)}, u32[]{:S(2)}) collective-permute-start(bf16[2,128,256]{2,1,0:T(8,128)(2,1)S(1)} %shard_map.115), channel_id=1, source_target_pairs={{0,4},{4,0},{8,16},{12,20},{16,8},{20,12},{24,28},{28,24},{1,5},{5... | collective-permute-start | bytes 393224 | tf_op jit(solution)/shard_map/ppermute | solution.py:51
  14.8 1.4 %collective-permute-done.1.in_ref.refs_0_ = bf16[2,128,256]{2,1,0:T(8,128)(2,1)S(1)} collective-permute-done((bf16[2,128,256]{2,1,0:T(8,128)(2,1)S(1)}, bf16[2,128,256]{2,1,0:T(8,128)(2,1)S(1)}, u32[]{:S(2)}, u32[]{:S(2)}) %collective-permute-start.1) | collective-permute-done | bytes 131104 | tf_op jit(solution)/shard_map/ppermute | solution.py:51
  16.2 1.0 %collective-permute-start.2 = (bf16[2,128,256]{2,1,0:T(8,128)(2,1)S(1)}, bf16[2,128,256]{2,1,0:T(8,128)(2,1)S(1)}, u32[]{:S(2)}, u32[]{:S(2)}) collective-permute-start(bf16[2,128,256]{2,1,0:T(8,128)(2,1)S(1)} %shard_map.107), channel_id=1, source_target_pairs={{0,4},{4,0},{8,16},{12,20},{16,8},{20,12},{24,28},{28,24},{1,5},{5... | collective-permute-start | bytes 393224 | tf_op jit(solution)/shard_map/ppermute | solution.py:51
  18.6 1.0 %shard_map.117 = (bf16[2,128,256]{2,1,0:T(8,128)(2,1)S(1)}, bf16[2,128,256]{2,1,0:T(8,128)(2,1)S(1)}, bf16[2,128,256]{2,1,0:T(8,128)(2,1)}) custom-call(bf16[2,128,256]{2,1,0:T(8,128)(2,1)S(1)} %collective-permute-done.8.in_ref.refs_0_, bf16[2,128,256]{2,1,0:T(8,128)(2,1)S(1)} %collective-permute-done.9.in_ref.refs_1_, ...), custom_call_target="tpu_custom_call" | custom-call | flops 100663296 | bytes 262144 | tf_op jit(solution)/shard_map/pallas_call | solution.py:23
  20.1 1.1 %shard_map.110 = (bf16[2,128,256]{2,1,0:T(8,128)(2,1)S(1)}, bf16[2,128,256]{2,1,0:T(8,128)(2,1)S(1)}, bf16[2,128,256]{2,1,0:T(8,128)(2,1)}) custom-call(bf16[2,128,256]{2,1,0:T(8,128)(2,1)S(1)} %collective-permute-done.1.in_ref.refs_0_, bf16[2,128,256]{2,1,0:T(8,128)(2,1)S(1)} %collective-permute-done.2.in_ref.refs_1_, ...), custom_call_target="tpu_custom_call" | custom-call | flops 100663296 | bytes 262144 | tf_op jit(solution)/shard_map/pallas_call | solution.py:23
  22.6 15.6 %collective-permute-start.16 = (bf16[8,128,256]{2,1,0:T(8,128)(2,1)S(1)}, bf16[8,128,256]{2,1,0:T(8,128)(2,1)S(1)}, u32[]{:S(2)}, u32[]{:S(2)}) collective-permute-start(bf16[8,128,256]{2,1,0:T(8,128)(2,1)S(1)} %bitcast.24), channel_id=1, source_target_pairs={{4,8},{12,16},{20,24},{8,4},{16,12},{24,20},{5,9},{13,17},{21,25},... | collective-permute-start | bytes 1572872 | tf_op jit(solution)/shard_map/ppermute | solution.py:78
  38.2 1.3 %collective-permute-start.18 = (bf16[8,128,256]{2,1,0:T(8,128)(2,1)S(1)}, bf16[8,128,256]{2,1,0:T(8,128)(2,1)}, u32[]{:S(2)}, u32[]{:S(2)}) collective-permute-start(bf16[8,128,256]{2,1,0:T(8,128)(2,1)S(1)} %bitcast.25), channel_id=1, source_target_pairs={{0,2},{2,0},{1,3},{3,1},{4,6},{6,4},{5,7},{7,5},{8,10},{10,8},{9,1... | collective-permute-start | bytes 1572872 | tf_op jit(solution)/shard_map/ppermute | solution.py:342
  40.9 1.2 %collective-permute-start.17 = (bf16[4,128,256]{2,1,0:T(8,128)(2,1)}, bf16[4,128,256]{2,1,0:T(8,128)(2,1)S(1)}, u32[]{:S(2)}, u32[]{:S(2)}) collective-permute-start(bf16[4,128,256]{2,1,0:T(8,128)(2,1)} %slice_bitcast_fusion), channel_id=1, source_target_pairs={{0,1},{1,0},{2,3},{3,2},{4,5},{5,4},{6,7},{7,6},{8,9},{9,8},{10,11... | collective-permute-start | bytes 786440 | tf_op jit(solution)/shard_map/ppermute | solution.py:336
  42.1 5.0 %collective-permute-done.13.refs_0_ = bf16[2,128,256]{2,1,0:T(8,128)(2,1)S(1)} collective-permute-done((bf16[2,128,256]{2,1,0:T(8,128)(2,1)S(1)}, bf16[2,128,256]{2,1,0:T(8,128)(2,1)S(1)}, u32[]{:S(2)}, u32[]{:S(2)}) %collective-permute-start.13) | collective-permute-done | bytes 131104 | tf_op jit(solution)/shard_map/ppermute | solution.py:51
  47.1 2.3 %collective-permute-start.7 = (bf16[2,128,256]{2,1,0:T(8,128)(2,1)S(1)}, bf16[2,128,256]{2,1,0:T(8,128)(2,1)S(1)}, u32[]{:S(2)}, u32[]{:S(2)}) collective-permute-start(bf16[2,128,256]{2,1,0:T(8,128)(2,1)S(1)} %shard_map.113), channel_id=1, source_target_pairs={{0,8},{4,12},{8,0},{12,4},{16,20},{20,16},{24,28},{28,24},{1,9},{5... | collective-permute-start | bytes 393224 | tf_op jit(solution)/shard_map/ppermute | solution.py:51
  49.4 1.0 %shard_map.120 = (bf16[2,128,256]{2,1,0:T(8,128)(2,1)S(1)}, bf16[2,128,256]{2,1,0:T(8,128)(2,1)}, bf16[2,128,256]{2,1,0:T(8,128)(2,1)}) custom-call(bf16[2,128,256]{2,1,0:T(8,128)(2,1)S(1)} %collective-permute-done.13.refs_0_, bf16[2,128,256]{2,1,0:T(8,128)(2,1)S(1)} %collective-permute-done.12.in_ref.refs_1_, ...), custom_call_target="tpu_custom_call" | custom-call | flops 67108864 | bytes 262144 | tf_op jit(solution)/shard_map/pallas_call | solution.py:23
  50.3 1.4 %collective-permute-done.7.refs_0_ = bf16[2,128,256]{2,1,0:T(8,128)(2,1)S(1)} collective-permute-done((bf16[2,128,256]{2,1,0:T(8,128)(2,1)S(1)}, bf16[2,128,256]{2,1,0:T(8,128)(2,1)S(1)}, u32[]{:S(2)}, u32[]{:S(2)}) %collective-permute-start.7) | collective-permute-done | bytes 131104 | tf_op jit(solution)/shard_map/ppermute | solution.py:51
  51.7 3.6 %collective-permute-start.15 = (bf16[2,128,256]{2,1,0:T(8,128)(2,1)}, bf16[2,128,256]{2,1,0:T(8,128)(2,1)}, u32[]{:S(2)}, u32[]{:S(2)}) collective-permute-start(bf16[2,128,256]{2,1,0:T(8,128)(2,1)} %get-tuple-element.25), channel_id=1, source_target_pairs={{0,4},{4,0},{8,12},{12,8},{16,20},{20,16},{24,28},{28,24},{1,5},{5... | collective-permute-start | bytes 393224 | tf_op jit(solution)/shard_map/ppermute | solution.py:43
  55.3 1.0 %shard_map.114 = (bf16[2,128,256]{2,1,0:T(8,128)(2,1)S(1)}, bf16[2,128,256]{2,1,0:T(8,128)(2,1)}, bf16[2,128,256]{2,1,0:T(8,128)(2,1)}) custom-call(bf16[2,128,256]{2,1,0:T(8,128)(2,1)S(1)} %collective-permute-done.7.refs_0_, bf16[2,128,256]{2,1,0:T(8,128)(2,1)S(1)} %collective-permute-done.6.in_ref.refs_1_, ...), custom_call_target="tpu_custom_call" | custom-call | flops 67108864 | bytes 262144 | tf_op jit(solution)/shard_map/pallas_call | solution.py:23
  58.5 1.2 %copy-done.5 = bf16[1,4,2,256,256]{4,3,2,1,0:T(8,128)(2,1)S(1)} copy-done((bf16[1,4,2,256,256]{4,3,2,1,0:T(8,128)(2,1)S(1)}, bf16[1,4,2,256,256]{4,3,2,1,0:T(8,128)(2,1)}, u32[]{:S(2)}) %copy-start.5) | copy-done | bytes 1048600
  59.8 1.0 %copy-done.10 = bf16[8,128,256]{2,1,0:T(8,128)(2,1)S(1)} copy-done((bf16[8,128,256]{2,1,0:T(8,128)(2,1)S(1)}, bf16[8,128,256]{2,1,0:T(8,128)(2,1)}, u32[]{:S(2)}) %copy-start.10) | copy-done | bytes 524312
  62.3 3.0 %shard_map.123 = f32[8,128,256]{2,1,0:T(8,128)} custom-call(s32[4,2]{1,0:T(4,128)S(1)} %copy.12.column_ref, bf16[8,128,256]{2,1,0:T(8,128)(2,1)S(1)} %bitcast.27, bf16[8,128,256]{2,1,0:T(8,128)(2,1)S(1)} %collective-permute-done.16.refs_1_, bf16[4,128,256]{2,1,0:T(8,128)(2,1)S(1)} %collective-permute-done.17.refs_2_, ...), custom_call_target="tpu_custom_call" | custom-call | flops 402653184 | bytes 4194304 | tf_op jit(solution)/shard_map/pallas_call | solution.py:421
  65.3 1.8 %shard_map.121 = bf16[8,128,256]{2,1,0:T(8,128)(2,1)} custom-call(bf16[2,128,256]{2,1,0:T(8,128)(2,1)S(1)} %copy-done.12, bf16[2,128,256]{2,1,0:T(8,128)(2,1)S(1)} %get-tuple-element.23.refs_1_, bf16[2,128,256]{2,1,0:T(8,128)(2,1)} %collective-permute-done.14.refs_2_, bf16[2,128,256]{2,1,0:T(8,128)(2,1)} %collective-permute-done.15.refs_3_), custom_call_target="tpu_custom_call" | custom-call | tf_op jit(solution)/shard_map/pallas_call | solution.py:326
  (67 shorter events, 10.9 us)
Async XLA Ops:
  0.6 1.2 %copy-start = (bf16[1,4,2,256,256]{4,3,2,1,0:T(8,128)(2,1)S(1)}, bf16[1,4,2,256,256]{4,3,2,1,0:T(8,128)(2,1)}, u32[]{:S(2)}) copy-start(bf16[1,4,2,256,256]{4,3,2,1,0:T(8,128)(2,1)} %param.12) | copy-start | bytes 3145732
  4.7 2.4 %collective-permute-start = (bf16[4,384,256]{2,1,0:T(8,128)(2,1)S(1)}, bf16[4,384,256]{2,1,0:T(8,128)(2,1)S(1)}, u32[]{:S(2)}, u32[]{:S(2)}) collective-permute-start(bf16[4,384,256]{2,1,0:T(8,128)(2,1)S(1)} %get-tuple-element.15), channel_id=1, source_target_pairs={{0,4},{4,0},{8,12},{12,8},{16,20},{20,16},{24,28},{28,24},{1,5},{5... | collective-permute-start | bytes 2359304 | tf_op jit(solution)/shard_map/ppermute | solution.py:43
  5.8 12.8 %collective-permute-start.4 = (bf16[4,256,256]{2,1,0:T(8,128)(2,1)S(1)}, bf16[4,256,256]{2,1,0:T(8,128)(2,1)S(1)}, u32[]{:S(2)}, u32[]{:S(2)}) collective-permute-start(bf16[4,256,256]{2,1,0:T(8,128)(2,1)S(1)} %get-tuple-element.17), channel_id=1, source_target_pairs={{0,4},{4,0},{8,12},{12,8},{16,20},{20,16},{24,28},{28,24},{1,5},{5... | collective-permute-start | bytes 1572872 | tf_op jit(solution)/shard_map/ppermute | solution.py:43
  7.3 6.1 %collective-permute-start.8 = (bf16[2,128,256]{2,1,0:T(8,128)(2,1)S(1)}, bf16[2,128,256]{2,1,0:T(8,128)(2,1)S(1)}, u32[]{:S(2)}, u32[]{:S(2)}) collective-permute-start(bf16[2,128,256]{2,1,0:T(8,128)(2,1)S(1)} %get-tuple-element.26), channel_id=1, source_target_pairs={{0,8},{4,12},{8,0},{12,4},{16,20},{20,16},{24,28},{28,24},{1,9},{5... | collective-permute-start | bytes 393224 | tf_op jit(solution)/shard_map/ppermute | solution.py:51
  9.8 6.4 %collective-permute-start.1 = (bf16[2,128,256]{2,1,0:T(8,128)(2,1)S(1)}, bf16[2,128,256]{2,1,0:T(8,128)(2,1)S(1)}, u32[]{:S(2)}, u32[]{:S(2)}) collective-permute-start(bf16[2,128,256]{2,1,0:T(8,128)(2,1)S(1)} %get-tuple-element.27), channel_id=1, source_target_pairs={{0,8},{4,12},{8,0},{12,4},{16,20},{20,16},{24,28},{28,24},{1,9},{5... | collective-permute-start | bytes 393224 | tf_op jit(solution)/shard_map/ppermute | solution.py:51
  13.4 3.8 %collective-permute-start.9 = (bf16[2,128,256]{2,1,0:T(8,128)(2,1)S(1)}, bf16[2,128,256]{2,1,0:T(8,128)(2,1)S(1)}, u32[]{:S(2)}, u32[]{:S(2)}) collective-permute-start(bf16[2,128,256]{2,1,0:T(8,128)(2,1)S(1)} %shard_map.115), channel_id=1, source_target_pairs={{0,4},{4,0},{8,16},{12,20},{16,8},{20,12},{24,28},{28,24},{1,5},{5... | collective-permute-start | bytes 393224 | tf_op jit(solution)/shard_map/ppermute | solution.py:51
  16.2 1.9 %collective-permute-start.2 = (bf16[2,128,256]{2,1,0:T(8,128)(2,1)S(1)}, bf16[2,128,256]{2,1,0:T(8,128)(2,1)S(1)}, u32[]{:S(2)}, u32[]{:S(2)}) collective-permute-start(bf16[2,128,256]{2,1,0:T(8,128)(2,1)S(1)} %shard_map.107), channel_id=1, source_target_pairs={{0,4},{4,0},{8,16},{12,20},{16,8},{20,12},{24,28},{28,24},{1,5},{5... | collective-permute-start | bytes 393224 | tf_op jit(solution)/shard_map/ppermute | solution.py:51
  17.2 1.4 %collective-permute-start.10 = (bf16[2,128,256]{2,1,0:T(8,128)(2,1)S(1)}, bf16[2,128,256]{2,1,0:T(8,128)(2,1)S(1)}, u32[]{:S(2)}, u32[]{:S(2)}) collective-permute-start(bf16[2,128,256]{2,1,0:T(8,128)(2,1)S(1)} %shard_map.116), channel_id=1, source_target_pairs={{0,4},{4,0},{8,12},{12,8},{16,24},{20,28},{24,16},{28,20},{1,5},{5... | collective-permute-start | bytes 393224 | tf_op jit(solution)/shard_map/ppermute | solution.py:51
  18.2 1.9 %collective-permute-start.3 = (bf16[2,128,256]{2,1,0:T(8,128)(2,1)S(1)}, bf16[2,128,256]{2,1,0:T(8,128)(2,1)S(1)}, u32[]{:S(2)}, u32[]{:S(2)}) collective-permute-start(bf16[2,128,256]{2,1,0:T(8,128)(2,1)S(1)} %shard_map.108), channel_id=1, source_target_pairs={{0,4},{4,0},{8,12},{12,8},{16,24},{20,28},{24,16},{28,20},{1,5},{5... | collective-permute-start | bytes 393224 | tf_op jit(solution)/shard_map/ppermute | solution.py:51
  19.6 1.9 %collective-permute-start.11 = (bf16[2,128,256]{2,1,0:T(8,128)(2,1)S(1)}, bf16[2,128,256]{2,1,0:T(8,128)(2,1)S(1)}, u32[]{:S(2)}, u32[]{:S(2)}) collective-permute-start(bf16[2,128,256]{2,1,0:T(8,128)(2,1)S(1)} %get-tuple-element.21.base_ref.refs_4_), channel_id=1, source_target_pairs={{0,4},{4,0},{8,12},{12,8},{16,24},{20,28},{24,16},{28,20},{1,5},{5... | collective-permute-start | bytes 393224 | tf_op jit(solution)/shard_map/ppermute | solution.py:51
  21.2 18.3 %collective-permute-start.5 = (bf16[2,128,256]{2,1,0:T(8,128)(2,1)S(1)}, bf16[2,128,256]{2,1,0:T(8,128)(2,1)S(1)}, u32[]{:S(2)}, u32[]{:S(2)}) collective-permute-start(bf16[2,128,256]{2,1,0:T(8,128)(2,1)S(1)} %get-tuple-element.18.base_ref.refs_4_), channel_id=1, source_target_pairs={{0,4},{4,0},{8,12},{12,8},{16,24},{20,28},{24,16},{28,20},{1,5},{5... | collective-permute-start | bytes 393224 | tf_op jit(solution)/shard_map/ppermute | solution.py:51
  21.6 18.0 %collective-permute-start.12 = (bf16[2,128,256]{2,1,0:T(8,128)(2,1)S(1)}, bf16[2,128,256]{2,1,0:T(8,128)(2,1)S(1)}, u32[]{:S(2)}, u32[]{:S(2)}) collective-permute-start(bf16[2,128,256]{2,1,0:T(8,128)(2,1)S(1)} %shard_map.118), channel_id=1, source_target_pairs={{0,4},{4,0},{8,16},{12,20},{16,8},{20,12},{24,28},{28,24},{1,5},{5... | collective-permute-start | bytes 393224 | tf_op jit(solution)/shard_map/ppermute | solution.py:51
  22.2 34.7 %collective-permute-start.19 = (bf16[8,128,256]{2,1,0:T(8,128)(2,1)S(1)}, bf16[8,128,256]{2,1,0:T(8,128)(2,1)S(1)}, u32[]{:S(2)}, u32[]{:S(2)}) collective-permute-start(bf16[8,128,256]{2,1,0:T(8,128)(2,1)S(1)} %bitcast.23), channel_id=1, source_target_pairs={{0,4},{4,0},{8,12},{12,8},{16,20},{20,16},{24,28},{28,24},{1,5},{5... | collective-permute-start | bytes 1572872 | tf_op jit(solution)/shard_map/ppermute | solution.py:43
  22.6 38.7 %collective-permute-start.16 = (bf16[8,128,256]{2,1,0:T(8,128)(2,1)S(1)}, bf16[8,128,256]{2,1,0:T(8,128)(2,1)S(1)}, u32[]{:S(2)}, u32[]{:S(2)}) collective-permute-start(bf16[8,128,256]{2,1,0:T(8,128)(2,1)S(1)} %bitcast.24), channel_id=1, source_target_pairs={{4,8},{12,16},{20,24},{8,4},{16,12},{24,20},{5,9},{13,17},{21,25},... | collective-permute-start | bytes 1572872 | tf_op jit(solution)/shard_map/ppermute | solution.py:78
  38.2 23.1 %collective-permute-start.18 = (bf16[8,128,256]{2,1,0:T(8,128)(2,1)S(1)}, bf16[8,128,256]{2,1,0:T(8,128)(2,1)}, u32[]{:S(2)}, u32[]{:S(2)}) collective-permute-start(bf16[8,128,256]{2,1,0:T(8,128)(2,1)S(1)} %bitcast.25), channel_id=1, source_target_pairs={{0,2},{2,0},{1,3},{3,1},{4,6},{6,4},{5,7},{7,5},{8,10},{10,8},{9,1... | collective-permute-start | bytes 1572872 | tf_op jit(solution)/shard_map/ppermute | solution.py:342
  39.5 1.4 %collective-permute-start.6 = (bf16[2,128,256]{2,1,0:T(8,128)(2,1)S(1)}, bf16[2,128,256]{2,1,0:T(8,128)(2,1)S(1)}, u32[]{:S(2)}, u32[]{:S(2)}) collective-permute-start(bf16[2,128,256]{2,1,0:T(8,128)(2,1)S(1)} %shard_map.112), channel_id=1, source_target_pairs={{0,4},{4,0},{8,16},{12,20},{16,8},{20,12},{24,28},{28,24},{1,5},{5... | collective-permute-start | bytes 393224 | tf_op jit(solution)/shard_map/ppermute | solution.py:51
  39.6 7.5 %collective-permute-start.13 = (bf16[2,128,256]{2,1,0:T(8,128)(2,1)S(1)}, bf16[2,128,256]{2,1,0:T(8,128)(2,1)S(1)}, u32[]{:S(2)}, u32[]{:S(2)}) collective-permute-start(bf16[2,128,256]{2,1,0:T(8,128)(2,1)S(1)} %shard_map.119), channel_id=1, source_target_pairs={{0,8},{4,12},{8,0},{12,4},{16,20},{20,16},{24,28},{28,24},{1,9},{5... | collective-permute-start | bytes 393224 | tf_op jit(solution)/shard_map/ppermute | solution.py:51
  40.9 20.4 %collective-permute-start.17 = (bf16[4,128,256]{2,1,0:T(8,128)(2,1)}, bf16[4,128,256]{2,1,0:T(8,128)(2,1)S(1)}, u32[]{:S(2)}, u32[]{:S(2)}) collective-permute-start(bf16[4,128,256]{2,1,0:T(8,128)(2,1)} %slice_bitcast_fusion), channel_id=1, source_target_pairs={{0,1},{1,0},{2,3},{3,2},{4,5},{5,4},{6,7},{7,6},{8,9},{9,8},{10,11... | collective-permute-start | bytes 786440 | tf_op jit(solution)/shard_map/ppermute | solution.py:336
  47.1 4.7 %collective-permute-start.7 = (bf16[2,128,256]{2,1,0:T(8,128)(2,1)S(1)}, bf16[2,128,256]{2,1,0:T(8,128)(2,1)S(1)}, u32[]{:S(2)}, u32[]{:S(2)}) collective-permute-start(bf16[2,128,256]{2,1,0:T(8,128)(2,1)S(1)} %shard_map.113), channel_id=1, source_target_pairs={{0,8},{4,12},{8,0},{12,4},{16,20},{20,16},{24,28},{28,24},{1,9},{5... | collective-permute-start | bytes 393224 | tf_op jit(solution)/shard_map/ppermute | solution.py:51
  51.7 13.6 %collective-permute-start.15 = (bf16[2,128,256]{2,1,0:T(8,128)(2,1)}, bf16[2,128,256]{2,1,0:T(8,128)(2,1)}, u32[]{:S(2)}, u32[]{:S(2)}) collective-permute-start(bf16[2,128,256]{2,1,0:T(8,128)(2,1)} %get-tuple-element.25), channel_id=1, source_target_pairs={{0,4},{4,0},{8,12},{12,8},{16,20},{20,16},{24,28},{28,24},{1,5},{5... | collective-permute-start | bytes 393224 | tf_op jit(solution)/shard_map/ppermute | solution.py:43
  55.3 3.2 %copy-start.1 = (bf16[1,4,2,256,256]{4,3,2,1,0:T(8,128)(2,1)S(1)}, bf16[1,4,2,256,256]{4,3,2,1,0:T(8,128)(2,1)}, u32[]{:S(2)}) copy-start(bf16[1,4,2,256,256]{4,3,2,1,0:T(8,128)(2,1)} %param.12) | copy-start | bytes 3145732
  57.8 7.6 %collective-permute-start.14 = (bf16[2,128,256]{2,1,0:T(8,128)(2,1)}, bf16[2,128,256]{2,1,0:T(8,128)(2,1)}, u32[]{:S(2)}, u32[]{:S(2)}) collective-permute-start(bf16[2,128,256]{2,1,0:T(8,128)(2,1)} %get-tuple-element.24), channel_id=1, source_target_pairs={{0,4},{4,0},{8,12},{12,8},{16,20},{20,16},{24,28},{28,24},{1,5},{5... | collective-permute-start | bytes 393224 | tf_op jit(solution)/shard_map/ppermute | solution.py:43
  60.8 1.5 %copy-start.7 = (bf16[1,4,2,256,256]{4,3,2,1,0:T(8,128)(2,1)S(1)}, bf16[1,4,2,256,256]{4,3,2,1,0:T(8,128)(2,1)}, u32[]{:S(2)}) copy-start(bf16[1,4,2,256,256]{4,3,2,1,0:T(8,128)(2,1)} %param.16) | copy-start | bytes 3145732
  62.3 3.0 %copy-start.12 = (bf16[2,128,256]{2,1,0:T(8,128)(2,1)S(1)}, bf16[2,128,256]{2,1,0:T(8,128)(2,1)}, u32[]{:S(2)}) copy-start(bf16[2,128,256]{2,1,0:T(8,128)(2,1)} %copy-done.11) | copy-start | bytes 393220
  (10 other events, 10.2 us)

commit v2 on v0

v2 whole, which is shorter than its diff:
```python
import functools

import jax
import jax.numpy as jnp
from jax import lax
from jax.experimental import pallas as pl
from jax.experimental.pallas import tpu as pltpu
from jax.sharding import PartitionSpec as P

BF16 = jnp.bfloat16
F32 = jnp.float32
VMEM = pltpu.MemorySpace.VMEM
HBM = pltpu.MemorySpace.HBM
GROUPS = 2


def dot(x, y):
    return jnp.dot(x, y, preferred_element_type=F32)


def call(kernel, outs, operands, hbm=(), after=(), scratch=(), products=1):
    spec = pl.BlockSpec(memory_space=pltpu.VMEM)
    anywhere = pl.BlockSpec(memory_space=pl.ANY)
    held = [pltpu.with_memory_space_constraint(x, VMEM) for x in operands]
    far = [pltpu.with_memory_space_constraint(x, HBM) for x in hbm]
    count = len(held) + len(far)

    def body(*refs):
        kernel(*refs[:count], *refs[count + len(after) :])

    return pl.pallas_call(
        body,
        out_shape=[VMEM(shape, dtype) for shape, dtype in outs],
        in_specs=[spec] * len(held) + [anywhere] * (len(far) + len(after)),
        out_specs=[spec] * len(outs),
        scratch_shapes=list(scratch),
        compiler_params=pltpu.CompilerParams(vmem_limit_bytes=8 << 20),
        cost_estimate=pl.CostEstimate(
            flops=products * 2 * 128 * 256 * 256, bytes_accessed=1 << 18, transcendentals=0
        ),
    )(*held, *far, *after)


def place():
    height = lax.axis_index("elev")
    return height // 2, lax.rem(height, 2)


def swap_cores(value):
    count = lax.axis_size("elev")
    return lax.ppermute(value, "elev", [(i, i ^ 1) for i in range(count)])


def swap_chips(value, low):
    pairs = []
    for i in range(lax.axis_size("elev")):
        chip = i // 2
        pairs.append((i, i + 2 if chip == low else i - 2 if chip == low + 1 else i ^ 1))
    return lax.ppermute(value, "elev", pairs)


def local(
    resid,
    direction,
    diag_blocks,
    lower_blocks,
    upper_blocks,
    inv_pivots,
    down_coupling,
    valley_coupling,
    coupled_column,
):
    _, valleys, downs, rows, size = resid.shape
    chains = valleys * downs
    half = chains // 2
    groups = GROUPS
    width = half // groups
    chips = lax.axis_size("elev") // 2
    vectors = lambda x: x.reshape(chains, rows, size)
    blocks = lambda x: x.reshape(chains, size, size)
    rhs, current = vectors(resid), vectors(direction)
    square = ((half, size, size), BF16)
    packed = ((half, size + rows, size), BF16)
    message = ((width, rows, size), BF16)
    every_block = ((chains, size, size), BF16)
    every_vector = ((chains, rows, size), BF16)
    every_sum = ((chains, rows, size), F32)
    spans = [slice(g * width, (g + 1) * width) for g in range(groups)]

    beside = swap_cores(current)

    def first(l_ref, p_ref, r_ref, d_ref, keep_ref, send_ref, lower_v, pivot_v, dir_v, rhs_v, sem):
        _, core = place()
        copies = []
        for side in (1 - core, core):
            part = pl.ds(side * half, half)
            for source, target in ((p_ref, pivot_v), (l_ref, lower_v), (r_ref, rhs_v)):
                copies.append(
                    pltpu.make_async_copy(
                        source.at[part], target.at[part], sem.at[len(copies)]
                    )
                )
        copies.append(pltpu.make_async_copy(d_ref, dir_v, sem.at[len(copies)]))
        for copy in copies:
            copy.start()
        for number, (ref, side) in enumerate(((send_ref, 1 - core), (keep_ref, core))):
            for copy in copies[3 * number : 3 * number + 3]:
                copy.wait()
            for i in range(half):
                block = pivot_v[side * half + i]
                ref[i, :size] = (-dot(lower_v[side * half + i], block)).astype(BF16)
                ref[i, size:] = dot(rhs_v[side * half + i], block).astype(BF16)
        copies[-1].wait()

    keep1, send1, lower_v, pivot_v, dir_v = call(
        first,
        [packed, packed, every_block, every_block, every_vector],
        [],
        hbm=[blocks(lower_blocks), blocks(inv_pivots), rhs, current],
        scratch=[pltpu.VMEM((chains, rows, size), BF16), pltpu.SemaphoreType.DMA((7,))],
        products=3 * chains,
    )
    recv1 = swap_cores(send1)

    def give(which, core, dir_ref, beside_ref, at, out_ref):
        @pl.when(core == which)
        def _():
            out_ref[...] = dir_ref[pl.ds(core * half + at, width)]

        @pl.when(core != which)
        def _():
            out_ref[...] = beside_ref[pl.ds(core * half + at, width)]

    def begin(keep_ref, recv_ref, dir_ref, beside_ref, start_ref, *out_refs):
        chip, core = place()

        def write(bottom, top):
            for i in range(half):
                start_ref[i] = (
                    top[i, size:].astype(F32) + dot(bottom[i, size:], top[i, :size])
                ).astype(BF16)

        pl.when(core == 0)(lambda: write(keep_ref, recv_ref))
        pl.when(core == 1)(lambda: write(recv_ref, keep_ref))
        for out_ref, span in zip(out_refs, spans):

            @pl.when(chip == 0)
            def _():
                out_ref[...] = start_ref[span]

            @pl.when(chip != 0)
            def _():
                give(0, core, dir_ref, beside_ref, span.start, out_ref)

    start, *fronts = call(
        begin,
        [((half, rows, size), BF16)] + [message] * groups,
        [keep1, recv1, dir_v, beside],
        products=half,
    )

    def second(p_ref, u_ref, keep_ref, send_ref, upper_v, sem):
        _, core = place()
        copies = []
        for side in (1 - core, core):
            part = pl.ds(side * half, half)
            copies.append(
                pltpu.make_async_copy(u_ref.at[part], upper_v.at[part], sem.at[len(copies)])
            )
        for copy in copies:
            copy.start()
        for copy, ref, side in zip(copies, (send_ref, keep_ref), (1 - core, core)):
            copy.wait()
            for i in range(half):
                at = side * half + i
                ref[i] = (-dot(upper_v[at], p_ref[at])).astype(BF16)

    keep2, send2, upper_v = call(
        second,
        [square, square, every_block],
        [pivot_v],
        hbm=[blocks(upper_blocks)],
        scratch=[pltpu.SemaphoreType.DMA((2,))],
        products=2 * chains,
    )

    def join(keep_ref, recv_ref, through_ref, bottom_ref):
        _, core = place()

        def write(bottom, top):
            bottom_ref[...] = bottom[...]
            for i in range(half):
                through_ref[i] = dot(bottom[i, :size], top[i, :size]).astype(BF16)

        pl.when(core == 0)(lambda: write(keep_ref, recv_ref))
        pl.when(core == 1)(lambda: write(recv_ref, keep_ref))

    through, bottom = call(join, [square, packed], [keep1, recv1], products=2 * half)
    recv2 = swap_cores(send2)

    def back(keep_ref, recv_ref, back_ref, low_ref, high_ref):
        _, core = place()

        def write(bottom, top):
            low_ref[...] = bottom[...]
            high_ref[...] = top[...]
            for i in range(half):
                back_ref[i] = dot(top[i], bottom[i]).astype(BF16)

        pl.when(core == 0)(lambda: write(keep_ref, recv_ref))
        pl.when(core == 1)(lambda: write(recv_ref, keep_ref))

    backward, back_low, back_high = call(
        back, [square] * 3, [keep2, recv2], products=2 * half
    )

    def near(dir_ref, beside_ref, lower_ref, upper_ref, diag_ref, out_ref, diag_v, sem):
        _, core = place()
        copy = pltpu.make_async_copy(diag_ref, diag_v, sem.at[0])
        copy.start()

        def write(block_ref):
            for i in range(chains):
                out_ref[i] = dot(beside_ref[i], block_ref[i])

        pl.when(core == 0)(lambda: write(upper_ref))
        pl.when(core == 1)(lambda: write(lower_ref))
        copy.wait()
        for i in range(chains):
            out_ref[i] += dot(dir_ref[i], diag_v[i])

    (near_sum,) = call(
        near,
        [every_sum],
        [dir_v, beside, lower_v, upper_v],
        hbm=[blocks(diag_blocks)],
        scratch=[pltpu.VMEM((chains, size, size), BF16), pltpu.SemaphoreType.DMA((1,))],
        products=2 * chains,
    )

    def advance(span, low, in_ref, start_ref, through_ref, dir_ref, beside_ref, out_ref):
        chip, core = place()
        at = span.start

        @pl.when(chip == low)
        def _():
            for i in range(width):
                out_ref[i] = (
                    start_ref[at + i].astype(F32) + dot(in_ref[i], through_ref[at + i])
                ).astype(BF16)

        @pl.when(chip != low)
        def _():
            give(0, core, dir_ref, beside_ref, at, out_ref)

    heard_up = [[] for _ in spans]
    for low in range(chips - 1):
        for g, span in enumerate(spans):
            arrived = swap_chips(fronts[g], low)
            heard_up[g].append(arrived)
            if low < chips - 2:
                (fronts[g],) = call(
                    functools.partial(advance, span, low + 1),
                    [message],
                    [arrived, start, through, dir_v, beside],
                    after=[near_sum] if low == 0 and g == 0 else [],
                    products=width,
                )

    downs_count, valley_count = lax.axis_size("down"), lax.axis_size("valley")
    rim = lax.ppermute(
        direction[0, :, -1],
        "down",
        [(i, (i + 1) % downs_count) for i in range(downs_count)],
    )
    others = [
        lax.ppermute(
            current, "valley", [(i, (i + by) % valley_count) for i in range(valley_count)]
        )
        for by in range(1, valley_count)
    ]

    def far(*refs):
        dir_ref, sum_ref, rim_ref = refs[:3]
        others_refs = refs[3 : 2 + valley_count]
        down_ref, valley_ref, column_ref, out_ref = refs[2 + valley_count : 6 + valley_count]
        partner_ref, down_v, valley_v, column_s, sem = refs[6 + valley_count :]
        mine = lax.axis_index("valley")
        edge = lax.axis_index("down")
        copies = [
            pltpu.make_async_copy(source, target, sem.at[i])
            for i, (source, target) in enumerate(
                ((column_ref, column_s), (down_ref, down_v), (valley_ref, valley_v))
            )
        ]
        for copy in copies:
            copy.start()
        copies[0].wait()
        for i in range(chains):
            column = column_s[i // downs, i % downs]
            owner = column // valleys
            spot = lax.rem(column, valleys) * downs + i % downs
            behind = lax.rem(mine - owner + valley_count, valley_count)

            @pl.when(behind == 0)
            def _():
                partner_ref[i] = dir_ref[spot]

            for by in range(1, valley_count):

                @pl.when(behind == by)
                def _():
                    partner_ref[i] = others_refs[by - 1][spot]

        copies[1].wait()
        for i in range(chains):
            if i % downs:
                out_ref[i] = sum_ref[i] + dot(dir_ref[i - 1], down_v[i])

        @pl.when(edge > 0)
        def _():
            for i in range(0, chains, downs):
                out_ref[i] = sum_ref[i] + dot(rim_ref[i // downs], down_v[i])

        @pl.when(edge == 0)
        def _():
            for i in range(0, chains, downs):
                out_ref[i] = sum_ref[i]

        copies[2].wait()
        for i in range(chains):
            out_ref[i] += dot(partner_ref[i], valley_v[i])

    (far_sum,) = call(
        far,
        [every_sum],
        [dir_v, near_sum, rim] + others,
        hbm=[blocks(down_coupling), blocks(valley_coupling), coupled_column[0]],
        scratch=[
            pltpu.VMEM((chains, rows, size), BF16),
            pltpu.VMEM((chains, size, size), BF16),
            pltpu.VMEM((chains, size, size), BF16),
            pltpu.SMEM((valleys, downs), jnp.int32),
            pltpu.SemaphoreType.DMA((3,)),
        ],
        products=2 * chains,
    )

    def turn(span, *refs):
        heard_refs = refs[: chips - 1]
        start_ref, through_ref, bottom_ref, low_ref, dir_ref, beside_ref = refs[chips - 1 : -4]
        top_ref, base_ref, out_ref, in_ref = refs[-4:]
        chip, core = place()
        at = span.start

        @pl.when(chip == 0)
        def _():
            in_ref[...] = jnp.zeros_like(in_ref)

        for low in range(chips - 1):

            @pl.when(chip == low + 1)
            def _():
                in_ref[...] = heard_refs[low][...]

        for i in range(width):
            arrived = in_ref[i]
            top = (start_ref[at + i].astype(F32) + dot(arrived, through_ref[at + i])).astype(BF16)
            base = bottom_ref[at + i, size:].astype(F32) + dot(arrived, bottom_ref[at + i, :size])
            top_ref[i] = top
            base_ref[i] = (base.astype(BF16).astype(F32) + dot(top, low_ref[at + i])).astype(BF16)

        @pl.when(chip == chips - 1)
        def _():
            out_ref[...] = base_ref[...]

        @pl.when(chip != chips - 1)
        def _():
            give(1, core, dir_ref, beside_ref, at, out_ref)

    tops, bases, solved = [], [], []
    for g, span in enumerate(spans):
        top, base, out = call(
            functools.partial(turn, span),
            [message] * 3,
            heard_up[g] + [start, through, bottom, back_low, dir_v, beside],
            scratch=[pltpu.VMEM(*message)],
            products=3 * width,
        )
        tops.append(top)
        bases.append(base)
        solved.append(out)

    def retreat(span, low, in_ref, base_ref, back_ref, dir_ref, beside_ref, out_ref):
        chip, core = place()
        at = span.start

        @pl.when(chip == low)
        def _():
            for i in range(width):
                out_ref[i] = (
                    base_ref[i].astype(F32) + dot(in_ref[i], back_ref[at + i])
                ).astype(BF16)

        @pl.when(chip != low)
        def _():
            give(1, core, dir_ref, beside_ref, at, out_ref)

    heard_down = [[] for _ in spans]
    for low in range(chips - 2, -1, -1):
        for g, span in enumerate(spans):
            arrived = swap_chips(solved[g], low)
            heard_down[g].insert(0, arrived)
            if low > 0:
                (solved[g],) = call(
                    functools.partial(retreat, span, low),
                    [message],
                    [arrived, bases[g], backward, dir_v, beside],
                    after=[far_sum] if low == chips - 2 and g == 0 else [],
                    products=width,
                )

    def finish(span, *refs):
        up_refs, down_refs = refs[: chips - 1], refs[chips - 1 : 2 * chips - 2]
        top_ref, base_ref, back_ref, high_ref = refs[2 * chips - 2 : -4]
        keep_ref, own_ref, send_ref, in_ref = refs[-4:]
        chip, core = place()
        at = span.start
        sent_halo = send_ref.at[pl.ds(width, width)]

        @pl.when(chip == chips - 1)
        def _():
            in_ref[...] = jnp.zeros_like(in_ref)

        for low in range(chips - 1):

            @pl.when(chip == low)
            def _():
                in_ref[...] = down_refs[low][...]

        for which, mine, other in ((0, own_ref, sent_halo), (1, sent_halo, own_ref)):

            @pl.when(core == which)
            def _():
                @pl.when(chip == 0)
                def _():
                    mine[...] = jnp.zeros_like(mine)

                @pl.when(chip == chips - 1)
                def _():
                    other[...] = jnp.zeros_like(other)

                for low in range(chips - 1):

                    @pl.when(chip == low + 1)
                    def _():
                        mine[...] = down_refs[low][...]

                    @pl.when(chip == low)
                    def _():
                        other[...] = up_refs[low][...]

        for i in range(width):
            arrived = in_ref[i]
            low = (base_ref[i].astype(F32) + dot(arrived, back_ref[at + i])).astype(BF16)
            high = (top_ref[i].astype(F32) + dot(arrived, high_ref[at + i])).astype(BF16)

            @pl.when(core == 0)
            def _():
                keep_ref[i] = low
                send_ref[i] = high

            @pl.when(core == 1)
            def _():
                keep_ref[i] = high
                send_ref[i] = low

    def final(span, *refs):
        keep_ref, own_ref, recv_ref, sum_ref, lower_ref, upper_ref = refs[:6]
        solved_ref, image_ref, total_ref, sem = refs[-4:]
        _, core = place()
        at = span.start
        copies = []
        for side, source in ((core, keep_ref), (1 - core, recv_ref.at[pl.ds(0, width)])):
            copies.append(
                pltpu.make_async_copy(
                    source, solved_ref.at[pl.ds(side * half + at, width)], sem.at[len(copies)]
                )
            )
            copies[-1].start()

        def write(block_ref):
            for number, side in enumerate((core, 1 - core)):
                base = side * half + at
                for i in range(width):
                    halo = own_ref[i] if number == 0 else recv_ref[width + i]
                    total_ref[number * width + i] = sum_ref[base + i] + dot(
                        halo, block_ref[base + i]
                    )

        pl.when(core == 0)(lambda: write(lower_ref))
        pl.when(core == 1)(lambda: write(upper_ref))
        for number, side in enumerate((core, 1 - core)):
            copies.append(
                pltpu.make_async_copy(
                    total_ref.at[pl.ds(number * width, width)],
                    image_ref.at[pl.ds(side * half + at, width)],
                    sem.at[len(copies)],
                )
            )
            copies[-1].start()
        for copy in copies:
            copy.wait()

    spec = pl.BlockSpec(memory_space=pltpu.VMEM)
    anywhere = pl.BlockSpec(memory_space=pl.ANY)
    outputs = []
    for g, span in enumerate(spans):
        keep, own, send = call(
            functools.partial(finish, span),
            [message, message, ((2 * width, rows, size), BF16)],
            heard_up[g] + heard_down[g] + [tops[g], bases[g], backward, back_high],
            scratch=[pltpu.VMEM(*message)],
            products=2 * width,
        )
        operands = [keep, own, swap_cores(send), far_sum, lower_v, upper_v]
        operands = [pltpu.with_memory_space_constraint(x, VMEM) for x in operands]
        outputs = pl.pallas_call(
            functools.partial(final, span),
            out_shape=[HBM(*every_vector), HBM(*every_sum)],
            in_specs=[spec] * len(operands) + [anywhere] * len(outputs),
            out_specs=[anywhere] * 2,
            input_output_aliases={len(operands) + i: i for i in range(len(outputs))},
            scratch_shapes=[
                pltpu.VMEM((2 * width, rows, size), F32),
                pltpu.SemaphoreType.DMA((4,)),
            ],
            compiler_params=pltpu.CompilerParams(vmem_limit_bytes=8 << 20),
            cost_estimate=pl.CostEstimate(
                flops=4 * width * rows * size * size, bytes_accessed=1 << 20, transcendentals=0
            ),
        )(*operands, *outputs)
    preconditioned, image = outputs
    return (preconditioned.reshape(resid.shape), image.reshape(resid.shape))


def solution(mesh):
    spec = P("elev", "valley", "down", None, None)
    in_specs = (spec,) * 8 + (P("elev", "valley", "down"),)
    return jax.shard_map(
        local, mesh=mesh, in_specs=in_specs, out_specs=(spec, spec), check_vma=False
    )
```

time: 253 us -> 57 us (0.23)
  waiting for transfers between devices: 140 us -> 3.07 us
  starting transfers between devices: 60.6 us -> 27.3 us
  Pallas kernels: 0 us -> 18.3 us
  local copies, waits for them, and re-layouts: 21.8 us -> 6.7 us
  matrix products: 15 us -> 0 us
  between operations: 14.1 us -> 0.89 us
    ppermute x19, waiting for transfers between devices: 128 us -> 3.07 us  [the longest x12 2.06 us: swap_chips(): return lax.ppermute(value, 'elev', pairs)]
    ppermute x19, starting transfers between devices: 60.5 us -> 27.3 us  [the longest x12 17 us: swap_chips(): return lax.ppermute(value, 'elev', pairs)]
    pallas_call x0 -> x21, Pallas kernels: none -> 18.3 us  [the longest x19 16.2 us: call(): pl.pallas_call(body, out_shape=[VMEM(shape, dtype) for shape, dtype in ou...]
    dot_general x8 -> x0, matrix products: 15 us -> none  [the longest x7 12.9 us: apply_blocks(): jnp.einsum('bqrs,bqst->bqrt', vectors, blocks, preferred_element_type=jnp...]
    another operation x18 -> x0, local copies, waits for them, and re-layouts: 14.9 us -> none
    all_gather x1 -> x0, waiting for transfers between devices: 12.6 us -> none  [local(): piece = lax.all_gather(current, 'valley', axis=0, tiled=True)]
    cond x2 -> x0, local copies, waits for them, and re-layouts: 3.75 us -> none
  transfers between devices with their start and end apart: 20 -> 19, of which waited for: 18 -> 5; matrix products, arithmetic and copies ran while one was open for 4% -> 4% of each run, Pallas kernels for 0% -> 27%
where the time goes in v2:
time: 57 us; the launch traced here: 56.3 us
  starting transfers between devices  27.3 us (48%)
  Pallas kernels  18.3 us (32%)
  local copies, waits for them, and re-layouts  6.7 us (12%)
  waiting for transfers between devices  3.07 us (5%)
  between operations  0.89 us (2%)
    ppermute x12, starting transfers between devices, swap_chips(): return lax.ppermute(value, 'elev', pairs)  17 us
    pallas_call x19, Pallas kernels, call(): pl.pallas_call(body, out_shape=[VMEM(shape, dtype) for shape, dtype in ou...  16.2 us
    ppermute x5, starting transfers between devices, swap_cores(): return lax.ppermute(value, 'elev', [(i, i ^ 1) for i in range(count)])  7.65 us
    unnamed x38, local copies, waits for them, and re-layouts  4.37 us
    pallas_call x2, Pallas kernels, local(): pl.pallas_call(functools.partial(final, span), out_shape=[HBM(*every_vect...  2.12 us
    ppermute x12, waiting for transfers between devices, swap_chips(): return lax.ppermute(value, 'elev', pairs)  2.06 us
    squeeze x1, local copies, waits for them, and re-layouts, local(): direction[0, :, -1]  1.67 us
    ppermute x1, starting transfers between devices, local(): lax.ppermute(direction[0, :, -1], 'down', [(i, (i + 1) % downs_count) for...  1.36 us
  transfers between devices with their start and end apart: 19, of which 5 were waited for; matrix products, arithmetic and copies ran while one was open for 4% of the time, Pallas kernels for 27%

profile of v2, /device:TPU:1, one launch (start us, length us, event | category | flops | bytes accessed | tf_op | source)
XLA Modules:
  0.0 56.3 jit_solution(14328501591857355689)
XLA Ops:
  0.6 2.1 %shard_map.104 = (bf16[4,384,256]{2,1,0:T(8,128)(2,1)S(1)}, bf16[4,384,256]{2,1,0:T(8,128)(2,1)S(1)}, bf16[8,256,256]{2,1,0:T(8,128)(2,1)S(1)}, bf16[8,256,256]{2,1,0:T(8,128)(2,1)S(1)}, bf16[8,128,256]{2,1,0:T(8,128)(2,1)S(1)}) custom-call(bf16[8,256,256]{2,1,0:T(8,128)(2,1)} %bitcast.15, bf16[8,256,256]{2,1,0:T(8,128)(2,1)} %bitcast.16, ...), custom_call_target="tpu_custom_call" | custom-call | flops 402653184 | bytes 262144 | tf_op jit(solution)/shard_map/pallas_call | solution.py:31
  3.3 1.7 %shard_map.109 = (bf16[4,256,256]{2,1,0:T(8,128)(2,1)S(1)}, bf16[4,256,256]{2,1,0:T(8,128)(2,1)S(1)}, bf16[8,256,256]{2,1,0:T(8,128)(2,1)S(1)}) custom-call(bf16[8,256,256]{2,1,0:T(8,128)(2,1)S(1)} %get-tuple-element.41.refs_0_, bf16[8,256,256]{2,1,0:T(8,128)(2,1)} %bitcast.21), custom_call_target="tpu_custom_call" | custom-call | flops 268435456 | bytes 262144 | tf_op jit(solution)/shard_map/pallas_call | solution.py:31
  5.2 0.9 %collective-permute-done.1.refs_3_.refs_4_.refs_8_.refs_1_ = bf16[8,128,256]{2,1,0:T(8,128)(2,1)S(1)} collective-permute-done((bf16[8,128,256]{2,1,0:T(8,128)(2,1)}, bf16[8,128,256]{2,1,0:T(8,128)(2,1)S(1)}, u32[]{:S(2)}, u32[]{:S(2)}) %collective-permute-start.1) | collective-permute-done | bytes 524320 | tf_op jit(solution)/shard_map/ppermute | solution.py:51
  6.3 2.5 %collective-permute-start.2 = (bf16[2,128,256]{2,1,0:T(8,128)(2,1)S(1)}, bf16[2,128,256]{2,1,0:T(8,128)(2,1)S(1)}, u32[]{:S(2)}, u32[]{:S(2)}) collective-permute-start(bf16[2,128,256]{2,1,0:T(8,128)(2,1)S(1)} %get-tuple-element.37), channel_id=1, source_target_pairs={{0,8},{4,12},{8,0},{12,4},{16,20},{20,16},{24,28},{28,24},{1,9},{5... | collective-permute-start | bytes 393224 | tf_op jit(solution)/shard_map/ppermute | solution.py:59
  8.9 1.3 %collective-permute-start.11 = (bf16[8,128,256]{2,1,0:T(8,128)(2,1)}, bf16[8,128,256]{2,1,0:T(8,128)(2,1)}, u32[]{:S(2)}, u32[]{:S(2)}) collective-permute-start(bf16[8,128,256]{2,1,0:T(8,128)(2,1)} %bitcast.3.refs_3_), channel_id=1, source_target_pairs={{0,2},{2,0},{1,3},{3,1},{4,6},{6,4},{5,7},{7,5},{8,10},{10,8},{9,1... | collective-permute-start | bytes 1572872 | tf_op jit(solution)/shard_map/ppermute | solution.py:277
  10.2 1.5 %shard_map.115.refs_1_.refs_5_ = f32[8,128,256]{2,1,0:T(8,128)S(1)} custom-call(bf16[8,128,256]{2,1,0:T(8,128)(2,1)S(1)} %get-tuple-element.36.refs_2_.refs_3_.refs_7_.refs_0_, bf16[8,128,256]{2,1,0:T(8,128)(2,1)S(1)} %collective-permute-done.1.refs_3_.refs_4_.refs_8_.refs_1_, bf16[8,256,256]{2,1,0:T(8,128)(2,1)S(1)} %get-tuple-element.53.refs_2_.refs_4_, ...), custom_call_target="tpu_custom_call" | custom-call | flops 268435456 | bytes 262144 | tf_op jit(solution)/shard_map/pallas_call | solution.py:31
  12.4 1.5 %collective-permute-start.3 = (bf16[2,128,256]{2,1,0:T(8,128)(2,1)S(1)}, bf16[2,128,256]{2,1,0:T(8,128)(2,1)S(1)}, u32[]{:S(2)}, u32[]{:S(2)}) collective-permute-start(bf16[2,128,256]{2,1,0:T(8,128)(2,1)S(1)} %shard_map.107), channel_id=1, source_target_pairs={{0,4},{4,0},{8,16},{12,20},{16,8},{20,12},{24,28},{28,24},{1,5},{5... | collective-permute-start | bytes 393224 | tf_op jit(solution)/shard_map/ppermute | solution.py:59
  13.9 1.4 %collective-permute-done.12.refs_0_ = bf16[2,128,256]{2,1,0:T(8,128)(2,1)S(1)} collective-permute-done((bf16[2,128,256]{2,1,0:T(8,128)(2,1)S(1)}, bf16[2,128,256]{2,1,0:T(8,128)(2,1)S(1)}, u32[]{:S(2)}, u32[]{:S(2)}) %collective-permute-start.12) | collective-permute-done | bytes 131104 | tf_op jit(solution)/shard_map/ppermute | solution.py:59
  16.2 1.7 %slice_bitcast_fusion = bf16[4,128,256]{2,1,0:T(8,128)(2,1)} fusion(bf16[1,4,2,128,256]{4,3,2,1,0:T(8,128)(2,1)} %param.10), kind=kLoop, calls=%fused_computation | loop fusion | bytes 524288 | tf_op jit(solution)/shard_map/squeeze | solution.py:272
  17.9 1.4 %collective-permute-start.10 = (bf16[4,128,256]{2,1,0:T(8,128)(2,1)}, bf16[4,128,256]{2,1,0:T(8,128)(2,1)}, u32[]{:S(2)}, u32[]{:S(2)}) collective-permute-start(bf16[4,128,256]{2,1,0:T(8,128)(2,1)} %slice_bitcast_fusion), channel_id=1, source_target_pairs={{0,1},{1,0},{2,3},{3,2},{4,5},{5,4},{6,7},{7,6},{8,9},{9,8},{10,11... | collective-permute-start | bytes 786440 | tf_op jit(solution)/shard_map/ppermute | solution.py:271
  20.7 1.1 %shard_map.119 = (bf16[2,128,256]{2,1,0:T(8,128)(2,1)S(1)}, bf16[2,128,256]{2,1,0:T(8,128)(2,1)S(1)}, bf16[2,128,256]{2,1,0:T(8,128)(2,1)}) custom-call(bf16[2,128,256]{2,1,0:T(8,128)(2,1)S(1)} %collective-permute-done.12.refs_0_, bf16[2,128,256]{2,1,0:T(8,128)(2,1)S(1)} %collective-permute-done.13.refs_0_.refs_1_, ...), custom_call_target="tpu_custom_call" | custom-call | flops 100663296 | bytes 262144 | tf_op jit(solution)/shard_map/pallas_call | solution.py:31
  23.3 1.0 %shard_map.111 = (bf16[2,128,256]{2,1,0:T(8,128)(2,1)S(1)}, bf16[2,128,256]{2,1,0:T(8,128)(2,1)S(1)}, bf16[2,128,256]{2,1,0:T(8,128)(2,1)}) custom-call(bf16[2,128,256]{2,1,0:T(8,128)(2,1)S(1)} %collective-permute-done.2.refs_0_, bf16[2,128,256]{2,1,0:T(8,128)(2,1)S(1)} %collective-permute-done.3.refs_0_.refs_1_, ...), custom_call_target="tpu_custom_call" | custom-call | flops 100663296 | bytes 262144 | tf_op jit(solution)/shard_map/pallas_call | solution.py:31
  27.1 1.2 %copy-done.3 = f32[8,128,256]{2,1,0:T(8,128)S(1)} copy-done((f32[8,128,256]{2,1,0:T(8,128)S(1)}, f32[8,128,256]{2,1,0:T(8,128)}, u32[]{:S(2)}) %copy-start.3) | copy-done | bytes 1048600
  28.3 3.0 %shard_map.116.refs_5_.refs_3_ = f32[8,128,256]{2,1,0:T(8,128)S(1)} custom-call(bf16[8,128,256]{2,1,0:T(8,128)(2,1)S(1)} %get-tuple-element.36.refs_2_.refs_3_.refs_7_.refs_0_, f32[8,128,256]{2,1,0:T(8,128)S(1)} %copy-done.3, bf16[4,128,256]{2,1,0:T(8,128)(2,1)} %collective-permute-done.10.refs_2_, bf16[8,128,256]{2,1,0:T(8,128)(2,1)} %collective-permute-done.11.refs_3_, ...), custom_call_target="tpu_custom_call" | custom-call | flops 268435456 | bytes 262144 | tf_op jit(solution)/shard_map/pallas_call | solution.py:31
  31.3 1.0 %shard_map.120 = bf16[2,128,256]{2,1,0:T(8,128)(2,1)S(1)} custom-call(bf16[2,128,256]{2,1,0:T(8,128)(2,1)} %collective-permute-done.15.refs_0_.refs_5_, bf16[2,128,256]{2,1,0:T(8,128)(2,1)S(1)} %copy-done.7, bf16[4,256,256]{2,1,0:T(8,128)(2,1)S(1)} %get-tuple-element.47.refs_2_.refs_8_, ...), custom_call_target="tpu_custom_call" | custom-call | flops 33554432 | bytes 262144 | tf_op jit(solution)/shard_map/pallas_call | solution.py:31
  32.6 0.9 %shard_map.112 = bf16[2,128,256]{2,1,0:T(8,128)(2,1)S(1)} custom-call(bf16[2,128,256]{2,1,0:T(8,128)(2,1)} %collective-permute-done.6.refs_0_.refs_5_, bf16[2,128,256]{2,1,0:T(8,128)(2,1)S(1)} %copy-done.9, bf16[4,256,256]{2,1,0:T(8,128)(2,1)S(1)} %get-tuple-element.47.refs_2_.refs_8_, ...), custom_call_target="tpu_custom_call" | custom-call | flops 33554432 | bytes 262144 | tf_op jit(solution)/shard_map/pallas_call | solution.py:31
  33.9 7.9 %collective-permute-start.17 = (bf16[2,128,256]{2,1,0:T(8,128)(2,1)S(1)}, bf16[2,128,256]{2,1,0:T(8,128)(2,1)S(1)}, u32[]{:S(2)}, u32[]{:S(2)}) collective-permute-start(bf16[2,128,256]{2,1,0:T(8,128)(2,1)S(1)} %shard_map.121), channel_id=1, source_target_pairs={{0,8},{4,12},{8,0},{12,4},{16,20},{20,16},{24,28},{28,24},{1,9},{5... | collective-permute-start | bytes 393224 | tf_op jit(solution)/shard_map/ppermute | solution.py:59
  41.8 2.4 %collective-permute-start.8 = (bf16[2,128,256]{2,1,0:T(8,128)(2,1)S(1)}, bf16[2,128,256]{2,1,0:T(8,128)(2,1)S(1)}, u32[]{:S(2)}, u32[]{:S(2)}) collective-permute-start(bf16[2,128,256]{2,1,0:T(8,128)(2,1)S(1)} %shard_map.113), channel_id=1, source_target_pairs={{0,8},{4,12},{8,0},{12,4},{16,20},{20,16},{24,28},{28,24},{1,9},{5... | collective-permute-start | bytes 393224 | tf_op jit(solution)/shard_map/ppermute | solution.py:59
  44.3 1.4 %shard_map.122 = (bf16[2,128,256]{2,1,0:T(8,128)(2,1)S(1)}, bf16[2,128,256]{2,1,0:T(8,128)(2,1)S(1)}, bf16[4,128,256]{2,1,0:T(8,128)(2,1)S(1)}) custom-call(bf16[2,128,256]{2,1,0:T(8,128)(2,1)S(1)} %collective-permute-done.12.refs_0_, bf16[2,128,256]{2,1,0:T(8,128)(2,1)S(1)} %copy-done.5, bf16[2,128,256]{2,1,0:T(8,128)(2,1)S(1)} %copy-done.13, ...), custom_call_target="tpu_custom_call" | custom-call | flops 67108864 | bytes 262144 | tf_op jit(solution)/shard_map/pallas_call | solution.py:31
  45.7 5.4 %collective-permute-start.18 = (bf16[4,128,256]{2,1,0:T(8,128)(2,1)S(1)}, bf16[4,128,256]{2,1,0:T(8,128)(2,1)S(1)}, u32[]{:S(2)}, u32[]{:S(2)}) collective-permute-start(bf16[4,128,256]{2,1,0:T(8,128)(2,1)S(1)} %get-tuple-element.61), channel_id=1, source_target_pairs={{0,4},{4,0},{8,12},{12,8},{16,20},{20,16},{24,28},{28,24},{1,5},{5... | collective-permute-start | bytes 786440 | tf_op jit(solution)/shard_map/ppermute | solution.py:51
  51.1 1.4 %shard_map.114 = (bf16[2,128,256]{2,1,0:T(8,128)(2,1)S(1)}, bf16[2,128,256]{2,1,0:T(8,128)(2,1)S(1)}, bf16[4,128,256]{2,1,0:T(8,128)(2,1)S(1)}) custom-call(bf16[2,128,256]{2,1,0:T(8,128)(2,1)S(1)} %collective-permute-done.2.refs_0_, bf16[2,128,256]{2,1,0:T(8,128)(2,1)S(1)} %collective-permute-done.3.refs_0_.refs_1_, bf16[2,128,256]{2,1,0:T(8,128)(2,1)S(1)} %copy-done.11, ...), custom_call_target="tpu_custom_call" | custom-call | flops 67108864 | bytes 262144 | tf_op jit(solution)/shard_map/pallas_call | solution.py:31
  52.6 1.5 %collective-permute-start.9 = (bf16[4,128,256]{2,1,0:T(8,128)(2,1)S(1)}, bf16[4,128,256]{2,1,0:T(8,128)(2,1)S(1)}, u32[]{:S(2)}, u32[]{:S(2)}) collective-permute-start(bf16[4,128,256]{2,1,0:T(8,128)(2,1)S(1)} %get-tuple-element.52), channel_id=1, source_target_pairs={{0,4},{4,0},{8,12},{12,8},{16,20},{20,16},{24,28},{28,24},{1,5},{5... | collective-permute-start | bytes 786440 | tf_op jit(solution)/shard_map/ppermute | solution.py:51
  54.1 1.1 %shard_map.123 = (bf16[8,128,256]{2,1,0:T(8,128)(2,1)}, f32[8,128,256]{2,1,0:T(8,128)}) custom-call(bf16[2,128,256]{2,1,0:T(8,128)(2,1)S(1)} %get-tuple-element.59.refs_0_, bf16[2,128,256]{2,1,0:T(8,128)(2,1)S(1)} %get-tuple-element.60.refs_1_, bf16[4,128,256]{2,1,0:T(8,128)(2,1)S(1)} %collective-permute-done.18.refs_2_, ...), custom_call_target="tpu_custom_call" | custom-call | flops 67108864 | bytes 1048576 | tf_op jit(solution)/shard_map/pallas_call | solution.py:528
  55.2 1.1 %shard_map.124 = (bf16[8,128,256]{2,1,0:T(8,128)(2,1)}, f32[8,128,256]{2,1,0:T(8,128)}) custom-call(bf16[2,128,256]{2,1,0:T(8,128)(2,1)S(1)} %get-tuple-element.50.refs_0_, bf16[2,128,256]{2,1,0:T(8,128)(2,1)S(1)} %get-tuple-element.51.refs_1_, ...), custom_call_target="tpu_custom_call", output_to_operand_aliasing={{0}: (6, {}), {1}: (7, {})} | custom-call | flops 67108864 | bytes 1048576 | tf_op jit(solution)/shard_map/pallas_call | solution.py:528
  (75 shorter events, 9.0 us)
Async XLA Ops:
  2.8 3.3 %collective-permute-start = (bf16[4,384,256]{2,1,0:T(8,128)(2,1)S(1)}, bf16[4,384,256]{2,1,0:T(8,128)(2,1)S(1)}, u32[]{:S(2)}, u32[]{:S(2)}) collective-permute-start(bf16[4,384,256]{2,1,0:T(8,128)(2,1)S(1)} %get-tuple-element.35), channel_id=1, source_target_pairs={{0,4},{4,0},{8,12},{12,8},{16,20},{20,16},{24,28},{28,24},{1,5},{5... | collective-permute-start | bytes 2359304 | tf_op jit(solution)/shard_map/ppermute | solution.py:51
  2.9 3.2 %collective-permute-start.1 = (bf16[8,128,256]{2,1,0:T(8,128)(2,1)}, bf16[8,128,256]{2,1,0:T(8,128)(2,1)S(1)}, u32[]{:S(2)}, u32[]{:S(2)}) collective-permute-start(bf16[8,128,256]{2,1,0:T(8,128)(2,1)} %bitcast.3.refs_3_), channel_id=1, source_target_pairs={{0,4},{4,0},{8,12},{12,8},{16,20},{20,16},{24,28},{28,24},{1,5},{5... | collective-permute-start | bytes 1572872 | tf_op jit(solution)/shard_map/ppermute | solution.py:51
  5.0 14.9 %collective-permute-start.5 = (bf16[4,256,256]{2,1,0:T(8,128)(2,1)S(1)}, bf16[4,256,256]{2,1,0:T(8,128)(2,1)S(1)}, u32[]{:S(2)}, u32[]{:S(2)}) collective-permute-start(bf16[4,256,256]{2,1,0:T(8,128)(2,1)S(1)} %get-tuple-element.43), channel_id=1, source_target_pairs={{0,4},{4,0},{8,12},{12,8},{16,20},{20,16},{24,28},{28,24},{1,5},{5... | collective-permute-start | bytes 1572872 | tf_op jit(solution)/shard_map/ppermute | solution.py:51
  6.3 6.1 %collective-permute-start.2 = (bf16[2,128,256]{2,1,0:T(8,128)(2,1)S(1)}, bf16[2,128,256]{2,1,0:T(8,128)(2,1)S(1)}, u32[]{:S(2)}, u32[]{:S(2)}) collective-permute-start(bf16[2,128,256]{2,1,0:T(8,128)(2,1)S(1)} %get-tuple-element.37), channel_id=1, source_target_pairs={{0,8},{4,12},{8,0},{12,4},{16,20},{20,16},{24,28},{28,24},{1,9},{5... | collective-permute-start | bytes 393224 | tf_op jit(solution)/shard_map/ppermute | solution.py:59
  8.8 6.5 %collective-permute-start.12 = (bf16[2,128,256]{2,1,0:T(8,128)(2,1)S(1)}, bf16[2,128,256]{2,1,0:T(8,128)(2,1)S(1)}, u32[]{:S(2)}, u32[]{:S(2)}) collective-permute-start(bf16[2,128,256]{2,1,0:T(8,128)(2,1)S(1)} %get-tuple-element.55), channel_id=1, source_target_pairs={{0,8},{4,12},{8,0},{12,4},{16,20},{20,16},{24,28},{28,24},{1,9},{5... | collective-permute-start | bytes 393224 | tf_op jit(solution)/shard_map/ppermute | solution.py:59
  8.9 18.1 %collective-permute-start.11 = (bf16[8,128,256]{2,1,0:T(8,128)(2,1)}, bf16[8,128,256]{2,1,0:T(8,128)(2,1)}, u32[]{:S(2)}, u32[]{:S(2)}) collective-permute-start(bf16[8,128,256]{2,1,0:T(8,128)(2,1)} %bitcast.3.refs_3_), channel_id=1, source_target_pairs={{0,2},{2,0},{1,3},{3,1},{4,6},{6,4},{5,7},{7,5},{8,10},{10,8},{9,1... | collective-permute-start | bytes 1572872 | tf_op jit(solution)/shard_map/ppermute | solution.py:277
  12.4 7.2 %collective-permute-start.3 = (bf16[2,128,256]{2,1,0:T(8,128)(2,1)S(1)}, bf16[2,128,256]{2,1,0:T(8,128)(2,1)S(1)}, u32[]{:S(2)}, u32[]{:S(2)}) collective-permute-start(bf16[2,128,256]{2,1,0:T(8,128)(2,1)S(1)} %shard_map.107), channel_id=1, source_target_pairs={{0,4},{4,0},{8,16},{12,20},{16,8},{20,12},{24,28},{28,24},{1,5},{5... | collective-permute-start | bytes 393224 | tf_op jit(solution)/shard_map/ppermute | solution.py:59
  15.3 3.9 %collective-permute-start.13 = (bf16[2,128,256]{2,1,0:T(8,128)(2,1)S(1)}, bf16[2,128,256]{2,1,0:T(8,128)(2,1)S(1)}, u32[]{:S(2)}, u32[]{:S(2)}) collective-permute-start(bf16[2,128,256]{2,1,0:T(8,128)(2,1)S(1)} %shard_map.117), channel_id=1, source_target_pairs={{0,4},{4,0},{8,16},{12,20},{16,8},{20,12},{24,28},{28,24},{1,5},{5... | collective-permute-start | bytes 393224 | tf_op jit(solution)/shard_map/ppermute | solution.py:59
  17.9 9.2 %collective-permute-start.10 = (bf16[4,128,256]{2,1,0:T(8,128)(2,1)}, bf16[4,128,256]{2,1,0:T(8,128)(2,1)}, u32[]{:S(2)}, u32[]{:S(2)}) collective-permute-start(bf16[4,128,256]{2,1,0:T(8,128)(2,1)} %slice_bitcast_fusion), channel_id=1, source_target_pairs={{0,1},{1,0},{2,3},{3,2},{4,5},{5,4},{6,7},{7,6},{8,9},{9,8},{10,11... | collective-permute-start | bytes 786440 | tf_op jit(solution)/shard_map/ppermute | solution.py:271
  19.2 1.4 %collective-permute-start.14 = (bf16[2,128,256]{2,1,0:T(8,128)(2,1)S(1)}, bf16[2,128,256]{2,1,0:T(8,128)(2,1)S(1)}, u32[]{:S(2)}, u32[]{:S(2)}) collective-permute-start(bf16[2,128,256]{2,1,0:T(8,128)(2,1)S(1)} %shard_map.118), channel_id=1, source_target_pairs={{0,4},{4,0},{8,12},{12,8},{16,24},{20,28},{24,16},{28,20},{1,5},{5... | collective-permute-start | bytes 393224 | tf_op jit(solution)/shard_map/ppermute | solution.py:59
  19.6 3.7 %collective-permute-start.4 = (bf16[2,128,256]{2,1,0:T(8,128)(2,1)S(1)}, bf16[2,128,256]{2,1,0:T(8,128)(2,1)S(1)}, u32[]{:S(2)}, u32[]{:S(2)}) collective-permute-start(bf16[2,128,256]{2,1,0:T(8,128)(2,1)S(1)} %shard_map.108), channel_id=1, source_target_pairs={{0,4},{4,0},{8,12},{12,8},{16,24},{20,28},{24,16},{28,20},{1,5},{5... | collective-permute-start | bytes 393224 | tf_op jit(solution)/shard_map/ppermute | solution.py:59
  23.0 8.3 %collective-permute-start.15 = (bf16[2,128,256]{2,1,0:T(8,128)(2,1)}, bf16[2,128,256]{2,1,0:T(8,128)(2,1)}, u32[]{:S(2)}, u32[]{:S(2)}) collective-permute-start(bf16[2,128,256]{2,1,0:T(8,128)(2,1)} %get-tuple-element.56), channel_id=1, source_target_pairs={{0,4},{4,0},{8,12},{12,8},{16,24},{20,28},{24,16},{28,20},{1,5},{5... | collective-permute-start | bytes 393224 | tf_op jit(solution)/shard_map/ppermute | solution.py:59
  25.7 6.9 %collective-permute-start.6 = (bf16[2,128,256]{2,1,0:T(8,128)(2,1)}, bf16[2,128,256]{2,1,0:T(8,128)(2,1)}, u32[]{:S(2)}, u32[]{:S(2)}) collective-permute-start(bf16[2,128,256]{2,1,0:T(8,128)(2,1)} %get-tuple-element.45), channel_id=1, source_target_pairs={{0,4},{4,0},{8,12},{12,8},{16,24},{20,28},{24,16},{28,20},{1,5},{5... | collective-permute-start | bytes 393224 | tf_op jit(solution)/shard_map/ppermute | solution.py:59
  32.3 1.6 %collective-permute-start.16 = (bf16[2,128,256]{2,1,0:T(8,128)(2,1)S(1)}, bf16[2,128,256]{2,1,0:T(8,128)(2,1)S(1)}, u32[]{:S(2)}, u32[]{:S(2)}) collective-permute-start(bf16[2,128,256]{2,1,0:T(8,128)(2,1)S(1)} %shard_map.120), channel_id=1, source_target_pairs={{0,4},{4,0},{8,16},{12,20},{16,8},{20,12},{24,28},{28,24},{1,5},{5... | collective-permute-start | bytes 393224 | tf_op jit(solution)/shard_map/ppermute | solution.py:59
  33.5 8.3 %collective-permute-start.7 = (bf16[2,128,256]{2,1,0:T(8,128)(2,1)S(1)}, bf16[2,128,256]{2,1,0:T(8,128)(2,1)S(1)}, u32[]{:S(2)}, u32[]{:S(2)}) collective-permute-start(bf16[2,128,256]{2,1,0:T(8,128)(2,1)S(1)} %shard_map.112), channel_id=1, source_target_pairs={{0,4},{4,0},{8,16},{12,20},{16,8},{20,12},{24,28},{28,24},{1,5},{5... | collective-permute-start | bytes 393224 | tf_op jit(solution)/shard_map/ppermute | solution.py:59
  33.9 10.3 %copy-start.5 = (bf16[2,128,256]{2,1,0:T(8,128)(2,1)S(1)}, bf16[2,128,256]{2,1,0:T(8,128)(2,1)}, u32[]{:S(2)}) copy-start(bf16[2,128,256]{2,1,0:T(8,128)(2,1)} %copy-done.4) | copy-start | bytes 393220
  33.9 10.3 %copy-start.13 = (bf16[2,128,256]{2,1,0:T(8,128)(2,1)S(1)}, bf16[2,128,256]{2,1,0:T(8,128)(2,1)}, u32[]{:S(2)}) copy-start(bf16[2,128,256]{2,1,0:T(8,128)(2,1)} %copy-done.12) | copy-start | bytes 393220
  33.9 10.3 %copy-start.17 = (bf16[2,128,256]{2,1,0:T(8,128)(2,1)S(1)}, bf16[2,128,256]{2,1,0:T(8,128)(2,1)}, u32[]{:S(2)}) copy-start(bf16[2,128,256]{2,1,0:T(8,128)(2,1)} %copy-done.16) | copy-start | bytes 393220
  33.9 10.3 %collective-permute-start.17 = (bf16[2,128,256]{2,1,0:T(8,128)(2,1)S(1)}, bf16[2,128,256]{2,1,0:T(8,128)(2,1)S(1)}, u32[]{:S(2)}, u32[]{:S(2)}) collective-permute-start(bf16[2,128,256]{2,1,0:T(8,128)(2,1)S(1)} %shard_map.121), channel_id=1, source_target_pairs={{0,8},{4,12},{8,0},{12,4},{16,20},{20,16},{24,28},{28,24},{1,9},{5... | collective-permute-start | bytes 393224 | tf_op jit(solution)/shard_map/ppermute | solution.py:59
  41.8 9.3 %collective-permute-start.8 = (bf16[2,128,256]{2,1,0:T(8,128)(2,1)S(1)}, bf16[2,128,256]{2,1,0:T(8,128)(2,1)S(1)}, u32[]{:S(2)}, u32[]{:S(2)}) collective-permute-start(bf16[2,128,256]{2,1,0:T(8,128)(2,1)S(1)} %shard_map.113), channel_id=1, source_target_pairs={{0,8},{4,12},{8,0},{12,4},{16,20},{20,16},{24,28},{28,24},{1,9},{5... | collective-permute-start | bytes 393224 | tf_op jit(solution)/shard_map/ppermute | solution.py:59
  44.3 6.9 %copy-start.11 = (bf16[2,128,256]{2,1,0:T(8,128)(2,1)S(1)}, bf16[2,128,256]{2,1,0:T(8,128)(2,1)}, u32[]{:S(2)}) copy-start(bf16[2,128,256]{2,1,0:T(8,128)(2,1)} %copy-done.10) | copy-start | bytes 393220
  44.3 6.9 %copy-start.15 = (bf16[2,128,256]{2,1,0:T(8,128)(2,1)S(1)}, bf16[2,128,256]{2,1,0:T(8,128)(2,1)}, u32[]{:S(2)}) copy-start(bf16[2,128,256]{2,1,0:T(8,128)(2,1)} %copy-done.14) | copy-start | bytes 393220
  45.7 8.4 %collective-permute-start.18 = (bf16[4,128,256]{2,1,0:T(8,128)(2,1)S(1)}, bf16[4,128,256]{2,1,0:T(8,128)(2,1)S(1)}, u32[]{:S(2)}, u32[]{:S(2)}) collective-permute-start(bf16[4,128,256]{2,1,0:T(8,128)(2,1)S(1)} %get-tuple-element.61), channel_id=1, source_target_pairs={{0,4},{4,0},{8,12},{12,8},{16,20},{20,16},{24,28},{28,24},{1,5},{5... | collective-permute-start | bytes 786440 | tf_op jit(solution)/shard_map/ppermute | solution.py:51
  52.6 2.7 %collective-permute-start.9 = (bf16[4,128,256]{2,1,0:T(8,128)(2,1)S(1)}, bf16[4,128,256]{2,1,0:T(8,128)(2,1)S(1)}, u32[]{:S(2)}, u32[]{:S(2)}) collective-permute-start(bf16[4,128,256]{2,1,0:T(8,128)(2,1)S(1)} %get-tuple-element.52), channel_id=1, source_target_pairs={{0,4},{4,0},{8,12},{12,8},{16,20},{20,16},{24,28},{28,24},{1,5},{5... | collective-permute-start | bytes 786440 | tf_op jit(solution)/shard_map/ppermute | solution.py:51
  (14 other events, 24.1 us)

commit v3 on v2

--- a/solution.py
+++ b/solution.py
@@ -18,7 +18,7 @@
     return jnp.dot(x, y, preferred_element_type=F32)
 
 
-def call(kernel, outs, operands, hbm=(), after=(), scratch=(), products=1):
+def call(kernel, outs, operands, hbm=(), after=(), scratch=(), products=1, room=1):
     spec = pl.BlockSpec(memory_space=pltpu.VMEM)
     anywhere = pl.BlockSpec(memory_space=pl.ANY)
     held = [pltpu.with_memory_space_constraint(x, VMEM) for x in operands]
@@ -34,7 +34,7 @@
         in_specs=[spec] * len(held) + [anywhere] * (len(far) + len(after)),
         out_specs=[spec] * len(outs),
         scratch_shapes=list(scratch),
-        compiler_params=pltpu.CompilerParams(vmem_limit_bytes=8 << 20),
+        compiler_params=pltpu.CompilerParams(vmem_limit_bytes=room << 20),
         cost_estimate=pl.CostEstimate(
             flops=products * 2 * 128 * 256 * 256, bytes_accessed=1 << 18, transcendentals=0
         ),
@@ -89,7 +89,9 @@
 
     beside = swap_cores(current)
 
-    def first(l_ref, p_ref, r_ref, d_ref, keep_ref, send_ref, lower_v, pivot_v, dir_v, rhs_v, sem):
+    def first(*refs):
+        l_ref, p_ref, r_ref, d_ref, keep_ref, send_ref, lower_v, pivot_v, dir_v, rim_ref = refs[:-2]
+        rhs_v, sem = refs[-2:]
         _, core = place()
         copies = []
         for side in (1 - core, core):
@@ -111,14 +113,17 @@
                 ref[i, :size] = (-dot(lower_v[side * half + i], block)).astype(BF16)
                 ref[i, size:] = dot(rhs_v[side * half + i], block).astype(BF16)
         copies[-1].wait()
-
-    keep1, send1, lower_v, pivot_v, dir_v = call(
+        for i in range(valleys):
+            rim_ref[i] = dir_v[i * downs + downs - 1]
+
+    keep1, send1, lower_v, pivot_v, dir_v, rim_out = call(
         first,
-        [packed, packed, every_block, every_block, every_vector],
+        [packed, packed, every_block, every_block, every_vector, ((valleys, rows, size), BF16)],
         [],
         hbm=[blocks(lower_blocks), blocks(inv_pivots), rhs, current],
         scratch=[pltpu.VMEM((chains, rows, size), BF16), pltpu.SemaphoreType.DMA((7,))],
         products=3 * chains,
+        room=2,
     )
     recv1 = swap_cores(send1)
 
@@ -236,6 +241,7 @@
         hbm=[blocks(diag_blocks)],
         scratch=[pltpu.VMEM((chains, size, size), BF16), pltpu.SemaphoreType.DMA((1,))],
         products=2 * chains,
+        room=2,
     )
 
     def advance(span, low, in_ref, start_ref, through_ref, dir_ref, beside_ref, out_ref):
@@ -269,7 +275,7 @@
 
     downs_count, valley_count = lax.axis_size("down"), lax.axis_size("valley")
     rim = lax.ppermute(
-        direction[0, :, -1],
+        rim_out,
         "down",
         [(i, (i + 1) % downs_count) for i in range(downs_count)],
     )
@@ -297,7 +303,7 @@
             copy.start()
         copies[0].wait()
         for i in range(chains):
-            column = column_s[i // downs, i % downs]
+            column = column_s[0, i % downs, i // downs]
             owner = column // valleys
             spot = lax.rem(column, valleys) * downs + i % downs
             behind = lax.rem(mine - owner + valley_count, valley_count)
@@ -335,15 +341,16 @@
         far,
         [every_sum],
         [dir_v, near_sum, rim] + others,
-        hbm=[blocks(down_coupling), blocks(valley_coupling), coupled_column[0]],
+        hbm=[blocks(down_coupling), blocks(valley_coupling), jnp.swapaxes(coupled_column, 1, 2)],
         scratch=[
             pltpu.VMEM((chains, rows, size), BF16),
             pltpu.VMEM((chains, size, size), BF16),
             pltpu.VMEM((chains, size, size), BF16),
-            pltpu.SMEM((valleys, downs), jnp.int32),
+            pltpu.SMEM((1, downs, valleys), jnp.int32),
             pltpu.SemaphoreType.DMA((3,)),
         ],
         products=2 * chains,
+        room=4,
     )
 
     def turn(span, *refs):
@@ -535,7 +542,7 @@
                 pltpu.VMEM((2 * width, rows, size), F32),
                 pltpu.SemaphoreType.DMA((4,)),
             ],
-            compiler_params=pltpu.CompilerParams(vmem_limit_bytes=8 << 20),
+            compiler_params=pltpu.CompilerParams(vmem_limit_bytes=2 << 20),
             cost_estimate=pl.CostEstimate(
                 flops=4 * width * rows * size * size, bytes_accessed=1 << 20, transcendentals=0
             ),

time: 57 us -> 47.8 us (0.84)
  local copies, waits for them, and re-layouts: 6.7 us -> 0.01 us
  Pallas kernels: 18.3 us -> 12.2 us
  waiting for transfers between devices: 3.07 us -> 7.21 us
    pallas_call x19, Pallas kernels: 16.2 us -> 10.1 us  [call(): pl.pallas_call(body, out_shape=[VMEM(shape, dtype) for shape, dtype in ou...]
    unnamed x38 -> x2, local copies, waits for them, and re-layouts: 4.37 us -> 0.01 us
    ppermute x1, waiting for transfers between devices: 0.01 us -> 3.77 us  [local(): lax.ppermute(rim_out, 'down', [(i, (i + 1) % downs_count) for i in range(...]
    squeeze x2 -> x0, local copies, waits for them, and re-layouts: 2.33 us -> none  [the longest x1 1.67 us: local(): direction[0, :, -1]]
    ppermute x1, starting transfers between devices: 1.32 us -> 2.67 us  [local(): lax.ppermute(current, 'valley', [(i, (i + by) % valley_count) for i in ra...]
    ppermute x12, waiting for transfers between devices: 2.06 us -> 3.33 us  [swap_chips(): return lax.ppermute(value, 'elev', pairs)]
    ppermute x5, waiting for transfers between devices: 1 us -> 0.1 us  [swap_cores(): return lax.ppermute(value, 'elev', [(i, i ^ 1) for i in range(count)])]
    ppermute x12, starting transfers between devices: 17 us -> 16.2 us  [swap_chips(): return lax.ppermute(value, 'elev', pairs)]
  transfers between devices with their start and end apart: 19 -> 19, of which waited for: 5 -> 6; matrix products, arithmetic and copies ran while one was open for 4% -> 0% of each run, Pallas kernels for 27% -> 19%
where the time goes in v3:
time: 47.8 us; the launch traced here: 47.3 us
  starting transfers between devices  27 us (56%)
  Pallas kernels  12.2 us (26%)
  waiting for transfers between devices  7.21 us (15%)
  between operations  0.81 us (2%)
    ppermute x12, starting transfers between devices, swap_chips(): return lax.ppermute(value, 'elev', pairs)  16.2 us
    pallas_call x19, Pallas kernels, call(): pl.pallas_call(body, out_shape=[VMEM(shape, dtype) for shape, dtype in ou...  10.1 us
    ppermute x5, starting transfers between devices, swap_cores(): return lax.ppermute(value, 'elev', [(i, i ^ 1) for i in range(count)])  6.91 us
    ppermute x1, waiting for transfers between devices, local(): lax.ppermute(rim_out, 'down', [(i, (i + 1) % downs_count) for i in range(...  3.77 us
    ppermute x12, waiting for transfers between devices, swap_chips(): return lax.ppermute(value, 'elev', pairs)  3.33 us
    ppermute x1, starting transfers between devices, local(): lax.ppermute(current, 'valley', [(i, (i + by) % valley_count) for i in ra...  2.67 us
    pallas_call x2, Pallas kernels, local(): pl.pallas_call(functools.partial(final, span), out_shape=[HBM(*every_vect...  2.12 us
    ppermute x1, starting transfers between devices, local(): lax.ppermute(rim_out, 'down', [(i, (i + 1) % downs_count) for i in range(...  1.22 us
  transfers between devices with their start and end apart: 19, of which 6 were waited for; matrix products, arithmetic and copies ran while one was open for 0% of the time, Pallas kernels for 19%

profile of v3, /device:TPU:1, one launch (start us, length us, event | category | flops | bytes accessed | tf_op | source)
XLA Modules:
  0.0 47.3 jit_solution(15200144896142567549)
XLA Ops:
  0.6 2.2 %shard_map.104 = (bf16[4,384,256]{2,1,0:T(8,128)(2,1)S(1)}, bf16[4,384,256]{2,1,0:T(8,128)(2,1)S(1)}, bf16[8,256,256]{2,1,0:T(8,128)(2,1)S(1)}, bf16[8,256,256]{...) custom-call(bf16[8,256,256]{2,1,0:T(8,128)(2,1)} %bitcast.11, ...), custom_call_target="tpu_custom_call" | custom-call | flops 402653184 | bytes 262144 | tf_op jit(solution)/shard_map/pallas_call | solution.py:31
  3.0 0.5 collective-permute-start.1
  3.4 1.7 %shard_map.109 = (bf16[4,256,256]{2,1,0:T(8,128)(2,1)S(1)}, bf16[4,256,256]{2,1,0:T(8,128)(2,1)S(1)}, bf16[8,256,256]{2,1,0:T(8,128)(2,1)S(1)}) custom-call(bf16[8,256,256]{2,1,0:T(8,128)(2,1)S(1)} %get-tuple-element.42.refs_0_, bf16[8,256,256]{2,1,0:T(8,128)(2,1)} %bitcast.15), custom_call_target="tpu_custom_call" | custom-call | flops 268435456 | bytes 262144 | tf_op jit(solution)/shard_map/pallas_call | solution.py:31
  5.2 2.7 %collective-permute-start.11 = (bf16[8,128,256]{2,1,0:T(8,128)(2,1)S(1)}, bf16[8,128,256]{2,1,0:T(8,128)(2,1)S(1)}, u32[]{:S(2)}, u32[]{:S(2)}) collective-permute-start(bf16[8,128,256]{2,1,0:T(8,128)(2,1)S(1)} %bitcast.22), channel_id=1, source_target_pairs={{0,2},{2,0},{1,3},{3,1},{4,6},{6,4},{5,7},{7,5},{8,10},{10,8},{9,1... | collective-permute-start | bytes 1572872 | tf_op jit(solution)/shard_map/ppermute | solution.py:283
  8.2 1.4 %collective-permute-start.12 = (bf16[2,128,256]{2,1,0:T(8,128)(2,1)S(1)}, bf16[2,128,256]{2,1,0:T(8,128)(2,1)S(1)}, u32[]{:S(2)}, u32[]{:S(2)}) collective-permute-start(bf16[2,128,256]{2,1,0:T(8,128)(2,1)S(1)} %get-tuple-element.57), channel_id=1, source_target_pairs={{0,8},{4,12},{8,0},{12,4},{16,20},{20,16},{24,28},{28,24},{1,9},{5... | collective-permute-start | bytes 393224 | tf_op jit(solution)/shard_map/ppermute | solution.py:59
  9.7 1.5 %shard_map.115.refs_1_.refs_5_ = f32[8,128,256]{2,1,0:T(8,128)S(1)} custom-call(bf16[8,128,256]{2,1,0:T(8,128)(2,1)S(1)} %get-tuple-element.37.refs_2_.refs_3_.refs_7_.refs_0_, bf16[8,128,256]{2,1,0:T(8,128)(2,1)S(1)} %collective-permute-done.1.refs_3_.refs_4_.refs_8_.refs_1_, bf16[8,256,256]{2,1,0:T(8,128)(2,1)S(1)} %get-tuple-element.54.refs_2_.refs_4_, ...), custom_call_target="tpu_custom_call" | custom-call | flops 268435456 | bytes 262144 | tf_op jit(solution)/shard_map/pallas_call | solution.py:31
  11.7 1.3 %collective-permute-done.12.refs_0_ = bf16[2,128,256]{2,1,0:T(8,128)(2,1)S(1)} collective-permute-done((bf16[2,128,256]{2,1,0:T(8,128)(2,1)S(1)}, bf16[2,128,256]{2,1,0:T(8,128)(2,1)S(1)}, u32[]{:S(2)}, u32[]{:S(2)}) %collective-permute-start.12) | collective-permute-done | bytes 131104 | tf_op jit(solution)/shard_map/ppermute | solution.py:59
  13.0 2.0 %collective-permute-start.13 = (bf16[2,128,256]{2,1,0:T(8,128)(2,1)S(1)}, bf16[2,128,256]{2,1,0:T(8,128)(2,1)S(1)}, u32[]{:S(2)}, u32[]{:S(2)}) collective-permute-start(bf16[2,128,256]{2,1,0:T(8,128)(2,1)S(1)} %shard_map.117), channel_id=1, source_target_pairs={{0,4},{4,0},{8,16},{12,20},{16,8},{20,12},{24,28},{28,24},{1,5},{5... | collective-permute-start | bytes 393224 | tf_op jit(solution)/shard_map/ppermute | solution.py:59
  15.0 0.8 %collective-permute-done.2.refs_0_ = bf16[2,128,256]{2,1,0:T(8,128)(2,1)S(1)} collective-permute-done((bf16[2,128,256]{2,1,0:T(8,128)(2,1)S(1)}, bf16[2,128,256]{2,1,0:T(8,128)(2,1)S(1)}, u32[]{:S(2)}, u32[]{:S(2)}) %collective-permute-start.2) | collective-permute-done | bytes 131104 | tf_op jit(solution)/shard_map/ppermute | solution.py:59
  15.8 1.3 %collective-permute-start.3 = (bf16[2,128,256]{2,1,0:T(8,128)(2,1)S(1)}, bf16[2,128,256]{2,1,0:T(8,128)(2,1)S(1)}, u32[]{:S(2)}, u32[]{:S(2)}) collective-permute-start(bf16[2,128,256]{2,1,0:T(8,128)(2,1)S(1)} %shard_map.107), channel_id=1, source_target_pairs={{0,4},{4,0},{8,16},{12,20},{16,8},{20,12},{24,28},{28,24},{1,5},{5... | collective-permute-start | bytes 393224 | tf_op jit(solution)/shard_map/ppermute | solution.py:59
  17.1 1.2 %collective-permute-start.10 = (bf16[4,128,256]{2,1,0:T(8,128)(2,1)S(1)}, bf16[4,128,256]{2,1,0:T(8,128)(2,1)S(1)}, u32[]{:S(2)}, u32[]{:S(2)}) collective-permute-start(bf16[4,128,256]{2,1,0:T(8,128)(2,1)S(1)} %get-tuple-element.56), channel_id=1, source_target_pairs={{0,1},{1,0},{2,3},{3,2},{4,5},{5,4},{6,7},{7,6},{8,9},{9,8},{10,11... | collective-permute-start | bytes 786440 | tf_op jit(solution)/shard_map/ppermute | solution.py:277
  18.3 0.4 collective-permute-start.14
  21.2 3.8 %collective-permute-done.10.refs_2_ = bf16[4,128,256]{2,1,0:T(8,128)(2,1)S(1)} collective-permute-done((bf16[4,128,256]{2,1,0:T(8,128)(2,1)S(1)}, bf16[4,128,256]{2,1,0:T(8,128)(2,1)S(1)}, u32[]{:S(2)}, u32[]{:S(2)}) %collective-permute-start.10) | collective-permute-done | bytes 262176 | tf_op jit(solution)/shard_map/ppermute | solution.py:277
  25.0 1.9 %shard_map.116.refs_5_.refs_3_ = f32[8,128,256]{2,1,0:T(8,128)S(1)} custom-call(bf16[8,128,256]{2,1,0:T(8,128)(2,1)S(1)} %get-tuple-element.37.refs_2_.refs_3_.refs_7_.refs_0_, f32[8,128,256]{2,1,0:T(8,128)S(1)} %shard_map.115.refs_1_.refs_5_, bf16[4,128,256]{2,1,0:T(8,128)(2,1)S(1)} %collective-permute-done.10.refs_2_, ...), custom_call_target="tpu_custom_call" | custom-call | flops 268435456 | bytes 262144 | tf_op jit(solution)/shard_map/pallas_call | solution.py:31
  26.9 0.9 %collective-permute-start.16 = (bf16[2,128,256]{2,1,0:T(8,128)(2,1)S(1)}, bf16[2,128,256]{2,1,0:T(8,128)(2,1)S(1)}, u32[]{:S(2)}, u32[]{:S(2)}) collective-permute-start(bf16[2,128,256]{2,1,0:T(8,128)(2,1)S(1)} %shard_map.120), channel_id=1, source_target_pairs={{0,4},{4,0},{8,16},{12,20},{16,8},{20,12},{24,28},{28,24},{1,5},{5... | collective-permute-start | bytes 393224 | tf_op jit(solution)/shard_map/ppermute | solution.py:59
  28.0 0.8 %collective-permute-done.16.refs_0_.refs_4_ = bf16[2,128,256]{2,1,0:T(8,128)(2,1)S(1)} collective-permute-done((bf16[2,128,256]{2,1,0:T(8,128)(2,1)S(1)}, bf16[2,128,256]{2,1,0:T(8,128)(2,1)S(1)}, u32[]{:S(2)}, u32[]{:S(2)}) %collective-permute-start.16) | collective-permute-done | bytes 131104 | tf_op jit(solution)/shard_map/ppermute | solution.py:59
  28.8 5.9 %collective-permute-start.17 = (bf16[2,128,256]{2,1,0:T(8,128)(2,1)S(1)}, bf16[2,128,256]{2,1,0:T(8,128)(2,1)S(1)}, u32[]{:S(2)}, u32[]{:S(2)}) collective-permute-start(bf16[2,128,256]{2,1,0:T(8,128)(2,1)S(1)} %shard_map.121), channel_id=1, source_target_pairs={{0,8},{4,12},{8,0},{12,4},{16,20},{20,16},{24,28},{28,24},{1,9},{5... | collective-permute-start | bytes 393224 | tf_op jit(solution)/shard_map/ppermute | solution.py:59
  34.8 3.2 %collective-permute-start.8 = (bf16[2,128,256]{2,1,0:T(8,128)(2,1)S(1)}, bf16[2,128,256]{2,1,0:T(8,128)(2,1)S(1)}, u32[]{:S(2)}, u32[]{:S(2)}) collective-permute-start(bf16[2,128,256]{2,1,0:T(8,128)(2,1)S(1)} %shard_map.113), channel_id=1, source_target_pairs={{0,8},{4,12},{8,0},{12,4},{16,20},{20,16},{24,28},{28,24},{1,9},{5... | collective-permute-start | bytes 393224 | tf_op jit(solution)/shard_map/ppermute | solution.py:59
  37.9 0.5 shard_map.122
  38.4 4.6 %collective-permute-start.18 = (bf16[4,128,256]{2,1,0:T(8,128)(2,1)S(1)}, bf16[4,128,256]{2,1,0:T(8,128)(2,1)S(1)}, u32[]{:S(2)}, u32[]{:S(2)}) collective-permute-start(bf16[4,128,256]{2,1,0:T(8,128)(2,1)S(1)} %get-tuple-element.63), channel_id=1, source_target_pairs={{0,4},{4,0},{8,12},{12,8},{16,20},{20,16},{24,28},{28,24},{1,5},{5... | collective-permute-start | bytes 786440 | tf_op jit(solution)/shard_map/ppermute | solution.py:51
  43.0 0.5 shard_map.114
  43.4 1.6 %collective-permute-start.9 = (bf16[4,128,256]{2,1,0:T(8,128)(2,1)S(1)}, bf16[4,128,256]{2,1,0:T(8,128)(2,1)S(1)}, u32[]{:S(2)}, u32[]{:S(2)}) collective-permute-start(bf16[4,128,256]{2,1,0:T(8,128)(2,1)S(1)} %get-tuple-element.53), channel_id=1, source_target_pairs={{0,4},{4,0},{8,12},{12,8},{16,20},{20,16},{24,28},{28,24},{1,5},{5... | collective-permute-start | bytes 786440 | tf_op jit(solution)/shard_map/ppermute | solution.py:51
  45.1 1.1 %shard_map.123 = (bf16[8,128,256]{2,1,0:T(8,128)(2,1)}, f32[8,128,256]{2,1,0:T(8,128)}) custom-call(bf16[2,128,256]{2,1,0:T(8,128)(2,1)S(1)} %get-tuple-element.61.refs_0_, bf16[2,128,256]{2,1,0:T(8,128)(2,1)S(1)} %get-tuple-element.62.refs_1_, bf16[4,128,256]{2,1,0:T(8,128)(2,1)S(1)} %collective-permute-done.18.refs_2_, ...), custom_call_target="tpu_custom_call" | custom-call | flops 67108864 | bytes 1048576 | tf_op jit(solution)/shard_map/pallas_call | solution.py:535
  46.2 1.1 %shard_map.124 = (bf16[8,128,256]{2,1,0:T(8,128)(2,1)}, f32[8,128,256]{2,1,0:T(8,128)}) custom-call(bf16[2,128,256]{2,1,0:T(8,128)(2,1)S(1)} %get-tuple-element.51.refs_0_, bf16[2,128,256]{2,1,0:T(8,128)(2,1)S(1)} %get-tuple-element.52.refs_1_, ...), custom_call_target="tpu_custom_call", output_to_operand_aliasing={{0}: (6, {}), {1}: (7, {})} | custom-call | flops 67108864 | bytes 1048576 | tf_op jit(solution)/shard_map/pallas_call | solution.py:535
  (37 shorter events, 3.8 us)
Async XLA Ops:
  0.6 2.3 %copy-start = (bf16[1,4,2,128,256]{4,3,2,1,0:T(8,128)(2,1)S(1)}, bf16[1,4,2,128,256]{4,3,2,1,0:T(8,128)(2,1)}, u32[]{:S(2)}) copy-start(bf16[1,4,2,128,256]{4,3,2,1,0:T(8,128)(2,1)} %param.10) | copy-start | bytes 1572868
  2.8 5.1 %collective-permute-start = (bf16[4,384,256]{2,1,0:T(8,128)(2,1)S(1)}, bf16[4,384,256]{2,1,0:T(8,128)(2,1)S(1)}, u32[]{:S(2)}, u32[]{:S(2)}) collective-permute-start(bf16[4,384,256]{2,1,0:T(8,128)(2,1)S(1)} %get-tuple-element.36), channel_id=1, source_target_pairs={{0,4},{4,0},{8,12},{12,8},{16,20},{20,16},{24,28},{28,24},{1,5},{5... | collective-permute-start | bytes 2359304 | tf_op jit(solution)/shard_map/ppermute | solution.py:51
  3.0 5.0 %collective-permute-start.1 = (bf16[8,128,256]{2,1,0:T(8,128)(2,1)S(1)}, bf16[8,128,256]{2,1,0:T(8,128)(2,1)S(1)}, u32[]{:S(2)}, u32[]{:S(2)}) collective-permute-start(bf16[8,128,256]{2,1,0:T(8,128)(2,1)S(1)} %bitcast.21), channel_id=1, source_target_pairs={{0,4},{4,0},{8,12},{12,8},{16,20},{20,16},{24,28},{28,24},{1,5},{5... | collective-permute-start | bytes 1572872 | tf_op jit(solution)/shard_map/ppermute | solution.py:51
  5.1 13.9 %collective-permute-start.5 = (bf16[4,256,256]{2,1,0:T(8,128)(2,1)S(1)}, bf16[4,256,256]{2,1,0:T(8,128)(2,1)S(1)}, u32[]{:S(2)}, u32[]{:S(2)}) collective-permute-start(bf16[4,256,256]{2,1,0:T(8,128)(2,1)S(1)} %get-tuple-element.44), channel_id=1, source_target_pairs={{0,4},{4,0},{8,12},{12,8},{16,20},{20,16},{24,28},{28,24},{1,5},{5... | collective-permute-start | bytes 1572872 | tf_op jit(solution)/shard_map/ppermute | solution.py:51
  5.2 19.7 %collective-permute-start.11 = (bf16[8,128,256]{2,1,0:T(8,128)(2,1)S(1)}, bf16[8,128,256]{2,1,0:T(8,128)(2,1)S(1)}, u32[]{:S(2)}, u32[]{:S(2)}) collective-permute-start(bf16[8,128,256]{2,1,0:T(8,128)(2,1)S(1)} %bitcast.22), channel_id=1, source_target_pairs={{0,2},{2,0},{1,3},{3,1},{4,6},{6,4},{5,7},{7,5},{8,10},{10,8},{9,1... | collective-permute-start | bytes 1572872 | tf_op jit(solution)/shard_map/ppermute | solution.py:283
  8.2 4.8 %collective-permute-start.12 = (bf16[2,128,256]{2,1,0:T(8,128)(2,1)S(1)}, bf16[2,128,256]{2,1,0:T(8,128)(2,1)S(1)}, u32[]{:S(2)}, u32[]{:S(2)}) collective-permute-start(bf16[2,128,256]{2,1,0:T(8,128)(2,1)S(1)} %get-tuple-element.57), channel_id=1, source_target_pairs={{0,8},{4,12},{8,0},{12,4},{16,20},{20,16},{24,28},{28,24},{1,9},{5... | collective-permute-start | bytes 393224 | tf_op jit(solution)/shard_map/ppermute | solution.py:59
  9.6 6.2 %collective-permute-start.2 = (bf16[2,128,256]{2,1,0:T(8,128)(2,1)S(1)}, bf16[2,128,256]{2,1,0:T(8,128)(2,1)S(1)}, u32[]{:S(2)}, u32[]{:S(2)}) collective-permute-start(bf16[2,128,256]{2,1,0:T(8,128)(2,1)S(1)} %get-tuple-element.38), channel_id=1, source_target_pairs={{0,8},{4,12},{8,0},{12,4},{16,20},{20,16},{24,28},{28,24},{1,9},{5... | collective-permute-start | bytes 393224 | tf_op jit(solution)/shard_map/ppermute | solution.py:59
  13.0 5.3 %collective-permute-start.13 = (bf16[2,128,256]{2,1,0:T(8,128)(2,1)S(1)}, bf16[2,128,256]{2,1,0:T(8,128)(2,1)S(1)}, u32[]{:S(2)}, u32[]{:S(2)}) collective-permute-start(bf16[2,128,256]{2,1,0:T(8,128)(2,1)S(1)} %shard_map.117), channel_id=1, source_target_pairs={{0,4},{4,0},{8,16},{12,20},{16,8},{20,12},{24,28},{28,24},{1,5},{5... | collective-permute-start | bytes 393224 | tf_op jit(solution)/shard_map/ppermute | solution.py:59
  15.8 2.9 %collective-permute-start.3 = (bf16[2,128,256]{2,1,0:T(8,128)(2,1)S(1)}, bf16[2,128,256]{2,1,0:T(8,128)(2,1)S(1)}, u32[]{:S(2)}, u32[]{:S(2)}) collective-permute-start(bf16[2,128,256]{2,1,0:T(8,128)(2,1)S(1)} %shard_map.107), channel_id=1, source_target_pairs={{0,4},{4,0},{8,16},{12,20},{16,8},{20,12},{24,28},{28,24},{1,5},{5... | collective-permute-start | bytes 393224 | tf_op jit(solution)/shard_map/ppermute | solution.py:59
  17.1 7.9 %collective-permute-start.10 = (bf16[4,128,256]{2,1,0:T(8,128)(2,1)S(1)}, bf16[4,128,256]{2,1,0:T(8,128)(2,1)S(1)}, u32[]{:S(2)}, u32[]{:S(2)}) collective-permute-start(bf16[4,128,256]{2,1,0:T(8,128)(2,1)S(1)} %get-tuple-element.56), channel_id=1, source_target_pairs={{0,1},{1,0},{2,3},{3,2},{4,5},{5,4},{6,7},{7,6},{8,9},{9,8},{10,11... | collective-permute-start | bytes 786440 | tf_op jit(solution)/shard_map/ppermute | solution.py:277
  18.3 1.4 %collective-permute-start.14 = (bf16[2,128,256]{2,1,0:T(8,128)(2,1)S(1)}, bf16[2,128,256]{2,1,0:T(8,128)(2,1)S(1)}, u32[]{:S(2)}, u32[]{:S(2)}) collective-permute-start(bf16[2,128,256]{2,1,0:T(8,128)(2,1)S(1)} %shard_map.118), channel_id=1, source_target_pairs={{0,4},{4,0},{8,12},{12,8},{16,24},{20,28},{24,16},{28,20},{1,5},{5... | collective-permute-start | bytes 393224 | tf_op jit(solution)/shard_map/ppermute | solution.py:59
  18.7 1.8 %collective-permute-start.4 = (bf16[2,128,256]{2,1,0:T(8,128)(2,1)S(1)}, bf16[2,128,256]{2,1,0:T(8,128)(2,1)S(1)}, u32[]{:S(2)}, u32[]{:S(2)}) collective-permute-start(bf16[2,128,256]{2,1,0:T(8,128)(2,1)S(1)} %shard_map.108), channel_id=1, source_target_pairs={{0,4},{4,0},{8,12},{12,8},{16,24},{20,28},{24,16},{28,20},{1,5},{5... | collective-permute-start | bytes 393224 | tf_op jit(solution)/shard_map/ppermute | solution.py:59
  20.1 6.7 %collective-permute-start.15 = (bf16[2,128,256]{2,1,0:T(8,128)(2,1)S(1)}, bf16[2,128,256]{2,1,0:T(8,128)(2,1)S(1)}, u32[]{:S(2)}, u32[]{:S(2)}) collective-permute-start(bf16[2,128,256]{2,1,0:T(8,128)(2,1)S(1)} %get-tuple-element.58), channel_id=1, source_target_pairs={{0,4},{4,0},{8,12},{12,8},{16,24},{20,28},{24,16},{28,20},{1,5},{5... | collective-permute-start | bytes 393224 | tf_op jit(solution)/shard_map/ppermute | solution.py:59
  21.0 6.9 %collective-permute-start.6 = (bf16[2,128,256]{2,1,0:T(8,128)(2,1)S(1)}, bf16[2,128,256]{2,1,0:T(8,128)(2,1)S(1)}, u32[]{:S(2)}, u32[]{:S(2)}) collective-permute-start(bf16[2,128,256]{2,1,0:T(8,128)(2,1)S(1)} %get-tuple-element.46), channel_id=1, source_target_pairs={{0,4},{4,0},{8,12},{12,8},{16,24},{20,28},{24,16},{28,20},{1,5},{5... | collective-permute-start | bytes 393224 | tf_op jit(solution)/shard_map/ppermute | solution.py:59
  26.9 1.9 %collective-permute-start.16 = (bf16[2,128,256]{2,1,0:T(8,128)(2,1)S(1)}, bf16[2,128,256]{2,1,0:T(8,128)(2,1)S(1)}, u32[]{:S(2)}, u32[]{:S(2)}) collective-permute-start(bf16[2,128,256]{2,1,0:T(8,128)(2,1)S(1)} %shard_map.120), channel_id=1, source_target_pairs={{0,4},{4,0},{8,16},{12,20},{16,8},{20,12},{24,28},{28,24},{1,5},{5... | collective-permute-start | bytes 393224 | tf_op jit(solution)/shard_map/ppermute | solution.py:59
  27.8 6.9 %collective-permute-start.7 = (bf16[2,128,256]{2,1,0:T(8,128)(2,1)S(1)}, bf16[2,128,256]{2,1,0:T(8,128)(2,1)S(1)}, u32[]{:S(2)}, u32[]{:S(2)}) collective-permute-start(bf16[2,128,256]{2,1,0:T(8,128)(2,1)S(1)} %shard_map.112), channel_id=1, source_target_pairs={{0,4},{4,0},{8,16},{12,20},{16,8},{20,12},{24,28},{28,24},{1,5},{5... | collective-permute-start | bytes 393224 | tf_op jit(solution)/shard_map/ppermute | solution.py:59
  28.8 9.1 %collective-permute-start.17 = (bf16[2,128,256]{2,1,0:T(8,128)(2,1)S(1)}, bf16[2,128,256]{2,1,0:T(8,128)(2,1)S(1)}, u32[]{:S(2)}, u32[]{:S(2)}) collective-permute-start(bf16[2,128,256]{2,1,0:T(8,128)(2,1)S(1)} %shard_map.121), channel_id=1, source_target_pairs={{0,8},{4,12},{8,0},{12,4},{16,20},{20,16},{24,28},{28,24},{1,9},{5... | collective-permute-start | bytes 393224 | tf_op jit(solution)/shard_map/ppermute | solution.py:59
  34.8 8.2 %collective-permute-start.8 = (bf16[2,128,256]{2,1,0:T(8,128)(2,1)S(1)}, bf16[2,128,256]{2,1,0:T(8,128)(2,1)S(1)}, u32[]{:S(2)}, u32[]{:S(2)}) collective-permute-start(bf16[2,128,256]{2,1,0:T(8,128)(2,1)S(1)} %shard_map.113), channel_id=1, source_target_pairs={{0,8},{4,12},{8,0},{12,4},{16,20},{20,16},{24,28},{28,24},{1,9},{5... | collective-permute-start | bytes 393224 | tf_op jit(solution)/shard_map/ppermute | solution.py:59
  38.4 6.7 %collective-permute-start.18 = (bf16[4,128,256]{2,1,0:T(8,128)(2,1)S(1)}, bf16[4,128,256]{2,1,0:T(8,128)(2,1)S(1)}, u32[]{:S(2)}, u32[]{:S(2)}) collective-permute-start(bf16[4,128,256]{2,1,0:T(8,128)(2,1)S(1)} %get-tuple-element.63), channel_id=1, source_target_pairs={{0,4},{4,0},{8,12},{12,8},{16,20},{20,16},{24,28},{28,24},{1,5},{5... | collective-permute-start | bytes 786440 | tf_op jit(solution)/shard_map/ppermute | solution.py:51
  43.4 2.8 %collective-permute-start.9 = (bf16[4,128,256]{2,1,0:T(8,128)(2,1)S(1)}, bf16[4,128,256]{2,1,0:T(8,128)(2,1)S(1)}, u32[]{:S(2)}, u32[]{:S(2)}) collective-permute-start(bf16[4,128,256]{2,1,0:T(8,128)(2,1)S(1)} %get-tuple-element.53), channel_id=1, source_target_pairs={{0,4},{4,0},{8,12},{12,8},{16,20},{20,16},{24,28},{28,24},{1,5},{5... | collective-permute-start | bytes 786440 | tf_op jit(solution)/shard_map/ppermute | solution.py:51

commit v4 on v3

v4 whole, which is shorter than its diff:
```python
import functools

import jax
import jax.numpy as jnp
from jax import lax
from jax.experimental import pallas as pl
from jax.experimental.pallas import tpu as pltpu
from jax.sharding import PartitionSpec as P

BF16 = jnp.bfloat16
F32 = jnp.float32
VMEM = pltpu.MemorySpace.VMEM
HBM = pltpu.MemorySpace.HBM
GROUPS = 2
WEIGHT = 190000000


def dot(x, y):
    return jnp.dot(x, y, preferred_element_type=F32)


def call(kernel, outs, operands, hbm=(), after=(), old=(), scratch=(), products=1, room=1, weight=1):
    spec = pl.BlockSpec(memory_space=pltpu.VMEM)
    anywhere = pl.BlockSpec(memory_space=pl.ANY)
    held = [pltpu.with_memory_space_constraint(x, VMEM) for x in operands]
    after = [*after, *old]
    far = [pltpu.with_memory_space_constraint(x, HBM) for x in hbm]
    count = len(held) + len(far)

    def body(*refs):
        kernel(*refs[:count], *refs[count + len(after) :])

    return pl.pallas_call(
        body,
        out_shape=[VMEM(shape, dtype) for shape, dtype in outs],
        in_specs=[spec] * len(held) + [anywhere] * (len(far) + len(after)),
        out_specs=[spec] * len(outs),
        scratch_shapes=list(scratch),
        input_output_aliases={count + len(after) - len(old) + i: i for i in range(len(old))},
        compiler_params=pltpu.CompilerParams(vmem_limit_bytes=room << 20),
        cost_estimate=pl.CostEstimate(
            flops=products * weight, bytes_accessed=1 << 10, transcendentals=0
        ),
    )(*held, *far, *after)


def place():
    height = lax.axis_index("elev")
    return height // 2, lax.rem(height, 2)


def swap_cores(value):
    count = lax.axis_size("elev")
    return lax.ppermute(value, "elev", [(i, i ^ 1) for i in range(count)])


def swap_chips(value, *lows):
    pairs = []
    for i in range(lax.axis_size("elev")):
        chip = i // 2
        step = 2 if chip in lows else -2 if chip - 1 in lows else 1 - 2 * (i % 2)
        pairs.append((i, i + step))
    return lax.ppermute(value, "elev", pairs)


def send_up(value, low):
    return lax.ppermute(value, "elev", [(2 * low, 2 * low + 2), (2 * low + 1, 2 * low + 3)])


def local(
    resid,
    direction,
    diag_blocks,
    lower_blocks,
    upper_blocks,
    inv_pivots,
    down_coupling,
    valley_coupling,
    coupled_column,
):
    _, valleys, downs, rows, size = resid.shape
    chains = valleys * downs
    half = chains // 2
    groups = GROUPS
    width = half // groups
    chips = lax.axis_size("elev") // 2
    vectors = lambda x: x.reshape(chains, rows, size)
    blocks = lambda x: x.reshape(chains, size, size)
    rhs, current = vectors(resid), vectors(direction)
    square = ((half, size, size), BF16)
    packed = ((half, size + rows, size), BF16)
    fuller = ((half, size + 2 * rows, size), BF16)
    message = ((width, rows, size), BF16)
    every_block = ((chains, size, size), BF16)
    every_vector = ((chains, rows, size), BF16)
    every_sum = ((chains, rows, size), F32)
    apart = chips > 3
    spans = [slice(g * width, (g + 1) * width) for g in range(groups)]

    half_blocks, half_vectors = ((half, size, size), BF16), ((half, rows, size), BF16)

    def send_products(l_ref, p_ref, r_ref, d_ref, out_ref, lower_v, pivot_v, rhs_v, sem):
        _, core = place()
        part = pl.ds((1 - core) * half, half)
        copies = [
            pltpu.make_async_copy(source.at[part], target, sem.at[i])
            for i, (source, target) in enumerate(
                (
                    (p_ref, pivot_v),
                    (r_ref, rhs_v),
                    (l_ref, lower_v),
                    (d_ref, out_ref.at[:, pl.ds(size + rows, rows)]),
                )
            )
        ]
        for copy in copies:
            copy.start()
        copies[0].wait()
        copies[1].wait()
        for i in range(half):
            out_ref[i, size : size + rows] = dot(rhs_v[i], pivot_v[i]).astype(BF16)
        copies[2].wait()
        for i in range(half):
            out_ref[i, :size] = (-dot(lower_v[i], pivot_v[i])).astype(BF16)
        copies[3].wait()

    send1, lower_other, pivot_other = call(
        send_products,
        [fuller, half_blocks, half_blocks],
        [],
        hbm=[blocks(lower_blocks), blocks(inv_pivots), rhs, current],
        scratch=[pltpu.VMEM(*half_vectors), pltpu.SemaphoreType.DMA((4,))],
        products=3 * half,
        room=2,
    )
    recv1 = swap_cores(send1)

    def keep_products(other_ref, l_ref, p_ref, u_ref, r_ref, d_ref, *refs):
        keep1_ref, keep2_ref, send2_ref, lower_v, own_v, other_v, dir_v = refs[:7]
        pivot_v, rhs_v, sem = refs[7:]
        _, core = place()
        own, other = pl.ds(core * half, half), pl.ds((1 - core) * half, half)
        copies = [
            pltpu.make_async_copy(source, target, sem.at[i])
            for i, (source, target) in enumerate(
                (
                    (p_ref.at[own], pivot_v),
                    (r_ref.at[own], rhs_v),
                    (l_ref.at[own], lower_v),
                    (d_ref, dir_v),
                    (u_ref.at[own], own_v),
                    (u_ref.at[other], other_v),
                    (d_ref.at[own], send2_ref.at[:, pl.ds(size, rows)]),
                )
            )
        ]
        for copy in copies:
            copy.start()
        copies[0].wait()
        copies[1].wait()
        for i in range(half):
            keep1_ref[i, size:] = dot(rhs_v[i], pivot_v[i]).astype(BF16)
        copies[2].wait()
        for i in range(half):
            keep1_ref[i, :size] = (-dot(lower_v[i], pivot_v[i])).astype(BF16)
        copies[3].wait()
        copies[4].wait()
        for i in range(half):
            keep2_ref[i] = (-dot(own_v[i], pivot_v[i])).astype(BF16)
        copies[5].wait()
        for i in range(half):
            send2_ref[i, :size] = (-dot(other_v[i], other_ref[i])).astype(BF16)
        copies[6].wait()

    keep1, keep2, send2, lower_own, upper_own, upper_other, dir_v = call(
        keep_products,
        [packed, square, packed, half_blocks, half_blocks, half_blocks, every_vector],
        [pivot_other],
        hbm=[blocks(lower_blocks), blocks(inv_pivots), blocks(upper_blocks), rhs, current],
        after=[send1],
        scratch=[
            pltpu.VMEM(*half_blocks),
            pltpu.VMEM(*half_vectors),
            pltpu.SemaphoreType.DMA((7,)),
        ],
        products=6 * half,
        room=2,
    )

    def give(which, core, dir_ref, beside_ref, at, out_ref):
        @pl.when(core == which)
        def _():
            out_ref[...] = dir_ref[pl.ds(core * half + at, width)]

        @pl.when(core != which)
        def _():
            out_ref[...] = beside_ref[pl.ds(at, width), pl.ds(size + rows, rows)]

    def begin(span, keep_ref, recv_ref, dir_ref, start_ref, out_ref):
        chip, core = place()
        at = span.start

        def write(bottom, top):
            for i in range(width):
                start_ref[i] = (
                    top[at + i, size : size + rows].astype(F32)
                    + dot(bottom[at + i, size : size + rows], top[at + i, :size])
                ).astype(BF16)

        pl.when(core == 0)(lambda: write(keep_ref, recv_ref))
        pl.when(core == 1)(lambda: write(recv_ref, keep_ref))

        @pl.when(chip == 0)
        def _():
            out_ref[...] = start_ref[...]

        @pl.when(chip != 0)
        def _():
            give(0, core, dir_ref, recv_ref, at, out_ref)

    def join(keep_ref, recv_ref, dir_ref, through_ref, bottom_ref, copy_ref, rim_ref):
        _, core = place()
        copy_ref[...] = dir_ref[...]
        for i in range(valleys):
            rim_ref[i] = dir_ref[i * downs + downs - 1]

        def write(bottom, top):
            bottom_ref[...] = bottom[:, : size + rows]
            for i in range(half):
                through_ref[i] = dot(bottom[i, :size], top[i, :size]).astype(BF16)

        pl.when(core == 0)(lambda: write(keep_ref, recv_ref))
        pl.when(core == 1)(lambda: write(recv_ref, keep_ref))

    def where(upper, work):
        chip, _ = place()
        pl.when((chip >= chips // 2) if upper else (chip < chips // 2))(work)

    def near(upper, dir_ref, recv_ref, lower_ref, upper_ref, diag_ref, out_ref, diag_v, sem):
        def work():
            _, core = place()
            copy = pltpu.make_async_copy(diag_ref, diag_v, sem.at[0])
            copy.start()

            def write(block_ref):
                for i in range(half):
                    out_ref[core * half + i] = dot(recv_ref[i, size + rows :], block_ref[i])

            pl.when(core == 0)(lambda: write(upper_ref))
            pl.when(core == 1)(lambda: write(lower_ref))
            copy.wait()
            for i in range(half):
                at = core * half + i
                out_ref[at] += dot(dir_ref[at], diag_v[at])
                at = (1 - core) * half + i
                out_ref[at] = dot(dir_ref[at], diag_v[at])

        where(upper, work)

    def make_near(upper, after, old):
        (result,) = call(
            functools.partial(near, upper),
            [every_sum],
            [dir_v, recv1, lower_own, upper_own],
            hbm=[blocks(diag_blocks)],
            after=after,
            old=old,
            scratch=[pltpu.VMEM((chains, size, size), BF16), pltpu.SemaphoreType.DMA((1,))],
            products=2 * chains,
            room=2,
        )
        return result

    def advance(span, low, in_ref, start_ref, through_ref, dir_ref, beside_ref, out_ref):
        chip, core = place()
        at = span.start

        @pl.when(chip == low)
        def _():
            for i in range(width):
                out_ref[i] = (
                    start_ref[i].astype(F32) + dot(in_ref[i], through_ref[at + i])
                ).astype(BF16)

        @pl.when(chip != low)
        def _():
            give(0, core, dir_ref, beside_ref, at, out_ref)

    downs_count, valley_count = lax.axis_size("down"), lax.axis_size("valley")

    def hop_up(value, low):
        return (send_up if apart and low == chips - 2 else swap_chips)(value, low)

    starts, fronts, heard_up = [], [], []
    for g, span in enumerate(spans):
        start, front = call(
            functools.partial(begin, span),
            [message] * 2,
            [keep1, recv1, dir_v],
            after=[near_sum] if g else [],
            products=width,
        )
        starts.append(start)
        fronts.append(front)
        heard_up.append([hop_up(front, 0)])
        if g == 0:
            through, bottom, dir_out, rim_out = call(
                join,
                [square, packed, every_vector, ((valleys, rows, size), BF16)],
                [keep1, recv1, dir_v],
                after=[start],
                products=2 * half,
            )
            others = [
                lax.ppermute(
                    dir_out, "valley", [(i, (i + by) % valley_count) for i in range(valley_count)]
                )
                for by in range(1, valley_count)
            ]
            near_sum = make_near(True, [start], [])
            recv2 = swap_cores(send2)
    rim = lax.ppermute(
        rim_out, "down", [(i, (i + 1) % downs_count) for i in range(downs_count)]
    )
    for low in range(1, chips - 1):
        for g, span in enumerate(spans):
            (fronts[g],) = call(
                functools.partial(advance, span, low),
                [message],
                [heard_up[g][-1], starts[g], through, dir_v, recv1],
                products=width,
                weight=WEIGHT,
            )
            heard_up[g].append(hop_up(fronts[g], low))
    near_sum = make_near(False, list(fronts), [near_sum])

    def back(keep_ref, recv_ref, back_ref, low_ref, high_ref):
        _, core = place()

        def write(bottom, top):
            low_ref[...] = bottom[:, :size]
            high_ref[...] = top[:, :size]
            for i in range(half):
                back_ref[i] = dot(top[i, :size], bottom[i, :size]).astype(BF16)

        pl.when(core == 0)(lambda: write(keep_ref, recv_ref))
        pl.when(core == 1)(lambda: write(recv_ref, keep_ref))

    backward, back_low, back_high = call(
        back, [square] * 3, [keep2, recv2], products=2 * half
    )

    def far(upper, *refs):
        where(upper, functools.partial(far_work, *refs))

    def far_work(*refs):
        dir_ref, sum_ref, rim_ref, recv_ref, lower_ref, upper_ref = refs[:6]
        others_refs = refs[6 : 5 + valley_count]
        down_ref, valley_ref, column_ref, out_ref = refs[5 + valley_count : 9 + valley_count]
        partner_ref, down_v, valley_v, column_s, sem = refs[9 + valley_count :]
        _, core = place()
        mine = lax.axis_index("valley")
        edge = lax.axis_index("down")
        copies = [
            pltpu.make_async_copy(source, target, sem.at[i])
            for i, (source, target) in enumerate(
                ((column_ref, column_s), (down_ref, down_v), (valley_ref, valley_v))
            )
        ]
        for copy in copies:
            copy.start()
        copies[0].wait()
        for i in range(chains):
            column = column_s[0, i % downs, i // downs]
            owner = column // valleys
            spot = lax.rem(column, valleys) * downs + i % downs
            behind = lax.rem(mine - owner + valley_count, valley_count)

            @pl.when(behind == 0)
            def _():
                partner_ref[i] = dir_ref[spot]

            for by in range(1, valley_count):

                @pl.when(behind == by)
                def _():
                    partner_ref[i] = others_refs[by - 1][spot]

        copies[1].wait()
        for i in range(chains):
            if i % downs:
                out_ref[i] = sum_ref[i] + dot(dir_ref[i - 1], down_v[i])

        @pl.when(edge > 0)
        def _():
            for i in range(0, chains, downs):
                out_ref[i] = sum_ref[i] + dot(rim_ref[i // downs], down_v[i])

        @pl.when(edge == 0)
        def _():
            for i in range(0, chains, downs):
                out_ref[i] = sum_ref[i]

        def add(block_ref):
            for i in range(half):
                out_ref[(1 - core) * half + i] += dot(recv_ref[i, size:], block_ref[i])

        pl.when(core == 0)(lambda: add(upper_ref))
        pl.when(core == 1)(lambda: add(lower_ref))
        copies[2].wait()
        for i in range(chains):
            out_ref[i] += dot(partner_ref[i], valley_v[i])

    def make_far(upper, after, old):
        (result,) = call(
            functools.partial(far, upper),
            [every_sum],
            [dir_v, near_sum, rim, recv2, lower_other, upper_other] + others,
            hbm=[
                blocks(down_coupling),
                blocks(valley_coupling),
                jnp.swapaxes(coupled_column, 1, 2),
            ],
            after=after,
            old=old,
            scratch=[
                pltpu.VMEM((chains, rows, size), BF16),
                pltpu.VMEM((chains, size, size), BF16),
                pltpu.VMEM((chains, size, size), BF16),
                pltpu.SMEM((1, downs, valleys), jnp.int32),
                pltpu.SemaphoreType.DMA((3,)),
            ],
            products=2 * chains,
            room=4,
        )
        return result

    def turn(span, *refs):
        heard_refs = refs[: chips - 1]
        start_ref, through_ref, bottom_ref, low_ref, dir_ref, beside_ref = refs[chips - 1 : chips + 5]
        top_ref, base_ref, out_ref, in_ref = refs[-4:]
        chip, core = place()
        at = span.start

        @pl.when(chip == 0)
        def _():
            in_ref[...] = jnp.zeros_like(in_ref)

        for low in range(chips - 1):

            @pl.when(chip == low + 1)
            def _():
                in_ref[...] = heard_refs[low][...]

        for i in range(width):
            arrived = in_ref[i]
            top = (start_ref[i].astype(F32) + dot(arrived, through_ref[at + i])).astype(BF16)
            base = bottom_ref[at + i, size:].astype(F32) + dot(arrived, bottom_ref[at + i, :size])
            top_ref[i] = top
            base_ref[i] = (base.astype(BF16).astype(F32) + dot(top, low_ref[at + i])).astype(BF16)

        @pl.when(chip == chips - 1)
        def _():
            out_ref[...] = base_ref[...]

        @pl.when(chip != chips - 1)
        def _():
            give(1, core, dir_ref, beside_ref, at, out_ref)

    def retreat(span, low, in_ref, base_ref, back_ref, dir_ref, beside_ref, out_ref):
        chip, core = place()
        at = span.start

        @pl.when(chip == low)
        def _():
            for i in range(width):
                out_ref[i] = (
                    base_ref[i].astype(F32) + dot(in_ref[i], back_ref[at + i])
                ).astype(BF16)

        @pl.when(chip != low)
        def _():
            give(1, core, dir_ref, beside_ref, at, out_ref)

        if apart and low == 1:

            @pl.when(chip == chips - 1)
            def _():
                give(0, core, dir_ref, beside_ref, at, out_ref)

    def hop_down(value, low):
        return swap_chips(value, *((0, chips - 2) if apart and low == 0 else (low,)))

    tops, bases, solved, heard_down = [], [], [], []
    for g, span in enumerate(spans):
        top, base, out = call(
            functools.partial(turn, span),
            [message] * 3,
            heard_up[g] + [starts[g], through, bottom, back_low, dir_v, recv1],
            after=[far_sum if g else near_sum],
            scratch=[pltpu.VMEM(*message)],
            products=3 * width,
            weight=WEIGHT,
        )
        tops.append(top)
        bases.append(base)
        solved.append(out)
        heard_down.append([hop_down(out, chips - 2)])
        if g == 0:
            far_sum = make_far(False, [top], [])
    for low in range(chips - 3, -1, -1):
        for g, span in enumerate(spans):
            (solved[g],) = call(
                functools.partial(retreat, span, low + 1),
                [message],
                [heard_down[g][0], bases[g], backward, dir_v, recv1],
                products=width,
                weight=WEIGHT,
            )
            heard_down[g].insert(0, hop_down(solved[g], low))
    far_sum = make_far(True, list(solved), [far_sum])

    def finish(span, *refs):
        up_refs, down_refs = refs[: chips - 1], refs[chips - 1 : 2 * chips - 2]
        top_ref, base_ref, back_ref, high_ref = refs[2 * chips - 2 : -4]
        keep_ref, own_ref, send_ref, in_ref = refs[-4:]
        chip, core = place()
        at = span.start
        sent_halo = send_ref.at[pl.ds(width, width)]

        @pl.when(chip == chips - 1)
        def _():
            in_ref[...] = jnp.zeros_like(in_ref)

        for low in range(chips - 1):

            @pl.when(chip == low)
            def _():
                in_ref[...] = down_refs[low][...]

        for which, mine, other in ((0, own_ref, sent_halo), (1, sent_halo, own_ref)):

            @pl.when(core == which)
            def _():
                @pl.when(chip == 0)
                def _():
                    mine[...] = jnp.zeros_like(mine)

                @pl.when(chip == chips - 1)
                def _():
                    other[...] = jnp.zeros_like(other)

                for low in range(chips - 1):

                    @pl.when(chip == low + 1)
                    def _():
                        mine[...] = down_refs[low][...]

                    late = apart and low == chips - 2

                    @pl.when(chip == low)
                    def _():
                        other[...] = (down_refs[0] if late else up_refs[low])[...]

        for i in range(width):
            arrived = in_ref[i]
            low = (base_ref[i].astype(F32) + dot(arrived, back_ref[at + i])).astype(BF16)
            high = (top_ref[i].astype(F32) + dot(arrived, high_ref[at + i])).astype(BF16)

            @pl.when(core == 0)
            def _():
                keep_ref[i] = low
                send_ref[i] = high

            @pl.when(core == 1)
            def _():
                keep_ref[i] = high
                send_ref[i] = low

    def final(span, *refs):
        keep_ref, own_ref, recv_ref, sum_ref = refs[:4]
        lower_refs, upper_refs = refs[4:6], refs[6:8]
        solved_ref, image_ref, total_ref, sem = refs[-4:]
        _, core = place()
        at = span.start
        copies = []
        for side, source in ((core, keep_ref), (1 - core, recv_ref.at[pl.ds(0, width)])):
            copies.append(
                pltpu.make_async_copy(
                    source, solved_ref.at[pl.ds(side * half + at, width)], sem.at[len(copies)]
                )
            )
            copies[-1].start()

        def write(block_refs):
            for number, side in enumerate((core, 1 - core)):
                base = side * half + at
                for i in range(width):
                    halo = own_ref[i] if number == 0 else recv_ref[width + i]
                    total_ref[number * width + i] = sum_ref[base + i] + dot(
                        halo, block_refs[number][at + i]
                    )

        pl.when(core == 0)(lambda: write(lower_refs))
        pl.when(core == 1)(lambda: write(upper_refs))
        for number, side in enumerate((core, 1 - core)):
            copies.append(
                pltpu.make_async_copy(
                    total_ref.at[pl.ds(number * width, width)],
                    image_ref.at[pl.ds(side * half + at, width)],
                    sem.at[len(copies)],
                )
            )
            copies[-1].start()
        for copy in copies:
            copy.wait()

    spec = pl.BlockSpec(memory_space=pltpu.VMEM)
    anywhere = pl.BlockSpec(memory_space=pl.ANY)
    outputs = []
    for g, span in enumerate(spans):
        keep, own, send = call(
            functools.partial(finish, span),
            [message, message, ((2 * width, rows, size), BF16)],
            heard_up[g] + heard_down[g] + [tops[g], bases[g], backward, back_high],
            after=[far_sum],
            scratch=[pltpu.VMEM(*message)],
            products=2 * width,
        )
        operands = [keep, own, swap_cores(send), far_sum]
        operands += [lower_own, lower_other, upper_own, upper_other]
        operands = [pltpu.with_memory_space_constraint(x, VMEM) for x in operands]
        outputs = pl.pallas_call(
            functools.partial(final, span),
            out_shape=[HBM(*every_vector), HBM(*every_sum)],
            in_specs=[spec] * len(operands) + [anywhere] * len(outputs),
            out_specs=[anywhere] * 2,
            input_output_aliases={len(operands) + i: i for i in range(len(outputs))},
            scratch_shapes=[
                pltpu.VMEM((2 * width, rows, size), F32),
                pltpu.SemaphoreType.DMA((4,)),
            ],
            compiler_params=pltpu.CompilerParams(vmem_limit_bytes=2 << 20),
            cost_estimate=pl.CostEstimate(
                flops=4 * width, bytes_accessed=1 << 10, transcendentals=0
            ),
        )(*operands, *outputs)
    preconditioned, image = outputs
    return (preconditioned.reshape(resid.shape), image.reshape(resid.shape))


def solution(mesh):
    spec = P("elev", "valley", "down", None, None)
    in_specs = (spec,) * 8 + (P("elev", "valley", "down"),)
    return jax.shard_map(
        local, mesh=mesh, in_specs=in_specs, out_specs=(spec, spec), check_vma=False
    )
```

time: 47.8 us -> 46 us (0.962)
  starting transfers between devices: 27 us -> 25.4 us
  waiting for transfers between devices: 7.21 us -> 6.15 us
  Pallas kernels: 12.2 us -> 13 us
    ppermute x1, waiting for transfers between devices: 3.77 us -> 2.32 us  [local(): lax.ppermute(rim_out, 'down', [(i, (i + 1) % downs_count) for i in range(...]
    ppermute x12 -> x10, starting transfers between devices: 16.2 us -> 15 us  [swap_chips(): return lax.ppermute(value, 'elev', pairs)]
    pallas_call x19 -> x22, Pallas kernels: 10.1 us -> 10.9 us  [call(): pl.pallas_call(body, out_shape=[VMEM(shape, dtype) for shape, dtype in ou...]
    ppermute x12 -> x10, waiting for transfers between devices: 3.33 us -> 3.73 us  [swap_chips(): return lax.ppermute(value, 'elev', pairs)]
    ppermute x5 -> x4, starting transfers between devices: 6.91 us -> 6.6 us  [swap_cores(): return lax.ppermute(value, 'elev', [(i, i ^ 1) for i in range(count)])]
    ppermute x1 -> x3, starting transfers between devices: 2.67 us -> 2.64 us  [the longest x2 1.34 us: send_up(): lax.ppermute(value, 'elev', [(2 * low, 2 * low + 2), (2 * low + 1, 2 * lo...]
  transfers between devices with their start and end apart: 19 -> 18, of which waited for: 6 -> 5; matrix products, arithmetic and copies ran while one was open for 0% -> 0% of each run, Pallas kernels for 19% -> 23%
where the time goes in v4:
time: 46 us; the launch traced here: 45.5 us
  starting transfers between devices  25.4 us (55%)
  Pallas kernels  13 us (28%)
  waiting for transfers between devices  6.15 us (13%)
  between operations  0.87 us (2%)
    ppermute x10, starting transfers between devices, swap_chips(): return lax.ppermute(value, 'elev', pairs)  15 us
    pallas_call x22, Pallas kernels, call(): pl.pallas_call(body, out_shape=[VMEM(shape, dtype) for shape, dtype in ou...  10.9 us
    ppermute x4, starting transfers between devices, swap_cores(): return lax.ppermute(value, 'elev', [(i, i ^ 1) for i in range(count)])  6.6 us
    ppermute x10, waiting for transfers between devices, swap_chips(): return lax.ppermute(value, 'elev', pairs)  3.73 us
    ppermute x1, waiting for transfers between devices, local(): lax.ppermute(rim_out, 'down', [(i, (i + 1) % downs_count) for i in range(...  2.32 us
    pallas_call x2, Pallas kernels, local(): pl.pallas_call(functools.partial(final, span), out_shape=[HBM(*every_vect...  2.12 us
    ppermute x2, starting transfers between devices, send_up(): lax.ppermute(value, 'elev', [(2 * low, 2 * low + 2), (2 * low + 1, 2 * lo...  1.34 us
    ppermute x1, starting transfers between devices, local(): lax.ppermute(dir_out, 'valley', [(i, (i + by) % valley_count) for i in ra...  1.3 us
  transfers between devices with their start and end apart: 18, of which 5 were waited for; matrix products, arithmetic and copies ran while one was open for 0% of the time, Pallas kernels for 23%

profile of v4, /device:TPU:1, one launch (start us, length us, event | category | flops | bytes accessed | tf_op | source)
XLA Modules:
  0.0 45.5 jit_solution(4074618579242369890)
XLA Ops:
  0.6 1.7 %shard_map.104 = (bf16[4,512,256]{2,1,0:T(8,128)(2,1)S(1)}, bf16[4,256,256]{2,1,0:T(8,128)(2,1)S(1)}, bf16[4,256,256]{2,1,0:T(8,128)(2,1)S(1)}) custom-call(bf16[8,256,256]{2,1,0:T(8,128)(2,1)} %bitcast.11, bf16[8,256,256]{2,1,0:T(8,128)(2,1)} %bitcast.13, bf16[8,128,256]{2,1,0:T(8,128)(2,1)} %bitcast.21, bf16[8,128,256]{2,1,0:T(8,128)(2,1)} %bitcast.23), custom_call_target="tpu_custom_call" | custom-call | flops 12 | bytes 1024 | tf_op jit(solution)/shard_map/pallas_call | solution.py:33
  2.5 2.3 %shard_map.105 = (bf16[4,384,256]{2,1,0:T(8,128)(2,1)S(1)}, bf16[4,256,256]{2,1,0:T(8,128)(2,1)S(1)}, bf16[4,384,256]{2,1,0:T(8,128)(2,1)S(1)}, bf16[4,256,256]{...) custom-call(bf16[4,256,256]{2,1,0:T(8,128)(2,1)S(1)} %get-tuple-elem, ...), custom_call_target="tpu_custom_call" | custom-call | flops 24 | bytes 1024 | tf_op jit(solution)/shard_map/pallas_call | solution.py:33
  4.8 0.5 %collective-permute-start.4 = (bf16[4,384,256]{2,1,0:T(8,128)(2,1)S(1)}, bf16[4,384,256]{2,1,0:T(8,128)(2,1)S(1)}, u32[]{:S(2)}, u32[]{:S(2)}) collective-permute-start(bf16[4,384,256]{2,1,0:T(8,128)(2,1)S(1)} %get-tuple-element.51), channel_id=1, source_target_pairs={{0,4},{4,0},{8,12},{12,8},{16,20},{20,16},{24,28},{28,24},{1,5},{5... | collective-permute-start | bytes 2359304 | tf_op jit(solution)/shard_map/ppermute | solution.py:54
  5.5 2.4 %collective-permute-start.5 = (bf16[2,128,256]{2,1,0:T(8,128)(2,1)S(1)}, bf16[2,128,256]{2,1,0:T(8,128)(2,1)S(1)}, u32[]{:S(2)}, u32[]{:S(2)}) collective-permute-start(bf16[2,128,256]{2,1,0:T(8,128)(2,1)S(1)} %get-tuple-element.53), channel_id=1, source_target_pairs={{0,8},{4,12},{8,0},{12,4},{16,20},{20,16},{24,28},{28,24},{1,9},{5... | collective-permute-start | bytes 393224 | tf_op jit(solution)/shard_map/ppermute | solution.py:63
  8.3 1.3 %collective-permute-start.8 = (bf16[8,128,256]{2,1,0:T(8,128)(2,1)S(1)}, bf16[8,128,256]{2,1,0:T(8,128)(2,1)S(1)}, u32[]{:S(2)}, u32[]{:S(2)}) collective-permute-start(bf16[8,128,256]{2,1,0:T(8,128)(2,1)S(1)} %get-tuple-element.57), channel_id=1, source_target_pairs={{0,2},{2,0},{1,3},{3,1},{4,6},{6,4},{5,7},{7,5},{8,10},{10,8},{9,1... | collective-permute-start | bytes 1572872 | tf_op jit(solution)/shard_map/ppermute | solution.py:315
  10.1 1.2 %collective-permute-done.5.refs_0_ = bf16[2,128,256]{2,1,0:T(8,128)(2,1)S(1)} collective-permute-done((bf16[2,128,256]{2,1,0:T(8,128)(2,1)S(1)}, bf16[2,128,256]{2,1,0:T(8,128)(2,1)S(1)}, u32[]{:S(2)}, u32[]{:S(2)}) %collective-permute-start.5) | collective-permute-done | bytes 131104 | tf_op jit(solution)/shard_map/ppermute | solution.py:63
  11.4 1.1 %collective-permute-start.6 = (bf16[2,128,256]{2,1,0:T(8,128)(2,1)S(1)}, bf16[2,128,256]{2,1,0:T(8,128)(2,1)S(1)}, u32[]{:S(2)}, u32[]{:S(2)}) collective-permute-start(bf16[2,128,256]{2,1,0:T(8,128)(2,1)S(1)} %shard_map.113), channel_id=1, source_target_pairs={{0,4},{4,0},{8,16},{12,20},{16,8},{20,12},{24,28},{28,24},{1,5},{5... | collective-permute-start | bytes 393224 | tf_op jit(solution)/shard_map/ppermute | solution.py:63
  12.5 1.6 %collective-permute-done.1.refs_0_ = bf16[2,128,256]{2,1,0:T(8,128)(2,1)S(1)} collective-permute-done((bf16[2,128,256]{2,1,0:T(8,128)(2,1)S(1)}, bf16[2,128,256]{2,1,0:T(8,128)(2,1)S(1)}, u32[]{:S(2)}, u32[]{:S(2)}) %collective-permute-start.1) | collective-permute-done | bytes 131104 | tf_op jit(solution)/shard_map/ppermute | solution.py:63
  14.1 2.0 %collective-permute-start.2 = (bf16[2,128,256]{2,1,0:T(8,128)(2,1)S(1)}, bf16[2,128,256]{2,1,0:T(8,128)(2,1)S(1)}, u32[]{:S(2)}, u32[]{:S(2)}) collective-permute-start(bf16[2,128,256]{2,1,0:T(8,128)(2,1)S(1)} %shard_map.110), channel_id=1, source_target_pairs={{0,4},{4,0},{8,16},{12,20},{16,8},{20,12},{24,28},{28,24},{1,5},{5... | collective-permute-start | bytes 393224 | tf_op jit(solution)/shard_map/ppermute | solution.py:63
  16.0 1.2 %collective-permute-start.7 = (bf16[4,128,256]{2,1,0:T(8,128)(2,1)S(1)}, bf16[4,128,256]{2,1,0:T(8,128)(2,1)S(1)}, u32[]{:S(2)}, u32[]{:S(2)}) collective-permute-start(bf16[4,128,256]{2,1,0:T(8,128)(2,1)S(1)} %get-tuple-element.54), channel_id=1, source_target_pairs={{0,1},{1,0},{2,3},{3,2},{4,5},{5,4},{6,7},{7,6},{8,9},{9,8},{10,11... | collective-permute-start | bytes 786440 | tf_op jit(solution)/shard_map/ppermute | solution.py:322
  17.3 0.7 %collective-permute-start.9 = (bf16[2,128,256]{2,1,0:T(8,128)(2,1)S(1)}, bf16[2,128,256]{2,1,0:T(8,128)(2,1)S(1)}, u32[]{:S(2)}, u32[]{:S(2)}) collective-permute-start(bf16[2,128,256]{2,1,0:T(8,128)(2,1)S(1)} %shard_map.114.refs_5_), channel_id=1, source_target_pairs={{16,24},{20,28},{17,25},{21,29},{18,26},{22,30},{19,27},{23,31}} | collective-permute-start | bytes 393224 | tf_op jit(solution)/shard_map/ppermute | solution.py:67
  18.0 0.7 %collective-permute-start.3 = (bf16[2,128,256]{2,1,0:T(8,128)(2,1)S(1)}, bf16[2,128,256]{2,1,0:T(8,128)(2,1)S(1)}, u32[]{:S(2)}, u32[]{:S(2)}) collective-permute-start(bf16[2,128,256]{2,1,0:T(8,128)(2,1)S(1)} %shard_map.111.refs_6_), channel_id=1, source_target_pairs={{16,24},{20,28},{17,25},{21,29},{18,26},{22,30},{19,27},{23,31}} | collective-permute-start | bytes 393224 | tf_op jit(solution)/shard_map/ppermute | solution.py:67
  19.1 1.7 %shard_map.115.refs_9_.refs_1_ = f32[8,128,256]{2,1,0:T(8,128)S(1)} custom-call(bf16[8,128,256]{2,1,0:T(8,128)(2,1)S(1)} %get-tuple-element.42.refs_2_.refs_0_.refs_3_.refs_7_, bf16[4,512,256]{2,1,0:T(8,128)(2,1)S(1)} %collective-permute-done.refs_1_.refs_4_.refs_8_, ...), custom_call_target="tpu_custom_call", output_to_operand_aliasing={{}: (7, {})} | custom-call | flops 16 | bytes 1024 | tf_op jit(solution)/shard_map/pallas_call | solution.py:33
  21.6 2.3 %collective-permute-done.7.refs_2_ = bf16[4,128,256]{2,1,0:T(8,128)(2,1)S(1)} collective-permute-done((bf16[4,128,256]{2,1,0:T(8,128)(2,1)S(1)}, bf16[4,128,256]{2,1,0:T(8,128)(2,1)S(1)}, u32[]{:S(2)}, u32[]{:S(2)}) %collective-permute-start.7) | collective-permute-done | bytes 262176 | tf_op jit(solution)/shard_map/ppermute | solution.py:322
  23.9 2.1 %shard_map.117.refs_9_.refs_12_ = f32[8,128,256]{2,1,0:T(8,128)S(1)} custom-call(bf16[8,128,256]{2,1,0:T(8,128)(2,1)S(1)} %get-tuple-element.42.refs_2_.refs_0_.refs_3_.refs_7_, f32[8,128,256]{2,1,0:T(8,128)S(1)} %shard_map.115.refs_9_.refs_1_, bf16[4,128,256]{2,1,0:T(8,128)(2,1)S(1)} %collective-permute-done.7.refs_2_, ...), custom_call_target="tpu_custom_call" | custom-call | flops 16 | bytes 1024 | tf_op jit(solution)/shard_map/pallas_call | solution.py:33
  26.4 0.9 %collective-permute-start.10 = (bf16[2,128,256]{2,1,0:T(8,128)(2,1)S(1)}, bf16[2,128,256]{2,1,0:T(8,128)(2,1)S(1)}, u32[]{:S(2)}, u32[]{:S(2)}) collective-permute-start(bf16[2,128,256]{2,1,0:T(8,128)(2,1)S(1)} %get-tuple-element.59), channel_id=1, source_target_pairs={{0,4},{4,0},{8,12},{12,8},{16,24},{20,28},{24,16},{28,20},{1,5},{5... | collective-permute-start | bytes 393224 | tf_op jit(solution)/shard_map/ppermute | solution.py:63
  27.5 0.9 %collective-permute-done.10.refs_0_.refs_5_ = bf16[2,128,256]{2,1,0:T(8,128)(2,1)S(1)} collective-permute-done((bf16[2,128,256]{2,1,0:T(8,128)(2,1)S(1)}, bf16[2,128,256]{2,1,0:T(8,128)(2,1)S(1)}, u32[]{:S(2)}, u32[]{:S(2)}) %collective-permute-start.10) | collective-permute-done | bytes 131104 | tf_op jit(solution)/shard_map/ppermute | solution.py:63
  28.8 4.1 %collective-permute-start.16 = (bf16[2,128,256]{2,1,0:T(8,128)(2,1)S(1)}, bf16[2,128,256]{2,1,0:T(8,128)(2,1)S(1)}, u32[]{:S(2)}, u32[]{:S(2)}) collective-permute-start(bf16[2,128,256]{2,1,0:T(8,128)(2,1)S(1)} %shard_map.122.refs_10_), channel_id=1, source_target_pairs={{0,8},{4,12},{8,0},{12,4},{16,24},{20,28},{24,16},{28,20},{1,9},{5... | collective-permute-start | bytes 393224 | tf_op jit(solution)/shard_map/ppermute | solution.py:63
  33.0 3.3 %collective-permute-start.12 = (bf16[2,128,256]{2,1,0:T(8,128)(2,1)S(1)}, bf16[2,128,256]{2,1,0:T(8,128)(2,1)S(1)}, u32[]{:S(2)}, u32[]{:S(2)}) collective-permute-start(bf16[2,128,256]{2,1,0:T(8,128)(2,1)S(1)} %shard_map.120.refs_11_), channel_id=1, source_target_pairs={{0,8},{4,12},{8,0},{12,4},{16,24},{20,28},{24,16},{28,20},{1,9},{5... | collective-permute-start | bytes 393224 | tf_op jit(solution)/shard_map/ppermute | solution.py:63
  36.3 0.5 %shard_map.125 = (bf16[2,128,256]{2,1,0:T(8,128)(2,1)S(1)}, bf16[2,128,256]{2,1,0:T(8,128)(2,1)S(1)}, bf16[4,128,256]{2,1,0:T(8,128)(2,1)S(1)}) custom-call(bf16[2,128,256]{2,1,0:T(8,128)(2,1)S(1)} %collective-permute-done.5.refs_0_, bf16[2,128,256]{2,1,0:T(8,128)(2,1)S(1)} %collective-permute-done.6.refs_0_.refs_1_, ...), custom_call_target="tpu_custom_call" | custom-call | flops 4 | bytes 1024 | tf_op jit(solution)/shard_map/pallas_call | solution.py:33
  36.8 4.4 %collective-permute-start.17 = (bf16[4,128,256]{2,1,0:T(8,128)(2,1)S(1)}, bf16[4,128,256]{2,1,0:T(8,128)(2,1)S(1)}, u32[]{:S(2)}, u32[]{:S(2)}) collective-permute-start(bf16[4,128,256]{2,1,0:T(8,128)(2,1)S(1)} %get-tuple-element.71), channel_id=1, source_target_pairs={{0,4},{4,0},{8,12},{12,8},{16,20},{20,16},{24,28},{28,24},{1,5},{5... | collective-permute-start | bytes 786440 | tf_op jit(solution)/shard_map/ppermute | solution.py:54
  41.7 1.5 %collective-permute-start.15 = (bf16[4,128,256]{2,1,0:T(8,128)(2,1)S(1)}, bf16[4,128,256]{2,1,0:T(8,128)(2,1)S(1)}, u32[]{:S(2)}, u32[]{:S(2)}) collective-permute-start(bf16[4,128,256]{2,1,0:T(8,128)(2,1)S(1)} %get-tuple-element.68), channel_id=1, source_target_pairs={{0,4},{4,0},{8,12},{12,8},{16,20},{20,16},{24,28},{28,24},{1,5},{5... | collective-permute-start | bytes 786440 | tf_op jit(solution)/shard_map/ppermute | solution.py:54
  43.2 1.1 %shard_map.126 = (bf16[8,128,256]{2,1,0:T(8,128)(2,1)}, f32[8,128,256]{2,1,0:T(8,128)}) custom-call(bf16[2,128,256]{2,1,0:T(8,128)(2,1)S(1)} %get-tuple-element.69.refs_0_, bf16[2,128,256]{2,1,0:T(8,128)(2,1)S(1)} %get-tuple-element.70.refs_1_, bf16[4,128,256]{2,1,0:T(8,128)(2,1)S(1)} %collective-permute-done.17.refs_2_, ...), custom_call_target="tpu_custom_call" | custom-call | flops 8 | bytes 1024 | tf_op jit(solution)/shard_map/pallas_call | solution.py:633
  44.4 1.1 %shard_map.127 = (bf16[8,128,256]{2,1,0:T(8,128)(2,1)}, f32[8,128,256]{2,1,0:T(8,128)}) custom-call(bf16[2,128,256]{2,1,0:T(8,128)(2,1)S(1)} %get-tuple-element.66.refs_0_, bf16[2,128,256]{2,1,0:T(8,128)(2,1)S(1)} %get-tuple-element.67.refs_1_, ...), custom_call_target="tpu_custom_call", output_to_operand_aliasing={{0}: (8, {}), {1}: (9, {})} | custom-call | flops 8 | bytes 1024 | tf_op jit(solution)/shard_map/pallas_call | solution.py:633
  (36 shorter events, 4.1 us)
Async XLA Ops:
  2.3 3.0 %collective-permute-start = (bf16[4,512,256]{2,1,0:T(8,128)(2,1)S(1)}, bf16[4,512,256]{2,1,0:T(8,128)(2,1)S(1)}, u32[]{:S(2)}, u32[]{:S(2)}) collective-permute-start(bf16[4,512,256]{2,1,0:T(8,128)(2,1)S(1)} %get-tuple-element.40.refs_6_), channel_id=1, source_target_pairs={{0,4},{4,0},{8,12},{12,8},{16,20},{20,16},{24,28},{28,24},{1,5},{5... | collective-permute-start | bytes 3145736 | tf_op jit(solution)/shard_map/ppermute | solution.py:54
  4.8 13.9 %collective-permute-start.4 = (bf16[4,384,256]{2,1,0:T(8,128)(2,1)S(1)}, bf16[4,384,256]{2,1,0:T(8,128)(2,1)S(1)}, u32[]{:S(2)}, u32[]{:S(2)}) collective-permute-start(bf16[4,384,256]{2,1,0:T(8,128)(2,1)S(1)} %get-tuple-element.51), channel_id=1, source_target_pairs={{0,4},{4,0},{8,12},{12,8},{16,20},{20,16},{24,28},{28,24},{1,5},{5... | collective-permute-start | bytes 2359304 | tf_op jit(solution)/shard_map/ppermute | solution.py:54
  5.5 5.9 %collective-permute-start.5 = (bf16[2,128,256]{2,1,0:T(8,128)(2,1)S(1)}, bf16[2,128,256]{2,1,0:T(8,128)(2,1)S(1)}, u32[]{:S(2)}, u32[]{:S(2)}) collective-permute-start(bf16[2,128,256]{2,1,0:T(8,128)(2,1)S(1)} %get-tuple-element.53), channel_id=1, source_target_pairs={{0,8},{4,12},{8,0},{12,4},{16,20},{20,16},{24,28},{28,24},{1,9},{5... | collective-permute-start | bytes 393224 | tf_op jit(solution)/shard_map/ppermute | solution.py:63
  8.3 15.6 %collective-permute-start.8 = (bf16[8,128,256]{2,1,0:T(8,128)(2,1)S(1)}, bf16[8,128,256]{2,1,0:T(8,128)(2,1)S(1)}, u32[]{:S(2)}, u32[]{:S(2)}) collective-permute-start(bf16[8,128,256]{2,1,0:T(8,128)(2,1)S(1)} %get-tuple-element.57), channel_id=1, source_target_pairs={{0,2},{2,0},{1,3},{3,1},{4,6},{6,4},{5,7},{7,5},{8,10},{10,8},{9,1... | collective-permute-start | bytes 1572872 | tf_op jit(solution)/shard_map/ppermute | solution.py:315
  9.9 4.2 %collective-permute-start.1 = (bf16[2,128,256]{2,1,0:T(8,128)(2,1)S(1)}, bf16[2,128,256]{2,1,0:T(8,128)(2,1)S(1)}, u32[]{:S(2)}, u32[]{:S(2)}) collective-permute-start(bf16[2,128,256]{2,1,0:T(8,128)(2,1)S(1)} %get-tuple-element.46), channel_id=1, source_target_pairs={{0,8},{4,12},{8,0},{12,4},{16,20},{20,16},{24,28},{28,24},{1,9},{5... | collective-permute-start | bytes 393224 | tf_op jit(solution)/shard_map/ppermute | solution.py:63
  11.4 5.9 %collective-permute-start.6 = (bf16[2,128,256]{2,1,0:T(8,128)(2,1)S(1)}, bf16[2,128,256]{2,1,0:T(8,128)(2,1)S(1)}, u32[]{:S(2)}, u32[]{:S(2)}) collective-permute-start(bf16[2,128,256]{2,1,0:T(8,128)(2,1)S(1)} %shard_map.113), channel_id=1, source_target_pairs={{0,4},{4,0},{8,16},{12,20},{16,8},{20,12},{24,28},{28,24},{1,5},{5... | collective-permute-start | bytes 393224 | tf_op jit(solution)/shard_map/ppermute | solution.py:63
  14.1 3.9 %collective-permute-start.2 = (bf16[2,128,256]{2,1,0:T(8,128)(2,1)S(1)}, bf16[2,128,256]{2,1,0:T(8,128)(2,1)S(1)}, u32[]{:S(2)}, u32[]{:S(2)}) collective-permute-start(bf16[2,128,256]{2,1,0:T(8,128)(2,1)S(1)} %shard_map.110), channel_id=1, source_target_pairs={{0,4},{4,0},{8,16},{12,20},{16,8},{20,12},{24,28},{28,24},{1,5},{5... | collective-permute-start | bytes 393224 | tf_op jit(solution)/shard_map/ppermute | solution.py:63
  16.0 7.9 %collective-permute-start.7 = (bf16[4,128,256]{2,1,0:T(8,128)(2,1)S(1)}, bf16[4,128,256]{2,1,0:T(8,128)(2,1)S(1)}, u32[]{:S(2)}, u32[]{:S(2)}) collective-permute-start(bf16[4,128,256]{2,1,0:T(8,128)(2,1)S(1)} %get-tuple-element.54), channel_id=1, source_target_pairs={{0,1},{1,0},{2,3},{3,2},{4,5},{5,4},{6,7},{7,6},{8,9},{9,8},{10,11... | collective-permute-start | bytes 786440 | tf_op jit(solution)/shard_map/ppermute | solution.py:322
  17.3 3.5 %collective-permute-start.9 = (bf16[2,128,256]{2,1,0:T(8,128)(2,1)S(1)}, bf16[2,128,256]{2,1,0:T(8,128)(2,1)S(1)}, u32[]{:S(2)}, u32[]{:S(2)}) collective-permute-start(bf16[2,128,256]{2,1,0:T(8,128)(2,1)S(1)} %shard_map.114.refs_5_), channel_id=1, source_target_pairs={{16,24},{20,28},{17,25},{21,29},{18,26},{22,30},{19,27},{23,31}} | collective-permute-start | bytes 393224 | tf_op jit(solution)/shard_map/ppermute | solution.py:67
  18.0 8.0 %collective-permute-start.3 = (bf16[2,128,256]{2,1,0:T(8,128)(2,1)S(1)}, bf16[2,128,256]{2,1,0:T(8,128)(2,1)S(1)}, u32[]{:S(2)}, u32[]{:S(2)}) collective-permute-start(bf16[2,128,256]{2,1,0:T(8,128)(2,1)S(1)} %shard_map.111.refs_6_), channel_id=1, source_target_pairs={{16,24},{20,28},{17,25},{21,29},{18,26},{22,30},{19,27},{23,31}} | collective-permute-start | bytes 393224 | tf_op jit(solution)/shard_map/ppermute | solution.py:67
  21.2 6.2 %collective-permute-start.13 = (bf16[2,128,256]{2,1,0:T(8,128)(2,1)S(1)}, bf16[2,128,256]{2,1,0:T(8,128)(2,1)S(1)}, u32[]{:S(2)}, u32[]{:S(2)}) collective-permute-start(bf16[2,128,256]{2,1,0:T(8,128)(2,1)S(1)} %get-tuple-element.64), channel_id=1, source_target_pairs={{0,4},{4,0},{8,12},{12,8},{16,24},{20,28},{24,16},{28,20},{1,5},{5... | collective-permute-start | bytes 393224 | tf_op jit(solution)/shard_map/ppermute | solution.py:63
  26.4 1.9 %collective-permute-start.10 = (bf16[2,128,256]{2,1,0:T(8,128)(2,1)S(1)}, bf16[2,128,256]{2,1,0:T(8,128)(2,1)S(1)}, u32[]{:S(2)}, u32[]{:S(2)}) collective-permute-start(bf16[2,128,256]{2,1,0:T(8,128)(2,1)S(1)} %get-tuple-element.59), channel_id=1, source_target_pairs={{0,4},{4,0},{8,12},{12,8},{16,24},{20,28},{24,16},{28,20},{1,5},{5... | collective-permute-start | bytes 393224 | tf_op jit(solution)/shard_map/ppermute | solution.py:63
  27.4 1.4 %collective-permute-start.14 = (bf16[2,128,256]{2,1,0:T(8,128)(2,1)S(1)}, bf16[2,128,256]{2,1,0:T(8,128)(2,1)S(1)}, u32[]{:S(2)}, u32[]{:S(2)}) collective-permute-start(bf16[2,128,256]{2,1,0:T(8,128)(2,1)S(1)} %shard_map.121), channel_id=1, source_target_pairs={{0,4},{4,0},{8,16},{12,20},{16,8},{20,12},{24,28},{28,24},{1,5},{5... | collective-permute-start | bytes 393224 | tf_op jit(solution)/shard_map/ppermute | solution.py:63
  28.4 4.6 %collective-permute-start.11 = (bf16[2,128,256]{2,1,0:T(8,128)(2,1)S(1)}, bf16[2,128,256]{2,1,0:T(8,128)(2,1)S(1)}, u32[]{:S(2)}, u32[]{:S(2)}) collective-permute-start(bf16[2,128,256]{2,1,0:T(8,128)(2,1)S(1)} %shard_map.119), channel_id=1, source_target_pairs={{0,4},{4,0},{8,16},{12,20},{16,8},{20,12},{24,28},{28,24},{1,5},{5... | collective-permute-start | bytes 393224 | tf_op jit(solution)/shard_map/ppermute | solution.py:63
  28.8 7.5 %collective-permute-start.16 = (bf16[2,128,256]{2,1,0:T(8,128)(2,1)S(1)}, bf16[2,128,256]{2,1,0:T(8,128)(2,1)S(1)}, u32[]{:S(2)}, u32[]{:S(2)}) collective-permute-start(bf16[2,128,256]{2,1,0:T(8,128)(2,1)S(1)} %shard_map.122.refs_10_), channel_id=1, source_target_pairs={{0,8},{4,12},{8,0},{12,4},{16,24},{20,28},{24,16},{28,20},{1,9},{5... | collective-permute-start | bytes 393224 | tf_op jit(solution)/shard_map/ppermute | solution.py:63
  33.0 8.3 %collective-permute-start.12 = (bf16[2,128,256]{2,1,0:T(8,128)(2,1)S(1)}, bf16[2,128,256]{2,1,0:T(8,128)(2,1)S(1)}, u32[]{:S(2)}, u32[]{:S(2)}) collective-permute-start(bf16[2,128,256]{2,1,0:T(8,128)(2,1)S(1)} %shard_map.120.refs_11_), channel_id=1, source_target_pairs={{0,8},{4,12},{8,0},{12,4},{16,24},{20,28},{24,16},{28,20},{1,9},{5... | collective-permute-start | bytes 393224 | tf_op jit(solution)/shard_map/ppermute | solution.py:63
  36.8 6.4 %collective-permute-start.17 = (bf16[4,128,256]{2,1,0:T(8,128)(2,1)S(1)}, bf16[4,128,256]{2,1,0:T(8,128)(2,1)S(1)}, u32[]{:S(2)}, u32[]{:S(2)}) collective-permute-start(bf16[4,128,256]{2,1,0:T(8,128)(2,1)S(1)} %get-tuple-element.71), channel_id=1, source_target_pairs={{0,4},{4,0},{8,12},{12,8},{16,20},{20,16},{24,28},{28,24},{1,5},{5... | collective-permute-start | bytes 786440 | tf_op jit(solution)/shard_map/ppermute | solution.py:54
  41.7 2.7 %collective-permute-start.15 = (bf16[4,128,256]{2,1,0:T(8,128)(2,1)S(1)}, bf16[4,128,256]{2,1,0:T(8,128)(2,1)S(1)}, u32[]{:S(2)}, u32[]{:S(2)}) collective-permute-start(bf16[4,128,256]{2,1,0:T(8,128)(2,1)S(1)} %get-tuple-element.68), channel_id=1, source_target_pairs={{0,4},{4,0},{8,12},{12,8},{16,20},{20,16},{24,28},{28,24},{1,5},{5... | collective-permute-start | bytes 786440 | tf_op jit(solution)/shard_map/ppermute | solution.py:54

commit v5 on v4

--- a/solution.py
+++ b/solution.py
@@ -12,7 +12,7 @@
 VMEM = pltpu.MemorySpace.VMEM
 HBM = pltpu.MemorySpace.HBM
 GROUPS = 2
-WEIGHT = 190000000
+WEIGHT = 50000000
 
 
 def dot(x, y):
@@ -61,10 +61,6 @@
         step = 2 if chip in lows else -2 if chip - 1 in lows else 1 - 2 * (i % 2)
         pairs.append((i, i + step))
     return lax.ppermute(value, "elev", pairs)
-
-
-def send_up(value, low):
-    return lax.ppermute(value, "elev", [(2 * low, 2 * low + 2), (2 * low + 1, 2 * low + 3)])
 
 
 def local(
@@ -94,7 +90,7 @@
     every_block = ((chains, size, size), BF16)
     every_vector = ((chains, rows, size), BF16)
     every_sum = ((chains, rows, size), F32)
-    apart = chips > 3
+    below_top, top_chip = chips - 2, chips - 1
     spans = [slice(g * width, (g + 1) * width) for g in range(groups)]
 
     half_blocks, half_vectors = ((half, size, size), BF16), ((half, rows, size), BF16)
@@ -288,9 +284,6 @@
 
     downs_count, valley_count = lax.axis_size("down"), lax.axis_size("valley")
 
-    def hop_up(value, low):
-        return (send_up if apart and low == chips - 2 else swap_chips)(value, low)
-
     starts, fronts, heard_up = [], [], []
     for g, span in enumerate(spans):
         start, front = call(
@@ -302,7 +295,7 @@
         )
         starts.append(start)
         fronts.append(front)
-        heard_up.append([hop_up(front, 0)])
+        heard_up.append([swap_chips(front, 0)])
         if g == 0:
             through, bottom, dir_out, rim_out = call(
                 join,
@@ -322,7 +315,7 @@
     rim = lax.ppermute(
         rim_out, "down", [(i, (i + 1) % downs_count) for i in range(downs_count)]
     )
-    for low in range(1, chips - 1):
+    for low in range(1, below_top):
         for g, span in enumerate(spans):
             (fronts[g],) = call(
                 functools.partial(advance, span, low),
@@ -331,7 +324,7 @@
                 products=width,
                 weight=WEIGHT,
             )
-            heard_up[g].append(hop_up(fronts[g], low))
+            heard_up[g].append(swap_chips(fronts[g], low))
     near_sum = make_near(False, list(fronts), [near_sum])
 
     def back(keep_ref, recv_ref, back_ref, low_ref, high_ref):
@@ -346,9 +339,37 @@
         pl.when(core == 0)(lambda: write(keep_ref, recv_ref))
         pl.when(core == 1)(lambda: write(recv_ref, keep_ref))
 
+    def reflect(span, start_ref, bottom_ref, through_ref, low_ref, dir_ref, beside_ref, out_ref):
+        chip, core = place()
+        at = span.start
+
+        @pl.when(chip == top_chip)
+        def _():
+            for i in range(width):
+                low_block = low_ref[at + i]
+                out_ref[i, :size] = (
+                    bottom_ref[at + i, :size].astype(F32) + dot(through_ref[at + i], low_block)
+                ).astype(BF16)
+                out_ref[i, size:] = (
+                    bottom_ref[at + i, size:].astype(F32) + dot(start_ref[i], low_block)
+                ).astype(BF16)
+
+        @pl.when(chip != top_chip)
+        def _():
+            give(1, core, dir_ref, beside_ref, at, out_ref.at[:, pl.ds(size, rows)])
+
     backward, back_low, back_high = call(
         back, [square] * 3, [keep2, recv2], products=2 * half
     )
+    answers = []
+    for g, span in enumerate(spans):
+        (answer,) = call(
+            functools.partial(reflect, span),
+            [((width, size + rows, size), BF16)],
+            [starts[g], bottom, through, back_low, dir_v, recv1],
+            products=3 * width,
+        )
+        answers.append(swap_chips(answer, below_top))
 
     def far(upper, *refs):
         where(upper, functools.partial(far_work, *refs))
@@ -435,10 +456,18 @@
         )
         return result
 
+    def fronts_of(at, arrived, i, start_ref, through_ref, bottom_ref, low_ref):
+        top = (start_ref[i].astype(F32) + dot(arrived, through_ref[at + i])).astype(BF16)
+        low = bottom_ref[at + i, size:].astype(F32) + dot(arrived, bottom_ref[at + i, :size])
+        return top, (low.astype(BF16).astype(F32) + dot(top, low_ref[at + i])).astype(BF16)
+
     def turn(span, *refs):
-        heard_refs = refs[: chips - 1]
-        start_ref, through_ref, bottom_ref, low_ref, dir_ref, beside_ref = refs[chips - 1 : chips + 5]
-        top_ref, base_ref, out_ref, in_ref = refs[-4:]
+        heard_refs = refs[:below_top]
+        answer_ref, start_ref, through_ref, bottom_ref, low_ref, back_ref = refs[
+            below_top : below_top + 6
+        ]
+        dir_ref, beside_ref = refs[below_top + 6 : below_top + 8]
+        top_ref, base_ref, down_ref, up_ref, echo_ref, in_ref = refs[-6:]
         chip, core = place()
         at = span.start
 
@@ -446,26 +475,47 @@
         def _():
             in_ref[...] = jnp.zeros_like(in_ref)
 
-        for low in range(chips - 1):
+        for low in range(below_top):
 
             @pl.when(chip == low + 1)
             def _():
                 in_ref[...] = heard_refs[low][...]
 
-        for i in range(width):
-            arrived = in_ref[i]
-            top = (start_ref[i].astype(F32) + dot(arrived, through_ref[at + i])).astype(BF16)
-            base = bottom_ref[at + i, size:].astype(F32) + dot(arrived, bottom_ref[at + i, :size])
-            top_ref[i] = top
-            base_ref[i] = (base.astype(BF16).astype(F32) + dot(top, low_ref[at + i])).astype(BF16)
-
-        @pl.when(chip == chips - 1)
-        def _():
-            out_ref[...] = base_ref[...]
-
-        @pl.when(chip != chips - 1)
-        def _():
-            give(1, core, dir_ref, beside_ref, at, out_ref)
+        @pl.when(chip < top_chip)
+        def _():
+            for i in range(width):
+                top, base = fronts_of(
+                    at, in_ref[i], i, start_ref, through_ref, bottom_ref, low_ref
+                )
+                top_ref[i] = top
+                base_ref[i] = base
+
+        @pl.when(chip == below_top)
+        def _():
+            for i in range(width):
+                echo = (
+                    answer_ref[i, size:].astype(F32) + dot(top_ref[i], answer_ref[i, :size])
+                ).astype(BF16)
+                echo_ref[i] = echo
+                down_ref[i] = (
+                    base_ref[i].astype(F32) + dot(echo, back_ref[at + i])
+                ).astype(BF16)
+            up_ref[...] = top_ref[...]
+
+        @pl.when(chip != below_top)
+        def _():
+            give(1, core, dir_ref, beside_ref, at, down_ref)
+            give(0, core, dir_ref, beside_ref, at, up_ref)
+
+    def crown(span, in_ref, start_ref, through_ref, bottom_ref, low_ref, top_ref, base_ref):
+        chip, _ = place()
+
+        @pl.when(chip == top_chip)
+        def _():
+            for i in range(width):
+                top_ref[i], base_ref[i] = fronts_of(
+                    span.start, in_ref[i], i, start_ref, through_ref, bottom_ref, low_ref
+                )
 
     def retreat(span, low, in_ref, base_ref, back_ref, dir_ref, beside_ref, out_ref):
         chip, core = place()
@@ -482,33 +532,27 @@
         def _():
             give(1, core, dir_ref, beside_ref, at, out_ref)
 
-        if apart and low == 1:
-
-            @pl.when(chip == chips - 1)
-            def _():
-                give(0, core, dir_ref, beside_ref, at, out_ref)
-
-    def hop_down(value, low):
-        return swap_chips(value, *((0, chips - 2) if apart and low == 0 else (low,)))
-
-    tops, bases, solved, heard_down = [], [], [], []
+    tops, bases, solved, echoes, ups, heard_down = [], [], [], [], [], []
     for g, span in enumerate(spans):
-        top, base, out = call(
+        top, base, down, up, echo = call(
             functools.partial(turn, span),
-            [message] * 3,
-            heard_up[g] + [starts[g], through, bottom, back_low, dir_v, recv1],
+            [message] * 5,
+            heard_up[g]
+            + [answers[g], starts[g], through, bottom, back_low, backward, dir_v, recv1],
             after=[far_sum if g else near_sum],
             scratch=[pltpu.VMEM(*message)],
-            products=3 * width,
+            products=5 * width,
             weight=WEIGHT,
         )
         tops.append(top)
         bases.append(base)
-        solved.append(out)
-        heard_down.append([hop_down(out, chips - 2)])
+        solved.append(down)
+        ups.append(up)
+        echoes.append(echo)
+        heard_down.append([swap_chips(down, below_top - 1)])
         if g == 0:
             far_sum = make_far(False, [top], [])
-    for low in range(chips - 3, -1, -1):
+    for low in range(below_top - 2, -1, -1):
         for g, span in enumerate(spans):
             (solved[g],) = call(
                 functools.partial(retreat, span, low + 1),
@@ -517,22 +561,35 @@
                 products=width,
                 weight=WEIGHT,
             )
-            heard_down[g].insert(0, hop_down(solved[g], low))
+            heard_down[g].insert(0, swap_chips(solved[g], low))
+    for g, span in enumerate(spans):
+        heard_up[g].append(swap_chips(ups[g], below_top))
+        tops[g], bases[g] = call(
+            functools.partial(crown, span),
+            [message] * 2,
+            [heard_up[g][-1], starts[g], through, bottom, back_low],
+            old=[tops[g], bases[g]],
+            products=3 * width,
+        )
     far_sum = make_far(True, list(solved), [far_sum])
 
     def finish(span, *refs):
-        up_refs, down_refs = refs[: chips - 1], refs[chips - 1 : 2 * chips - 2]
-        top_ref, base_ref, back_ref, high_ref = refs[2 * chips - 2 : -4]
+        up_refs, down_refs = refs[:top_chip], refs[top_chip : 2 * top_chip - 1]
+        echo_ref, answer_ref, top_ref, base_ref, back_ref, high_ref = refs[2 * top_chip - 1 : -4]
         keep_ref, own_ref, send_ref, in_ref = refs[-4:]
         chip, core = place()
         at = span.start
         sent_halo = send_ref.at[pl.ds(width, width)]
 
-        @pl.when(chip == chips - 1)
+        @pl.when(chip == top_chip)
         def _():
             in_ref[...] = jnp.zeros_like(in_ref)
 
-        for low in range(chips - 1):
+        @pl.when(chip == below_top)
+        def _():
+            in_ref[...] = echo_ref[...]
+
+        for low in range(below_top):
 
             @pl.when(chip == low)
             def _():
@@ -546,21 +603,25 @@
                 def _():
                     mine[...] = jnp.zeros_like(mine)
 
-                @pl.when(chip == chips - 1)
+                @pl.when(chip == top_chip)
                 def _():
                     other[...] = jnp.zeros_like(other)
 
-                for low in range(chips - 1):
+                @pl.when(chip == top_chip)
+                def _():
+                    mine[...] = answer_ref[:, pl.ds(size, rows)]
+
+                for low in range(top_chip):
+
+                    @pl.when(chip == low)
+                    def _():
+                        other[...] = up_refs[low][...]
+
+                for low in range(below_top):
 
                     @pl.when(chip == low + 1)
                     def _():
                         mine[...] = down_refs[low][...]
-
-                    late = apart and low == chips - 2
-
-                    @pl.when(chip == low)
-                    def _():
-                        other[...] = (down_refs[0] if late else up_refs[low])[...]
 
         for i in range(width):
             arrived = in_ref[i]
@@ -622,7 +683,9 @@
         keep, own, send = call(
             functools.partial(finish, span),
             [message, message, ((2 * width, rows, size), BF16)],
-            heard_up[g] + heard_down[g] + [tops[g], bases[g], backward, back_high],
+            heard_up[g]
+            + heard_down[g]
+            + [echoes[g], answers[g], tops[g], bases[g], backward, back_high],
             after=[far_sum],
             scratch=[pltpu.VMEM(*message)],
             products=2 * width,

time: 46 us -> 43.6 us (0.948)
  starting transfers between devices: 25.4 us -> 20.2 us
  waiting for transfers between devices: 6.15 us -> 9.09 us
    ppermute x10 -> x12, waiting for transfers between devices: 3.73 us -> 8.98 us  [swap_chips(): return lax.ppermute(value, 'elev', pairs)]
    ppermute x4, starting transfers between devices: 6.6 us -> 2.74 us  [swap_cores(): return lax.ppermute(value, 'elev', [(i, i ^ 1) for i in range(count)])]
    ppermute x1, waiting for transfers between devices: 2.32 us -> 0.01 us  [local(): lax.ppermute(rim_out, 'down', [(i, (i + 1) % downs_count) for i in range(...]
    ppermute x2 -> x0, starting transfers between devices: 1.34 us -> none  [send_up(): lax.ppermute(value, 'elev', [(2 * low, 2 * low + 2), (2 * low + 1, 2 * lo...]
    ppermute x10 -> x12, starting transfers between devices: 15 us -> 13.9 us  [swap_chips(): return lax.ppermute(value, 'elev', pairs)]
    ppermute x1, starting transfers between devices: 1.3 us -> 2.34 us  [local(): lax.ppermute(dir_out, 'valley', [(i, (i + by) % valley_count) for i in ra...]
  transfers between devices with their start and end apart: 18 -> 18, of which waited for: 5 -> 6; matrix products, arithmetic and copies ran while one was open for 0% -> 0% of each run, Pallas kernels for 23% -> 24%
where the time goes in v5:
time: 43.6 us; the launch traced here: 43 us
  starting transfers between devices  20.2 us (46%)
  Pallas kernels  12.9 us (30%)
  waiting for transfers between devices  9.09 us (21%)
  between operations  0.83 us (2%)
    ppermute x12, starting transfers between devices, swap_chips(): return lax.ppermute(value, 'elev', pairs)  13.9 us
    pallas_call x22, Pallas kernels, call(): pl.pallas_call(body, out_shape=[VMEM(shape, dtype) for shape, dtype in ou...  10.8 us
    ppermute x12, waiting for transfers between devices, swap_chips(): return lax.ppermute(value, 'elev', pairs)  8.98 us
    ppermute x4, starting transfers between devices, swap_cores(): return lax.ppermute(value, 'elev', [(i, i ^ 1) for i in range(count)])  2.74 us
    ppermute x1, starting transfers between devices, local(): lax.ppermute(dir_out, 'valley', [(i, (i + by) % valley_count) for i in ra...  2.34 us
    pallas_call x2, Pallas kernels, local(): pl.pallas_call(functools.partial(final, span), out_shape=[HBM(*every_vect...  2.12 us
    ppermute x1, starting transfers between devices, local(): lax.ppermute(rim_out, 'down', [(i, (i + 1) % downs_count) for i in range(...  1.21 us
  transfers between devices with their start and end apart: 18, of which 6 were waited for; matrix products, arithmetic and copies ran while one was open for 0% of the time, Pallas kernels for 24%

profile of v5, /device:TPU:1, one launch (start us, length us, event | category | flops | bytes accessed | tf_op | source)
XLA Modules:
  0.0 43.0 jit_solution(17794023974023159840)
XLA Ops:
  0.6 1.7 %shard_map.104 = (bf16[4,512,256]{2,1,0:T(8,128)(2,1)S(1)}, bf16[4,256,256]{2,1,0:T(8,128)(2,1)S(1)}, bf16[4,256,256]{2,1,0:T(8,128)(2,1)S(1)}) custom-call(bf16[8,256,256]{2,1,0:T(8,128)(2,1)} %bitcast.11, bf16[8,256,256]{2,1,0:T(8,128)(2,1)} %bitcast.13, bf16[8,128,256]{2,1,0:T(8,128)(2,1)} %bitcast.21, bf16[8,128,256]{2,1,0:T(8,128)(2,1)} %bitcast.23), custom_call_target="tpu_custom_call" | custom-call | flops 12 | bytes 1024 | tf_op jit(solution)/shard_map/pallas_call | solution.py:33
  2.5 2.3 %shard_map.105 = (bf16[4,384,256]{2,1,0:T(8,128)(2,1)S(1)}, bf16[4,256,256]{2,1,0:T(8,128)(2,1)S(1)}, bf16[4,384,256]{2,1,0:T(8,128)(2,1)S(1)}, bf16[4,256,256]{...) custom-call(bf16[4,256,256]{2,1,0:T(8,128)(2,1)S(1)} %get-tuple-elem, ...), custom_call_target="tpu_custom_call" | custom-call | flops 24 | bytes 1024 | tf_op jit(solution)/shard_map/pallas_call | solution.py:33
  4.8 0.5 %collective-permute-start.3 = (bf16[4,384,256]{2,1,0:T(8,128)(2,1)S(1)}, bf16[4,384,256]{2,1,0:T(8,128)(2,1)S(1)}, u32[]{:S(2)}, u32[]{:S(2)}) collective-permute-start(bf16[4,384,256]{2,1,0:T(8,128)(2,1)S(1)} %get-tuple-element.59), channel_id=1, source_target_pairs={{0,4},{4,0},{8,12},{12,8},{16,20},{20,16},{24,28},{28,24},{1,5},{5... | collective-permute-start | bytes 2359304 | tf_op jit(solution)/shard_map/ppermute | solution.py:54
  5.9 2.3 %collective-permute-start.7 = (bf16[8,128,256]{2,1,0:T(8,128)(2,1)S(1)}, bf16[8,128,256]{2,1,0:T(8,128)(2,1)S(1)}, u32[]{:S(2)}, u32[]{:S(2)}) collective-permute-start(bf16[8,128,256]{2,1,0:T(8,128)(2,1)S(1)} %get-tuple-element.66), channel_id=1, source_target_pairs={{0,2},{2,0},{1,3},{3,1},{4,6},{6,4},{5,7},{7,5},{8,10},{10,8},{9,1... | collective-permute-start | bytes 1572872 | tf_op jit(solution)/shard_map/ppermute | solution.py:308
  8.7 0.8 %collective-permute-start.9 = (bf16[2,384,256]{2,1,0:T(8,128)(2,1)S(1)}, bf16[2,384,256]{2,1,0:T(8,128)(2,1)S(1)}, u32[]{:S(2)}, u32[]{:S(2)}) collective-permute-start(bf16[2,384,256]{2,1,0:T(8,128)(2,1)S(1)} %shard_map.115), channel_id=1, source_target_pairs={{0,4},{4,0},{8,12},{12,8},{16,24},{20,28},{24,16},{28,20},{1,5},{5... | collective-permute-start | bytes 1179656 | tf_op jit(solution)/shard_map/ppermute | solution.py:63
  9.5 1.3 %collective-permute-start.5 = (bf16[2,128,256]{2,1,0:T(8,128)(2,1)S(1)}, bf16[2,128,256]{2,1,0:T(8,128)(2,1)S(1)}, u32[]{:S(2)}, u32[]{:S(2)}) collective-permute-start(bf16[2,128,256]{2,1,0:T(8,128)(2,1)S(1)} %get-tuple-element.62), channel_id=1, source_target_pairs={{0,8},{4,12},{8,0},{12,4},{16,20},{20,16},{24,28},{28,24},{1,9},{5... | collective-permute-start | bytes 393224 | tf_op jit(solution)/shard_map/ppermute | solution.py:63
  11.3 0.7 %collective-permute-start.4 = (bf16[2,384,256]{2,1,0:T(8,128)(2,1)S(1)}, bf16[2,384,256]{2,1,0:T(8,128)(2,1)S(1)}, u32[]{:S(2)}, u32[]{:S(2)}) collective-permute-start(bf16[2,384,256]{2,1,0:T(8,128)(2,1)S(1)} %shard_map.112), channel_id=1, source_target_pairs={{0,4},{4,0},{8,12},{12,8},{16,24},{20,28},{24,16},{28,20},{1,5},{5... | collective-permute-start | bytes 1179656 | tf_op jit(solution)/shard_map/ppermute | solution.py:63
  12.0 2.6 %collective-permute-done.5.refs_0_ = bf16[2,128,256]{2,1,0:T(8,128)(2,1)S(1)} collective-permute-done((bf16[2,128,256]{2,1,0:T(8,128)(2,1)S(1)}, bf16[2,128,256]{2,1,0:T(8,128)(2,1)S(1)}, u32[]{:S(2)}, u32[]{:S(2)}) %collective-permute-start.5) | collective-permute-done | bytes 131104 | tf_op jit(solution)/shard_map/ppermute | solution.py:63
  14.6 1.2 %collective-permute-start.6 = (bf16[4,128,256]{2,1,0:T(8,128)(2,1)S(1)}, bf16[4,128,256]{2,1,0:T(8,128)(2,1)S(1)}, u32[]{:S(2)}, u32[]{:S(2)}) collective-permute-start(bf16[4,128,256]{2,1,0:T(8,128)(2,1)S(1)} %get-tuple-element.63), channel_id=1, source_target_pairs={{0,1},{1,0},{2,3},{3,2},{4,5},{5,4},{6,7},{7,6},{8,9},{9,8},{10,11... | collective-permute-start | bytes 786440 | tf_op jit(solution)/shard_map/ppermute | solution.py:315
  15.8 1.6 %collective-permute-done.1.refs_0_ = bf16[2,128,256]{2,1,0:T(8,128)(2,1)S(1)} collective-permute-done((bf16[2,128,256]{2,1,0:T(8,128)(2,1)S(1)}, bf16[2,128,256]{2,1,0:T(8,128)(2,1)S(1)}, u32[]{:S(2)}, u32[]{:S(2)}) %collective-permute-start.1) | collective-permute-done | bytes 131104 | tf_op jit(solution)/shard_map/ppermute | solution.py:63
  17.4 0.8 %collective-permute-start.8 = (bf16[2,128,256]{2,1,0:T(8,128)(2,1)S(1)}, bf16[2,128,256]{2,1,0:T(8,128)(2,1)S(1)}, u32[]{:S(2)}, u32[]{:S(2)}) collective-permute-start(bf16[2,128,256]{2,1,0:T(8,128)(2,1)S(1)} %shard_map.113.refs_5_), channel_id=1, source_target_pairs={{0,4},{4,0},{8,16},{12,20},{16,8},{20,12},{24,28},{28,24},{1,5},{5... | collective-permute-start | bytes 393224 | tf_op jit(solution)/shard_map/ppermute | solution.py:63
  18.3 1.0 %collective-permute-done.8.refs_1_ = bf16[2,128,256]{2,1,0:T(8,128)(2,1)S(1)} collective-permute-done((bf16[2,128,256]{2,1,0:T(8,128)(2,1)S(1)}, bf16[2,128,256]{2,1,0:T(8,128)(2,1)S(1)}, u32[]{:S(2)}, u32[]{:S(2)}) %collective-permute-start.8) | collective-permute-done | bytes 131104 | tf_op jit(solution)/shard_map/ppermute | solution.py:63
  19.6 1.6 %shard_map.114.refs_10_.refs_1_ = f32[8,128,256]{2,1,0:T(8,128)S(1)} custom-call(bf16[8,128,256]{2,1,0:T(8,128)(2,1)S(1)} %get-tuple-element.50.refs_2_.refs_0_.refs_3_.refs_4_.refs_8_, bf16[4,512,256]{2,1,0:T(8,128)(2,1)S(1)} %collective-permute-done.refs_1_.refs_4_.refs_5_.refs_9_, ...), custom_call_target="tpu_custom_call", output_to_operand_aliasing={{}: (7, {})} | custom-call | flops 16 | bytes 1024 | tf_op jit(solution)/shard_map/pallas_call | solution.py:33
  21.9 2.1 %shard_map.117.refs_10_.refs_12_ = f32[8,128,256]{2,1,0:T(8,128)S(1)} custom-call(bf16[8,128,256]{2,1,0:T(8,128)(2,1)S(1)} %get-tuple-element.50.refs_2_.refs_0_.refs_3_.refs_4_.refs_8_, f32[8,128,256]{2,1,0:T(8,128)S(1)} %shard_map.114.refs_10_.refs_1_, bf16[4,128,256]{2,1,0:T(8,128)(2,1)S(1)} %collective-permute-done.6.refs_2_, ...), custom_call_target="tpu_custom_call" | custom-call | flops 16 | bytes 1024 | tf_op jit(solution)/shard_map/pallas_call | solution.py:33
  24.5 1.5 %collective-permute-start.11 = (bf16[2,128,256]{2,1,0:T(8,128)(2,1)S(1)}, bf16[2,128,256]{2,1,0:T(8,128)(2,1)S(1)}, u32[]{:S(2)}, u32[]{:S(2)}) collective-permute-start(bf16[2,128,256]{2,1,0:T(8,128)(2,1)S(1)} %get-tuple-element.69), channel_id=1, source_target_pairs={{0,4},{4,0},{8,16},{12,20},{16,8},{20,12},{24,28},{28,24},{1,5},{5... | collective-permute-start | bytes 393224 | tf_op jit(solution)/shard_map/ppermute | solution.py:63
  26.0 7.0 %collective-permute-start.16 = (bf16[2,128,256]{2,1,0:T(8,128)(2,1)S(1)}, bf16[2,128,256]{2,1,0:T(8,128)(2,1)S(1)}, u32[]{:S(2)}, u32[]{:S(2)}) collective-permute-start(bf16[2,128,256]{2,1,0:T(8,128)(2,1)S(1)} %shard_map.121.refs_10_), channel_id=1, source_target_pairs={{0,8},{4,12},{8,0},{12,4},{16,20},{20,16},{24,28},{28,24},{1,9},{5... | collective-permute-start | bytes 393224 | tf_op jit(solution)/shard_map/ppermute | solution.py:63
  33.3 0.6 %collective-permute-start.12 = (bf16[2,128,256]{2,1,0:T(8,128)(2,1)S(1)}, bf16[2,128,256]{2,1,0:T(8,128)(2,1)S(1)}, u32[]{:S(2)}, u32[]{:S(2)}) collective-permute-start(bf16[2,128,256]{2,1,0:T(8,128)(2,1)S(1)} %shard_map.119.refs_11_), channel_id=1, source_target_pairs={{0,8},{4,12},{8,0},{12,4},{16,20},{20,16},{24,28},{28,24},{1,9},{5... | collective-permute-start | bytes 393224 | tf_op jit(solution)/shard_map/ppermute | solution.py:63
  34.0 3.0 %collective-permute-done.16.refs_3_ = bf16[2,128,256]{2,1,0:T(8,128)(2,1)S(1)} collective-permute-done((bf16[2,128,256]{2,1,0:T(8,128)(2,1)S(1)}, bf16[2,128,256]{2,1,0:T(8,128)(2,1)S(1)}, u32[]{:S(2)}, u32[]{:S(2)}) %collective-permute-start.16) | collective-permute-done | bytes 131104 | tf_op jit(solution)/shard_map/ppermute | solution.py:63
  37.4 0.8 %collective-permute-start.17 = (bf16[4,128,256]{2,1,0:T(8,128)(2,1)S(1)}, bf16[4,128,256]{2,1,0:T(8,128)(2,1)S(1)}, u32[]{:S(2)}, u32[]{:S(2)}) collective-permute-start(bf16[4,128,256]{2,1,0:T(8,128)(2,1)S(1)} %get-tuple-element.87), channel_id=1, source_target_pairs={{0,4},{4,0},{8,12},{12,8},{16,20},{20,16},{24,28},{28,24},{1,5},{5... | collective-permute-start | bytes 786440 | tf_op jit(solution)/shard_map/ppermute | solution.py:54
  38.2 0.9 %collective-permute-done.12.refs_3_ = bf16[2,128,256]{2,1,0:T(8,128)(2,1)S(1)} collective-permute-done((bf16[2,128,256]{2,1,0:T(8,128)(2,1)S(1)}, bf16[2,128,256]{2,1,0:T(8,128)(2,1)S(1)}, u32[]{:S(2)}, u32[]{:S(2)}) %collective-permute-start.12) | collective-permute-done | bytes 131104 | tf_op jit(solution)/shard_map/ppermute | solution.py:63
  39.1 0.5 %shard_map.123 = (bf16[2,128,256]{2,1,0:T(8,128)(2,1)S(1)}, bf16[2,128,256]{2,1,0:T(8,128)(2,1)S(1)}, bf16[4,128,256]{2,1,0:T(8,128)(2,1)S(1)}) custom-call(bf16[2,128,256]{2,1,0:T(8,128)(2,1)S(1)} %collective-permute-done.1.refs_0_, bf16[2,128,256]{2,1,0:T(8,128)(2,1)S(1)} %collective-permute-done.2.refs_1_, ...), custom_call_target="tpu_custom_call" | custom-call | flops 4 | bytes 1024 | tf_op jit(solution)/shard_map/pallas_call | solution.py:33
  39.5 1.3 %collective-permute-start.14 = (bf16[4,128,256]{2,1,0:T(8,128)(2,1)S(1)}, bf16[4,128,256]{2,1,0:T(8,128)(2,1)S(1)}, u32[]{:S(2)}, u32[]{:S(2)}) collective-permute-start(bf16[4,128,256]{2,1,0:T(8,128)(2,1)S(1)} %get-tuple-element.80), channel_id=1, source_target_pairs={{0,4},{4,0},{8,12},{12,8},{16,20},{20,16},{24,28},{28,24},{1,5},{5... | collective-permute-start | bytes 786440 | tf_op jit(solution)/shard_map/ppermute | solution.py:54
  40.8 1.1 %shard_map.126 = (bf16[8,128,256]{2,1,0:T(8,128)(2,1)}, f32[8,128,256]{2,1,0:T(8,128)}) custom-call(bf16[2,128,256]{2,1,0:T(8,128)(2,1)S(1)} %get-tuple-element.85.refs_0_, bf16[2,128,256]{2,1,0:T(8,128)(2,1)S(1)} %get-tuple-element.86.refs_1_, bf16[4,128,256]{2,1,0:T(8,128)(2,1)S(1)} %collective-permute-done.17.refs_2_, ...), custom_call_target="tpu_custom_call" | custom-call | flops 8 | bytes 1024 | tf_op jit(solution)/shard_map/pallas_call | solution.py:696
  42.0 1.1 %shard_map.127 = (bf16[8,128,256]{2,1,0:T(8,128)(2,1)}, f32[8,128,256]{2,1,0:T(8,128)}) custom-call(bf16[2,128,256]{2,1,0:T(8,128)(2,1)S(1)} %get-tuple-element.78.refs_0_, bf16[2,128,256]{2,1,0:T(8,128)(2,1)S(1)} %get-tuple-element.79.refs_1_, ...), custom_call_target="tpu_custom_call", output_to_operand_aliasing={{0}: (8, {}), {1}: (9, {})} | custom-call | flops 8 | bytes 1024 | tf_op jit(solution)/shard_map/pallas_call | solution.py:696
  (36 shorter events, 4.1 us)
Async XLA Ops:
  2.3 3.0 %collective-permute-start = (bf16[4,512,256]{2,1,0:T(8,128)(2,1)S(1)}, bf16[4,512,256]{2,1,0:T(8,128)(2,1)S(1)}, u32[]{:S(2)}, u32[]{:S(2)}) collective-permute-start(bf16[4,512,256]{2,1,0:T(8,128)(2,1)S(1)} %get-tuple-element.48.refs_6_), channel_id=1, source_target_pairs={{0,4},{4,0},{8,12},{12,8},{16,20},{20,16},{24,28},{28,24},{1,5},{5... | collective-permute-start | bytes 3145736 | tf_op jit(solution)/shard_map/ppermute | solution.py:54
  4.8 3.5 %collective-permute-start.3 = (bf16[4,384,256]{2,1,0:T(8,128)(2,1)S(1)}, bf16[4,384,256]{2,1,0:T(8,128)(2,1)S(1)}, u32[]{:S(2)}, u32[]{:S(2)}) collective-permute-start(bf16[4,384,256]{2,1,0:T(8,128)(2,1)S(1)} %get-tuple-element.59), channel_id=1, source_target_pairs={{0,4},{4,0},{8,12},{12,8},{16,20},{20,16},{24,28},{28,24},{1,5},{5... | collective-permute-start | bytes 2359304 | tf_op jit(solution)/shard_map/ppermute | solution.py:54
  5.9 16.0 %collective-permute-start.7 = (bf16[8,128,256]{2,1,0:T(8,128)(2,1)S(1)}, bf16[8,128,256]{2,1,0:T(8,128)(2,1)S(1)}, u32[]{:S(2)}, u32[]{:S(2)}) collective-permute-start(bf16[8,128,256]{2,1,0:T(8,128)(2,1)S(1)} %get-tuple-element.66), channel_id=1, source_target_pairs={{0,2},{2,0},{1,3},{3,1},{4,6},{6,4},{5,7},{7,5},{8,10},{10,8},{9,1... | collective-permute-start | bytes 1572872 | tf_op jit(solution)/shard_map/ppermute | solution.py:308
  8.7 12.5 %collective-permute-start.9 = (bf16[2,384,256]{2,1,0:T(8,128)(2,1)S(1)}, bf16[2,384,256]{2,1,0:T(8,128)(2,1)S(1)}, u32[]{:S(2)}, u32[]{:S(2)}) collective-permute-start(bf16[2,384,256]{2,1,0:T(8,128)(2,1)S(1)} %shard_map.115), channel_id=1, source_target_pairs={{0,4},{4,0},{8,12},{12,8},{16,24},{20,28},{24,16},{28,20},{1,5},{5... | collective-permute-start | bytes 1179656 | tf_op jit(solution)/shard_map/ppermute | solution.py:63
  9.5 5.1 %collective-permute-start.5 = (bf16[2,128,256]{2,1,0:T(8,128)(2,1)S(1)}, bf16[2,128,256]{2,1,0:T(8,128)(2,1)S(1)}, u32[]{:S(2)}, u32[]{:S(2)}) collective-permute-start(bf16[2,128,256]{2,1,0:T(8,128)(2,1)S(1)} %get-tuple-element.62), channel_id=1, source_target_pairs={{0,8},{4,12},{8,0},{12,4},{16,20},{20,16},{24,28},{28,24},{1,9},{5... | collective-permute-start | bytes 393224 | tf_op jit(solution)/shard_map/ppermute | solution.py:63
  11.1 6.3 %collective-permute-start.1 = (bf16[2,128,256]{2,1,0:T(8,128)(2,1)S(1)}, bf16[2,128,256]{2,1,0:T(8,128)(2,1)S(1)}, u32[]{:S(2)}, u32[]{:S(2)}) collective-permute-start(bf16[2,128,256]{2,1,0:T(8,128)(2,1)S(1)} %get-tuple-element.54), channel_id=1, source_target_pairs={{0,8},{4,12},{8,0},{12,4},{16,20},{20,16},{24,28},{28,24},{1,9},{5... | collective-permute-start | bytes 393224 | tf_op jit(solution)/shard_map/ppermute | solution.py:63
  11.3 12.7 %collective-permute-start.4 = (bf16[2,384,256]{2,1,0:T(8,128)(2,1)S(1)}, bf16[2,384,256]{2,1,0:T(8,128)(2,1)S(1)}, u32[]{:S(2)}, u32[]{:S(2)}) collective-permute-start(bf16[2,384,256]{2,1,0:T(8,128)(2,1)S(1)} %shard_map.112), channel_id=1, source_target_pairs={{0,4},{4,0},{8,12},{12,8},{16,24},{20,28},{24,16},{28,20},{1,5},{5... | collective-permute-start | bytes 1179656 | tf_op jit(solution)/shard_map/ppermute | solution.py:63
  14.6 7.3 %collective-permute-start.6 = (bf16[4,128,256]{2,1,0:T(8,128)(2,1)S(1)}, bf16[4,128,256]{2,1,0:T(8,128)(2,1)S(1)}, u32[]{:S(2)}, u32[]{:S(2)}) collective-permute-start(bf16[4,128,256]{2,1,0:T(8,128)(2,1)S(1)} %get-tuple-element.63), channel_id=1, source_target_pairs={{0,1},{1,0},{2,3},{3,2},{4,5},{5,4},{6,7},{7,6},{8,9},{9,8},{10,11... | collective-permute-start | bytes 786440 | tf_op jit(solution)/shard_map/ppermute | solution.py:315
  17.4 1.8 %collective-permute-start.8 = (bf16[2,128,256]{2,1,0:T(8,128)(2,1)S(1)}, bf16[2,128,256]{2,1,0:T(8,128)(2,1)S(1)}, u32[]{:S(2)}, u32[]{:S(2)}) collective-permute-start(bf16[2,128,256]{2,1,0:T(8,128)(2,1)S(1)} %shard_map.113.refs_5_), channel_id=1, source_target_pairs={{0,4},{4,0},{8,16},{12,20},{16,8},{20,12},{24,28},{28,24},{1,5},{5... | collective-permute-start | bytes 393224 | tf_op jit(solution)/shard_map/ppermute | solution.py:63
  19.2 4.8 %collective-permute-start.2 = (bf16[2,128,256]{2,1,0:T(8,128)(2,1)S(1)}, bf16[2,128,256]{2,1,0:T(8,128)(2,1)S(1)}, u32[]{:S(2)}, u32[]{:S(2)}) collective-permute-start(bf16[2,128,256]{2,1,0:T(8,128)(2,1)S(1)} %shard_map.110.refs_6_), channel_id=1, source_target_pairs={{0,4},{4,0},{8,16},{12,20},{16,8},{20,12},{24,28},{28,24},{1,5},{5... | collective-permute-start | bytes 393224 | tf_op jit(solution)/shard_map/ppermute | solution.py:63
  21.7 4.3 %collective-permute-start.13 = (bf16[2,128,256]{2,1,0:T(8,128)(2,1)S(1)}, bf16[2,128,256]{2,1,0:T(8,128)(2,1)S(1)}, u32[]{:S(2)}, u32[]{:S(2)}) collective-permute-start(bf16[2,128,256]{2,1,0:T(8,128)(2,1)S(1)} %get-tuple-element.76), channel_id=1, source_target_pairs={{0,4},{4,0},{8,16},{12,20},{16,8},{20,12},{24,28},{28,24},{1,5},{5... | collective-permute-start | bytes 393224 | tf_op jit(solution)/shard_map/ppermute | solution.py:63
  24.5 8.9 %collective-permute-start.11 = (bf16[2,128,256]{2,1,0:T(8,128)(2,1)S(1)}, bf16[2,128,256]{2,1,0:T(8,128)(2,1)S(1)}, u32[]{:S(2)}, u32[]{:S(2)}) collective-permute-start(bf16[2,128,256]{2,1,0:T(8,128)(2,1)S(1)} %get-tuple-element.69), channel_id=1, source_target_pairs={{0,4},{4,0},{8,16},{12,20},{16,8},{20,12},{24,28},{28,24},{1,5},{5... | collective-permute-start | bytes 393224 | tf_op jit(solution)/shard_map/ppermute | solution.py:63
  25.9 8.0 %collective-permute-start.15 = (bf16[2,128,256]{2,1,0:T(8,128)(2,1)S(1)}, bf16[2,128,256]{2,1,0:T(8,128)(2,1)S(1)}, u32[]{:S(2)}, u32[]{:S(2)}) collective-permute-start(bf16[2,128,256]{2,1,0:T(8,128)(2,1)S(1)} %get-tuple-element.81), channel_id=1, source_target_pairs={{0,4},{4,0},{8,12},{12,8},{16,24},{20,28},{24,16},{28,20},{1,5},{5... | collective-permute-start | bytes 393224 | tf_op jit(solution)/shard_map/ppermute | solution.py:63
  26.0 10.9 %collective-permute-start.16 = (bf16[2,128,256]{2,1,0:T(8,128)(2,1)S(1)}, bf16[2,128,256]{2,1,0:T(8,128)(2,1)S(1)}, u32[]{:S(2)}, u32[]{:S(2)}) collective-permute-start(bf16[2,128,256]{2,1,0:T(8,128)(2,1)S(1)} %shard_map.121.refs_10_), channel_id=1, source_target_pairs={{0,8},{4,12},{8,0},{12,4},{16,20},{20,16},{24,28},{28,24},{1,9},{5... | collective-permute-start | bytes 393224 | tf_op jit(solution)/shard_map/ppermute | solution.py:63
  33.0 5.2 %collective-permute-start.10 = (bf16[2,128,256]{2,1,0:T(8,128)(2,1)S(1)}, bf16[2,128,256]{2,1,0:T(8,128)(2,1)S(1)}, u32[]{:S(2)}, u32[]{:S(2)}) collective-permute-start(bf16[2,128,256]{2,1,0:T(8,128)(2,1)S(1)} %get-tuple-element.68), channel_id=1, source_target_pairs={{0,4},{4,0},{8,12},{12,8},{16,24},{20,28},{24,16},{28,20},{1,5},{5... | collective-permute-start | bytes 393224 | tf_op jit(solution)/shard_map/ppermute | solution.py:63
  33.3 5.7 %collective-permute-start.12 = (bf16[2,128,256]{2,1,0:T(8,128)(2,1)S(1)}, bf16[2,128,256]{2,1,0:T(8,128)(2,1)S(1)}, u32[]{:S(2)}, u32[]{:S(2)}) collective-permute-start(bf16[2,128,256]{2,1,0:T(8,128)(2,1)S(1)} %shard_map.119.refs_11_), channel_id=1, source_target_pairs={{0,8},{4,12},{8,0},{12,4},{16,20},{20,16},{24,28},{28,24},{1,9},{5... | collective-permute-start | bytes 393224 | tf_op jit(solution)/shard_map/ppermute | solution.py:63
  37.4 3.5 %collective-permute-start.17 = (bf16[4,128,256]{2,1,0:T(8,128)(2,1)S(1)}, bf16[4,128,256]{2,1,0:T(8,128)(2,1)S(1)}, u32[]{:S(2)}, u32[]{:S(2)}) collective-permute-start(bf16[4,128,256]{2,1,0:T(8,128)(2,1)S(1)} %get-tuple-element.87), channel_id=1, source_target_pairs={{0,4},{4,0},{8,12},{12,8},{16,20},{20,16},{24,28},{28,24},{1,5},{5... | collective-permute-start | bytes 786440 | tf_op jit(solution)/shard_map/ppermute | solution.py:54
  39.5 2.4 %collective-permute-start.14 = (bf16[4,128,256]{2,1,0:T(8,128)(2,1)S(1)}, bf16[4,128,256]{2,1,0:T(8,128)(2,1)S(1)}, u32[]{:S(2)}, u32[]{:S(2)}) collective-permute-start(bf16[4,128,256]{2,1,0:T(8,128)(2,1)S(1)} %get-tuple-element.80), channel_id=1, source_target_pairs={{0,4},{4,0},{8,12},{12,8},{16,20},{20,16},{24,28},{28,24},{1,5},{5... | collective-permute-start | bytes 786440 | tf_op jit(solution)/shard_map/ppermute | solution.py:54

commit v6 on v5

v6 whole, which is shorter than its diff:
```python
import functools

import jax
import jax.numpy as jnp
from jax import lax
from jax.experimental import pallas as pl
from jax.experimental.pallas import tpu as pltpu
from jax.sharding import PartitionSpec as P

BF16 = jnp.bfloat16
F32 = jnp.float32
VMEM = pltpu.MemorySpace.VMEM
HBM = pltpu.MemorySpace.HBM
LAST = 1
WEIGHT = 190000000


def dot(x, y):
    return jnp.dot(x, y, preferred_element_type=F32)


def call(kernel, outs, operands, hbm=(), after=(), old=(), scratch=(), products=1, room=1, weight=1):
    spec = pl.BlockSpec(memory_space=pltpu.VMEM)
    anywhere = pl.BlockSpec(memory_space=pl.ANY)
    held = [pltpu.with_memory_space_constraint(x, VMEM) for x in operands]
    after = [*after, *old]
    far = [pltpu.with_memory_space_constraint(x, HBM) for x in hbm]
    count = len(held) + len(far)

    def body(*refs):
        kernel(*refs[:count], *refs[count + len(after) :])

    return pl.pallas_call(
        body,
        out_shape=[VMEM(shape, dtype) for shape, dtype in outs],
        in_specs=[spec] * len(held) + [anywhere] * (len(far) + len(after)),
        out_specs=[spec] * len(outs),
        scratch_shapes=list(scratch),
        input_output_aliases={count + len(after) - len(old) + i: i for i in range(len(old))},
        compiler_params=pltpu.CompilerParams(vmem_limit_bytes=room << 20),
        cost_estimate=pl.CostEstimate(
            flops=products * weight, bytes_accessed=1 << 10, transcendentals=0
        ),
    )(*held, *far, *after)


def place():
    height = lax.axis_index("elev")
    return height // 2, lax.rem(height, 2)


def swap_cores(value):
    count = lax.axis_size("elev")
    return lax.ppermute(value, "elev", [(i, i ^ 1) for i in range(count)])


def swap_chips(value, *lows):
    pairs = []
    for i in range(lax.axis_size("elev")):
        chip = i // 2
        step = 2 if chip in lows else -2 if chip - 1 in lows else 1 - 2 * (i % 2)
        pairs.append((i, i + step))
    return lax.ppermute(value, "elev", pairs)


def local(
    resid,
    direction,
    diag_blocks,
    lower_blocks,
    upper_blocks,
    inv_pivots,
    down_coupling,
    valley_coupling,
    coupled_column,
):
    _, valleys, downs, rows, size = resid.shape
    chains = valleys * downs
    half = chains // 2
    spans = [slice(0, half // 2), slice(half // 2, half)]
    first = half - max(1, LAST * half // 4)
    answer_spans = [slice(0, first), slice(first, half)]
    chips = lax.axis_size("elev") // 2
    below_top, top_chip = chips - 2, chips - 1
    vectors = lambda x: x.reshape(chains, rows, size)
    blocks = lambda x: x.reshape(chains, size, size)
    rhs, current = vectors(resid), vectors(direction)
    square = ((half, size, size), BF16)
    packed = ((half, 2 * size + rows, size), BF16)
    LOWER, RIGHT, UPPER = slice(0, size), slice(size, size + rows), slice(size + rows, None)
    every_block = ((chains, size, size), BF16)
    every_vector = ((chains, rows, size), BF16)
    every_sum = ((chains, rows, size), F32)
    downs_count, valley_count = lax.axis_size("down"), lax.axis_size("valley")

    def wide(span):
        return span.stop - span.start

    def message(span, more=0):
        return ((wide(span), rows + more, size), BF16)

    half_blocks, half_vectors = ((half, size, size), BF16), ((half, rows, size), BF16)

    half_blocks, half_vectors = ((half, size, size), BF16), ((half, rows, size), BF16)

    def multiply(pivot_ref, rhs_ref, lower_ref, upper_ref, copies, out_ref):
        copies[0].wait()
        copies[1].wait()
        for i in range(half):
            out_ref[i, RIGHT] = dot(rhs_ref[i], pivot_ref[i]).astype(BF16)
        copies[2].wait()
        for i in range(half):
            out_ref[i, LOWER] = (-dot(lower_ref[i], pivot_ref[i])).astype(BF16)
        copies[3].wait()
        for i in range(half):
            out_ref[i, UPPER] = (-dot(upper_ref[i], pivot_ref[i])).astype(BF16)

    def send_products(p_ref, r_ref, l_ref, u_ref, out_ref, lower_v, upper_v, pivot_v, rhs_v, sem):
        _, core = place()
        part = pl.ds((1 - core) * half, half)
        copies = [
            pltpu.make_async_copy(source.at[part], target, sem.at[i])
            for i, (source, target) in enumerate(
                ((p_ref, pivot_v), (r_ref, rhs_v), (l_ref, lower_v), (u_ref, upper_v))
            )
        ]
        for copy in copies:
            copy.start()
        multiply(pivot_v, rhs_v, lower_v, upper_v, copies, out_ref)

    def keep_products(p_ref, r_ref, l_ref, u_ref, d_ref, *refs):
        out_ref, lower_v, upper_v, dir_v, pivot_v, rhs_v, sem = refs
        _, core = place()
        part = pl.ds(core * half, half)
        copies = [
            pltpu.make_async_copy(source, target, sem.at[i])
            for i, (source, target) in enumerate(
                (
                    (p_ref.at[part], pivot_v),
                    (r_ref.at[part], rhs_v),
                    (l_ref.at[part], lower_v),
                    (u_ref.at[part], upper_v),
                    (d_ref, dir_v),
                )
            )
        ]
        for copy in copies:
            copy.start()
        multiply(pivot_v, rhs_v, lower_v, upper_v, copies, out_ref)
        copies[4].wait()

    layer = [blocks(inv_pivots), rhs, blocks(lower_blocks), blocks(upper_blocks)]
    room_for = [pltpu.VMEM(*half_blocks), pltpu.VMEM(*half_vectors)]
    send1, lower_other, upper_other = call(
        send_products,
        [packed, half_blocks, half_blocks],
        [],
        hbm=layer,
        scratch=room_for + [pltpu.SemaphoreType.DMA((4,))],
        products=5 * half,
        room=2,
    )
    recv1 = swap_cores(send1)
    keep1, lower_own, upper_own, dir_v = call(
        keep_products,
        [packed, half_blocks, half_blocks, every_vector],
        [],
        hbm=layer + [current],
        after=[send1],
        scratch=room_for + [pltpu.SemaphoreType.DMA((5,))],
        products=5 * half,
        room=2,
    )
    beside = swap_cores(dir_v)

    def reflect(span, keep_ref, recv_ref, out_ref):
        chip, core = place()

        def write(bottom, top):
            for i, at in enumerate(range(span.start, span.stop)):
                lower, upper = top[at, LOWER], bottom[at, UPPER]
                through = dot(bottom[at, LOWER], lower).astype(BF16)
                out_ref[i, :size] = (
                    bottom[at, LOWER].astype(F32) + dot(through, upper)
                ).astype(BF16)
                start = top[at, RIGHT].astype(F32) + dot(bottom[at, RIGHT], lower)
                out_ref[i, size : size + rows] = (
                    bottom[at, RIGHT].astype(F32) + dot(start.astype(BF16), upper)
                ).astype(BF16)

        here = chip == top_chip
        pl.when(jnp.logical_and(here, core == 0))(lambda: write(keep_ref, recv_ref))
        pl.when(jnp.logical_and(here, core == 1))(lambda: write(recv_ref, keep_ref))

    def answer_of(span, after):
        (answer,) = call(
            functools.partial(reflect, span),
            [message(span, size)],
            [keep1, recv1],
            after=after,
            products=4 * wide(span),
        )
        return answer

    answer = answer_of(answer_spans[0], [])
    answers, echoing = [swap_chips(answer, below_top)], [answer]

    late_rows = max(size + rows, half * rows // wide(answer_spans[1]))

    def reflect_late(keep_ref, recv_ref, dir_ref, beside_ref, out_ref):
        chip, core = place()
        reflect(answer_spans[1], keep_ref, recv_ref, out_ref)

        @pl.when(chip == below_top)
        def _():
            for at in range(half):
                part, line = divmod(at * rows, late_rows)
                target = out_ref.at[part, pl.ds(line, rows)]

                @pl.when(core == 1)
                def _():
                    target[...] = dir_ref[core * half + at]

                @pl.when(core == 0)
                def _():
                    target[...] = beside_ref[core * half + at]

    def give(which, core, dir_ref, beside_ref, span, out_ref):
        part = pl.ds(core * half + span.start, wide(span))

        @pl.when(core == which)
        def _():
            out_ref[...] = dir_ref[part]

        @pl.when(core != which)
        def _():
            out_ref[...] = beside_ref[part]

    def begin(span, keep_ref, recv_ref, dir_ref, beside_ref, start_ref, out_ref):
        chip, core = place()

        def write(bottom, top):
            for i, at in enumerate(range(span.start, span.stop)):
                start_ref[i] = (
                    top[at, RIGHT].astype(F32) + dot(bottom[at, RIGHT], top[at, LOWER])
                ).astype(BF16)

        pl.when(core == 0)(lambda: write(keep_ref, recv_ref))
        pl.when(core == 1)(lambda: write(recv_ref, keep_ref))

        @pl.when(chip == 0)
        def _():
            out_ref[...] = start_ref[...]

        @pl.when(chip != 0)
        def _():
            give(0, core, dir_ref, beside_ref, span, out_ref)

    def join(keep_ref, recv_ref, dir_ref, *refs):
        through_ref, backward_ref, bottom_ref, low_ref, high_ref, copy_ref, rim_ref = refs
        _, core = place()
        copy_ref[...] = dir_ref[...]
        for i in range(valleys):
            rim_ref[i] = dir_ref[i * downs + downs - 1]

        def write(bottom, top):
            bottom_ref[...] = bottom[:, : size + rows]
            low_ref[...] = bottom[:, UPPER]
            high_ref[...] = top[:, UPPER]
            for i in range(half):
                through_ref[i] = dot(bottom[i, LOWER], top[i, LOWER]).astype(BF16)
                backward_ref[i] = dot(top[i, UPPER], bottom[i, UPPER]).astype(BF16)

        pl.when(core == 0)(lambda: write(keep_ref, recv_ref))
        pl.when(core == 1)(lambda: write(recv_ref, keep_ref))

    def where(upper, work):
        chip, _ = place()
        pl.when((chip >= chips // 2) if upper else (chip < chips // 2))(work)

    def near(upper, dir_ref, beside_ref, lower_ref, upper_ref, diag_ref, out_ref, diag_v, sem):
        def work():
            _, core = place()
            copy = pltpu.make_async_copy(diag_ref, diag_v, sem.at[0])
            copy.start()

            def write(block_ref):
                for i in range(half):
                    at = core * half + i
                    out_ref[at] = dot(beside_ref[at], block_ref[i])

            pl.when(core == 0)(lambda: write(upper_ref))
            pl.when(core == 1)(lambda: write(lower_ref))
            copy.wait()
            for i in range(half):
                at = core * half + i
                out_ref[at] += dot(dir_ref[at], diag_v[at])
                at = (1 - core) * half + i
                out_ref[at] = dot(dir_ref[at], diag_v[at])

        where(upper, work)

    def make_near(upper, after, old):
        (result,) = call(
            functools.partial(near, upper),
            [every_sum],
            [dir_v, beside, lower_own, upper_own],
            hbm=[blocks(diag_blocks)],
            after=after,
            old=old,
            scratch=[pltpu.VMEM((chains, size, size), BF16), pltpu.SemaphoreType.DMA((1,))],
            products=2 * chains,
            room=2,
        )
        return result

    def advance(span, low, in_ref, start_ref, through_ref, dir_ref, beside_ref, out_ref):
        chip, core = place()

        @pl.when(chip == low)
        def _():
            for i, at in enumerate(range(span.start, span.stop)):
                out_ref[i] = (
                    start_ref[i].astype(F32) + dot(in_ref[i], through_ref[at])
                ).astype(BF16)

        @pl.when(chip != low)
        def _():
            give(0, core, dir_ref, beside_ref, span, out_ref)

    downs_count, valley_count = lax.axis_size("down"), lax.axis_size("valley")

    starts, fronts, heard_up = [], [], []
    for g, span in enumerate(spans):
        start, front = call(
            functools.partial(begin, span),
            [message(span)] * 2,
            [keep1, recv1, dir_v, beside],
            after=[near_sum] if g else echoing,
            products=wide(span),
        )
        starts.append(start)
        fronts.append(front)
        heard_up.append([swap_chips(front, 0)])
        if g == 0:
            through, backward, bottom, back_low, back_high, dir_out, rim_out = call(
                join,
                [square, square, ((half, size + rows, size), BF16), square, square]
                + [every_vector, ((valleys, rows, size), BF16)],
                [keep1, recv1, dir_v],
                after=[start],
                products=4 * half,
            )
            others = [
                lax.ppermute(
                    dir_out, "valley", [(i, (i + by) % valley_count) for i in range(valley_count)]
                )
                for by in range(1, valley_count)
            ]
            near_sum = make_near(True, [start], [])
    (answer,) = call(
        reflect_late,
        [((wide(answer_spans[1]), late_rows, size), BF16)],
        [keep1, recv1, dir_v, beside],
        after=echoing,
        products=4 * wide(answer_spans[1]),
    )
    answers.append(swap_chips(answer, below_top))
    rim = lax.ppermute(
        rim_out, "down", [(i, (i + 1) % downs_count) for i in range(downs_count)]
    )
    for low in range(1, below_top):
        for g, span in enumerate(spans):
            (fronts[g],) = call(
                functools.partial(advance, span, low),
                [message(span)],
                [heard_up[g][-1], starts[g], through, dir_v, beside],
                products=wide(span),
                weight=WEIGHT,
            )
            heard_up[g].append(swap_chips(fronts[g], low))
    near_sum = make_near(False, list(fronts) + [rim], [near_sum])

    def far(upper, *refs):
        where(upper, functools.partial(far_work, *refs))

    def far_work(*refs):
        dir_ref, sum_ref, rim_ref, beside_ref, lower_ref, upper_ref = refs[:6]
        others_refs = refs[6 : 5 + valley_count]
        down_ref, valley_ref, column_ref, out_ref = refs[5 + valley_count : 9 + valley_count]
        partner_ref, down_v, valley_v, column_s, sem = refs[9 + valley_count :]
        _, core = place()
        mine = lax.axis_index("valley")
        edge = lax.axis_index("down")
        copies = [
            pltpu.make_async_copy(source, target, sem.at[i])
            for i, (source, target) in enumerate(
                ((column_ref, column_s), (down_ref, down_v), (valley_ref, valley_v))
            )
        ]
        for copy in copies:
            copy.start()
        copies[0].wait()
        for i in range(chains):
            column = column_s[0, i % downs, i // downs]
            owner = column // valleys
            spot = lax.rem(column, valleys) * downs + i % downs
            behind = lax.rem(mine - owner + valley_count, valley_count)

            @pl.when(behind == 0)
            def _():
                partner_ref[i] = dir_ref[spot]

            for by in range(1, valley_count):

                @pl.when(behind == by)
                def _():
                    partner_ref[i] = others_refs[by - 1][spot]

        copies[1].wait()
        for i in range(chains):
            if i % downs:
                out_ref[i] = sum_ref[i] + dot(dir_ref[i - 1], down_v[i])

        @pl.when(edge > 0)
        def _():
            for i in range(0, chains, downs):
                out_ref[i] = sum_ref[i] + dot(rim_ref[i // downs], down_v[i])

        @pl.when(edge == 0)
        def _():
            for i in range(0, chains, downs):
                out_ref[i] = sum_ref[i]

        def add(block_ref):
            for i in range(half):
                at = (1 - core) * half + i
                out_ref[at] += dot(beside_ref[at], block_ref[i])

        pl.when(core == 0)(lambda: add(upper_ref))
        pl.when(core == 1)(lambda: add(lower_ref))
        copies[2].wait()
        for i in range(chains):
            out_ref[i] += dot(partner_ref[i], valley_v[i])

    def make_far(upper, after, old):
        (result,) = call(
            functools.partial(far, upper),
            [every_sum],
            [dir_v, near_sum, rim, beside, lower_other, upper_other] + others,
            hbm=[
                blocks(down_coupling),
                blocks(valley_coupling),
                jnp.swapaxes(coupled_column, 1, 2),
            ],
            after=after,
            old=old,
            scratch=[
                pltpu.VMEM((chains, rows, size), BF16),
                pltpu.VMEM((chains, size, size), BF16),
                pltpu.VMEM((chains, size, size), BF16),
                pltpu.SMEM((1, downs, valleys), jnp.int32),
                pltpu.SemaphoreType.DMA((3,)),
            ],
            products=2 * chains,
            room=4,
        )
        return result

    def fronts_of(span, in_ref, start_ref, through_ref, bottom_ref, low_ref, top_ref, base_ref):
        for i, at in enumerate(range(span.start, span.stop)):
            top = (start_ref[i].astype(F32) + dot(in_ref[i], through_ref[at])).astype(BF16)
            low = bottom_ref[at, size:].astype(F32) + dot(in_ref[i], bottom_ref[at, :size])
            top_ref[i] = top
            base_ref[i] = (low.astype(BF16).astype(F32) + dot(top, low_ref[at])).astype(BF16)

    def arrive(span, *refs):
        heard_refs = refs[:below_top]
        start_ref, through_ref, bottom_ref, low_ref, dir_ref, beside_ref = refs[
            below_top : below_top + 6
        ]
        top_ref, base_ref, up_ref, in_ref = refs[-4:]
        chip, core = place()

        @pl.when(chip == 0)
        def _():
            in_ref[...] = jnp.zeros_like(in_ref)

        for low in range(below_top):

            @pl.when(chip == low + 1)
            def _():
                in_ref[...] = heard_refs[low][...]

        @pl.when(chip < top_chip)
        def _():
            fronts_of(span, in_ref, start_ref, through_ref, bottom_ref, low_ref, top_ref, base_ref)

        @pl.when(chip == below_top)
        def _():
            up_ref[...] = top_ref[...]

        @pl.when(chip != below_top)
        def _():
            give(0, core, dir_ref, beside_ref, span, up_ref)

    def turn(span, *refs):
        answer_refs = refs[:2]
        top_ref, base_ref, back_ref, dir_ref, beside_ref, down_ref, echo_ref = refs[2:]
        chip, core = place()

        @pl.when(chip == below_top)
        def _():
            for i, at in enumerate(range(span.start, span.stop)):
                late = at >= first
                answer = answer_refs[late].at[at - first * late]
                echo = (
                    answer[size : size + rows, :].astype(F32) + dot(top_ref[i], answer[:size, :])
                ).astype(BF16)
                echo_ref[i] = echo
                down_ref[i] = (base_ref[i].astype(F32) + dot(echo, back_ref[at])).astype(BF16)

        @pl.when(chip != below_top)
        def _():
            give(1, core, dir_ref, beside_ref, span, down_ref)

    def crown(span, in_ref, start_ref, through_ref, bottom_ref, low_ref, top_ref, base_ref):
        chip, _ = place()

        @pl.when(chip == top_chip)
        def _():
            fronts_of(span, in_ref, start_ref, through_ref, bottom_ref, low_ref, top_ref, base_ref)

    def retreat(span, low, in_ref, base_ref, back_ref, dir_ref, beside_ref, out_ref):
        chip, core = place()

        @pl.when(chip == low)
        def _():
            for i, at in enumerate(range(span.start, span.stop)):
                out_ref[i] = (base_ref[i].astype(F32) + dot(in_ref[i], back_ref[at])).astype(BF16)

        @pl.when(chip != low)
        def _():
            give(1, core, dir_ref, beside_ref, span, out_ref)

    tops, bases, ups, solved, echoes, heard_down = [], [], [], [], [], []
    for g, span in enumerate(spans):
        top, base, up = call(
            functools.partial(arrive, span),
            [message(span)] * 3,
            heard_up[g] + [starts[g], through, bottom, back_low, dir_v, beside],
            after=[near_sum],
            scratch=[pltpu.VMEM(*message(span))],
            products=3 * wide(span),
            weight=WEIGHT,
        )
        tops.append(top)
        bases.append(base)
        ups.append(up)
    for g, span in enumerate(spans):
        down, echo = call(
            functools.partial(turn, span),
            [message(span)] * 2,
            [answers[0], answers[0] if span.stop <= first else answers[1]]
            + [tops[g], bases[g], backward, dir_v, beside],
            after=[far_sum] if g else [],
            products=2 * wide(span),
            weight=WEIGHT,
        )
        solved.append(down)
        echoes.append(echo)
        heard_down.append([swap_chips(down, below_top - 1)])
        if g == 0:
            far_sum = make_far(False, [down], [])
    for g, span in enumerate(spans):
        heard_up[g].append(swap_chips(ups[g], below_top))
        tops[g], bases[g] = call(
            functools.partial(crown, span),
            [message(span)] * 2,
            [heard_up[g][-1], starts[g], through, bottom, back_low],
            old=[tops[g], bases[g]],
            products=3 * wide(span),
        )
    for low in range(below_top - 2, -1, -1):
        for g, span in enumerate(spans):
            (solved[g],) = call(
                functools.partial(retreat, span, low + 1),
                [message(span)],
                [heard_down[g][0], bases[g], backward, dir_v, beside],
                products=wide(span),
                weight=WEIGHT,
            )
            heard_down[g].insert(0, swap_chips(solved[g], low))
    far_sum = make_far(True, list(solved), [far_sum])

    def finish(span, *refs):
        up_refs, down_refs = refs[:top_chip], refs[top_chip : 2 * top_chip - 1]
        answer_ref, echo_ref, top_ref, base_ref, back_ref, high_ref = refs[2 * top_chip - 1 : -4]
        keep_ref, own_ref, send_ref, in_ref = refs[-4:]
        chip, core = place()
        sent_halo = send_ref.at[pl.ds(wide(span), wide(span))]

        @pl.when(chip == top_chip)
        def _():
            in_ref[...] = jnp.zeros_like(in_ref)

        @pl.when(chip == below_top)
        def _():
            in_ref[...] = echo_ref[...]

        for low in range(below_top):

            @pl.when(chip == low)
            def _():
                in_ref[...] = down_refs[low][...]

        for which, mine, other in ((0, own_ref, sent_halo), (1, sent_halo, own_ref)):

            @pl.when(core == which)
            def _():
                @pl.when(chip == 0)
                def _():
                    mine[...] = jnp.zeros_like(mine)

                @pl.when(chip == top_chip)
                def _():
                    other[...] = jnp.zeros_like(other)

                @pl.when(chip == top_chip)
                def _():
                    for i, at in enumerate(range(span.start, span.stop)):
                        part, line = divmod(at * rows, late_rows)
                        mine[i] = answer_ref[part, pl.ds(line, rows)]

                for low in range(top_chip):

                    @pl.when(chip == low)
                    def _():
                        other[...] = up_refs[low][...]

                for low in range(below_top):

                    @pl.when(chip == low + 1)
                    def _():
                        mine[...] = down_refs[low][...]

        for i, at in enumerate(range(span.start, span.stop)):
            low = (base_ref[i].astype(F32) + dot(in_ref[i], back_ref[at])).astype(BF16)
            high = (top_ref[i].astype(F32) + dot(in_ref[i], high_ref[at])).astype(BF16)

            @pl.when(core == 0)
            def _():
                keep_ref[i] = low
                send_ref[i] = high

            @pl.when(core == 1)
            def _():
                keep_ref[i] = high
                send_ref[i] = low

    def final(span, *refs):
        keep_ref, own_ref, recv_ref, sum_ref = refs[:4]
        lower_refs, upper_refs = refs[4:6], refs[6:8]
        solved_ref, image_ref, total_ref, sem = refs[-4:]
        _, core = place()
        at, width = span.start, wide(span)
        copies = []
        for side, source in ((core, keep_ref), (1 - core, recv_ref.at[pl.ds(0, width)])):
            copies.append(
                pltpu.make_async_copy(
                    source, solved_ref.at[pl.ds(side * half + at, width)], sem.at[len(copies)]
                )
            )
            copies[-1].start()

        def write(block_refs):
            for number, side in enumerate((core, 1 - core)):
                base = side * half + at
                for i in range(width):
                    halo = own_ref[i] if number == 0 else recv_ref[width + i]
                    total_ref[number * width + i] = sum_ref[base + i] + dot(
                        halo, block_refs[number][at + i]
                    )

        pl.when(core == 0)(lambda: write(lower_refs))
        pl.when(core == 1)(lambda: write(upper_refs))
        for number, side in enumerate((core, 1 - core)):
            copies.append(
                pltpu.make_async_copy(
                    total_ref.at[pl.ds(number * width, width)],
                    image_ref.at[pl.ds(side * half + at, width)],
                    sem.at[len(copies)],
                )
            )
            copies[-1].start()
        for copy in copies:
            copy.wait()

    spec = pl.BlockSpec(memory_space=pltpu.VMEM)
    anywhere = pl.BlockSpec(memory_space=pl.ANY)
    outputs = []
    for g, span in enumerate(spans):
        keep, own, send = call(
            functools.partial(finish, span),
            [message(span), message(span), ((2 * wide(span), rows, size), BF16)],
            heard_up[g]
            + heard_down[g]
            + [answers[1], echoes[g], tops[g], bases[g], backward, back_high],
            after=[far_sum],
            scratch=[pltpu.VMEM(*message(span))],
            products=2 * wide(span),
        )
        operands = [keep, own, swap_cores(send), far_sum]
        operands += [lower_own, lower_other, upper_own, upper_other]
        operands = [pltpu.with_memory_space_constraint(x, VMEM) for x in operands]
        outputs = pl.pallas_call(
            functools.partial(final, span),
            out_shape=[HBM(*every_vector), HBM(*every_sum)],
            in_specs=[spec] * len(operands) + [anywhere] * len(outputs),
            out_specs=[anywhere] * 2,
            input_output_aliases={len(operands) + i: i for i in range(len(outputs))},
            scratch_shapes=[
                pltpu.VMEM((2 * wide(span), rows, size), F32),
                pltpu.SemaphoreType.DMA((4,)),
            ],
            compiler_params=pltpu.CompilerParams(vmem_limit_bytes=2 << 20),
            cost_estimate=pl.CostEstimate(
                flops=4 * wide(span), bytes_accessed=1 << 10, transcendentals=0
            ),
        )(*operands, *outputs)
    preconditioned, image = outputs
    return (preconditioned.reshape(resid.shape), image.reshape(resid.shape))


def solution(mesh):
    spec = P("elev", "valley", "down", None, None)
    in_specs = (spec,) * 8 + (P("elev", "valley", "down"),)
    return jax.shard_map(
        local, mesh=mesh, in_specs=in_specs, out_specs=(spec, spec), check_vma=False
    )
```

time: 43.6 us -> 42.2 us (0.968)
  waiting for transfers between devices: 9.09 us -> 5.73 us
  starting transfers between devices: 20.2 us -> 22.4 us
    ppermute x12, waiting for transfers between devices: 8.98 us -> 2.8 us  [swap_chips(): return lax.ppermute(value, 'elev', pairs)]
    ppermute x4, starting transfers between devices: 2.74 us -> 5.6 us  [swap_cores(): return lax.ppermute(value, 'elev', [(i, i ^ 1) for i in range(count)])]
    ppermute x1, waiting for transfers between devices: 0.01 us -> 1.43 us  [local(): lax.ppermute(dir_out, 'valley', [(i, (i + by) % valley_count) for i in ra...]
    ppermute x4, waiting for transfers between devices: 0.1 us -> 1.49 us  [swap_cores(): return lax.ppermute(value, 'elev', [(i, i ^ 1) for i in range(count)])]
    ppermute x1, starting transfers between devices: 2.34 us -> 1.24 us  [local(): lax.ppermute(dir_out, 'valley', [(i, (i + by) % valley_count) for i in ra...]
    pallas_call x22 -> x23, Pallas kernels: 10.8 us -> 10.6 us  [call(): pl.pallas_call(body, out_shape=[VMEM(shape, dtype) for shape, dtype in ou...]
  transfers between devices with their start and end apart: 18 -> 18, of which waited for: 6 -> 7; matrix products, arithmetic and copies ran while one was open for 0% -> 0% of each run, Pallas kernels for 24% -> 23%
where the time goes in v6:
time: 42.2 us; the launch traced here: 41.7 us
  starting transfers between devices  22.4 us (53%)
  Pallas kernels  12.7 us (30%)
  waiting for transfers between devices  5.73 us (14%)
  between operations  0.82 us (2%)
    ppermute x12, starting transfers between devices, swap_chips(): return lax.ppermute(value, 'elev', pairs)  14.3 us
    pallas_call x23, Pallas kernels, call(): pl.pallas_call(body, out_shape=[VMEM(shape, dtype) for shape, dtype in ou...  10.6 us
    ppermute x4, starting transfers between devices, swap_cores(): return lax.ppermute(value, 'elev', [(i, i ^ 1) for i in range(count)])  5.6 us
    ppermute x12, waiting for transfers between devices, swap_chips(): return lax.ppermute(value, 'elev', pairs)  2.8 us
    pallas_call x2, Pallas kernels, local(): pl.pallas_call(functools.partial(final, span), out_shape=[HBM(*every_vect...  2.12 us
    ppermute x4, waiting for transfers between devices, swap_cores(): return lax.ppermute(value, 'elev', [(i, i ^ 1) for i in range(count)])  1.49 us
    ppermute x1, waiting for transfers between devices, local(): lax.ppermute(dir_out, 'valley', [(i, (i + by) % valley_count) for i in ra...  1.43 us
    ppermute x1, starting transfers between devices, local(): lax.ppermute(rim_out, 'down', [(i, (i + 1) % downs_count) for i in range(...  1.28 us
  transfers between devices with their start and end apart: 18, of which 7 were waited for; matrix products, arithmetic and copies ran while one was open for 0% of the time, Pallas kernels for 23%

profile of v6, /device:TPU:1, one launch (start us, length us, event | category | flops | bytes accessed | tf_op | source)
XLA Modules:
  0.0 41.7 jit_solution(1956365036321304552)
XLA Ops:
  0.6 2.0 %shard_map.104 = (bf16[4,640,256]{2,1,0:T(8,128)(2,1)S(1)}, bf16[4,256,256]{2,1,0:T(8,128)(2,1)S(1)}, bf16[4,256,256]{2,1,0:T(8,128)(2,1)S(1)}) custom-call(bf16[8,256,256]{2,1,0:T(8,128)(2,1)} %bitcast.11, bf16[8,128,256]{2,1,0:T(8,128)(2,1)} %bitcast.23, bf16[8,256,256]{2,1,0:T(8,128)(2,1)} %bitcast.13, bf16[8,256,256]{2,1,0:T(8,128)(2,1)} %bitcast.15), custom_call_target="tpu_custom_call" | custom-call | flops 20 | bytes 1024 | tf_op jit(solution)/shard_map/pallas_call | solution.py:33
  2.8 2.0 %shard_map.105 = (bf16[4,640,256]{2,1,0:T(8,128)(2,1)S(1)}, bf16[4,256,256]{2,1,0:T(8,128)(2,1)S(1)}, bf16[4,256,256]{2,1,0:T(8,128)(2,1)S(1)}, bf16[8,128,256]{2,1,0:T(8,128)(2,1)S(1)}) custom-call(bf16[8,256,256]{2,1,0:T(8,128)(2,1)} %bitcast.12, bf16[8,128,256]{2,1,0:T(8,128)(2,1)} %bitcast.24, bf16[8,256,256]{2,1,0:T(8,128)(2,1)} %bitcast.14, ...), custom_call_target="tpu_custom_call" | custom-call | flops 20 | bytes 1024 | tf_op jit(solution)/shard_map/pallas_call | solution.py:33
  4.8 0.5 %collective-permute-start.1 = (bf16[8,128,256]{2,1,0:T(8,128)(2,1)S(1)}, bf16[8,128,256]{2,1,0:T(8,128)(2,1)S(1)}, u32[]{:S(2)}, u32[]{:S(2)}) collective-permute-start(bf16[8,128,256]{2,1,0:T(8,128)(2,1)S(1)} %get-tuple-element.46.refs_2_.refs_0_.refs_3_.refs_6_.refs_5_), channel_id=1, source_target_pairs={{0,4},{4,0},{8,12},{12,8},{16,20},{20,16},{24,28},{28,24},{1,5},{5... | collective-permute-start | bytes 1572872 | tf_op jit(solution)/shard_map/ppermute | solution.py:54
  5.3 0.5 %collective-permute-done.refs_1_ = bf16[4,640,256]{2,1,0:T(8,128)(2,1)S(1)} collective-permute-done((bf16[4,640,256]{2,1,0:T(8,128)(2,1)S(1)}, bf16[4,640,256]{2,1,0:T(8,128)(2,1)S(1)}, u32[]{:S(2)}, u32[]{:S(2)}) %collective-permute-start) | collective-permute-done | bytes 1310752 | tf_op jit(solution)/shard_map/ppermute | solution.py:54
  5.9 0.9 %collective-permute-done.1.refs_3_.refs_1_.refs_4_.refs_7_.refs_6_ = bf16[8,128,256]{2,1,0:T(8,128)(2,1)S(1)} collective-permute-done((bf16[8,128,256]{2,1,0:T(8,128)(2,1)S(1)}, bf16[8,128,256]{2,1,0:T(8,128)(2,1)S(1)}, u32[]{:S(2)}, u32[]{:S(2)}) %collective-permute-start.1) | collective-permute-done | bytes 524320 | tf_op jit(solution)/shard_map/ppermute | solution.py:54
  7.0 2.7 %collective-permute-start.4 = (bf16[2,128,256]{2,1,0:T(8,128)(2,1)S(1)}, bf16[2,128,256]{2,1,0:T(8,128)(2,1)S(1)}, u32[]{:S(2)}, u32[]{:S(2)}) collective-permute-start(bf16[2,128,256]{2,1,0:T(8,128)(2,1)S(1)} %get-tuple-element.55), channel_id=1, source_target_pairs={{0,8},{4,12},{8,0},{12,4},{16,20},{20,16},{24,28},{28,24},{1,9},{5... | collective-permute-start | bytes 393224 | tf_op jit(solution)/shard_map/ppermute | solution.py:63
  9.8 0.6 %shard_map.110 = (bf16[4,256,256]{2,1,0:T(8,128)(2,1)S(1)}, bf16[4,256,256]{2,1,0:T(8,128)(2,1)S(1)}, bf16[4,384,256]{2,1,0:T(8,128)(2,1)S(1)}, bf16[4,256,256]{...) custom-call(bf16[4,640,256]{2,1,0:T(8,128)(2,1)S(1)} %get-tuple-elem, ...), custom_call_target="tpu_custom_call" | custom-call | flops 16 | bytes 1024 | tf_op jit(solution)/shard_map/pallas_call | solution.py:33
  10.4 1.3 %collective-permute-start.5 = (bf16[4,128,256]{2,1,0:T(8,128)(2,1)S(1)}, bf16[4,128,256]{2,1,0:T(8,128)(2,1)S(1)}, u32[]{:S(2)}, u32[]{:S(2)}) collective-permute-start(bf16[4,128,256]{2,1,0:T(8,128)(2,1)S(1)} %get-tuple-element.56), channel_id=1, source_target_pairs={{0,1},{1,0},{2,3},{3,2},{4,5},{5,4},{6,7},{7,6},{8,9},{9,8},{10,11... | collective-permute-start | bytes 786440 | tf_op jit(solution)/shard_map/ppermute | solution.py:369
  11.7 1.2 %collective-permute-start.9 = (bf16[8,128,256]{2,1,0:T(8,128)(2,1)S(1)}, bf16[8,128,256]{2,1,0:T(8,128)(2,1)S(1)}, u32[]{:S(2)}, u32[]{:S(2)}) collective-permute-start(bf16[8,128,256]{2,1,0:T(8,128)(2,1)S(1)} %get-tuple-element.63), channel_id=1, source_target_pairs={{0,2},{2,0},{1,3},{3,1},{4,6},{6,4},{5,7},{7,5},{8,10},{10,8},{9,1... | collective-permute-start | bytes 1572872 | tf_op jit(solution)/shard_map/ppermute | solution.py:355
  13.5 1.2 %collective-permute-start.10 = (bf16[2,128,256]{2,1,0:T(8,128)(2,1)S(1)}, bf16[2,128,256]{2,1,0:T(8,128)(2,1)S(1)}, u32[]{:S(2)}, u32[]{:S(2)}) collective-permute-start(bf16[2,128,256]{2,1,0:T(8,128)(2,1)S(1)} %shard_map.112.refs_5_), channel_id=1, source_target_pairs={{0,4},{4,0},{8,16},{12,20},{16,8},{20,12},{24,28},{28,24},{1,5},{5... | collective-permute-start | bytes 393224 | tf_op jit(solution)/shard_map/ppermute | solution.py:63
  14.7 2.6 %collective-permute-done.2.refs_0_ = bf16[2,128,256]{2,1,0:T(8,128)(2,1)S(1)} collective-permute-done((bf16[2,128,256]{2,1,0:T(8,128)(2,1)S(1)}, bf16[2,128,256]{2,1,0:T(8,128)(2,1)S(1)}, u32[]{:S(2)}, u32[]{:S(2)}) %collective-permute-start.2) | collective-permute-done | bytes 131104 | tf_op jit(solution)/shard_map/ppermute | solution.py:63
  17.3 1.9 %collective-permute-start.3 = (bf16[2,128,256]{2,1,0:T(8,128)(2,1)S(1)}, bf16[2,128,256]{2,1,0:T(8,128)(2,1)S(1)}, u32[]{:S(2)}, u32[]{:S(2)}) collective-permute-start(bf16[2,128,256]{2,1,0:T(8,128)(2,1)S(1)} %shard_map.111.refs_6_), channel_id=1, source_target_pairs={{0,4},{4,0},{8,16},{12,20},{16,8},{20,12},{24,28},{28,24},{1,5},{5... | collective-permute-start | bytes 393224 | tf_op jit(solution)/shard_map/ppermute | solution.py:63
  19.4 1.6 %shard_map.113.refs_8_.refs_1_ = f32[8,128,256]{2,1,0:T(8,128)S(1)} custom-call(bf16[8,128,256]{2,1,0:T(8,128)(2,1)S(1)} %get-tuple-element.46.refs_2_.refs_0_.refs_3_.refs_6_.refs_5_, bf16[8,128,256]{2,1,0:T(8,128)(2,1)S(1)} %collective-permute-done.1.refs_3_.refs_1_.refs_4_.refs_7_.refs_6_, ...), custom_call_target="tpu_custom_call", output_to_operand_aliasing={{}: (8, {})} | custom-call | flops 16 | bytes 1024 | tf_op jit(solution)/shard_map/pallas_call | solution.py:33
  21.5 0.5 %collective-permute-start.14 = (bf16[2,128,256]{2,1,0:T(8,128)(2,1)S(1)}, bf16[2,128,256]{2,1,0:T(8,128)(2,1)S(1)}, u32[]{:S(2)}, u32[]{:S(2)}) collective-permute-start(bf16[2,128,256]{2,1,0:T(8,128)(2,1)S(1)} %get-tuple-element.72), channel_id=1, source_target_pairs={{0,4},{4,0},{8,12},{12,8},{16,24},{20,28},{24,16},{28,20},{1,5},{5... | collective-permute-start | bytes 393224 | tf_op jit(solution)/shard_map/ppermute | solution.py:63
  23.0 1.4 %collective-permute-done.9.refs_6_ = bf16[8,128,256]{2,1,0:T(8,128)(2,1)S(1)} collective-permute-done((bf16[8,128,256]{2,1,0:T(8,128)(2,1)S(1)}, bf16[8,128,256]{2,1,0:T(8,128)(2,1)S(1)}, u32[]{:S(2)}, u32[]{:S(2)}) %collective-permute-start.9) | collective-permute-done | bytes 524320 | tf_op jit(solution)/shard_map/ppermute | solution.py:355
  24.4 2.1 %shard_map.118.refs_7_.refs_12_ = f32[8,128,256]{2,1,0:T(8,128)S(1)} custom-call(bf16[8,128,256]{2,1,0:T(8,128)(2,1)S(1)} %get-tuple-element.46.refs_2_.refs_0_.refs_3_.refs_6_.refs_5_, f32[8,128,256]{2,1,0:T(8,128)S(1)} %shard_map.113.refs_8_.refs_1_, bf16[4,128,256]{2,1,0:T(8,128)(2,1)S(1)} %collective-permute-done.5.refs_7_.refs_2_, ...), custom_call_target="tpu_custom_call" | custom-call | flops 16 | bytes 1024 | tf_op jit(solution)/shard_map/pallas_call | solution.py:33
  26.6 1.7 %collective-permute-start.11 = (bf16[2,128,256]{2,1,0:T(8,128)(2,1)S(1)}, bf16[2,128,256]{2,1,0:T(8,128)(2,1)S(1)}, u32[]{:S(2)}, u32[]{:S(2)}) collective-permute-start(bf16[2,128,256]{2,1,0:T(8,128)(2,1)S(1)} %get-tuple-element.67), channel_id=1, source_target_pairs={{0,4},{4,0},{8,16},{12,20},{16,8},{20,12},{24,28},{28,24},{1,5},{5... | collective-permute-start | bytes 393224 | tf_op jit(solution)/shard_map/ppermute | solution.py:63
  28.3 2.9 %collective-permute-start.16 = (bf16[2,128,256]{2,1,0:T(8,128)(2,1)S(1)}, bf16[2,128,256]{2,1,0:T(8,128)(2,1)S(1)}, u32[]{:S(2)}, u32[]{:S(2)}) collective-permute-start(bf16[2,128,256]{2,1,0:T(8,128)(2,1)S(1)} %shard_map.123.refs_10_), channel_id=1, source_target_pairs={{0,8},{4,12},{8,0},{12,4},{16,20},{20,16},{24,28},{28,24},{1,9},{5... | collective-permute-start | bytes 393224 | tf_op jit(solution)/shard_map/ppermute | solution.py:63
  31.2 2.2 %collective-permute-start.12 = (bf16[2,128,256]{2,1,0:T(8,128)(2,1)S(1)}, bf16[2,128,256]{2,1,0:T(8,128)(2,1)S(1)}, u32[]{:S(2)}, u32[]{:S(2)}) collective-permute-start(bf16[2,128,256]{2,1,0:T(8,128)(2,1)S(1)} %shard_map.121.refs_11_), channel_id=1, source_target_pairs={{0,8},{4,12},{8,0},{12,4},{16,20},{20,16},{24,28},{28,24},{1,9},{5... | collective-permute-start | bytes 393224 | tf_op jit(solution)/shard_map/ppermute | solution.py:63
  34.0 3.5 %collective-permute-start.17 = (bf16[4,128,256]{2,1,0:T(8,128)(2,1)S(1)}, bf16[4,128,256]{2,1,0:T(8,128)(2,1)S(1)}, u32[]{:S(2)}, u32[]{:S(2)}) collective-permute-start(bf16[4,128,256]{2,1,0:T(8,128)(2,1)S(1)} %get-tuple-element.81), channel_id=1, source_target_pairs={{0,4},{4,0},{8,12},{12,8},{16,20},{20,16},{24,28},{28,24},{1,5},{5... | collective-permute-start | bytes 786440 | tf_op jit(solution)/shard_map/ppermute | solution.py:54
  37.5 0.5 %shard_map.125 = (bf16[2,128,256]{2,1,0:T(8,128)(2,1)S(1)}, bf16[2,128,256]{2,1,0:T(8,128)(2,1)S(1)}, bf16[4,128,256]{2,1,0:T(8,128)(2,1)S(1)}) custom-call(bf16[2,128,256]{2,1,0:T(8,128)(2,1)S(1)} %collective-permute-done.2.refs_0_, bf16[2,128,256]{2,1,0:T(8,128)(2,1)S(1)} %collective-permute-done.3.refs_1_, ...), custom_call_target="tpu_custom_call" | custom-call | flops 4 | bytes 1024 | tf_op jit(solution)/shard_map/pallas_call | solution.py:33
  38.0 1.4 %collective-permute-start.15 = (bf16[4,128,256]{2,1,0:T(8,128)(2,1)S(1)}, bf16[4,128,256]{2,1,0:T(8,128)(2,1)S(1)}, u32[]{:S(2)}, u32[]{:S(2)}) collective-permute-start(bf16[4,128,256]{2,1,0:T(8,128)(2,1)S(1)} %get-tuple-element.76), channel_id=1, source_target_pairs={{0,4},{4,0},{8,12},{12,8},{16,20},{20,16},{24,28},{28,24},{1,5},{5... | collective-permute-start | bytes 786440 | tf_op jit(solution)/shard_map/ppermute | solution.py:54
  39.5 1.1 %shard_map.127 = (bf16[8,128,256]{2,1,0:T(8,128)(2,1)}, f32[8,128,256]{2,1,0:T(8,128)}) custom-call(bf16[2,128,256]{2,1,0:T(8,128)(2,1)S(1)} %get-tuple-element.79.refs_0_, bf16[2,128,256]{2,1,0:T(8,128)(2,1)S(1)} %get-tuple-element.80.refs_1_, bf16[4,128,256]{2,1,0:T(8,128)(2,1)S(1)} %collective-permute-done.17.refs_2_, ...), custom_call_target="tpu_custom_call" | custom-call | flops 8 | bytes 1024 | tf_op jit(solution)/shard_map/pallas_call | solution.py:716
  40.6 1.1 %shard_map.128 = (bf16[8,128,256]{2,1,0:T(8,128)(2,1)}, f32[8,128,256]{2,1,0:T(8,128)}) custom-call(bf16[2,128,256]{2,1,0:T(8,128)(2,1)S(1)} %get-tuple-element.74.refs_0_, bf16[2,128,256]{2,1,0:T(8,128)(2,1)S(1)} %get-tuple-element.75.refs_1_, ...), custom_call_target="tpu_custom_call", output_to_operand_aliasing={{0}: (8, {}), {1}: (9, {})} | custom-call | flops 8 | bytes 1024 | tf_op jit(solution)/shard_map/pallas_call | solution.py:716
  (37 shorter events, 3.4 us)
Async XLA Ops:
  2.6 3.1 %collective-permute-start = (bf16[4,640,256]{2,1,0:T(8,128)(2,1)S(1)}, bf16[4,640,256]{2,1,0:T(8,128)(2,1)S(1)}, u32[]{:S(2)}, u32[]{:S(2)}) collective-permute-start(bf16[4,640,256]{2,1,0:T(8,128)(2,1)S(1)} %get-tuple-element.44.refs_5_), channel_id=1, source_target_pairs={{0,4},{4,0},{8,12},{12,8},{16,20},{20,16},{24,28},{28,24},{1,5},{5... | collective-permute-start | bytes 3932168 | tf_op jit(solution)/shard_map/ppermute | solution.py:54
  4.8 2.1 %collective-permute-start.1 = (bf16[8,128,256]{2,1,0:T(8,128)(2,1)S(1)}, bf16[8,128,256]{2,1,0:T(8,128)(2,1)S(1)}, u32[]{:S(2)}, u32[]{:S(2)}) collective-permute-start(bf16[8,128,256]{2,1,0:T(8,128)(2,1)S(1)} %get-tuple-element.46.refs_2_.refs_0_.refs_3_.refs_6_.refs_5_), channel_id=1, source_target_pairs={{0,4},{4,0},{8,12},{12,8},{16,20},{20,16},{24,28},{28,24},{1,5},{5... | collective-permute-start | bytes 1572872 | tf_op jit(solution)/shard_map/ppermute | solution.py:54
  5.7 16.8 %collective-permute-start.7 = (bf16[3,384,256]{2,1,0:T(8,128)(2,1)S(1)}, bf16[3,384,256]{2,1,0:T(8,128)(2,1)S(1)}, u32[]{:S(2)}, u32[]{:S(2)}) collective-permute-start(bf16[3,384,256]{2,1,0:T(8,128)(2,1)S(1)} %shard_map.106.refs_4_), channel_id=1, source_target_pairs={{0,4},{4,0},{8,12},{12,8},{16,24},{20,28},{24,16},{28,20},{1,5},{5... | collective-permute-start | bytes 1769480 | tf_op jit(solution)/shard_map/ppermute | solution.py:63
  7.0 6.5 %collective-permute-start.4 = (bf16[2,128,256]{2,1,0:T(8,128)(2,1)S(1)}, bf16[2,128,256]{2,1,0:T(8,128)(2,1)S(1)}, u32[]{:S(2)}, u32[]{:S(2)}) collective-permute-start(bf16[2,128,256]{2,1,0:T(8,128)(2,1)S(1)} %get-tuple-element.55), channel_id=1, source_target_pairs={{0,8},{4,12},{8,0},{12,4},{16,20},{20,16},{24,28},{28,24},{1,9},{5... | collective-permute-start | bytes 393224 | tf_op jit(solution)/shard_map/ppermute | solution.py:63
  10.4 8.9 %collective-permute-start.5 = (bf16[4,128,256]{2,1,0:T(8,128)(2,1)S(1)}, bf16[4,128,256]{2,1,0:T(8,128)(2,1)S(1)}, u32[]{:S(2)}, u32[]{:S(2)}) collective-permute-start(bf16[4,128,256]{2,1,0:T(8,128)(2,1)S(1)} %get-tuple-element.56), channel_id=1, source_target_pairs={{0,1},{1,0},{2,3},{3,2},{4,5},{5,4},{6,7},{7,6},{8,9},{9,8},{10,11... | collective-permute-start | bytes 786440 | tf_op jit(solution)/shard_map/ppermute | solution.py:369
  11.7 12.8 %collective-permute-start.9 = (bf16[8,128,256]{2,1,0:T(8,128)(2,1)S(1)}, bf16[8,128,256]{2,1,0:T(8,128)(2,1)S(1)}, u32[]{:S(2)}, u32[]{:S(2)}) collective-permute-start(bf16[8,128,256]{2,1,0:T(8,128)(2,1)S(1)} %get-tuple-element.63), channel_id=1, source_target_pairs={{0,2},{2,0},{1,3},{3,1},{4,6},{6,4},{5,7},{7,5},{8,10},{10,8},{9,1... | collective-permute-start | bytes 1572872 | tf_op jit(solution)/shard_map/ppermute | solution.py:355
  13.2 4.2 %collective-permute-start.2 = (bf16[2,128,256]{2,1,0:T(8,128)(2,1)S(1)}, bf16[2,128,256]{2,1,0:T(8,128)(2,1)S(1)}, u32[]{:S(2)}, u32[]{:S(2)}) collective-permute-start(bf16[2,128,256]{2,1,0:T(8,128)(2,1)S(1)} %get-tuple-element.50), channel_id=1, source_target_pairs={{0,8},{4,12},{8,0},{12,4},{16,20},{20,16},{24,28},{28,24},{1,9},{5... | collective-permute-start | bytes 393224 | tf_op jit(solution)/shard_map/ppermute | solution.py:63
  13.5 7.5 %collective-permute-start.10 = (bf16[2,128,256]{2,1,0:T(8,128)(2,1)S(1)}, bf16[2,128,256]{2,1,0:T(8,128)(2,1)S(1)}, u32[]{:S(2)}, u32[]{:S(2)}) collective-permute-start(bf16[2,128,256]{2,1,0:T(8,128)(2,1)S(1)} %shard_map.112.refs_5_), channel_id=1, source_target_pairs={{0,4},{4,0},{8,16},{12,20},{16,8},{20,12},{24,28},{28,24},{1,5},{5... | collective-permute-start | bytes 393224 | tf_op jit(solution)/shard_map/ppermute | solution.py:63
  17.3 4.6 %collective-permute-start.3 = (bf16[2,128,256]{2,1,0:T(8,128)(2,1)S(1)}, bf16[2,128,256]{2,1,0:T(8,128)(2,1)S(1)}, u32[]{:S(2)}, u32[]{:S(2)}) collective-permute-start(bf16[2,128,256]{2,1,0:T(8,128)(2,1)S(1)} %shard_map.111.refs_6_), channel_id=1, source_target_pairs={{0,4},{4,0},{8,16},{12,20},{16,8},{20,12},{24,28},{28,24},{1,5},{5... | collective-permute-start | bytes 393224 | tf_op jit(solution)/shard_map/ppermute | solution.py:63
  19.3 7.2 %collective-permute-start.8 = (bf16[1,512,256]{2,1,0:T(8,128)(2,1)S(1)}, bf16[1,512,256]{2,1,0:T(8,128)(2,1)S(1)}, u32[]{:S(2)}, u32[]{:S(2)}) collective-permute-start(bf16[1,512,256]{2,1,0:T(8,128)(2,1)S(1)} %shard_map.115), channel_id=1, source_target_pairs={{0,4},{4,0},{8,12},{12,8},{16,24},{20,28},{24,16},{28,20},{1,5},{5... | collective-permute-start | bytes 786440 | tf_op jit(solution)/shard_map/ppermute | solution.py:63
  21.5 6.7 %collective-permute-start.14 = (bf16[2,128,256]{2,1,0:T(8,128)(2,1)S(1)}, bf16[2,128,256]{2,1,0:T(8,128)(2,1)S(1)}, u32[]{:S(2)}, u32[]{:S(2)}) collective-permute-start(bf16[2,128,256]{2,1,0:T(8,128)(2,1)S(1)} %get-tuple-element.72), channel_id=1, source_target_pairs={{0,4},{4,0},{8,12},{12,8},{16,24},{20,28},{24,16},{28,20},{1,5},{5... | collective-permute-start | bytes 393224 | tf_op jit(solution)/shard_map/ppermute | solution.py:63
  22.3 5.9 %collective-permute-start.6 = (bf16[2,128,256]{2,1,0:T(8,128)(2,1)S(1)}, bf16[2,128,256]{2,1,0:T(8,128)(2,1)S(1)}, u32[]{:S(2)}, u32[]{:S(2)}) collective-permute-start(bf16[2,128,256]{2,1,0:T(8,128)(2,1)S(1)} %get-tuple-element.57), channel_id=1, source_target_pairs={{0,4},{4,0},{8,12},{12,8},{16,24},{20,28},{24,16},{28,20},{1,5},{5... | collective-permute-start | bytes 393224 | tf_op jit(solution)/shard_map/ppermute | solution.py:63
  22.5 5.7 %collective-permute-start.13 = (bf16[2,128,256]{2,1,0:T(8,128)(2,1)S(1)}, bf16[2,128,256]{2,1,0:T(8,128)(2,1)S(1)}, u32[]{:S(2)}, u32[]{:S(2)}) collective-permute-start(bf16[2,128,256]{2,1,0:T(8,128)(2,1)S(1)} %get-tuple-element.66.refs_10_), channel_id=1, source_target_pairs={{0,4},{4,0},{8,16},{12,20},{16,8},{20,12},{24,28},{28,24},{1,5},{5... | collective-permute-start | bytes 393224 | tf_op jit(solution)/shard_map/ppermute | solution.py:63
  26.6 4.7 %collective-permute-start.11 = (bf16[2,128,256]{2,1,0:T(8,128)(2,1)S(1)}, bf16[2,128,256]{2,1,0:T(8,128)(2,1)S(1)}, u32[]{:S(2)}, u32[]{:S(2)}) collective-permute-start(bf16[2,128,256]{2,1,0:T(8,128)(2,1)S(1)} %get-tuple-element.67), channel_id=1, source_target_pairs={{0,4},{4,0},{8,16},{12,20},{16,8},{20,12},{24,28},{28,24},{1,5},{5... | collective-permute-start | bytes 393224 | tf_op jit(solution)/shard_map/ppermute | solution.py:63
  28.3 5.3 %collective-permute-start.16 = (bf16[2,128,256]{2,1,0:T(8,128)(2,1)S(1)}, bf16[2,128,256]{2,1,0:T(8,128)(2,1)S(1)}, u32[]{:S(2)}, u32[]{:S(2)}) collective-permute-start(bf16[2,128,256]{2,1,0:T(8,128)(2,1)S(1)} %shard_map.123.refs_10_), channel_id=1, source_target_pairs={{0,8},{4,12},{8,0},{12,4},{16,20},{20,16},{24,28},{28,24},{1,9},{5... | collective-permute-start | bytes 393224 | tf_op jit(solution)/shard_map/ppermute | solution.py:63
  31.2 6.3 %collective-permute-start.12 = (bf16[2,128,256]{2,1,0:T(8,128)(2,1)S(1)}, bf16[2,128,256]{2,1,0:T(8,128)(2,1)S(1)}, u32[]{:S(2)}, u32[]{:S(2)}) collective-permute-start(bf16[2,128,256]{2,1,0:T(8,128)(2,1)S(1)} %shard_map.121.refs_11_), channel_id=1, source_target_pairs={{0,8},{4,12},{8,0},{12,4},{16,20},{20,16},{24,28},{28,24},{1,9},{5... | collective-permute-start | bytes 393224 | tf_op jit(solution)/shard_map/ppermute | solution.py:63
  34.0 5.4 %collective-permute-start.17 = (bf16[4,128,256]{2,1,0:T(8,128)(2,1)S(1)}, bf16[4,128,256]{2,1,0:T(8,128)(2,1)S(1)}, u32[]{:S(2)}, u32[]{:S(2)}) collective-permute-start(bf16[4,128,256]{2,1,0:T(8,128)(2,1)S(1)} %get-tuple-element.81), channel_id=1, source_target_pairs={{0,4},{4,0},{8,12},{12,8},{16,20},{20,16},{24,28},{28,24},{1,5},{5... | collective-permute-start | bytes 786440 | tf_op jit(solution)/shard_map/ppermute | solution.py:54
  38.0 2.6 %collective-permute-start.15 = (bf16[4,128,256]{2,1,0:T(8,128)(2,1)S(1)}, bf16[4,128,256]{2,1,0:T(8,128)(2,1)S(1)}, u32[]{:S(2)}, u32[]{:S(2)}) collective-permute-start(bf16[4,128,256]{2,1,0:T(8,128)(2,1)S(1)} %get-tuple-element.76), channel_id=1, source_target_pairs={{0,4},{4,0},{8,12},{12,8},{16,20},{20,16},{24,28},{28,24},{1,5},{5... | collective-permute-start | bytes 786440 | tf_op jit(solution)/shard_map/ppermute | solution.py:54

commit v7 on v6

--- a/solution.py
+++ b/solution.py
@@ -205,7 +205,7 @@
     answer = answer_of(answer_spans[0], [])
     answers, echoing = [swap_chips(answer, below_top)], [answer]
 
-    late_rows = max(size + rows, half * rows // wide(answer_spans[1]))
+    late_rows = max(size + rows, spans[0].stop * rows // wide(answer_spans[1]))
 
     def reflect_late(keep_ref, recv_ref, dir_ref, beside_ref, out_ref):
         chip, core = place()
@@ -213,7 +213,7 @@
 
         @pl.when(chip == below_top)
         def _():
-            for at in range(half):
+            for at in range(spans[0].stop):
                 part, line = divmod(at * rows, late_rows)
                 target = out_ref.at[part, pl.ds(line, rows)]
 
@@ -274,9 +274,9 @@
         pl.when(core == 0)(lambda: write(keep_ref, recv_ref))
         pl.when(core == 1)(lambda: write(recv_ref, keep_ref))
 
-    def where(upper, work):
+    def where(upper, edge, work):
         chip, _ = place()
-        pl.when((chip >= chips // 2) if upper else (chip < chips // 2))(work)
+        pl.when((chip >= edge) if upper else (chip < edge))(work)
 
     def near(upper, dir_ref, beside_ref, lower_ref, upper_ref, diag_ref, out_ref, diag_v, sem):
         def work():
@@ -298,7 +298,7 @@
                 at = (1 - core) * half + i
                 out_ref[at] = dot(dir_ref[at], diag_v[at])
 
-        where(upper, work)
+        where(upper, chips // 2, work)
 
     def make_near(upper, after, old):
         (result,) = call(
@@ -382,7 +382,7 @@
     near_sum = make_near(False, list(fronts) + [rim], [near_sum])
 
     def far(upper, *refs):
-        where(upper, functools.partial(far_work, *refs))
+        where(upper, 1, functools.partial(far_work, *refs))
 
     def far_work(*refs):
         dir_ref, sum_ref, rim_ref, beside_ref, lower_ref, upper_ref = refs[:6]
@@ -590,7 +590,8 @@
                 products=wide(span),
                 weight=WEIGHT,
             )
-            heard_down[g].insert(0, swap_chips(solved[g], low))
+            lows = (low, below_top) if g and low == 0 else (low,)
+            heard_down[g].insert(0, swap_chips(solved[g], *lows))
     far_sum = make_far(True, list(solved), [far_sum])
 
     def finish(span, *refs):
@@ -628,9 +629,12 @@
 
                 @pl.when(chip == top_chip)
                 def _():
-                    for i, at in enumerate(range(span.start, span.stop)):
-                        part, line = divmod(at * rows, late_rows)
-                        mine[i] = answer_ref[part, pl.ds(line, rows)]
+                    if span.start:
+                        mine[...] = down_refs[0][...]
+                    else:
+                        for at in range(span.stop):
+                            part, line = divmod(at * rows, late_rows)
+                            mine[at] = answer_ref[part, pl.ds(line, rows)]
 
                 for low in range(top_chip):
 

time: 42.2 us -> 41.9 us (level)
  starting transfers between devices: 22.4 us -> 21.7 us
    ppermute x4, starting transfers between devices: 5.6 us -> 4.79 us  [swap_cores(): return lax.ppermute(value, 'elev', [(i, i ^ 1) for i in range(count)])]
where the time goes in v7:
time: 41.9 us; the launch traced here: 41.3 us
  starting transfers between devices  21.7 us (52%)
  Pallas kernels  12.8 us (31%)
  waiting for transfers between devices  6 us (14%)
  between operations  0.83 us (2%)
    ppermute x12, starting transfers between devices, swap_chips(): return lax.ppermute(value, 'elev', pairs)  14.4 us
    pallas_call x23, Pallas kernels, call(): pl.pallas_call(body, out_shape=[VMEM(shape, dtype) for shape, dtype in ou...  10.6 us
    ppermute x4, starting transfers between devices, swap_cores(): return lax.ppermute(value, 'elev', [(i, i ^ 1) for i in range(count)])  4.79 us
    ppermute x12, waiting for transfers between devices, swap_chips(): return lax.ppermute(value, 'elev', pairs)  3.08 us
    pallas_call x2, Pallas kernels, local(): pl.pallas_call(functools.partial(final, span), out_shape=[HBM(*every_vect...  2.12 us
    ppermute x4, waiting for transfers between devices, swap_cores(): return lax.ppermute(value, 'elev', [(i, i ^ 1) for i in range(count)])  1.49 us
    ppermute x1, waiting for transfers between devices, local(): lax.ppermute(dir_out, 'valley', [(i, (i + by) % valley_count) for i in ra...  1.43 us
    ppermute x1, starting transfers between devices, local(): lax.ppermute(rim_out, 'down', [(i, (i + 1) % downs_count) for i in range(...  1.28 us
  transfers between devices with their start and end apart: 18, of which 7 were waited for; matrix products, arithmetic and copies ran while one was open for 0% of the time, Pallas kernels for 23%

profile of v7, /device:TPU:1, one launch (start us, length us, event | category | flops | bytes accessed | tf_op | source)
XLA Modules:
  0.0 41.3 jit_solution(335095268029829466)
XLA Ops:
  0.6 2.0 %shard_map.104 = (bf16[4,640,256]{2,1,0:T(8,128)(2,1)S(1)}, bf16[4,256,256]{2,1,0:T(8,128)(2,1)S(1)}, bf16[4,256,256]{2,1,0:T(8,128)(2,1)S(1)}) custom-call(bf16[8,256,256]{2,1,0:T(8,128)(2,1)} %bitcast.11, bf16[8,128,256]{2,1,0:T(8,128)(2,1)} %bitcast.23, bf16[8,256,256]{2,1,0:T(8,128)(2,1)} %bitcast.13, bf16[8,256,256]{2,1,0:T(8,128)(2,1)} %bitcast.15), custom_call_target="tpu_custom_call" | custom-call | flops 20 | bytes 1024 | tf_op jit(solution)/shard_map/pallas_call | solution.py:33
  2.8 2.0 %shard_map.105 = (bf16[4,640,256]{2,1,0:T(8,128)(2,1)S(1)}, bf16[4,256,256]{2,1,0:T(8,128)(2,1)S(1)}, bf16[4,256,256]{2,1,0:T(8,128)(2,1)S(1)}, bf16[8,128,256]{2,1,0:T(8,128)(2,1)S(1)}) custom-call(bf16[8,256,256]{2,1,0:T(8,128)(2,1)} %bitcast.12, bf16[8,128,256]{2,1,0:T(8,128)(2,1)} %bitcast.24, bf16[8,256,256]{2,1,0:T(8,128)(2,1)} %bitcast.14, ...), custom_call_target="tpu_custom_call" | custom-call | flops 20 | bytes 1024 | tf_op jit(solution)/shard_map/pallas_call | solution.py:33
  4.8 0.5 %collective-permute-start.1 = (bf16[8,128,256]{2,1,0:T(8,128)(2,1)S(1)}, bf16[8,128,256]{2,1,0:T(8,128)(2,1)S(1)}, u32[]{:S(2)}, u32[]{:S(2)}) collective-permute-start(bf16[8,128,256]{2,1,0:T(8,128)(2,1)S(1)} %get-tuple-element.46.refs_2_.refs_0_.refs_3_.refs_6_.refs_5_), channel_id=1, source_target_pairs={{0,4},{4,0},{8,12},{12,8},{16,20},{20,16},{24,28},{28,24},{1,5},{5... | collective-permute-start | bytes 1572872 | tf_op jit(solution)/shard_map/ppermute | solution.py:54
  5.3 0.5 %collective-permute-done.refs_1_ = bf16[4,640,256]{2,1,0:T(8,128)(2,1)S(1)} collective-permute-done((bf16[4,640,256]{2,1,0:T(8,128)(2,1)S(1)}, bf16[4,640,256]{2,1,0:T(8,128)(2,1)S(1)}, u32[]{:S(2)}, u32[]{:S(2)}) %collective-permute-start) | collective-permute-done | bytes 1310752 | tf_op jit(solution)/shard_map/ppermute | solution.py:54
  5.9 0.9 %collective-permute-done.1.refs_3_.refs_1_.refs_4_.refs_7_.refs_6_ = bf16[8,128,256]{2,1,0:T(8,128)(2,1)S(1)} collective-permute-done((bf16[8,128,256]{2,1,0:T(8,128)(2,1)S(1)}, bf16[8,128,256]{2,1,0:T(8,128)(2,1)S(1)}, u32[]{:S(2)}, u32[]{:S(2)}) %collective-permute-start.1) | collective-permute-done | bytes 524320 | tf_op jit(solution)/shard_map/ppermute | solution.py:54
  7.0 2.7 %collective-permute-start.4 = (bf16[2,128,256]{2,1,0:T(8,128)(2,1)S(1)}, bf16[2,128,256]{2,1,0:T(8,128)(2,1)S(1)}, u32[]{:S(2)}, u32[]{:S(2)}) collective-permute-start(bf16[2,128,256]{2,1,0:T(8,128)(2,1)S(1)} %get-tuple-element.55), channel_id=1, source_target_pairs={{0,8},{4,12},{8,0},{12,4},{16,20},{20,16},{24,28},{28,24},{1,9},{5... | collective-permute-start | bytes 393224 | tf_op jit(solution)/shard_map/ppermute | solution.py:63
  9.8 0.6 %shard_map.110 = (bf16[4,256,256]{2,1,0:T(8,128)(2,1)S(1)}, bf16[4,256,256]{2,1,0:T(8,128)(2,1)S(1)}, bf16[4,384,256]{2,1,0:T(8,128)(2,1)S(1)}, bf16[4,256,256]{...) custom-call(bf16[4,640,256]{2,1,0:T(8,128)(2,1)S(1)} %get-tuple-elem, ...), custom_call_target="tpu_custom_call" | custom-call | flops 16 | bytes 1024 | tf_op jit(solution)/shard_map/pallas_call | solution.py:33
  10.4 1.3 %collective-permute-start.5 = (bf16[4,128,256]{2,1,0:T(8,128)(2,1)S(1)}, bf16[4,128,256]{2,1,0:T(8,128)(2,1)S(1)}, u32[]{:S(2)}, u32[]{:S(2)}) collective-permute-start(bf16[4,128,256]{2,1,0:T(8,128)(2,1)S(1)} %get-tuple-element.56), channel_id=1, source_target_pairs={{0,1},{1,0},{2,3},{3,2},{4,5},{5,4},{6,7},{7,6},{8,9},{9,8},{10,11... | collective-permute-start | bytes 786440 | tf_op jit(solution)/shard_map/ppermute | solution.py:369
  11.7 1.2 %collective-permute-start.9 = (bf16[8,128,256]{2,1,0:T(8,128)(2,1)S(1)}, bf16[8,128,256]{2,1,0:T(8,128)(2,1)S(1)}, u32[]{:S(2)}, u32[]{:S(2)}) collective-permute-start(bf16[8,128,256]{2,1,0:T(8,128)(2,1)S(1)} %get-tuple-element.63), channel_id=1, source_target_pairs={{0,2},{2,0},{1,3},{3,1},{4,6},{6,4},{5,7},{7,5},{8,10},{10,8},{9,1... | collective-permute-start | bytes 1572872 | tf_op jit(solution)/shard_map/ppermute | solution.py:355
  13.5 1.2 %collective-permute-start.10 = (bf16[2,128,256]{2,1,0:T(8,128)(2,1)S(1)}, bf16[2,128,256]{2,1,0:T(8,128)(2,1)S(1)}, u32[]{:S(2)}, u32[]{:S(2)}) collective-permute-start(bf16[2,128,256]{2,1,0:T(8,128)(2,1)S(1)} %shard_map.112.refs_5_), channel_id=1, source_target_pairs={{0,4},{4,0},{8,16},{12,20},{16,8},{20,12},{24,28},{28,24},{1,5},{5... | collective-permute-start | bytes 393224 | tf_op jit(solution)/shard_map/ppermute | solution.py:63
  14.7 2.6 %collective-permute-done.2.refs_0_ = bf16[2,128,256]{2,1,0:T(8,128)(2,1)S(1)} collective-permute-done((bf16[2,128,256]{2,1,0:T(8,128)(2,1)S(1)}, bf16[2,128,256]{2,1,0:T(8,128)(2,1)S(1)}, u32[]{:S(2)}, u32[]{:S(2)}) %collective-permute-start.2) | collective-permute-done | bytes 131104 | tf_op jit(solution)/shard_map/ppermute | solution.py:63
  17.3 1.9 %collective-permute-start.3 = (bf16[2,128,256]{2,1,0:T(8,128)(2,1)S(1)}, bf16[2,128,256]{2,1,0:T(8,128)(2,1)S(1)}, u32[]{:S(2)}, u32[]{:S(2)}) collective-permute-start(bf16[2,128,256]{2,1,0:T(8,128)(2,1)S(1)} %shard_map.111.refs_6_), channel_id=1, source_target_pairs={{0,4},{4,0},{8,16},{12,20},{16,8},{20,12},{24,28},{28,24},{1,5},{5... | collective-permute-start | bytes 393224 | tf_op jit(solution)/shard_map/ppermute | solution.py:63
  19.4 1.6 %shard_map.113.refs_8_.refs_1_ = f32[8,128,256]{2,1,0:T(8,128)S(1)} custom-call(bf16[8,128,256]{2,1,0:T(8,128)(2,1)S(1)} %get-tuple-element.46.refs_2_.refs_0_.refs_3_.refs_6_.refs_5_, bf16[8,128,256]{2,1,0:T(8,128)(2,1)S(1)} %collective-permute-done.1.refs_3_.refs_1_.refs_4_.refs_7_.refs_6_, ...), custom_call_target="tpu_custom_call", output_to_operand_aliasing={{}: (8, {})} | custom-call | flops 16 | bytes 1024 | tf_op jit(solution)/shard_map/pallas_call | solution.py:33
  21.5 0.5 %collective-permute-start.14 = (bf16[2,128,256]{2,1,0:T(8,128)(2,1)S(1)}, bf16[2,128,256]{2,1,0:T(8,128)(2,1)S(1)}, u32[]{:S(2)}, u32[]{:S(2)}) collective-permute-start(bf16[2,128,256]{2,1,0:T(8,128)(2,1)S(1)} %get-tuple-element.72), channel_id=1, source_target_pairs={{0,4},{4,0},{8,12},{12,8},{16,24},{20,28},{24,16},{28,20},{1,5},{5... | collective-permute-start | bytes 393224 | tf_op jit(solution)/shard_map/ppermute | solution.py:63
  23.0 1.4 %collective-permute-done.9.refs_6_ = bf16[8,128,256]{2,1,0:T(8,128)(2,1)S(1)} collective-permute-done((bf16[8,128,256]{2,1,0:T(8,128)(2,1)S(1)}, bf16[8,128,256]{2,1,0:T(8,128)(2,1)S(1)}, u32[]{:S(2)}, u32[]{:S(2)}) %collective-permute-start.9) | collective-permute-done | bytes 524320 | tf_op jit(solution)/shard_map/ppermute | solution.py:355
  24.4 2.1 %shard_map.118.refs_7_.refs_12_ = f32[8,128,256]{2,1,0:T(8,128)S(1)} custom-call(bf16[8,128,256]{2,1,0:T(8,128)(2,1)S(1)} %get-tuple-element.46.refs_2_.refs_0_.refs_3_.refs_6_.refs_5_, f32[8,128,256]{2,1,0:T(8,128)S(1)} %shard_map.113.refs_8_.refs_1_, bf16[4,128,256]{2,1,0:T(8,128)(2,1)S(1)} %collective-permute-done.5.refs_7_.refs_2_, ...), custom_call_target="tpu_custom_call" | custom-call | flops 16 | bytes 1024 | tf_op jit(solution)/shard_map/pallas_call | solution.py:33
  26.6 1.7 %collective-permute-start.11 = (bf16[2,128,256]{2,1,0:T(8,128)(2,1)S(1)}, bf16[2,128,256]{2,1,0:T(8,128)(2,1)S(1)}, u32[]{:S(2)}, u32[]{:S(2)}) collective-permute-start(bf16[2,128,256]{2,1,0:T(8,128)(2,1)S(1)} %get-tuple-element.67), channel_id=1, source_target_pairs={{0,4},{4,0},{8,16},{12,20},{16,8},{20,12},{24,28},{28,24},{1,5},{5... | collective-permute-start | bytes 393224 | tf_op jit(solution)/shard_map/ppermute | solution.py:63
  28.3 2.9 %collective-permute-start.16 = (bf16[2,128,256]{2,1,0:T(8,128)(2,1)S(1)}, bf16[2,128,256]{2,1,0:T(8,128)(2,1)S(1)}, u32[]{:S(2)}, u32[]{:S(2)}) collective-permute-start(bf16[2,128,256]{2,1,0:T(8,128)(2,1)S(1)} %shard_map.123.refs_10_), channel_id=1, source_target_pairs={{0,8},{4,12},{8,0},{12,4},{16,20},{20,16},{24,28},{28,24},{1,9},{5... | collective-permute-start | bytes 393224 | tf_op jit(solution)/shard_map/ppermute | solution.py:63
  31.2 2.4 %collective-permute-start.12 = (bf16[2,128,256]{2,1,0:T(8,128)(2,1)S(1)}, bf16[2,128,256]{2,1,0:T(8,128)(2,1)S(1)}, u32[]{:S(2)}, u32[]{:S(2)}) collective-permute-start(bf16[2,128,256]{2,1,0:T(8,128)(2,1)S(1)} %shard_map.121.refs_11_), channel_id=1, source_target_pairs={{0,8},{4,12},{8,0},{12,4},{16,24},{20,28},{24,16},{28,20},{1,9},{5... | collective-permute-start | bytes 393224 | tf_op jit(solution)/shard_map/ppermute | solution.py:63
  33.6 0.5 %shard_map.126 = (bf16[2,128,256]{2,1,0:T(8,128)(2,1)S(1)}, bf16[2,128,256]{2,1,0:T(8,128)(2,1)S(1)}, bf16[4,128,256]{2,1,0:T(8,128)(2,1)S(1)}) custom-call(bf16[2,128,256]{2,1,0:T(8,128)(2,1)S(1)} %collective-permute-done.4.refs_0_, bf16[2,128,256]{2,1,0:T(8,128)(2,1)S(1)} %collective-permute-done.10.refs_1_, ...), custom_call_target="tpu_custom_call" | custom-call | flops 4 | bytes 1024 | tf_op jit(solution)/shard_map/pallas_call | solution.py:33
  34.1 2.7 %collective-permute-start.17 = (bf16[4,128,256]{2,1,0:T(8,128)(2,1)S(1)}, bf16[4,128,256]{2,1,0:T(8,128)(2,1)S(1)}, u32[]{:S(2)}, u32[]{:S(2)}) collective-permute-start(bf16[4,128,256]{2,1,0:T(8,128)(2,1)S(1)} %get-tuple-element.81), channel_id=1, source_target_pairs={{0,4},{4,0},{8,12},{12,8},{16,20},{20,16},{24,28},{28,24},{1,5},{5... | collective-permute-start | bytes 786440 | tf_op jit(solution)/shard_map/ppermute | solution.py:54
  37.6 1.5 %collective-permute-start.15 = (bf16[4,128,256]{2,1,0:T(8,128)(2,1)S(1)}, bf16[4,128,256]{2,1,0:T(8,128)(2,1)S(1)}, u32[]{:S(2)}, u32[]{:S(2)}) collective-permute-start(bf16[4,128,256]{2,1,0:T(8,128)(2,1)S(1)} %get-tuple-element.76), channel_id=1, source_target_pairs={{0,4},{4,0},{8,12},{12,8},{16,20},{20,16},{24,28},{28,24},{1,5},{5... | collective-permute-start | bytes 786440 | tf_op jit(solution)/shard_map/ppermute | solution.py:54
  39.1 1.1 %shard_map.127 = (bf16[8,128,256]{2,1,0:T(8,128)(2,1)}, f32[8,128,256]{2,1,0:T(8,128)}) custom-call(bf16[2,128,256]{2,1,0:T(8,128)(2,1)S(1)} %get-tuple-element.79.refs_0_, bf16[2,128,256]{2,1,0:T(8,128)(2,1)S(1)} %get-tuple-element.80.refs_1_, bf16[4,128,256]{2,1,0:T(8,128)(2,1)S(1)} %collective-permute-done.17.refs_2_, ...), custom_call_target="tpu_custom_call" | custom-call | flops 8 | bytes 1024 | tf_op jit(solution)/shard_map/pallas_call | solution.py:720
  40.3 1.1 %shard_map.128 = (bf16[8,128,256]{2,1,0:T(8,128)(2,1)}, f32[8,128,256]{2,1,0:T(8,128)}) custom-call(bf16[2,128,256]{2,1,0:T(8,128)(2,1)S(1)} %get-tuple-element.74.refs_0_, bf16[2,128,256]{2,1,0:T(8,128)(2,1)S(1)} %get-tuple-element.75.refs_1_, ...), custom_call_target="tpu_custom_call", output_to_operand_aliasing={{0}: (8, {}), {1}: (9, {})} | custom-call | flops 8 | bytes 1024 | tf_op jit(solution)/shard_map/pallas_call | solution.py:720
  (37 shorter events, 3.7 us)
Async XLA Ops:
  2.6 3.1 %collective-permute-start = (bf16[4,640,256]{2,1,0:T(8,128)(2,1)S(1)}, bf16[4,640,256]{2,1,0:T(8,128)(2,1)S(1)}, u32[]{:S(2)}, u32[]{:S(2)}) collective-permute-start(bf16[4,640,256]{2,1,0:T(8,128)(2,1)S(1)} %get-tuple-element.44.refs_5_), channel_id=1, source_target_pairs={{0,4},{4,0},{8,12},{12,8},{16,20},{20,16},{24,28},{28,24},{1,5},{5... | collective-permute-start | bytes 3932168 | tf_op jit(solution)/shard_map/ppermute | solution.py:54
  4.8 2.1 %collective-permute-start.1 = (bf16[8,128,256]{2,1,0:T(8,128)(2,1)S(1)}, bf16[8,128,256]{2,1,0:T(8,128)(2,1)S(1)}, u32[]{:S(2)}, u32[]{:S(2)}) collective-permute-start(bf16[8,128,256]{2,1,0:T(8,128)(2,1)S(1)} %get-tuple-element.46.refs_2_.refs_0_.refs_3_.refs_6_.refs_5_), channel_id=1, source_target_pairs={{0,4},{4,0},{8,12},{12,8},{16,20},{20,16},{24,28},{28,24},{1,5},{5... | collective-permute-start | bytes 1572872 | tf_op jit(solution)/shard_map/ppermute | solution.py:54
  5.7 16.8 %collective-permute-start.7 = (bf16[3,384,256]{2,1,0:T(8,128)(2,1)S(1)}, bf16[3,384,256]{2,1,0:T(8,128)(2,1)S(1)}, u32[]{:S(2)}, u32[]{:S(2)}) collective-permute-start(bf16[3,384,256]{2,1,0:T(8,128)(2,1)S(1)} %shard_map.106.refs_4_), channel_id=1, source_target_pairs={{0,4},{4,0},{8,12},{12,8},{16,24},{20,28},{24,16},{28,20},{1,5},{5... | collective-permute-start | bytes 1769480 | tf_op jit(solution)/shard_map/ppermute | solution.py:63
  7.0 6.5 %collective-permute-start.4 = (bf16[2,128,256]{2,1,0:T(8,128)(2,1)S(1)}, bf16[2,128,256]{2,1,0:T(8,128)(2,1)S(1)}, u32[]{:S(2)}, u32[]{:S(2)}) collective-permute-start(bf16[2,128,256]{2,1,0:T(8,128)(2,1)S(1)} %get-tuple-element.55), channel_id=1, source_target_pairs={{0,8},{4,12},{8,0},{12,4},{16,20},{20,16},{24,28},{28,24},{1,9},{5... | collective-permute-start | bytes 393224 | tf_op jit(solution)/shard_map/ppermute | solution.py:63
  10.4 8.9 %collective-permute-start.5 = (bf16[4,128,256]{2,1,0:T(8,128)(2,1)S(1)}, bf16[4,128,256]{2,1,0:T(8,128)(2,1)S(1)}, u32[]{:S(2)}, u32[]{:S(2)}) collective-permute-start(bf16[4,128,256]{2,1,0:T(8,128)(2,1)S(1)} %get-tuple-element.56), channel_id=1, source_target_pairs={{0,1},{1,0},{2,3},{3,2},{4,5},{5,4},{6,7},{7,6},{8,9},{9,8},{10,11... | collective-permute-start | bytes 786440 | tf_op jit(solution)/shard_map/ppermute | solution.py:369
  11.7 12.8 %collective-permute-start.9 = (bf16[8,128,256]{2,1,0:T(8,128)(2,1)S(1)}, bf16[8,128,256]{2,1,0:T(8,128)(2,1)S(1)}, u32[]{:S(2)}, u32[]{:S(2)}) collective-permute-start(bf16[8,128,256]{2,1,0:T(8,128)(2,1)S(1)} %get-tuple-element.63), channel_id=1, source_target_pairs={{0,2},{2,0},{1,3},{3,1},{4,6},{6,4},{5,7},{7,5},{8,10},{10,8},{9,1... | collective-permute-start | bytes 1572872 | tf_op jit(solution)/shard_map/ppermute | solution.py:355
  13.2 4.2 %collective-permute-start.2 = (bf16[2,128,256]{2,1,0:T(8,128)(2,1)S(1)}, bf16[2,128,256]{2,1,0:T(8,128)(2,1)S(1)}, u32[]{:S(2)}, u32[]{:S(2)}) collective-permute-start(bf16[2,128,256]{2,1,0:T(8,128)(2,1)S(1)} %get-tuple-element.50), channel_id=1, source_target_pairs={{0,8},{4,12},{8,0},{12,4},{16,20},{20,16},{24,28},{28,24},{1,9},{5... | collective-permute-start | bytes 393224 | tf_op jit(solution)/shard_map/ppermute | solution.py:63
  13.5 7.5 %collective-permute-start.10 = (bf16[2,128,256]{2,1,0:T(8,128)(2,1)S(1)}, bf16[2,128,256]{2,1,0:T(8,128)(2,1)S(1)}, u32[]{:S(2)}, u32[]{:S(2)}) collective-permute-start(bf16[2,128,256]{2,1,0:T(8,128)(2,1)S(1)} %shard_map.112.refs_5_), channel_id=1, source_target_pairs={{0,4},{4,0},{8,16},{12,20},{16,8},{20,12},{24,28},{28,24},{1,5},{5... | collective-permute-start | bytes 393224 | tf_op jit(solution)/shard_map/ppermute | solution.py:63
  17.3 4.6 %collective-permute-start.3 = (bf16[2,128,256]{2,1,0:T(8,128)(2,1)S(1)}, bf16[2,128,256]{2,1,0:T(8,128)(2,1)S(1)}, u32[]{:S(2)}, u32[]{:S(2)}) collective-permute-start(bf16[2,128,256]{2,1,0:T(8,128)(2,1)S(1)} %shard_map.111.refs_6_), channel_id=1, source_target_pairs={{0,4},{4,0},{8,16},{12,20},{16,8},{20,12},{24,28},{28,24},{1,5},{5... | collective-permute-start | bytes 393224 | tf_op jit(solution)/shard_map/ppermute | solution.py:63
  19.3 7.2 %collective-permute-start.8 = (bf16[1,384,256]{2,1,0:T(8,128)(2,1)S(1)}, bf16[1,384,256]{2,1,0:T(8,128)(2,1)S(1)}, u32[]{:S(2)}, u32[]{:S(2)}) collective-permute-start(bf16[1,384,256]{2,1,0:T(8,128)(2,1)S(1)} %shard_map.115), channel_id=1, source_target_pairs={{0,4},{4,0},{8,12},{12,8},{16,24},{20,28},{24,16},{28,20},{1,5},{5... | collective-permute-start | bytes 589832 | tf_op jit(solution)/shard_map/ppermute | solution.py:63
  21.5 6.7 %collective-permute-start.14 = (bf16[2,128,256]{2,1,0:T(8,128)(2,1)S(1)}, bf16[2,128,256]{2,1,0:T(8,128)(2,1)S(1)}, u32[]{:S(2)}, u32[]{:S(2)}) collective-permute-start(bf16[2,128,256]{2,1,0:T(8,128)(2,1)S(1)} %get-tuple-element.72), channel_id=1, source_target_pairs={{0,4},{4,0},{8,12},{12,8},{16,24},{20,28},{24,16},{28,20},{1,5},{5... | collective-permute-start | bytes 393224 | tf_op jit(solution)/shard_map/ppermute | solution.py:63
  22.3 5.9 %collective-permute-start.6 = (bf16[2,128,256]{2,1,0:T(8,128)(2,1)S(1)}, bf16[2,128,256]{2,1,0:T(8,128)(2,1)S(1)}, u32[]{:S(2)}, u32[]{:S(2)}) collective-permute-start(bf16[2,128,256]{2,1,0:T(8,128)(2,1)S(1)} %get-tuple-element.57), channel_id=1, source_target_pairs={{0,4},{4,0},{8,12},{12,8},{16,24},{20,28},{24,16},{28,20},{1,5},{5... | collective-permute-start | bytes 393224 | tf_op jit(solution)/shard_map/ppermute | solution.py:63
  22.5 5.7 %collective-permute-start.13 = (bf16[2,128,256]{2,1,0:T(8,128)(2,1)S(1)}, bf16[2,128,256]{2,1,0:T(8,128)(2,1)S(1)}, u32[]{:S(2)}, u32[]{:S(2)}) collective-permute-start(bf16[2,128,256]{2,1,0:T(8,128)(2,1)S(1)} %get-tuple-element.66.refs_10_), channel_id=1, source_target_pairs={{0,4},{4,0},{8,16},{12,20},{16,8},{20,12},{24,28},{28,24},{1,5},{5... | collective-permute-start | bytes 393224 | tf_op jit(solution)/shard_map/ppermute | solution.py:63
  26.6 4.7 %collective-permute-start.11 = (bf16[2,128,256]{2,1,0:T(8,128)(2,1)S(1)}, bf16[2,128,256]{2,1,0:T(8,128)(2,1)S(1)}, u32[]{:S(2)}, u32[]{:S(2)}) collective-permute-start(bf16[2,128,256]{2,1,0:T(8,128)(2,1)S(1)} %get-tuple-element.67), channel_id=1, source_target_pairs={{0,4},{4,0},{8,16},{12,20},{16,8},{20,12},{24,28},{28,24},{1,5},{5... | collective-permute-start | bytes 393224 | tf_op jit(solution)/shard_map/ppermute | solution.py:63
  28.3 5.4 %collective-permute-start.16 = (bf16[2,128,256]{2,1,0:T(8,128)(2,1)S(1)}, bf16[2,128,256]{2,1,0:T(8,128)(2,1)S(1)}, u32[]{:S(2)}, u32[]{:S(2)}) collective-permute-start(bf16[2,128,256]{2,1,0:T(8,128)(2,1)S(1)} %shard_map.123.refs_10_), channel_id=1, source_target_pairs={{0,8},{4,12},{8,0},{12,4},{16,20},{20,16},{24,28},{28,24},{1,9},{5... | collective-permute-start | bytes 393224 | tf_op jit(solution)/shard_map/ppermute | solution.py:63
  31.2 5.9 %collective-permute-start.12 = (bf16[2,128,256]{2,1,0:T(8,128)(2,1)S(1)}, bf16[2,128,256]{2,1,0:T(8,128)(2,1)S(1)}, u32[]{:S(2)}, u32[]{:S(2)}) collective-permute-start(bf16[2,128,256]{2,1,0:T(8,128)(2,1)S(1)} %shard_map.121.refs_11_), channel_id=1, source_target_pairs={{0,8},{4,12},{8,0},{12,4},{16,24},{20,28},{24,16},{28,20},{1,9},{5... | collective-permute-start | bytes 393224 | tf_op jit(solution)/shard_map/ppermute | solution.py:63
  34.1 5.0 %collective-permute-start.17 = (bf16[4,128,256]{2,1,0:T(8,128)(2,1)S(1)}, bf16[4,128,256]{2,1,0:T(8,128)(2,1)S(1)}, u32[]{:S(2)}, u32[]{:S(2)}) collective-permute-start(bf16[4,128,256]{2,1,0:T(8,128)(2,1)S(1)} %get-tuple-element.81), channel_id=1, source_target_pairs={{0,4},{4,0},{8,12},{12,8},{16,20},{20,16},{24,28},{28,24},{1,5},{5... | collective-permute-start | bytes 786440 | tf_op jit(solution)/shard_map/ppermute | solution.py:54
  37.6 2.6 %collective-permute-start.15 = (bf16[4,128,256]{2,1,0:T(8,128)(2,1)S(1)}, bf16[4,128,256]{2,1,0:T(8,128)(2,1)S(1)}, u32[]{:S(2)}, u32[]{:S(2)}) collective-permute-start(bf16[4,128,256]{2,1,0:T(8,128)(2,1)S(1)} %get-tuple-element.76), channel_id=1, source_target_pairs={{0,4},{4,0},{8,12},{12,8},{16,20},{20,16},{24,28},{28,24},{1,5},{5... | collective-permute-start | bytes 786440 | tf_op jit(solution)/shard_map/ppermute | solution.py:54

commit v8 on v7

--- a/solution.py
+++ b/solution.py
@@ -382,7 +382,7 @@
     near_sum = make_near(False, list(fronts) + [rim], [near_sum])
 
     def far(upper, *refs):
-        where(upper, 1, functools.partial(far_work, *refs))
+        where(upper, chips // 2, functools.partial(far_work, *refs))
 
     def far_work(*refs):
         dir_ref, sum_ref, rim_ref, beside_ref, lower_ref, upper_ref = refs[:6]
@@ -572,7 +572,7 @@
         heard_down.append([swap_chips(down, below_top - 1)])
         if g == 0:
             far_sum = make_far(False, [down], [])
-    for g, span in enumerate(spans):
+    def take_in(g, span):
         heard_up[g].append(swap_chips(ups[g], below_top))
         tops[g], bases[g] = call(
             functools.partial(crown, span),
@@ -581,6 +581,8 @@
             old=[tops[g], bases[g]],
             products=3 * wide(span),
         )
+
+    take_in(0, spans[0])
     for low in range(below_top - 2, -1, -1):
         for g, span in enumerate(spans):
             (solved[g],) = call(
@@ -592,6 +594,7 @@
             )
             lows = (low, below_top) if g and low == 0 else (low,)
             heard_down[g].insert(0, swap_chips(solved[g], *lows))
+    take_in(1, spans[1])
     far_sum = make_far(True, list(solved), [far_sum])
 
     def finish(span, *refs):

time: 41.9 us -> 41.9 us (level)
  waiting for transfers between devices: 6 us -> 8.01 us
  starting transfers between devices: 21.7 us -> 19.8 us
    ppermute x12, waiting for transfers between devices: 3.08 us -> 4.67 us  [swap_chips(): return lax.ppermute(value, 'elev', pairs)]
    ppermute x4, starting transfers between devices: 4.79 us -> 3.78 us  [swap_cores(): return lax.ppermute(value, 'elev', [(i, i ^ 1) for i in range(count)])]
    ppermute x12, starting transfers between devices: 14.4 us -> 13.5 us  [swap_chips(): return lax.ppermute(value, 'elev', pairs)]
where the time goes in v8:
time: 41.9 us; the launch traced here: 41.4 us
  starting transfers between devices  19.8 us (47%)
  Pallas kernels  12.7 us (30%)
  waiting for transfers between devices  8.01 us (19%)
  between operations  0.82 us (2%)
    ppermute x12, starting transfers between devices, swap_chips(): return lax.ppermute(value, 'elev', pairs)  13.5 us
    pallas_call x23, Pallas kernels, call(): pl.pallas_call(body, out_shape=[VMEM(shape, dtype) for shape, dtype in ou...  10.6 us
    ppermute x12, waiting for transfers between devices, swap_chips(): return lax.ppermute(value, 'elev', pairs)  4.67 us
    ppermute x4, starting transfers between devices, swap_cores(): return lax.ppermute(value, 'elev', [(i, i ^ 1) for i in range(count)])  3.78 us
    pallas_call x2, Pallas kernels, local(): pl.pallas_call(functools.partial(final, span), out_shape=[HBM(*every_vect...  2.12 us
    ppermute x1, waiting for transfers between devices, local(): lax.ppermute(dir_out, 'valley', [(i, (i + by) % valley_count) for i in ra...  1.85 us
    ppermute x4, waiting for transfers between devices, swap_cores(): return lax.ppermute(value, 'elev', [(i, i ^ 1) for i in range(count)])  1.49 us
    ppermute x1, starting transfers between devices, local(): lax.ppermute(rim_out, 'down', [(i, (i + 1) % downs_count) for i in range(...  1.28 us
  transfers between devices with their start and end apart: 18, of which 7 were waited for; matrix products, arithmetic and copies ran while one was open for 0% of the time, Pallas kernels for 23%

profile of v8, /device:TPU:1, one launch (start us, length us, event | category | flops | bytes accessed | tf_op | source)
XLA Modules:
  0.0 41.4 jit_solution(17166445618569834287)
XLA Ops:
  0.6 2.0 %shard_map.104 = (bf16[4,640,256]{2,1,0:T(8,128)(2,1)S(1)}, bf16[4,256,256]{2,1,0:T(8,128)(2,1)S(1)}, bf16[4,256,256]{2,1,0:T(8,128)(2,1)S(1)}) custom-call(bf16[8,256,256]{2,1,0:T(8,128)(2,1)} %bitcast.11, bf16[8,128,256]{2,1,0:T(8,128)(2,1)} %bitcast.23, bf16[8,256,256]{2,1,0:T(8,128)(2,1)} %bitcast.13, bf16[8,256,256]{2,1,0:T(8,128)(2,1)} %bitcast.15), custom_call_target="tpu_custom_call" | custom-call | flops 20 | bytes 1024 | tf_op jit(solution)/shard_map/pallas_call | solution.py:33
  2.8 2.0 %shard_map.105 = (bf16[4,640,256]{2,1,0:T(8,128)(2,1)S(1)}, bf16[4,256,256]{2,1,0:T(8,128)(2,1)S(1)}, bf16[4,256,256]{2,1,0:T(8,128)(2,1)S(1)}, bf16[8,128,256]{2,1,0:T(8,128)(2,1)S(1)}) custom-call(bf16[8,256,256]{2,1,0:T(8,128)(2,1)} %bitcast.12, bf16[8,128,256]{2,1,0:T(8,128)(2,1)} %bitcast.24, bf16[8,256,256]{2,1,0:T(8,128)(2,1)} %bitcast.14, ...), custom_call_target="tpu_custom_call" | custom-call | flops 20 | bytes 1024 | tf_op jit(solution)/shard_map/pallas_call | solution.py:33
  4.8 0.5 %collective-permute-start.1 = (bf16[8,128,256]{2,1,0:T(8,128)(2,1)S(1)}, bf16[8,128,256]{2,1,0:T(8,128)(2,1)S(1)}, u32[]{:S(2)}, u32[]{:S(2)}) collective-permute-start(bf16[8,128,256]{2,1,0:T(8,128)(2,1)S(1)} %get-tuple-element.46.refs_2_.refs_0_.refs_3_.refs_6_.refs_5_), channel_id=1, source_target_pairs={{0,4},{4,0},{8,12},{12,8},{16,20},{20,16},{24,28},{28,24},{1,5},{5... | collective-permute-start | bytes 1572872 | tf_op jit(solution)/shard_map/ppermute | solution.py:54
  5.3 0.5 %collective-permute-done.refs_1_ = bf16[4,640,256]{2,1,0:T(8,128)(2,1)S(1)} collective-permute-done((bf16[4,640,256]{2,1,0:T(8,128)(2,1)S(1)}, bf16[4,640,256]{2,1,0:T(8,128)(2,1)S(1)}, u32[]{:S(2)}, u32[]{:S(2)}) %collective-permute-start) | collective-permute-done | bytes 1310752 | tf_op jit(solution)/shard_map/ppermute | solution.py:54
  5.9 0.9 %collective-permute-done.1.refs_3_.refs_1_.refs_4_.refs_7_.refs_6_ = bf16[8,128,256]{2,1,0:T(8,128)(2,1)S(1)} collective-permute-done((bf16[8,128,256]{2,1,0:T(8,128)(2,1)S(1)}, bf16[8,128,256]{2,1,0:T(8,128)(2,1)S(1)}, u32[]{:S(2)}, u32[]{:S(2)}) %collective-permute-start.1) | collective-permute-done | bytes 524320 | tf_op jit(solution)/shard_map/ppermute | solution.py:54
  7.0 2.7 %collective-permute-start.4 = (bf16[2,128,256]{2,1,0:T(8,128)(2,1)S(1)}, bf16[2,128,256]{2,1,0:T(8,128)(2,1)S(1)}, u32[]{:S(2)}, u32[]{:S(2)}) collective-permute-start(bf16[2,128,256]{2,1,0:T(8,128)(2,1)S(1)} %get-tuple-element.55), channel_id=1, source_target_pairs={{0,8},{4,12},{8,0},{12,4},{16,20},{20,16},{24,28},{28,24},{1,9},{5... | collective-permute-start | bytes 393224 | tf_op jit(solution)/shard_map/ppermute | solution.py:63
  9.8 0.6 %shard_map.110 = (bf16[4,256,256]{2,1,0:T(8,128)(2,1)S(1)}, bf16[4,256,256]{2,1,0:T(8,128)(2,1)S(1)}, bf16[4,384,256]{2,1,0:T(8,128)(2,1)S(1)}, bf16[4,256,256]{...) custom-call(bf16[4,640,256]{2,1,0:T(8,128)(2,1)S(1)} %get-tuple-elem, ...), custom_call_target="tpu_custom_call" | custom-call | flops 16 | bytes 1024 | tf_op jit(solution)/shard_map/pallas_call | solution.py:33
  10.4 1.3 %collective-permute-start.5 = (bf16[4,128,256]{2,1,0:T(8,128)(2,1)S(1)}, bf16[4,128,256]{2,1,0:T(8,128)(2,1)S(1)}, u32[]{:S(2)}, u32[]{:S(2)}) collective-permute-start(bf16[4,128,256]{2,1,0:T(8,128)(2,1)S(1)} %get-tuple-element.56), channel_id=1, source_target_pairs={{0,1},{1,0},{2,3},{3,2},{4,5},{5,4},{6,7},{7,6},{8,9},{9,8},{10,11... | collective-permute-start | bytes 786440 | tf_op jit(solution)/shard_map/ppermute | solution.py:369
  11.7 1.2 %collective-permute-start.9 = (bf16[8,128,256]{2,1,0:T(8,128)(2,1)S(1)}, bf16[8,128,256]{2,1,0:T(8,128)(2,1)S(1)}, u32[]{:S(2)}, u32[]{:S(2)}) collective-permute-start(bf16[8,128,256]{2,1,0:T(8,128)(2,1)S(1)} %get-tuple-element.63), channel_id=1, source_target_pairs={{0,2},{2,0},{1,3},{3,1},{4,6},{6,4},{5,7},{7,5},{8,10},{10,8},{9,1... | collective-permute-start | bytes 1572872 | tf_op jit(solution)/shard_map/ppermute | solution.py:355
  13.5 1.2 %collective-permute-start.10 = (bf16[2,128,256]{2,1,0:T(8,128)(2,1)S(1)}, bf16[2,128,256]{2,1,0:T(8,128)(2,1)S(1)}, u32[]{:S(2)}, u32[]{:S(2)}) collective-permute-start(bf16[2,128,256]{2,1,0:T(8,128)(2,1)S(1)} %shard_map.112.refs_5_), channel_id=1, source_target_pairs={{0,4},{4,0},{8,16},{12,20},{16,8},{20,12},{24,28},{28,24},{1,5},{5... | collective-permute-start | bytes 393224 | tf_op jit(solution)/shard_map/ppermute | solution.py:63
  14.7 2.6 %collective-permute-done.2.refs_0_ = bf16[2,128,256]{2,1,0:T(8,128)(2,1)S(1)} collective-permute-done((bf16[2,128,256]{2,1,0:T(8,128)(2,1)S(1)}, bf16[2,128,256]{2,1,0:T(8,128)(2,1)S(1)}, u32[]{:S(2)}, u32[]{:S(2)}) %collective-permute-start.2) | collective-permute-done | bytes 131104 | tf_op jit(solution)/shard_map/ppermute | solution.py:63
  17.3 1.9 %collective-permute-start.3 = (bf16[2,128,256]{2,1,0:T(8,128)(2,1)S(1)}, bf16[2,128,256]{2,1,0:T(8,128)(2,1)S(1)}, u32[]{:S(2)}, u32[]{:S(2)}) collective-permute-start(bf16[2,128,256]{2,1,0:T(8,128)(2,1)S(1)} %shard_map.111.refs_6_), channel_id=1, source_target_pairs={{0,4},{4,0},{8,16},{12,20},{16,8},{20,12},{24,28},{28,24},{1,5},{5... | collective-permute-start | bytes 393224 | tf_op jit(solution)/shard_map/ppermute | solution.py:63
  19.4 1.6 %shard_map.113.refs_8_.refs_1_ = f32[8,128,256]{2,1,0:T(8,128)S(1)} custom-call(bf16[8,128,256]{2,1,0:T(8,128)(2,1)S(1)} %get-tuple-element.46.refs_2_.refs_0_.refs_3_.refs_6_.refs_5_, bf16[8,128,256]{2,1,0:T(8,128)(2,1)S(1)} %collective-permute-done.1.refs_3_.refs_1_.refs_4_.refs_7_.refs_6_, ...), custom_call_target="tpu_custom_call", output_to_operand_aliasing={{}: (8, {})} | custom-call | flops 16 | bytes 1024 | tf_op jit(solution)/shard_map/pallas_call | solution.py:33
  21.5 0.5 %collective-permute-start.14 = (bf16[2,128,256]{2,1,0:T(8,128)(2,1)S(1)}, bf16[2,128,256]{2,1,0:T(8,128)(2,1)S(1)}, u32[]{:S(2)}, u32[]{:S(2)}) collective-permute-start(bf16[2,128,256]{2,1,0:T(8,128)(2,1)S(1)} %get-tuple-element.72), channel_id=1, source_target_pairs={{0,4},{4,0},{8,12},{12,8},{16,24},{20,28},{24,16},{28,20},{1,5},{5... | collective-permute-start | bytes 393224 | tf_op jit(solution)/shard_map/ppermute | solution.py:63
  22.6 1.8 %collective-permute-done.9.refs_6_ = bf16[8,128,256]{2,1,0:T(8,128)(2,1)S(1)} collective-permute-done((bf16[8,128,256]{2,1,0:T(8,128)(2,1)S(1)}, bf16[8,128,256]{2,1,0:T(8,128)(2,1)S(1)}, u32[]{:S(2)}, u32[]{:S(2)}) %collective-permute-start.9) | collective-permute-done | bytes 524320 | tf_op jit(solution)/shard_map/ppermute | solution.py:355
  24.4 2.1 %shard_map.118.refs_7_.refs_12_ = f32[8,128,256]{2,1,0:T(8,128)S(1)} custom-call(bf16[8,128,256]{2,1,0:T(8,128)(2,1)S(1)} %get-tuple-element.46.refs_2_.refs_0_.refs_3_.refs_6_.refs_5_, f32[8,128,256]{2,1,0:T(8,128)S(1)} %shard_map.113.refs_8_.refs_1_, bf16[4,128,256]{2,1,0:T(8,128)(2,1)S(1)} %collective-permute-done.5.refs_7_.refs_2_, ...), custom_call_target="tpu_custom_call" | custom-call | flops 16 | bytes 1024 | tf_op jit(solution)/shard_map/pallas_call | solution.py:33
  26.6 1.7 %collective-permute-start.11 = (bf16[2,128,256]{2,1,0:T(8,128)(2,1)S(1)}, bf16[2,128,256]{2,1,0:T(8,128)(2,1)S(1)}, u32[]{:S(2)}, u32[]{:S(2)}) collective-permute-start(bf16[2,128,256]{2,1,0:T(8,128)(2,1)S(1)} %get-tuple-element.67), channel_id=1, source_target_pairs={{0,4},{4,0},{8,16},{12,20},{16,8},{20,12},{24,28},{28,24},{1,5},{5... | collective-permute-start | bytes 393224 | tf_op jit(solution)/shard_map/ppermute | solution.py:63
  28.3 3.0 %collective-permute-start.16 = (bf16[2,128,256]{2,1,0:T(8,128)(2,1)S(1)}, bf16[2,128,256]{2,1,0:T(8,128)(2,1)S(1)}, u32[]{:S(2)}, u32[]{:S(2)}) collective-permute-start(bf16[2,128,256]{2,1,0:T(8,128)(2,1)S(1)} %shard_map.123.refs_10_), channel_id=1, source_target_pairs={{0,8},{4,12},{8,0},{12,4},{16,20},{20,16},{24,28},{28,24},{1,9},{5... | collective-permute-start | bytes 393224 | tf_op jit(solution)/shard_map/ppermute | solution.py:63
  31.4 1.7 %collective-permute-start.12 = (bf16[2,128,256]{2,1,0:T(8,128)(2,1)S(1)}, bf16[2,128,256]{2,1,0:T(8,128)(2,1)S(1)}, u32[]{:S(2)}, u32[]{:S(2)}) collective-permute-start(bf16[2,128,256]{2,1,0:T(8,128)(2,1)S(1)} %shard_map.120.refs_11_), channel_id=1, source_target_pairs={{0,8},{4,12},{8,0},{12,4},{16,24},{20,28},{24,16},{28,20},{1,9},{5... | collective-permute-start | bytes 393224 | tf_op jit(solution)/shard_map/ppermute | solution.py:63
  33.1 1.9 %collective-permute-done.16.refs_3_ = bf16[2,128,256]{2,1,0:T(8,128)(2,1)S(1)} collective-permute-done((bf16[2,128,256]{2,1,0:T(8,128)(2,1)S(1)}, bf16[2,128,256]{2,1,0:T(8,128)(2,1)S(1)}, u32[]{:S(2)}, u32[]{:S(2)}) %collective-permute-start.16) | collective-permute-done | bytes 131104 | tf_op jit(solution)/shard_map/ppermute | solution.py:63
  35.5 1.1 %collective-permute-start.17 = (bf16[4,128,256]{2,1,0:T(8,128)(2,1)S(1)}, bf16[4,128,256]{2,1,0:T(8,128)(2,1)S(1)}, u32[]{:S(2)}, u32[]{:S(2)}) collective-permute-start(bf16[4,128,256]{2,1,0:T(8,128)(2,1)S(1)} %get-tuple-element.81), channel_id=1, source_target_pairs={{0,4},{4,0},{8,12},{12,8},{16,20},{20,16},{24,28},{28,24},{1,5},{5... | collective-permute-start | bytes 786440 | tf_op jit(solution)/shard_map/ppermute | solution.py:54
  37.1 2.0 %collective-permute-start.15 = (bf16[4,128,256]{2,1,0:T(8,128)(2,1)S(1)}, bf16[4,128,256]{2,1,0:T(8,128)(2,1)S(1)}, u32[]{:S(2)}, u32[]{:S(2)}) collective-permute-start(bf16[4,128,256]{2,1,0:T(8,128)(2,1)S(1)} %get-tuple-element.76), channel_id=1, source_target_pairs={{0,4},{4,0},{8,12},{12,8},{16,20},{20,16},{24,28},{28,24},{1,5},{5... | collective-permute-start | bytes 786440 | tf_op jit(solution)/shard_map/ppermute | solution.py:54
  39.1 1.1 %shard_map.127 = (bf16[8,128,256]{2,1,0:T(8,128)(2,1)}, f32[8,128,256]{2,1,0:T(8,128)}) custom-call(bf16[2,128,256]{2,1,0:T(8,128)(2,1)S(1)} %get-tuple-element.79.refs_0_, bf16[2,128,256]{2,1,0:T(8,128)(2,1)S(1)} %get-tuple-element.80.refs_1_, bf16[4,128,256]{2,1,0:T(8,128)(2,1)S(1)} %collective-permute-done.17.refs_2_, ...), custom_call_target="tpu_custom_call" | custom-call | flops 8 | bytes 1024 | tf_op jit(solution)/shard_map/pallas_call | solution.py:723
  40.3 1.1 %shard_map.128 = (bf16[8,128,256]{2,1,0:T(8,128)(2,1)}, f32[8,128,256]{2,1,0:T(8,128)}) custom-call(bf16[2,128,256]{2,1,0:T(8,128)(2,1)S(1)} %get-tuple-element.74.refs_0_, bf16[2,128,256]{2,1,0:T(8,128)(2,1)S(1)} %get-tuple-element.75.refs_1_, ...), custom_call_target="tpu_custom_call", output_to_operand_aliasing={{0}: (8, {}), {1}: (9, {})} | custom-call | flops 8 | bytes 1024 | tf_op jit(solution)/shard_map/pallas_call | solution.py:723
  (37 shorter events, 3.4 us)
Async XLA Ops:
  2.6 3.1 %collective-permute-start = (bf16[4,640,256]{2,1,0:T(8,128)(2,1)S(1)}, bf16[4,640,256]{2,1,0:T(8,128)(2,1)S(1)}, u32[]{:S(2)}, u32[]{:S(2)}) collective-permute-start(bf16[4,640,256]{2,1,0:T(8,128)(2,1)S(1)} %get-tuple-element.44.refs_5_), channel_id=1, source_target_pairs={{0,4},{4,0},{8,12},{12,8},{16,20},{20,16},{24,28},{28,24},{1,5},{5... | collective-permute-start | bytes 3932168 | tf_op jit(solution)/shard_map/ppermute | solution.py:54
  4.8 2.1 %collective-permute-start.1 = (bf16[8,128,256]{2,1,0:T(8,128)(2,1)S(1)}, bf16[8,128,256]{2,1,0:T(8,128)(2,1)S(1)}, u32[]{:S(2)}, u32[]{:S(2)}) collective-permute-start(bf16[8,128,256]{2,1,0:T(8,128)(2,1)S(1)} %get-tuple-element.46.refs_2_.refs_0_.refs_3_.refs_6_.refs_5_), channel_id=1, source_target_pairs={{0,4},{4,0},{8,12},{12,8},{16,20},{20,16},{24,28},{28,24},{1,5},{5... | collective-permute-start | bytes 1572872 | tf_op jit(solution)/shard_map/ppermute | solution.py:54
  5.7 16.6 %collective-permute-start.7 = (bf16[3,384,256]{2,1,0:T(8,128)(2,1)S(1)}, bf16[3,384,256]{2,1,0:T(8,128)(2,1)S(1)}, u32[]{:S(2)}, u32[]{:S(2)}) collective-permute-start(bf16[3,384,256]{2,1,0:T(8,128)(2,1)S(1)} %shard_map.106.refs_4_), channel_id=1, source_target_pairs={{0,4},{4,0},{8,12},{12,8},{16,24},{20,28},{24,16},{28,20},{1,5},{5... | collective-permute-start | bytes 1769480 | tf_op jit(solution)/shard_map/ppermute | solution.py:63
  7.0 6.5 %collective-permute-start.4 = (bf16[2,128,256]{2,1,0:T(8,128)(2,1)S(1)}, bf16[2,128,256]{2,1,0:T(8,128)(2,1)S(1)}, u32[]{:S(2)}, u32[]{:S(2)}) collective-permute-start(bf16[2,128,256]{2,1,0:T(8,128)(2,1)S(1)} %get-tuple-element.55), channel_id=1, source_target_pairs={{0,8},{4,12},{8,0},{12,4},{16,20},{20,16},{24,28},{28,24},{1,9},{5... | collective-permute-start | bytes 393224 | tf_op jit(solution)/shard_map/ppermute | solution.py:63
  10.4 8.9 %collective-permute-start.5 = (bf16[4,128,256]{2,1,0:T(8,128)(2,1)S(1)}, bf16[4,128,256]{2,1,0:T(8,128)(2,1)S(1)}, u32[]{:S(2)}, u32[]{:S(2)}) collective-permute-start(bf16[4,128,256]{2,1,0:T(8,128)(2,1)S(1)} %get-tuple-element.56), channel_id=1, source_target_pairs={{0,1},{1,0},{2,3},{3,2},{4,5},{5,4},{6,7},{7,6},{8,9},{9,8},{10,11... | collective-permute-start | bytes 786440 | tf_op jit(solution)/shard_map/ppermute | solution.py:369
  11.7 12.8 %collective-permute-start.9 = (bf16[8,128,256]{2,1,0:T(8,128)(2,1)S(1)}, bf16[8,128,256]{2,1,0:T(8,128)(2,1)S(1)}, u32[]{:S(2)}, u32[]{:S(2)}) collective-permute-start(bf16[8,128,256]{2,1,0:T(8,128)(2,1)S(1)} %get-tuple-element.63), channel_id=1, source_target_pairs={{0,2},{2,0},{1,3},{3,1},{4,6},{6,4},{5,7},{7,5},{8,10},{10,8},{9,1... | collective-permute-start | bytes 1572872 | tf_op jit(solution)/shard_map/ppermute | solution.py:355
  13.2 4.2 %collective-permute-start.2 = (bf16[2,128,256]{2,1,0:T(8,128)(2,1)S(1)}, bf16[2,128,256]{2,1,0:T(8,128)(2,1)S(1)}, u32[]{:S(2)}, u32[]{:S(2)}) collective-permute-start(bf16[2,128,256]{2,1,0:T(8,128)(2,1)S(1)} %get-tuple-element.50), channel_id=1, source_target_pairs={{0,8},{4,12},{8,0},{12,4},{16,20},{20,16},{24,28},{28,24},{1,9},{5... | collective-permute-start | bytes 393224 | tf_op jit(solution)/shard_map/ppermute | solution.py:63
  13.5 7.5 %collective-permute-start.10 = (bf16[2,128,256]{2,1,0:T(8,128)(2,1)S(1)}, bf16[2,128,256]{2,1,0:T(8,128)(2,1)S(1)}, u32[]{:S(2)}, u32[]{:S(2)}) collective-permute-start(bf16[2,128,256]{2,1,0:T(8,128)(2,1)S(1)} %shard_map.112.refs_5_), channel_id=1, source_target_pairs={{0,4},{4,0},{8,16},{12,20},{16,8},{20,12},{24,28},{28,24},{1,5},{5... | collective-permute-start | bytes 393224 | tf_op jit(solution)/shard_map/ppermute | solution.py:63
  17.3 4.6 %collective-permute-start.3 = (bf16[2,128,256]{2,1,0:T(8,128)(2,1)S(1)}, bf16[2,128,256]{2,1,0:T(8,128)(2,1)S(1)}, u32[]{:S(2)}, u32[]{:S(2)}) collective-permute-start(bf16[2,128,256]{2,1,0:T(8,128)(2,1)S(1)} %shard_map.111.refs_6_), channel_id=1, source_target_pairs={{0,4},{4,0},{8,16},{12,20},{16,8},{20,12},{24,28},{28,24},{1,5},{5... | collective-permute-start | bytes 393224 | tf_op jit(solution)/shard_map/ppermute | solution.py:63
  19.3 7.2 %collective-permute-start.8 = (bf16[1,384,256]{2,1,0:T(8,128)(2,1)S(1)}, bf16[1,384,256]{2,1,0:T(8,128)(2,1)S(1)}, u32[]{:S(2)}, u32[]{:S(2)}) collective-permute-start(bf16[1,384,256]{2,1,0:T(8,128)(2,1)S(1)} %shard_map.115), channel_id=1, source_target_pairs={{0,4},{4,0},{8,12},{12,8},{16,24},{20,28},{24,16},{28,20},{1,5},{5... | collective-permute-start | bytes 589832 | tf_op jit(solution)/shard_map/ppermute | solution.py:63
  21.5 6.8 %collective-permute-start.14 = (bf16[2,128,256]{2,1,0:T(8,128)(2,1)S(1)}, bf16[2,128,256]{2,1,0:T(8,128)(2,1)S(1)}, u32[]{:S(2)}, u32[]{:S(2)}) collective-permute-start(bf16[2,128,256]{2,1,0:T(8,128)(2,1)S(1)} %get-tuple-element.72), channel_id=1, source_target_pairs={{0,4},{4,0},{8,12},{12,8},{16,24},{20,28},{24,16},{28,20},{1,5},{5... | collective-permute-start | bytes 393224 | tf_op jit(solution)/shard_map/ppermute | solution.py:63
  22.4 5.9 %collective-permute-start.13 = (bf16[2,128,256]{2,1,0:T(8,128)(2,1)S(1)}, bf16[2,128,256]{2,1,0:T(8,128)(2,1)S(1)}, u32[]{:S(2)}, u32[]{:S(2)}) collective-permute-start(bf16[2,128,256]{2,1,0:T(8,128)(2,1)S(1)} %get-tuple-element.66.refs_10_), channel_id=1, source_target_pairs={{0,4},{4,0},{8,16},{12,20},{16,8},{20,12},{24,28},{28,24},{1,5},{5... | collective-permute-start | bytes 393224 | tf_op jit(solution)/shard_map/ppermute | solution.py:63
  26.6 4.8 %collective-permute-start.11 = (bf16[2,128,256]{2,1,0:T(8,128)(2,1)S(1)}, bf16[2,128,256]{2,1,0:T(8,128)(2,1)S(1)}, u32[]{:S(2)}, u32[]{:S(2)}) collective-permute-start(bf16[2,128,256]{2,1,0:T(8,128)(2,1)S(1)} %get-tuple-element.67), channel_id=1, source_target_pairs={{0,4},{4,0},{8,16},{12,20},{16,8},{20,12},{24,28},{28,24},{1,5},{5... | collective-permute-start | bytes 393224 | tf_op jit(solution)/shard_map/ppermute | solution.py:63
  28.2 4.9 %collective-permute-start.6 = (bf16[2,128,256]{2,1,0:T(8,128)(2,1)S(1)}, bf16[2,128,256]{2,1,0:T(8,128)(2,1)S(1)}, u32[]{:S(2)}, u32[]{:S(2)}) collective-permute-start(bf16[2,128,256]{2,1,0:T(8,128)(2,1)S(1)} %get-tuple-element.57), channel_id=1, source_target_pairs={{0,4},{4,0},{8,12},{12,8},{16,24},{20,28},{24,16},{28,20},{1,5},{5... | collective-permute-start | bytes 393224 | tf_op jit(solution)/shard_map/ppermute | solution.py:63
  28.3 6.8 %collective-permute-start.16 = (bf16[2,128,256]{2,1,0:T(8,128)(2,1)S(1)}, bf16[2,128,256]{2,1,0:T(8,128)(2,1)S(1)}, u32[]{:S(2)}, u32[]{:S(2)}) collective-permute-start(bf16[2,128,256]{2,1,0:T(8,128)(2,1)S(1)} %shard_map.123.refs_10_), channel_id=1, source_target_pairs={{0,8},{4,12},{8,0},{12,4},{16,20},{20,16},{24,28},{28,24},{1,9},{5... | collective-permute-start | bytes 393224 | tf_op jit(solution)/shard_map/ppermute | solution.py:63
  31.4 5.3 %collective-permute-start.12 = (bf16[2,128,256]{2,1,0:T(8,128)(2,1)S(1)}, bf16[2,128,256]{2,1,0:T(8,128)(2,1)S(1)}, u32[]{:S(2)}, u32[]{:S(2)}) collective-permute-start(bf16[2,128,256]{2,1,0:T(8,128)(2,1)S(1)} %shard_map.120.refs_11_), channel_id=1, source_target_pairs={{0,8},{4,12},{8,0},{12,4},{16,24},{20,28},{24,16},{28,20},{1,9},{5... | collective-permute-start | bytes 393224 | tf_op jit(solution)/shard_map/ppermute | solution.py:63
  35.5 3.6 %collective-permute-start.17 = (bf16[4,128,256]{2,1,0:T(8,128)(2,1)S(1)}, bf16[4,128,256]{2,1,0:T(8,128)(2,1)S(1)}, u32[]{:S(2)}, u32[]{:S(2)}) collective-permute-start(bf16[4,128,256]{2,1,0:T(8,128)(2,1)S(1)} %get-tuple-element.81), channel_id=1, source_target_pairs={{0,4},{4,0},{8,12},{12,8},{16,20},{20,16},{24,28},{28,24},{1,5},{5... | collective-permute-start | bytes 786440 | tf_op jit(solution)/shard_map/ppermute | solution.py:54
  37.1 3.2 %collective-permute-start.15 = (bf16[4,128,256]{2,1,0:T(8,128)(2,1)S(1)}, bf16[4,128,256]{2,1,0:T(8,128)(2,1)S(1)}, u32[]{:S(2)}, u32[]{:S(2)}) collective-permute-start(bf16[4,128,256]{2,1,0:T(8,128)(2,1)S(1)} %get-tuple-element.76), channel_id=1, source_target_pairs={{0,4},{4,0},{8,12},{12,8},{16,20},{20,16},{24,28},{28,24},{1,5},{5... | collective-permute-start | bytes 786440 | tf_op jit(solution)/shard_map/ppermute | solution.py:54

commit v9 on v8

--- a/solution.py
+++ b/solution.py
@@ -382,7 +382,7 @@
     near_sum = make_near(False, list(fronts) + [rim], [near_sum])
 
     def far(upper, *refs):
-        where(upper, chips // 2, functools.partial(far_work, *refs))
+        where(upper, 1, functools.partial(far_work, *refs))
 
     def far_work(*refs):
         dir_ref, sum_ref, rim_ref, beside_ref, lower_ref, upper_ref = refs[:6]

time: 41.9 us -> 41.9 us (level)
  starting transfers between devices: 19.8 us -> 17.8 us
  waiting for transfers between devices: 8.01 us -> 10 us
    ppermute x12, waiting for transfers between devices: 4.67 us -> 6.66 us  [swap_chips(): return lax.ppermute(value, 'elev', pairs)]
    ppermute x4, starting transfers between devices: 3.78 us -> 2.65 us  [swap_cores(): return lax.ppermute(value, 'elev', [(i, i ^ 1) for i in range(count)])]
    ppermute x12, starting transfers between devices: 13.5 us -> 12.6 us  [swap_chips(): return lax.ppermute(value, 'elev', pairs)]
  transfers between devices with their start and end apart: 18 -> 18, of which waited for: 7 -> 8; matrix products, arithmetic and copies ran while one was open for 0% -> 0% of each run, Pallas kernels for 23% -> 23%
where the time goes in v9:
time: 41.9 us; the launch traced here: 41.4 us
  starting transfers between devices  17.8 us (42%)
  Pallas kernels  12.7 us (30%)
  waiting for transfers between devices  10 us (24%)
  between operations  0.82 us (2%)
    ppermute x12, starting transfers between devices, swap_chips(): return lax.ppermute(value, 'elev', pairs)  12.6 us
    pallas_call x23, Pallas kernels, call(): pl.pallas_call(body, out_shape=[VMEM(shape, dtype) for shape, dtype in ou...  10.6 us
    ppermute x12, waiting for transfers between devices, swap_chips(): return lax.ppermute(value, 'elev', pairs)  6.66 us
    ppermute x4, starting transfers between devices, swap_cores(): return lax.ppermute(value, 'elev', [(i, i ^ 1) for i in range(count)])  2.65 us
    pallas_call x2, Pallas kernels, local(): pl.pallas_call(functools.partial(final, span), out_shape=[HBM(*every_vect...  2.12 us
    ppermute x1, waiting for transfers between devices, local(): lax.ppermute(dir_out, 'valley', [(i, (i + by) % valley_count) for i in ra...  1.85 us
    ppermute x4, waiting for transfers between devices, swap_cores(): return lax.ppermute(value, 'elev', [(i, i ^ 1) for i in range(count)])  1.49 us
    ppermute x1, starting transfers between devices, local(): lax.ppermute(rim_out, 'down', [(i, (i + 1) % downs_count) for i in range(...  1.28 us
  transfers between devices with their start and end apart: 18, of which 8 were waited for; matrix products, arithmetic and copies ran while one was open for 0% of the time, Pallas kernels for 23%

profile of v9, /device:TPU:1, one launch (start us, length us, event | category | flops | bytes accessed | tf_op | source)
XLA Modules:
  0.0 41.4 jit_solution(8604279069138726658)
XLA Ops:
  0.6 2.0 %shard_map.104 = (bf16[4,640,256]{2,1,0:T(8,128)(2,1)S(1)}, bf16[4,256,256]{2,1,0:T(8,128)(2,1)S(1)}, bf16[4,256,256]{2,1,0:T(8,128)(2,1)S(1)}) custom-call(bf16[8,256,256]{2,1,0:T(8,128)(2,1)} %bitcast.11, bf16[8,128,256]{2,1,0:T(8,128)(2,1)} %bitcast.23, bf16[8,256,256]{2,1,0:T(8,128)(2,1)} %bitcast.13, bf16[8,256,256]{2,1,0:T(8,128)(2,1)} %bitcast.15), custom_call_target="tpu_custom_call" | custom-call | flops 20 | bytes 1024 | tf_op jit(solution)/shard_map/pallas_call | solution.py:33
  2.8 2.0 %shard_map.105 = (bf16[4,640,256]{2,1,0:T(8,128)(2,1)S(1)}, bf16[4,256,256]{2,1,0:T(8,128)(2,1)S(1)}, bf16[4,256,256]{2,1,0:T(8,128)(2,1)S(1)}, bf16[8,128,256]{2,1,0:T(8,128)(2,1)S(1)}) custom-call(bf16[8,256,256]{2,1,0:T(8,128)(2,1)} %bitcast.12, bf16[8,128,256]{2,1,0:T(8,128)(2,1)} %bitcast.24, bf16[8,256,256]{2,1,0:T(8,128)(2,1)} %bitcast.14, ...), custom_call_target="tpu_custom_call" | custom-call | flops 20 | bytes 1024 | tf_op jit(solution)/shard_map/pallas_call | solution.py:33
  4.8 0.5 %collective-permute-start.1 = (bf16[8,128,256]{2,1,0:T(8,128)(2,1)S(1)}, bf16[8,128,256]{2,1,0:T(8,128)(2,1)S(1)}, u32[]{:S(2)}, u32[]{:S(2)}) collective-permute-start(bf16[8,128,256]{2,1,0:T(8,128)(2,1)S(1)} %get-tuple-element.46.refs_2_.refs_0_.refs_3_.refs_6_.refs_5_), channel_id=1, source_target_pairs={{0,4},{4,0},{8,12},{12,8},{16,20},{20,16},{24,28},{28,24},{1,5},{5... | collective-permute-start | bytes 1572872 | tf_op jit(solution)/shard_map/ppermute | solution.py:54
  5.9 0.9 %collective-permute-done.1.refs_3_.refs_1_.refs_4_.refs_7_.refs_6_ = bf16[8,128,256]{2,1,0:T(8,128)(2,1)S(1)} collective-permute-done((bf16[8,128,256]{2,1,0:T(8,128)(2,1)S(1)}, bf16[8,128,256]{2,1,0:T(8,128)(2,1)S(1)}, u32[]{:S(2)}, u32[]{:S(2)}) %collective-permute-start.1) | collective-permute-done | bytes 524320 | tf_op jit(solution)/shard_map/ppermute | solution.py:54
  7.0 2.7 %collective-permute-start.4 = (bf16[2,128,256]{2,1,0:T(8,128)(2,1)S(1)}, bf16[2,128,256]{2,1,0:T(8,128)(2,1)S(1)}, u32[]{:S(2)}, u32[]{:S(2)}) collective-permute-start(bf16[2,128,256]{2,1,0:T(8,128)(2,1)S(1)} %get-tuple-element.55), channel_id=1, source_target_pairs={{0,8},{4,12},{8,0},{12,4},{16,20},{20,16},{24,28},{28,24},{1,9},{5... | collective-permute-start | bytes 393224 | tf_op jit(solution)/shard_map/ppermute | solution.py:63
  9.8 0.6 %shard_map.110 = (bf16[4,256,256]{2,1,0:T(8,128)(2,1)S(1)}, bf16[4,256,256]{2,1,0:T(8,128)(2,1)S(1)}, bf16[4,384,256]{2,1,0:T(8,128)(2,1)S(1)}, bf16[4,256,256]{...) custom-call(bf16[4,640,256]{2,1,0:T(8,128)(2,1)S(1)} %get-tuple-elem, ...), custom_call_target="tpu_custom_call" | custom-call | flops 16 | bytes 1024 | tf_op jit(solution)/shard_map/pallas_call | solution.py:33
  10.4 1.3 %collective-permute-start.5 = (bf16[4,128,256]{2,1,0:T(8,128)(2,1)S(1)}, bf16[4,128,256]{2,1,0:T(8,128)(2,1)S(1)}, u32[]{:S(2)}, u32[]{:S(2)}) collective-permute-start(bf16[4,128,256]{2,1,0:T(8,128)(2,1)S(1)} %get-tuple-element.56), channel_id=1, source_target_pairs={{0,1},{1,0},{2,3},{3,2},{4,5},{5,4},{6,7},{7,6},{8,9},{9,8},{10,11... | collective-permute-start | bytes 786440 | tf_op jit(solution)/shard_map/ppermute | solution.py:369
  11.7 1.2 %collective-permute-start.9 = (bf16[8,128,256]{2,1,0:T(8,128)(2,1)S(1)}, bf16[8,128,256]{2,1,0:T(8,128)(2,1)S(1)}, u32[]{:S(2)}, u32[]{:S(2)}) collective-permute-start(bf16[8,128,256]{2,1,0:T(8,128)(2,1)S(1)} %get-tuple-element.63), channel_id=1, source_target_pairs={{0,2},{2,0},{1,3},{3,1},{4,6},{6,4},{5,7},{7,5},{8,10},{10,8},{9,1... | collective-permute-start | bytes 1572872 | tf_op jit(solution)/shard_map/ppermute | solution.py:355
  13.5 1.2 %collective-permute-start.10 = (bf16[2,128,256]{2,1,0:T(8,128)(2,1)S(1)}, bf16[2,128,256]{2,1,0:T(8,128)(2,1)S(1)}, u32[]{:S(2)}, u32[]{:S(2)}) collective-permute-start(bf16[2,128,256]{2,1,0:T(8,128)(2,1)S(1)} %shard_map.112.refs_5_), channel_id=1, source_target_pairs={{0,4},{4,0},{8,16},{12,20},{16,8},{20,12},{24,28},{28,24},{1,5},{5... | collective-permute-start | bytes 393224 | tf_op jit(solution)/shard_map/ppermute | solution.py:63
  14.7 2.6 %collective-permute-done.2.refs_0_ = bf16[2,128,256]{2,1,0:T(8,128)(2,1)S(1)} collective-permute-done((bf16[2,128,256]{2,1,0:T(8,128)(2,1)S(1)}, bf16[2,128,256]{2,1,0:T(8,128)(2,1)S(1)}, u32[]{:S(2)}, u32[]{:S(2)}) %collective-permute-start.2) | collective-permute-done | bytes 131104 | tf_op jit(solution)/shard_map/ppermute | solution.py:63
  17.3 1.9 %collective-permute-start.3 = (bf16[2,128,256]{2,1,0:T(8,128)(2,1)S(1)}, bf16[2,128,256]{2,1,0:T(8,128)(2,1)S(1)}, u32[]{:S(2)}, u32[]{:S(2)}) collective-permute-start(bf16[2,128,256]{2,1,0:T(8,128)(2,1)S(1)} %shard_map.111.refs_6_), channel_id=1, source_target_pairs={{0,4},{4,0},{8,16},{12,20},{16,8},{20,12},{24,28},{28,24},{1,5},{5... | collective-permute-start | bytes 393224 | tf_op jit(solution)/shard_map/ppermute | solution.py:63
  19.4 1.6 %shard_map.113.refs_8_.refs_1_ = f32[8,128,256]{2,1,0:T(8,128)S(1)} custom-call(bf16[8,128,256]{2,1,0:T(8,128)(2,1)S(1)} %get-tuple-element.46.refs_2_.refs_0_.refs_3_.refs_6_.refs_5_, bf16[8,128,256]{2,1,0:T(8,128)(2,1)S(1)} %collective-permute-done.1.refs_3_.refs_1_.refs_4_.refs_7_.refs_6_, ...), custom_call_target="tpu_custom_call", output_to_operand_aliasing={{}: (8, {})} | custom-call | flops 16 | bytes 1024 | tf_op jit(solution)/shard_map/pallas_call | solution.py:33
  21.5 0.5 %collective-permute-start.14 = (bf16[2,128,256]{2,1,0:T(8,128)(2,1)S(1)}, bf16[2,128,256]{2,1,0:T(8,128)(2,1)S(1)}, u32[]{:S(2)}, u32[]{:S(2)}) collective-permute-start(bf16[2,128,256]{2,1,0:T(8,128)(2,1)S(1)} %get-tuple-element.72), channel_id=1, source_target_pairs={{0,4},{4,0},{8,12},{12,8},{16,24},{20,28},{24,16},{28,20},{1,5},{5... | collective-permute-start | bytes 393224 | tf_op jit(solution)/shard_map/ppermute | solution.py:63
  22.6 1.8 %collective-permute-done.9.refs_6_ = bf16[8,128,256]{2,1,0:T(8,128)(2,1)S(1)} collective-permute-done((bf16[8,128,256]{2,1,0:T(8,128)(2,1)S(1)}, bf16[8,128,256]{2,1,0:T(8,128)(2,1)S(1)}, u32[]{:S(2)}, u32[]{:S(2)}) %collective-permute-start.9) | collective-permute-done | bytes 524320 | tf_op jit(solution)/shard_map/ppermute | solution.py:355
  24.4 2.1 %shard_map.118.refs_7_.refs_12_ = f32[8,128,256]{2,1,0:T(8,128)S(1)} custom-call(bf16[8,128,256]{2,1,0:T(8,128)(2,1)S(1)} %get-tuple-element.46.refs_2_.refs_0_.refs_3_.refs_6_.refs_5_, f32[8,128,256]{2,1,0:T(8,128)S(1)} %shard_map.113.refs_8_.refs_1_, bf16[4,128,256]{2,1,0:T(8,128)(2,1)S(1)} %collective-permute-done.5.refs_7_.refs_2_, ...), custom_call_target="tpu_custom_call" | custom-call | flops 16 | bytes 1024 | tf_op jit(solution)/shard_map/pallas_call | solution.py:33
  26.6 1.7 %collective-permute-start.11 = (bf16[2,128,256]{2,1,0:T(8,128)(2,1)S(1)}, bf16[2,128,256]{2,1,0:T(8,128)(2,1)S(1)}, u32[]{:S(2)}, u32[]{:S(2)}) collective-permute-start(bf16[2,128,256]{2,1,0:T(8,128)(2,1)S(1)} %get-tuple-element.67), channel_id=1, source_target_pairs={{0,4},{4,0},{8,16},{12,20},{16,8},{20,12},{24,28},{28,24},{1,5},{5... | collective-permute-start | bytes 393224 | tf_op jit(solution)/shard_map/ppermute | solution.py:63
  28.3 3.0 %collective-permute-start.16 = (bf16[2,128,256]{2,1,0:T(8,128)(2,1)S(1)}, bf16[2,128,256]{2,1,0:T(8,128)(2,1)S(1)}, u32[]{:S(2)}, u32[]{:S(2)}) collective-permute-start(bf16[2,128,256]{2,1,0:T(8,128)(2,1)S(1)} %shard_map.123.refs_10_), channel_id=1, source_target_pairs={{0,8},{4,12},{8,0},{12,4},{16,20},{20,16},{24,28},{28,24},{1,9},{5... | collective-permute-start | bytes 393224 | tf_op jit(solution)/shard_map/ppermute | solution.py:63
  31.4 0.8 %collective-permute-start.12 = (bf16[2,128,256]{2,1,0:T(8,128)(2,1)S(1)}, bf16[2,128,256]{2,1,0:T(8,128)(2,1)S(1)}, u32[]{:S(2)}, u32[]{:S(2)}) collective-permute-start(bf16[2,128,256]{2,1,0:T(8,128)(2,1)S(1)} %shard_map.120.refs_11_), channel_id=1, source_target_pairs={{0,8},{4,12},{8,0},{12,4},{16,24},{20,28},{24,16},{28,20},{1,9},{5... | collective-permute-start | bytes 393224 | tf_op jit(solution)/shard_map/ppermute | solution.py:63
  32.3 2.8 %collective-permute-done.16.refs_3_ = bf16[2,128,256]{2,1,0:T(8,128)(2,1)S(1)} collective-permute-done((bf16[2,128,256]{2,1,0:T(8,128)(2,1)S(1)}, bf16[2,128,256]{2,1,0:T(8,128)(2,1)S(1)}, u32[]{:S(2)}, u32[]{:S(2)}) %collective-permute-start.16) | collective-permute-done | bytes 131104 | tf_op jit(solution)/shard_map/ppermute | solution.py:63
  35.5 1.2 %collective-permute-start.17 = (bf16[4,128,256]{2,1,0:T(8,128)(2,1)S(1)}, bf16[4,128,256]{2,1,0:T(8,128)(2,1)S(1)}, u32[]{:S(2)}, u32[]{:S(2)}) collective-permute-start(bf16[4,128,256]{2,1,0:T(8,128)(2,1)S(1)} %get-tuple-element.81), channel_id=1, source_target_pairs={{0,4},{4,0},{8,12},{12,8},{16,20},{20,16},{24,28},{28,24},{1,5},{5... | collective-permute-start | bytes 786440 | tf_op jit(solution)/shard_map/ppermute | solution.py:54
  36.7 1.2 %collective-permute-done.12.refs_3_ = bf16[2,128,256]{2,1,0:T(8,128)(2,1)S(1)} collective-permute-done((bf16[2,128,256]{2,1,0:T(8,128)(2,1)S(1)}, bf16[2,128,256]{2,1,0:T(8,128)(2,1)S(1)}, u32[]{:S(2)}, u32[]{:S(2)}) %collective-permute-start.12) | collective-permute-done | bytes 131104 | tf_op jit(solution)/shard_map/ppermute | solution.py:63
  38.3 0.8 %collective-permute-start.15 = (bf16[4,128,256]{2,1,0:T(8,128)(2,1)S(1)}, bf16[4,128,256]{2,1,0:T(8,128)(2,1)S(1)}, u32[]{:S(2)}, u32[]{:S(2)}) collective-permute-start(bf16[4,128,256]{2,1,0:T(8,128)(2,1)S(1)} %get-tuple-element.76), channel_id=1, source_target_pairs={{0,4},{4,0},{8,12},{12,8},{16,20},{20,16},{24,28},{28,24},{1,5},{5... | collective-permute-start | bytes 786440 | tf_op jit(solution)/shard_map/ppermute | solution.py:54
  39.1 1.1 %shard_map.127 = (bf16[8,128,256]{2,1,0:T(8,128)(2,1)}, f32[8,128,256]{2,1,0:T(8,128)}) custom-call(bf16[2,128,256]{2,1,0:T(8,128)(2,1)S(1)} %get-tuple-element.79.refs_0_, bf16[2,128,256]{2,1,0:T(8,128)(2,1)S(1)} %get-tuple-element.80.refs_1_, bf16[4,128,256]{2,1,0:T(8,128)(2,1)S(1)} %collective-permute-done.17.refs_2_, ...), custom_call_target="tpu_custom_call" | custom-call | flops 8 | bytes 1024 | tf_op jit(solution)/shard_map/pallas_call | solution.py:723
  40.3 1.1 %shard_map.128 = (bf16[8,128,256]{2,1,0:T(8,128)(2,1)}, f32[8,128,256]{2,1,0:T(8,128)}) custom-call(bf16[2,128,256]{2,1,0:T(8,128)(2,1)S(1)} %get-tuple-element.74.refs_0_, bf16[2,128,256]{2,1,0:T(8,128)(2,1)S(1)} %get-tuple-element.75.refs_1_, ...), custom_call_target="tpu_custom_call", output_to_operand_aliasing={{0}: (8, {}), {1}: (9, {})} | custom-call | flops 8 | bytes 1024 | tf_op jit(solution)/shard_map/pallas_call | solution.py:723
  (37 shorter events, 3.9 us)
Async XLA Ops:
  2.6 3.1 %collective-permute-start = (bf16[4,640,256]{2,1,0:T(8,128)(2,1)S(1)}, bf16[4,640,256]{2,1,0:T(8,128)(2,1)S(1)}, u32[]{:S(2)}, u32[]{:S(2)}) collective-permute-start(bf16[4,640,256]{2,1,0:T(8,128)(2,1)S(1)} %get-tuple-element.44.refs_5_), channel_id=1, source_target_pairs={{0,4},{4,0},{8,12},{12,8},{16,20},{20,16},{24,28},{28,24},{1,5},{5... | collective-permute-start | bytes 3932168 | tf_op jit(solution)/shard_map/ppermute | solution.py:54
  4.8 2.1 %collective-permute-start.1 = (bf16[8,128,256]{2,1,0:T(8,128)(2,1)S(1)}, bf16[8,128,256]{2,1,0:T(8,128)(2,1)S(1)}, u32[]{:S(2)}, u32[]{:S(2)}) collective-permute-start(bf16[8,128,256]{2,1,0:T(8,128)(2,1)S(1)} %get-tuple-element.46.refs_2_.refs_0_.refs_3_.refs_6_.refs_5_), channel_id=1, source_target_pairs={{0,4},{4,0},{8,12},{12,8},{16,20},{20,16},{24,28},{28,24},{1,5},{5... | collective-permute-start | bytes 1572872 | tf_op jit(solution)/shard_map/ppermute | solution.py:54
  5.7 16.6 %collective-permute-start.7 = (bf16[3,384,256]{2,1,0:T(8,128)(2,1)S(1)}, bf16[3,384,256]{2,1,0:T(8,128)(2,1)S(1)}, u32[]{:S(2)}, u32[]{:S(2)}) collective-permute-start(bf16[3,384,256]{2,1,0:T(8,128)(2,1)S(1)} %shard_map.106.refs_4_), channel_id=1, source_target_pairs={{0,4},{4,0},{8,12},{12,8},{16,24},{20,28},{24,16},{28,20},{1,5},{5... | collective-permute-start | bytes 1769480 | tf_op jit(solution)/shard_map/ppermute | solution.py:63
  7.0 6.5 %collective-permute-start.4 = (bf16[2,128,256]{2,1,0:T(8,128)(2,1)S(1)}, bf16[2,128,256]{2,1,0:T(8,128)(2,1)S(1)}, u32[]{:S(2)}, u32[]{:S(2)}) collective-permute-start(bf16[2,128,256]{2,1,0:T(8,128)(2,1)S(1)} %get-tuple-element.55), channel_id=1, source_target_pairs={{0,8},{4,12},{8,0},{12,4},{16,20},{20,16},{24,28},{28,24},{1,9},{5... | collective-permute-start | bytes 393224 | tf_op jit(solution)/shard_map/ppermute | solution.py:63
  10.4 8.9 %collective-permute-start.5 = (bf16[4,128,256]{2,1,0:T(8,128)(2,1)S(1)}, bf16[4,128,256]{2,1,0:T(8,128)(2,1)S(1)}, u32[]{:S(2)}, u32[]{:S(2)}) collective-permute-start(bf16[4,128,256]{2,1,0:T(8,128)(2,1)S(1)} %get-tuple-element.56), channel_id=1, source_target_pairs={{0,1},{1,0},{2,3},{3,2},{4,5},{5,4},{6,7},{7,6},{8,9},{9,8},{10,11... | collective-permute-start | bytes 786440 | tf_op jit(solution)/shard_map/ppermute | solution.py:369
  11.7 12.8 %collective-permute-start.9 = (bf16[8,128,256]{2,1,0:T(8,128)(2,1)S(1)}, bf16[8,128,256]{2,1,0:T(8,128)(2,1)S(1)}, u32[]{:S(2)}, u32[]{:S(2)}) collective-permute-start(bf16[8,128,256]{2,1,0:T(8,128)(2,1)S(1)} %get-tuple-element.63), channel_id=1, source_target_pairs={{0,2},{2,0},{1,3},{3,1},{4,6},{6,4},{5,7},{7,5},{8,10},{10,8},{9,1... | collective-permute-start | bytes 1572872 | tf_op jit(solution)/shard_map/ppermute | solution.py:355
  13.2 4.2 %collective-permute-start.2 = (bf16[2,128,256]{2,1,0:T(8,128)(2,1)S(1)}, bf16[2,128,256]{2,1,0:T(8,128)(2,1)S(1)}, u32[]{:S(2)}, u32[]{:S(2)}) collective-permute-start(bf16[2,128,256]{2,1,0:T(8,128)(2,1)S(1)} %get-tuple-element.50), channel_id=1, source_target_pairs={{0,8},{4,12},{8,0},{12,4},{16,20},{20,16},{24,28},{28,24},{1,9},{5... | collective-permute-start | bytes 393224 | tf_op jit(solution)/shard_map/ppermute | solution.py:63
  13.5 7.5 %collective-permute-start.10 = (bf16[2,128,256]{2,1,0:T(8,128)(2,1)S(1)}, bf16[2,128,256]{2,1,0:T(8,128)(2,1)S(1)}, u32[]{:S(2)}, u32[]{:S(2)}) collective-permute-start(bf16[2,128,256]{2,1,0:T(8,128)(2,1)S(1)} %shard_map.112.refs_5_), channel_id=1, source_target_pairs={{0,4},{4,0},{8,16},{12,20},{16,8},{20,12},{24,28},{28,24},{1,5},{5... | collective-permute-start | bytes 393224 | tf_op jit(solution)/shard_map/ppermute | solution.py:63
  17.3 4.6 %collective-permute-start.3 = (bf16[2,128,256]{2,1,0:T(8,128)(2,1)S(1)}, bf16[2,128,256]{2,1,0:T(8,128)(2,1)S(1)}, u32[]{:S(2)}, u32[]{:S(2)}) collective-permute-start(bf16[2,128,256]{2,1,0:T(8,128)(2,1)S(1)} %shard_map.111.refs_6_), channel_id=1, source_target_pairs={{0,4},{4,0},{8,16},{12,20},{16,8},{20,12},{24,28},{28,24},{1,5},{5... | collective-permute-start | bytes 393224 | tf_op jit(solution)/shard_map/ppermute | solution.py:63
  19.3 7.2 %collective-permute-start.8 = (bf16[1,384,256]{2,1,0:T(8,128)(2,1)S(1)}, bf16[1,384,256]{2,1,0:T(8,128)(2,1)S(1)}, u32[]{:S(2)}, u32[]{:S(2)}) collective-permute-start(bf16[1,384,256]{2,1,0:T(8,128)(2,1)S(1)} %shard_map.115), channel_id=1, source_target_pairs={{0,4},{4,0},{8,12},{12,8},{16,24},{20,28},{24,16},{28,20},{1,5},{5... | collective-permute-start | bytes 589832 | tf_op jit(solution)/shard_map/ppermute | solution.py:63
  21.5 6.8 %collective-permute-start.14 = (bf16[2,128,256]{2,1,0:T(8,128)(2,1)S(1)}, bf16[2,128,256]{2,1,0:T(8,128)(2,1)S(1)}, u32[]{:S(2)}, u32[]{:S(2)}) collective-permute-start(bf16[2,128,256]{2,1,0:T(8,128)(2,1)S(1)} %get-tuple-element.72), channel_id=1, source_target_pairs={{0,4},{4,0},{8,12},{12,8},{16,24},{20,28},{24,16},{28,20},{1,5},{5... | collective-permute-start | bytes 393224 | tf_op jit(solution)/shard_map/ppermute | solution.py:63
  22.4 5.9 %collective-permute-start.13 = (bf16[2,128,256]{2,1,0:T(8,128)(2,1)S(1)}, bf16[2,128,256]{2,1,0:T(8,128)(2,1)S(1)}, u32[]{:S(2)}, u32[]{:S(2)}) collective-permute-start(bf16[2,128,256]{2,1,0:T(8,128)(2,1)S(1)} %get-tuple-element.66.refs_10_), channel_id=1, source_target_pairs={{0,4},{4,0},{8,16},{12,20},{16,8},{20,12},{24,28},{28,24},{1,5},{5... | collective-permute-start | bytes 393224 | tf_op jit(solution)/shard_map/ppermute | solution.py:63
  26.6 4.8 %collective-permute-start.11 = (bf16[2,128,256]{2,1,0:T(8,128)(2,1)S(1)}, bf16[2,128,256]{2,1,0:T(8,128)(2,1)S(1)}, u32[]{:S(2)}, u32[]{:S(2)}) collective-permute-start(bf16[2,128,256]{2,1,0:T(8,128)(2,1)S(1)} %get-tuple-element.67), channel_id=1, source_target_pairs={{0,4},{4,0},{8,16},{12,20},{16,8},{20,12},{24,28},{28,24},{1,5},{5... | collective-permute-start | bytes 393224 | tf_op jit(solution)/shard_map/ppermute | solution.py:63
  28.2 4.0 %collective-permute-start.6 = (bf16[2,128,256]{2,1,0:T(8,128)(2,1)S(1)}, bf16[2,128,256]{2,1,0:T(8,128)(2,1)S(1)}, u32[]{:S(2)}, u32[]{:S(2)}) collective-permute-start(bf16[2,128,256]{2,1,0:T(8,128)(2,1)S(1)} %get-tuple-element.57), channel_id=1, source_target_pairs={{0,4},{4,0},{8,12},{12,8},{16,24},{20,28},{24,16},{28,20},{1,5},{5... | collective-permute-start | bytes 393224 | tf_op jit(solution)/shard_map/ppermute | solution.py:63
  28.3 6.7 %collective-permute-start.16 = (bf16[2,128,256]{2,1,0:T(8,128)(2,1)S(1)}, bf16[2,128,256]{2,1,0:T(8,128)(2,1)S(1)}, u32[]{:S(2)}, u32[]{:S(2)}) collective-permute-start(bf16[2,128,256]{2,1,0:T(8,128)(2,1)S(1)} %shard_map.123.refs_10_), channel_id=1, source_target_pairs={{0,8},{4,12},{8,0},{12,4},{16,20},{20,16},{24,28},{28,24},{1,9},{5... | collective-permute-start | bytes 393224 | tf_op jit(solution)/shard_map/ppermute | solution.py:63
  31.4 6.5 %collective-permute-start.12 = (bf16[2,128,256]{2,1,0:T(8,128)(2,1)S(1)}, bf16[2,128,256]{2,1,0:T(8,128)(2,1)S(1)}, u32[]{:S(2)}, u32[]{:S(2)}) collective-permute-start(bf16[2,128,256]{2,1,0:T(8,128)(2,1)S(1)} %shard_map.120.refs_11_), channel_id=1, source_target_pairs={{0,8},{4,12},{8,0},{12,4},{16,24},{20,28},{24,16},{28,20},{1,9},{5... | collective-permute-start | bytes 393224 | tf_op jit(solution)/shard_map/ppermute | solution.py:63
  35.5 3.6 %collective-permute-start.17 = (bf16[4,128,256]{2,1,0:T(8,128)(2,1)S(1)}, bf16[4,128,256]{2,1,0:T(8,128)(2,1)S(1)}, u32[]{:S(2)}, u32[]{:S(2)}) collective-permute-start(bf16[4,128,256]{2,1,0:T(8,128)(2,1)S(1)} %get-tuple-element.81), channel_id=1, source_target_pairs={{0,4},{4,0},{8,12},{12,8},{16,20},{20,16},{24,28},{28,24},{1,5},{5... | collective-permute-start | bytes 786440 | tf_op jit(solution)/shard_map/ppermute | solution.py:54
  38.3 2.0 %collective-permute-start.15 = (bf16[4,128,256]{2,1,0:T(8,128)(2,1)S(1)}, bf16[4,128,256]{2,1,0:T(8,128)(2,1)S(1)}, u32[]{:S(2)}, u32[]{:S(2)}) collective-permute-start(bf16[4,128,256]{2,1,0:T(8,128)(2,1)S(1)} %get-tuple-element.76), channel_id=1, source_target_pairs={{0,4},{4,0},{8,12},{12,8},{16,20},{20,16},{24,28},{28,24},{1,5},{5... | collective-permute-start | bytes 786440 | tf_op jit(solution)/shard_map/ppermute | solution.py:54
